TPU v7x, 32 devices: a whole 2x2x4 slice. The times are simulated.
32 devices in a mesh: section: 16 (over z, y, core), coil: 2 (over x).
Axes of the slice: x: 2, y: 2, z: 4, core: 2. Of those that a mesh axis runs over, the one named last changes fastest.
Arguments:
- kspace: bfloat16 [16, 16, 16, 640], P('coil', None, 'section'), may hold values from -6 to 6
- coil_maps: bfloat16 [16, 16, 16, 640], P('coil', 'section'), may hold values from -1.5 to 1.5
- sampling: int32 [2, 8, 320], replicated, may hold values 0 or 1
- dc_weight: float32 [2], replicated, may hold values from 0.5 to 2.5
- kernel_in: float32 [2, 9, 18, 2], replicated, may hold values from -1.5 to 1.5
- bias_in: float32 [2, 18], replicated, may hold values from -0.5 to 0.5
- kernel_out: float32 [2, 9, 2, 18], replicated, may hold values from -0.5 to 0.5
- bias_out: float32 [2, 2], replicated, may hold values from -0.5 to 0.5
- cotangent: bfloat16 [16, 16, 640], P('section'), may hold values from -6 to 6
Outputs:
- image_out: float32 [16, 16, 640], P('section')
- grad_kspace: float32 [16, 16, 16, 640], P('coil', None, 'section')
All inputs are finite; a program needn't handle non-finite values.
Results may differ from a plain program's by a relative error of at most 0.035.
Values may be sent and summed in bfloat16 or wider, within the bound.
No kernel may reach another device: no remote copies, remote signals or barrier semaphores. Data moves between devices by JAX's collectives and lax.ppermute only.
A program may use at most 64 MiB of HBM per device.

v0:
```python
import math

import jax
import jax.numpy as jnp
from jax import lax
from jax.sharding import PartitionSpec as P

CASCADES = 2
VOLUMES = 2


PRECISE = lax.Precision.HIGHEST


def line_table(count, exponent_sign):
    indices = jnp.arange(count, dtype=jnp.int32)
    product = indices[:, None] * indices[None, :] % count
    angles = product.astype(jnp.float32) * (2.0 * math.pi / count)
    factor = 1.0 / math.sqrt(count)
    return (jnp.cos(angles) * factor, exponent_sign * jnp.sin(angles) * factor)


def line_matrix(count, exponent_sign):
    real_part, imag_part = line_table(count, exponent_sign)
    upper_rows = jnp.concatenate([real_part, imag_part], axis=1)
    lower_rows = jnp.concatenate([-imag_part, real_part], axis=1)
    return jnp.concatenate([upper_rows, lower_rows], axis=0).astype(jnp.bfloat16)


def line_transform(values, matrix):
    return jnp.dot(values.astype(jnp.bfloat16), matrix, preferred_element_type=jnp.float32)


def depth_transform(values, volumes, exponent_sign):
    layout_shape = values.shape
    width_two = layout_shape[-1]
    half_width = width_two // 2
    depth_count = layout_shape[1] // volumes
    real_part, imag_part = line_table(depth_count, exponent_sign)
    blocks = values.astype(jnp.bfloat16).reshape(
        layout_shape[0], volumes, depth_count, layout_shape[2], width_two
    )
    straight = jnp.einsum(
        "kz,cvzrw->cvkrw",
        real_part.astype(jnp.bfloat16),
        blocks,
        preferred_element_type=jnp.float32,
    )
    crossed = jnp.einsum(
        "kz,cvzrw->cvkrw",
        imag_part.astype(jnp.bfloat16),
        blocks,
        preferred_element_type=jnp.float32,
    )
    turned = jnp.concatenate([-crossed[..., half_width:], crossed[..., :half_width]], axis=-1)
    return (straight + turned).reshape(layout_shape)


def spread(coil_maps, picture):
    half_width = coil_maps.shape[-1] // 2
    maps_real = coil_maps[..., :half_width].astype(jnp.float32)
    maps_imag = coil_maps[..., half_width:].astype(jnp.float32)
    pic_real = picture[..., :half_width].astype(jnp.float32)
    pic_imag = picture[..., half_width:].astype(jnp.float32)
    return jnp.concatenate(
        [maps_real * pic_real - maps_imag * pic_imag, maps_real * pic_imag + maps_imag * pic_real],
        axis=-1,
    )


def collect(coil_maps, coil_images):
    half_width = coil_maps.shape[-1] // 2
    maps_real = coil_maps[..., :half_width].astype(jnp.float32)
    maps_imag = coil_maps[..., half_width:].astype(jnp.float32)
    img_real = coil_images[..., :half_width]
    img_imag = coil_images[..., half_width:]
    summed = jnp.concatenate(
        [maps_real * img_real + maps_imag * img_imag, maps_real * img_imag - maps_imag * img_real],
        axis=-1,
    )
    return jnp.sum(summed, axis=0)


def shifted_windows(planes):
    row_count, col_count = (planes.shape[-2], planes.shape[-1])
    padded = jnp.pad(planes, ((0, 0), (1, 1), (1, 1)))
    return jnp.stack(
        [
            padded[:, row_shift : row_shift + row_count, col_shift : col_shift + col_count]
            for row_shift in range(3)
            for col_shift in range(3)
        ],
        axis=0,
    )


def conv_out(hidden, kernel, bias):
    row_count, col_count = (hidden.shape[-2], hidden.shape[-1])
    projected = jnp.einsum("toc,cxy->toxy", kernel, hidden, precision=PRECISE)
    padded = jnp.pad(projected, ((0, 0), (0, 0), (1, 1), (1, 1)))
    summed = jnp.zeros((kernel.shape[1], row_count, col_count), jnp.float32) + bias[:, None, None]
    for tap_index in range(9):
        row_shift = tap_index // 3
        col_shift = tap_index % 3
        summed = (
            summed
            + padded[
                tap_index, :, row_shift : row_shift + row_count, col_shift : col_shift + col_count
            ]
        )
    return summed


def refine(picture, kernel_in, bias_in, kernel_out, bias_out):
    half_width = picture.shape[-1] // 2
    planes = jnp.stack([picture[:, :half_width], picture[:, half_width:]], axis=0)
    hidden = (
        jnp.einsum("toc,tcxy->oxy", kernel_in, shifted_windows(planes), precision=PRECISE)
        + bias_in[:, None, None]
    )
    hidden = jax.nn.silu(hidden)
    output = conv_out(hidden, kernel_out, bias_out)
    return jnp.concatenate([output[0], output[1]], axis=1)


def body(
    kspace, coil_maps, sampling, dc_weight, kernel_in, bias_in, kernel_out, bias_out, cotangent
):
    width_two = kspace.shape[-1]
    slot_count = kspace.shape[1]
    lines_used = sampling.astype(jnp.float32).reshape(slot_count, width_two // 2)
    sampled = jnp.concatenate([lines_used, lines_used], axis=1)[None, :, None, :]
    measured = sampled * kspace.astype(jnp.float32)
    forward_line = line_matrix(width_two // 2, -1.0)
    inverse_line = line_matrix(width_two // 2, 1.0)
    maps_rows = lax.all_to_all(coil_maps, "section", split_axis=2, concat_axis=1, tiled=True)

    def expand(picture):
        moved = lax.all_to_all(picture, "section", split_axis=1, concat_axis=0, tiled=True)
        spreaded = spread(maps_rows, moved[None])
        return depth_transform(line_transform(spreaded, forward_line), VOLUMES, -1.0)

    def combine(kstate, is_final):
        coil_images = line_transform(depth_transform(kstate, VOLUMES, 1.0), inverse_line)
        partial_sum = collect(maps_rows, coil_images)
        summed = lax.psum(partial_sum.astype(jnp.bfloat16), "coil").astype(jnp.float32)
        if is_final:
            return lax.all_to_all(
                summed.astype(jnp.bfloat16), "section", split_axis=0, concat_axis=1, tiled=True
            ).astype(summed.dtype)
        return lax.all_to_all(
            summed.astype(jnp.bfloat16), "section", split_axis=0, concat_axis=1, tiled=True
        )

    kstate = measured
    stored = []
    for cascade in range(CASCADES):
        picture = combine(kstate, False)[0].astype(jnp.float32)
        stored.append(picture)
        model = refine(
            picture, kernel_in[cascade], bias_in[cascade], kernel_out[cascade], bias_out[cascade]
        )
        update = expand(model.astype(jnp.bfloat16)[None])
        kstate = kstate - dc_weight[cascade] * sampled * (kstate - measured) + update
    image_out = combine(kstate, True)
    adjoint = expand(cotangent)
    grad_measured = jnp.zeros(measured.shape, jnp.float32)
    for cascade in reversed(range(CASCADES)):
        weighted = dc_weight[cascade] * sampled
        grad_measured = grad_measured + weighted * adjoint
        model_bar = combine(adjoint, False)[0].astype(jnp.float32)
        adjoint = adjoint - weighted * adjoint

        def local_model(flat, index=cascade):
            return refine(
                flat, kernel_in[index], bias_in[index], kernel_out[index], bias_out[index]
            )

        unused, pull_back = jax.vjp(local_model, stored[cascade])
        picture_bar = pull_back(model_bar)[0]
        adjoint = adjoint + expand(picture_bar.astype(jnp.bfloat16)[None])
    grad_measured = grad_measured + adjoint
    return (image_out, sampled * grad_measured)


def solution(mesh):
    return jax.shard_map(
        body,
        mesh=mesh,
        in_specs=(
            P("coil", None, "section", None),
            P("coil", "section", None, None),
            P(),
            P(),
            P(),
            P(),
            P(),
            P(),
            P("section", None, None),
        ),
        out_specs=(P("section", None, None), P("coil", None, "section", None)),
        check_vma=False,
    )
```

profile of v0, /device:TPU:0, one launch (start us, length us, event | category | flops | bytes accessed | tf_op | source)
XLA Modules:
  0.0 184.6 jit_solution(4112808005718965084)
XLA Ops:
  0.7 1.6 copy.176
  2.3 7.4 %all-to-all-start = ((bf16[8,1,16,640]{3,0,1,2:T(8,128)(2,1)}), bf16[8,1,16,640]{3,0,1,2:T(8,128)(2,1)S(1)}, u32[]{:S(2)}, u32[]{:S(2)}) async-start(bf16[8,1,16,640]{3,0,1,2:T(8,128)(2,1)} %copy.176), calls=%async_computation | async-start | bytes 327680 | tf_op jit(solution)/shard_map/all_to_all | solution.py:136
  9.7 2.2 %negate_convert_fusion = (bf16[320,320]{1,0:T(8,128)(2,1)S(1)}, bf16[320,320]{1,0:T(8,128)(2,1)S(1)}) fusion(), kind=kLoop, calls=%fused_computation.156 | loop fusion | flops 1433600 | bytes 409600 | tf_op jit(solution)/shard_map/convert.37
  11.9 2.0 %negate_convert_fusion.1 = (bf16[320,320]{1,0:T(8,128)(2,1)S(1)}, bf16[320,320]{1,0:T(8,128)(2,1)S(1)}) fusion(), kind=kLoop, calls=%fused_computation.157 | loop fusion | flops 1331200 | bytes 409600 | tf_op jit(solution)/shard_map/convert.51
  21.3 6.0 %all-to-all-start.6 = ((bf16[16,2,320]{2,1,0:T(2,128)(2,1)}), bf16[16,2,320]{2,1,0:T(2,128)(2,1)S(1)}, u32[]{:S(2)}, u32[]{:S(2)}) async-start(bf16[16,2,320]{2,1,0:T(2,128)(2,1)} %reshape.608), calls=%async_computation.6 | async-start | bytes 49152 | tf_op jit(solution)/shard_map/all_to_all | solution.py:139
  27.6 8.3 %psum.35 = bf16[16,1,640]{2,0,1:T(8,128)(2,1)S(1)} all-reduce(bf16[16,1,640]{2,0,1:T(8,128)(2,1)S(1)} %bitcast.768), channel_id=1, replica_groups=mesh['section'=16,'coil'=2] {'coil'}, use_global_device_ids=true, to_apply=%region_1.2 | all-reduce | flops 10240 | bytes 40960 | tf_op jit(solution)/shard_map/psum | solution.py:146
  37.1 6.0 %all-to-all-start.1 = ((bf16[16,2,320]{2,1,0:T(2,128)(2,1)}), bf16[16,2,320]{2,1,0:T(2,128)(2,1)S(1)}, u32[]{:S(2)}, u32[]{:S(2)}) async-start(bf16[16,2,320]{2,1,0:T(2,128)(2,1)} %reshape.598), calls=%async_computation.1 | async-start | bytes 49152 | tf_op jit(solution)/shard_map/all_to_all | solution.py:151
  43.2 2.0 %fusion.63 = bf16[320,320]{1,0:T(8,128)(2,1)S(1)} fusion(), kind=kLoop, calls=%fused_computation.167 | loop fusion | flops 1126400 | bytes 204800 | tf_op jit(solution)/shard_map/convert.40
  45.3 4.5 %all-to-all-done.1 = bf16[16,2,320]{2,1,0:T(2,128)(2,1)S(1)} async-done(((bf16[16,2,320]{2,1,0:T(2,128)(2,1)}), bf16[16,2,320]{2,1,0:T(2,128)(2,1)S(1)}, u32[]{:S(2)}, u32[]{:S(2)}) %all-to-all-start.1) | async-done | bytes 20512 | tf_op jit(solution)/shard_map/all_to_all | solution.py:151
  55.6 3.7 %all-to-all-start.2 = ((bf16[16,2,320]{2,1,0:T(2,128)(2,1)}), bf16[16,2,320]{2,1,0:T(2,128)(2,1)S(1)}, u32[]{:S(2)}, u32[]{:S(2)}) async-start(bf16[16,2,320]{2,1,0:T(2,128)(2,1)} %reshape.600), calls=%async_computation.2 | async-start | bytes 49152 | tf_op jit(solution)/shard_map/all_to_all | solution.py:139
  59.3 6.3 %all-to-all-done.2 = bf16[16,2,320]{2,1,0:T(2,128)(2,1)S(1)} async-done(((bf16[16,2,320]{2,1,0:T(2,128)(2,1)}), bf16[16,2,320]{2,1,0:T(2,128)(2,1)S(1)}, u32[]{:S(2)}, u32[]{:S(2)}) %all-to-all-start.2) | async-done | bytes 20512 | tf_op jit(solution)/shard_map/all_to_all | solution.py:139
  72.1 1.6 convolution_bitcast_fusion.11
  74.2 7.6 %all-reduce.49 = (bf16[16,1,640]{2,0,1:T(8,128)(2,1)S(1)}, bf16[16,1,640]{2,0,1:T(8,128)(2,1)S(1)}) all-reduce(bf16[16,1,640]{2,0,1:T(8,128)(2,1)S(1)} %bitcast.764, bf16[16,1,640]{2,0,1:T(8,128)(2,1)S(1)} %bitcast.766), channel_id=1, replica_groups=mesh['section'=16,'coil'=2] {'coil'}, use_global_device_ids=true, to_apply=%region_3.4 | all-reduce | flops 20480 | bytes 81920 | tf_op jit(solution)/shard_map/psum | solution.py:146
  83.0 3.5 %all-to-all-start.3 = ((bf16[16,2,320]{2,1,0:T(2,128)(2,1)}), bf16[16,2,320]{2,1,0:T(2,128)(2,1)S(1)}, u32[]{:S(2)}, u32[]{:S(2)}) async-start(bf16[16,2,320]{2,1,0:T(2,128)(2,1)} %reshape.602), calls=%async_computation.3 | async-start | bytes 49152 | tf_op jit(solution)/shard_map/all_to_all | solution.py:151
  88.6 4.5 %all-to-all-done.3 = bf16[16,2,320]{2,1,0:T(2,128)(2,1)S(1)} async-done(((bf16[16,2,320]{2,1,0:T(2,128)(2,1)}), bf16[16,2,320]{2,1,0:T(2,128)(2,1)S(1)}, u32[]{:S(2)}, u32[]{:S(2)}) %all-to-all-start.3) | async-done | bytes 20512 | tf_op jit(solution)/shard_map/all_to_all | solution.py:151
  93.1 3.5 %all-to-all-start.7 = ((bf16[16,2,320]{2,1,0:T(2,128)(2,1)}), bf16[16,2,320]{2,1,0:T(2,128)(2,1)S(1)}, u32[]{:S(2)}, u32[]{:S(2)}) async-start(bf16[16,2,320]{2,1,0:T(2,128)(2,1)} %reshape.610), calls=%async_computation.7 | async-start | bytes 49152 | tf_op jit(solution)/shard_map/all_to_all | solution.py:151
  101.2 1.9 %all-to-all-done.7 = bf16[16,2,320]{2,1,0:T(2,128)(2,1)S(1)} async-done(((bf16[16,2,320]{2,1,0:T(2,128)(2,1)}), bf16[16,2,320]{2,1,0:T(2,128)(2,1)S(1)}, u32[]{:S(2)}, u32[]{:S(2)}) %all-to-all-start.7) | async-done | bytes 20512 | tf_op jit(solution)/shard_map/all_to_all | solution.py:151
  103.8 1.6 convolution_bitcast_fusion.5
  109.2 4.1 %all-to-all-start.8 = ((bf16[16,2,320]{2,1,0:T(2,128)(2,1)}), bf16[16,2,320]{2,1,0:T(2,128)(2,1)S(1)}, u32[]{:S(2)}, u32[]{:S(2)}) async-start(bf16[16,2,320]{2,1,0:T(2,128)(2,1)} %reshape.612), calls=%async_computation.8 | async-start | bytes 49152 | tf_op jit(solution)/shard_map/all_to_all | solution.py:139
  115.3 4.6 %all-to-all-done.8 = bf16[16,2,320]{2,1,0:T(2,128)(2,1)S(1)} async-done(((bf16[16,2,320]{2,1,0:T(2,128)(2,1)}), bf16[16,2,320]{2,1,0:T(2,128)(2,1)S(1)}, u32[]{:S(2)}, u32[]{:S(2)}) %all-to-all-start.8) | async-done | bytes 20512 | tf_op jit(solution)/shard_map/all_to_all | solution.py:139
  119.9 3.7 %all-to-all-start.4 = ((bf16[16,2,320]{2,1,0:T(2,128)(2,1)}), bf16[16,2,320]{2,1,0:T(2,128)(2,1)S(1)}, u32[]{:S(2)}, u32[]{:S(2)}) async-start(bf16[16,2,320]{2,1,0:T(2,128)(2,1)} %reshape.604), calls=%async_computation.4 | async-start | bytes 49152 | tf_op jit(solution)/shard_map/all_to_all | solution.py:139
  123.8 6.1 %all-to-all-done.4 = bf16[16,2,320]{2,1,0:T(2,128)(2,1)S(1)} async-done(((bf16[16,2,320]{2,1,0:T(2,128)(2,1)}), bf16[16,2,320]{2,1,0:T(2,128)(2,1)S(1)}, u32[]{:S(2)}, u32[]{:S(2)}) %all-to-all-start.4) | async-done | bytes 20512 | tf_op jit(solution)/shard_map/all_to_all | solution.py:139
  135.2 1.7 convolution_bitcast_fusion.8
  136.9 1.7 convolution_bitcast_fusion.10
  139.1 8.5 %all-reduce.48 = (bf16[16,1,640]{2,0,1:T(8,128)(2,1)S(1)}, bf16[16,1,640]{2,0,1:T(8,128)(2,1)S(1)}) all-reduce(bf16[16,1,640]{2,0,1:T(8,128)(2,1)S(1)} %bitcast.765, bf16[16,1,640]{2,0,1:T(8,128)(2,1)S(1)} %bitcast.767), channel_id=1, replica_groups=mesh['section'=16,'coil'=2] {'coil'}, use_global_device_ids=true, to_apply=%region_5.6 | all-reduce | flops 20480 | bytes 81920 | tf_op jit(solution)/shard_map/psum | solution.py:146
  148.9 3.5 %all-to-all-start.9 = ((bf16[16,2,320]{2,1,0:T(2,128)(2,1)}), bf16[16,2,320]{2,1,0:T(2,128)(2,1)S(1)}, u32[]{:S(2)}, u32[]{:S(2)}) async-start(bf16[16,2,320]{2,1,0:T(2,128)(2,1)} %reshape.614), calls=%async_computation.9 | async-start | bytes 49152 | tf_op jit(solution)/shard_map/all_to_all | solution.py:151
  153.7 5.3 %all-to-all-done.9 = bf16[16,2,320]{2,1,0:T(2,128)(2,1)S(1)} async-done(((bf16[16,2,320]{2,1,0:T(2,128)(2,1)}), bf16[16,2,320]{2,1,0:T(2,128)(2,1)S(1)}, u32[]{:S(2)}, u32[]{:S(2)}) %all-to-all-start.9) | async-done | bytes 20512 | tf_op jit(solution)/shard_map/all_to_all | solution.py:151
  158.9 3.5 %all-to-all-start.5 = ((bf16[16,2,320]{2,1,0:T(2,128)(2,1)}), bf16[16,2,320]{2,1,0:T(2,128)(2,1)S(1)}, u32[]{:S(2)}, u32[]{:S(2)}) async-start(bf16[16,2,320]{2,1,0:T(2,128)(2,1)} %reshape.606), calls=%async_computation.5 | async-start | bytes 49152 | tf_op jit(solution)/shard_map/all_to_all | solution.py:148
  163.2 1.6 convolution_bitcast_fusion.4
  168.9 5.6 %all-to-all-start.10 = ((bf16[16,2,320]{2,1,0:T(2,128)(2,1)}), bf16[16,2,320]{2,1,0:T(2,128)(2,1)S(1)}, u32[]{:S(2)}, u32[]{:S(2)}) async-start(bf16[16,2,320]{2,1,0:T(2,128)(2,1)} %reshape.616), calls=%async_computation.10 | async-start | bytes 49152 | tf_op jit(solution)/shard_map/all_to_all | solution.py:139
  175.3 5.8 %all-to-all-done.10 = bf16[16,2,320]{2,1,0:T(2,128)(2,1)S(1)} async-done(((bf16[16,2,320]{2,1,0:T(2,128)(2,1)}), bf16[16,2,320]{2,1,0:T(2,128)(2,1)S(1)}, u32[]{:S(2)}, u32[]{:S(2)}) %all-to-all-start.10) | async-done | bytes 20512 | tf_op jit(solution)/shard_map/all_to_all | solution.py:139
  182.9 1.6 fusion.86
  (259 shorter events, 51.2 us)
Async XLA Ops:
  0.6 13.3 %copy-start.28 = (f32[2]{0:T(128)S(1)}, f32[2]{0:T(128)}, u32[]{:S(2)}) copy-start(f32[2]{0:T(128)} %param.12) | copy-start | bytes 28
  0.6 14.0 %copy-start.19 = (s32[2,8,320]{2,1,0:T(8,128)S(1)}, s32[2,8,320]{2,1,0:T(8,128)}, u32[]{:S(2)}) copy-start(s32[2,8,320]{2,1,0:T(8,128)} %param.11) | copy-start | bytes 61444
  0.7 15.4 %copy-start = (bf16[8,16,1,640]{3,1,2,0:T(8,128)(2,1)S(1)}, bf16[8,16,1,640]{3,1,2,0:T(8,128)(2,1)}, u32[]{:S(2)}) copy-start(bf16[8,16,1,640]{3,1,2,0:T(8,128)(2,1)} %param.9) | copy-start | bytes 491524
  2.3 18.9 %all-to-all-start = ((bf16[8,1,16,640]{3,0,1,2:T(8,128)(2,1)}), bf16[8,1,16,640]{3,0,1,2:T(8,128)(2,1)S(1)}, u32[]{:S(2)}, u32[]{:S(2)}) async-start(bf16[8,1,16,640]{3,0,1,2:T(8,128)(2,1)} %copy.176), calls=%async_computation | async-start | bytes 327680 | tf_op jit(solution)/shard_map/all_to_all | solution.py:136
  11.9 56.1 %copy-start.5 = (bf16[320,320]{1,0:T(8,128)(2,1)}, bf16[320,320]{1,0:T(8,128)(2,1)S(1)}, u32[]{:S(2)}) copy-start(bf16[320,320]{1,0:T(8,128)(2,1)S(1)} %get-tuple-element.141) | copy-start | bytes 614404
  11.9 60.2 %copy-start.8 = (bf16[320,320]{1,0:T(8,128)(2,1)}, bf16[320,320]{1,0:T(8,128)(2,1)S(1)}, u32[]{:S(2)}) copy-start(bf16[320,320]{1,0:T(8,128)(2,1)S(1)} %get-tuple-element.142) | copy-start | bytes 614404
  13.9 58.2 %copy-start.15 = (bf16[320,320]{1,0:T(8,128)(2,1)}, bf16[320,320]{1,0:T(8,128)(2,1)S(1)}, u32[]{:S(2)}) copy-start(bf16[320,320]{1,0:T(8,128)(2,1)S(1)} %get-tuple-element.139) | copy-start | bytes 614404
  13.9 58.2 %copy-start.17 = (bf16[320,320]{1,0:T(8,128)(2,1)}, bf16[320,320]{1,0:T(8,128)(2,1)S(1)}, u32[]{:S(2)}) copy-start(bf16[320,320]{1,0:T(8,128)(2,1)S(1)} %get-tuple-element.140) | copy-start | bytes 614404
  16.1 52.9 %copy-start.3 = (f32[16,640]{1,0:T(8,128)}, f32[16,640]{1,0:T(8,128)S(1)}, u32[]{:S(2)}) copy-start(f32[16,640]{1,0:T(8,128)S(1)} %get-tuple-element.113) | copy-start | bytes 122884
  16.1 117.5 %copy-start.1 = (f32[16,640]{1,0:T(8,128)}, f32[16,640]{1,0:T(8,128)S(1)}, u32[]{:S(2)}) copy-start(f32[16,640]{1,0:T(8,128)S(1)} %get-tuple-element.112) | copy-start | bytes 122884
  18.0 2.7 %copy-start.22 = (f32[2,9,2,18]{3,2,1,0:T(2,128)S(1)}, f32[2,9,2,18]{3,2,1,0:T(2,128)}, u32[]{:S(2)}) copy-start(f32[2,9,2,18]{3,2,1,0:T(2,128)} %param.15) | copy-start | bytes 7780
  21.2 31.2 %copy-start.23 = (f32[1,9,2,18]{3,2,1,0:T(2,128)}, f32[1,9,2,18]{3,2,1,0:T(2,128)S(1)}, u32[]{:S(2)}) copy-start(f32[1,9,2,18]{3,2,1,0:T(2,128)S(1)} %get-tuple-element.130) | copy-start | bytes 3892
  21.3 15.9 %all-to-all-start.6 = ((bf16[16,2,320]{2,1,0:T(2,128)(2,1)}), bf16[16,2,320]{2,1,0:T(2,128)(2,1)S(1)}, u32[]{:S(2)}, u32[]{:S(2)}) async-start(bf16[16,2,320]{2,1,0:T(2,128)(2,1)} %reshape.608), calls=%async_computation.6 | async-start | bytes 49152 | tf_op jit(solution)/shard_map/all_to_all | solution.py:139
  37.1 12.6 %all-to-all-start.1 = ((bf16[16,2,320]{2,1,0:T(2,128)(2,1)}), bf16[16,2,320]{2,1,0:T(2,128)(2,1)S(1)}, u32[]{:S(2)}, u32[]{:S(2)}) async-start(bf16[16,2,320]{2,1,0:T(2,128)(2,1)} %reshape.598), calls=%async_computation.1 | async-start | bytes 49152 | tf_op jit(solution)/shard_map/all_to_all | solution.py:151
  45.1 22.9 %copy-start.12 = (bf16[320,320]{1,0:T(8,128)(2,1)}, bf16[320,320]{1,0:T(8,128)(2,1)S(1)}, u32[]{:S(2)}) copy-start(bf16[320,320]{1,0:T(8,128)(2,1)S(1)} %fusion.63) | copy-start | bytes 614404
  55.6 10.0 %all-to-all-start.2 = ((bf16[16,2,320]{2,1,0:T(2,128)(2,1)}), bf16[16,2,320]{2,1,0:T(2,128)(2,1)S(1)}, u32[]{:S(2)}, u32[]{:S(2)}) async-start(bf16[16,2,320]{2,1,0:T(2,128)(2,1)} %reshape.600), calls=%async_computation.2 | async-start | bytes 49152 | tf_op jit(solution)/shard_map/all_to_all | solution.py:139
  83.0 10.0 %all-to-all-start.3 = ((bf16[16,2,320]{2,1,0:T(2,128)(2,1)}), bf16[16,2,320]{2,1,0:T(2,128)(2,1)S(1)}, u32[]{:S(2)}, u32[]{:S(2)}) async-start(bf16[16,2,320]{2,1,0:T(2,128)(2,1)} %reshape.602), calls=%async_computation.3 | async-start | bytes 49152 | tf_op jit(solution)/shard_map/all_to_all | solution.py:151
  93.1 10.0 %all-to-all-start.7 = ((bf16[16,2,320]{2,1,0:T(2,128)(2,1)}), bf16[16,2,320]{2,1,0:T(2,128)(2,1)S(1)}, u32[]{:S(2)}, u32[]{:S(2)}) async-start(bf16[16,2,320]{2,1,0:T(2,128)(2,1)} %reshape.610), calls=%async_computation.7 | async-start | bytes 49152 | tf_op jit(solution)/shard_map/all_to_all | solution.py:151
  101.2 2.7 %copy-start.26 = (f32[1,9,2,18]{3,2,1,0:T(2,128)S(1)}, f32[1,9,2,18]{3,2,1,0:T(2,128)}, u32[]{:S(2)}) copy-start(f32[1,9,2,18]{3,2,1,0:T(2,128)} %get-tuple-element.129) | copy-start | bytes 3892
  106.9 6.5 %copy-start.27 = (f32[2]{0:T(128)S(1)}, f32[2]{0:T(128)}, u32[]{:S(2)}) copy-start(f32[2]{0:T(128)} %get-tuple-element.133) | copy-start | bytes 28
  109.2 10.7 %all-to-all-start.8 = ((bf16[16,2,320]{2,1,0:T(2,128)(2,1)}), bf16[16,2,320]{2,1,0:T(2,128)(2,1)S(1)}, u32[]{:S(2)}, u32[]{:S(2)}) async-start(bf16[16,2,320]{2,1,0:T(2,128)(2,1)} %reshape.612), calls=%async_computation.8 | async-start | bytes 49152 | tf_op jit(solution)/shard_map/all_to_all | solution.py:139
  113.4 17.0 %copy-start.6 = (bf16[320,320]{1,0:T(8,128)(2,1)S(1)}, bf16[320,320]{1,0:T(8,128)(2,1)}, u32[]{:S(2)}) copy-start(bf16[320,320]{1,0:T(8,128)(2,1)} %copy-done.5) | copy-start | bytes 614404
  113.4 17.0 %copy-start.9 = (bf16[320,320]{1,0:T(8,128)(2,1)S(1)}, bf16[320,320]{1,0:T(8,128)(2,1)}, u32[]{:S(2)}) copy-start(bf16[320,320]{1,0:T(8,128)(2,1)} %copy-done.8) | copy-start | bytes 614404
  113.4 17.0 %copy-start.13 = (bf16[320,320]{1,0:T(8,128)(2,1)S(1)}, bf16[320,320]{1,0:T(8,128)(2,1)}, u32[]{:S(2)}) copy-start(bf16[320,320]{1,0:T(8,128)(2,1)} %copy-done.12) | copy-start | bytes 614404
  119.9 10.0 %all-to-all-start.4 = ((bf16[16,2,320]{2,1,0:T(2,128)(2,1)}), bf16[16,2,320]{2,1,0:T(2,128)(2,1)S(1)}, u32[]{:S(2)}, u32[]{:S(2)}) async-start(bf16[16,2,320]{2,1,0:T(2,128)(2,1)} %reshape.604), calls=%async_computation.4 | async-start | bytes 49152 | tf_op jit(solution)/shard_map/all_to_all | solution.py:139
  147.6 15.6 %copy-start.24 = (f32[1,9,2,18]{3,2,1,0:T(2,128)S(1)}, f32[1,9,2,18]{3,2,1,0:T(2,128)}, u32[]{:S(2)}) copy-start(f32[1,9,2,18]{3,2,1,0:T(2,128)} %copy-done.23) | copy-start | bytes 3892
  148.9 10.0 %all-to-all-start.9 = ((bf16[16,2,320]{2,1,0:T(2,128)(2,1)}), bf16[16,2,320]{2,1,0:T(2,128)(2,1)S(1)}, u32[]{:S(2)}, u32[]{:S(2)}) async-start(bf16[16,2,320]{2,1,0:T(2,128)(2,1)} %reshape.614), calls=%async_computation.9 | async-start | bytes 49152 | tf_op jit(solution)/shard_map/all_to_all | solution.py:151
  158.9 10.0 %all-to-all-start.5 = ((bf16[16,2,320]{2,1,0:T(2,128)(2,1)}), bf16[16,2,320]{2,1,0:T(2,128)(2,1)S(1)}, u32[]{:S(2)}, u32[]{:S(2)}) async-start(bf16[16,2,320]{2,1,0:T(2,128)(2,1)} %reshape.606), calls=%async_computation.5 | async-start | bytes 49152 | tf_op jit(solution)/shard_map/all_to_all | solution.py:148
  166.5 15.0 %copy-start.7 = (bf16[320,320]{1,0:T(8,128)(2,1)S(1)}, bf16[320,320]{1,0:T(8,128)(2,1)}, u32[]{:S(2)}) copy-start(bf16[320,320]{1,0:T(8,128)(2,1)} %copy-done.5) | copy-start | bytes 614404
  166.5 15.0 %copy-start.11 = (bf16[320,320]{1,0:T(8,128)(2,1)S(1)}, bf16[320,320]{1,0:T(8,128)(2,1)}, u32[]{:S(2)}) copy-start(bf16[320,320]{1,0:T(8,128)(2,1)} %copy-done.8) | copy-start | bytes 614404
  166.5 15.0 %copy-start.14 = (bf16[320,320]{1,0:T(8,128)(2,1)S(1)}, bf16[320,320]{1,0:T(8,128)(2,1)}, u32[]{:S(2)}) copy-start(bf16[320,320]{1,0:T(8,128)(2,1)} %copy-done.12) | copy-start | bytes 614404
  168.9 12.2 %all-to-all-start.10 = ((bf16[16,2,320]{2,1,0:T(2,128)(2,1)}), bf16[16,2,320]{2,1,0:T(2,128)(2,1)S(1)}, u32[]{:S(2)}, u32[]{:S(2)}) async-start(bf16[16,2,320]{2,1,0:T(2,128)(2,1)} %reshape.616), calls=%async_computation.10 | async-start | bytes 49152 | tf_op jit(solution)/shard_map/all_to_all | solution.py:139
  (10 other events, 10.9 us)
where the time goes:
time: 186 us; the launch traced here: 185 us
  starting transfers between devices  50.5 us (27%)
  waiting for transfers between devices  39.2 us (21%)
  other arithmetic  26.5 us (14%)
  blocking collectives  24.4 us (13%)
  matrix products  21.7 us (12%)
  local copies, waits for them, and re-layouts  20.2 us (11%)
  between operations  2.13 us (1%)
    psum x3, blocking collectives, combine(): lax.psum(partial_sum.astype(jnp.bfloat16), 'coil').astype(jnp.float32)  24.4 us
    all_to_all x5, starting transfers between devices, expand(): lax.all_to_all(picture, 'section', split_axis=1, concat_axis=0, tiled=True)  23.1 us
    all_to_all x5, waiting for transfers between devices, expand(): lax.all_to_all(picture, 'section', split_axis=1, concat_axis=0, tiled=True)  22.8 us
    all_to_all x5, starting transfers between devices, combine(): lax.all_to_all(summed.astype(jnp.bfloat16), 'section', split_axis=0, conc...  20 us
    all_to_all x5, waiting for transfers between devices, combine(): lax.all_to_all(summed.astype(jnp.bfloat16), 'section', split_axis=0, conc...  16.4 us
    unnamed x115, local copies, waits for them, and re-layouts  12.3 us
    dot_general x10, matrix products, line_transform(): jnp.dot(values.astype(jnp.bfloat16), matrix, preferred_element_type=jnp.f...  9.03 us
    all_to_all x1, starting transfers between devices, body(): lax.all_to_all(coil_maps, 'section', split_axis=2, concat_axis=1, tiled=T...  7.39 us
  transfers between devices with their start and end apart: 11, of which 9 were waited for; matrix products, arithmetic and copies ran while one was open for 17% of the time, Pallas kernels for 0%

commit v1 on v0

v1 whole, which is shorter than its diff:
```python
import functools
import math

import jax
import jax.numpy as jnp
import ml_dtypes
import numpy as np
from jax import lax
from jax.experimental import pallas as pl
from jax.experimental.pallas import tpu as pltpu
from jax.sharding import PartitionSpec as P

CASCADES = 2
VOLUMES = 2
LANES = 128
VMEM_BYTES = 48 * 1024 * 1024

F32 = jnp.float32
BF16 = jnp.bfloat16


def padded(size, unit):
    return -(-size // unit) * unit


def dft_parts(count):
    indices = np.arange(count)
    angles = (indices[:, None] * indices[None, :] % count) * (2.0 * math.pi / count)
    factor = 1.0 / math.sqrt(count)
    return np.cos(angles) * factor, np.sin(angles) * factor


def line_constant(lines):
    width = padded(lines, LANES)
    cosine, sine = dft_parts(lines)
    table = np.zeros((width, 2 * width), np.float32)
    table[:lines, :lines] = cosine
    table[:lines, width : width + lines] = sine
    return table.astype(ml_dtypes.bfloat16)


def depth_constant(coils, slots, volumes, sign):
    cosine, sine = dft_parts(slots // volumes)
    spread_over = np.eye(coils * volumes)
    real, imag = np.kron(spread_over, cosine), sign * np.kron(spread_over, sine)
    return np.block([[real, -imag], [imag, real]]).astype(np.float32).astype(ml_dtypes.bfloat16)


def conv_constants(rows, channels):
    groups = 6
    width = padded(groups * rows, LANES)
    repeat = np.kron(np.eye(channels), np.ones((rows, 1))).astype(np.float32)
    taps = CASCADES * 3
    place = np.zeros((padded(2 * taps * groups + CASCADES, LANES), 2 * taps * width), np.float32)
    for kind in range(2):
        for tap in range(taps):
            for group in range(groups):
                start = (kind * taps + tap) * width + group * rows
                place[(kind * taps + tap) * groups + group, start : start + rows] = 1.0
    offset = np.full((channels * rows, width), -9.0, np.float32)
    row = np.arange(rows)
    offset[:, : groups * rows] = np.tile(row[None, :] - row[:, None] + 1.0, (channels, groups))
    offset = np.clip(offset, -9.0, 9.0)
    return repeat, place.astype(ml_dtypes.bfloat16), offset


def lane_index(shape):
    return lax.broadcasted_iota(jnp.int32, shape, len(shape) - 1)


def split_complex(chunks, lines):
    whole, rest = divmod(lines, LANES)
    count = padded(lines, LANES) // LANES
    if rest == 0:
        return jnp.concatenate(chunks[:count], 1), jnp.concatenate(chunks[count:], 1)
    lane = lane_index(chunks[0].shape)
    real = chunks[:whole] + [jnp.where(lane < rest, chunks[whole], 0.0)]
    turned = [pltpu.roll(chunk, LANES - rest, 1) for chunk in chunks[whole:]]
    turned.append(jnp.zeros_like(turned[0]))
    imag = [jnp.where(lane < LANES - rest, turned[k], turned[k + 1]) for k in range(count)]
    imag[-1] = jnp.where(lane < rest, imag[-1], 0.0)
    return jnp.concatenate(real, 1), jnp.concatenate(imag, 1)


def lane_chunks(value):
    return [value[:, start : start + LANES] for start in range(0, value.shape[1], LANES)]


def join_complex(real, imag, lines):
    whole, rest = divmod(lines, LANES)
    real, imag = lane_chunks(real), lane_chunks(imag)
    if rest == 0:
        return real + imag
    lane = lane_index(real[0].shape)
    turned = [real[whole]] + [pltpu.roll(chunk, rest, 1) for chunk in imag]
    mixed = [jnp.where(lane < rest, turned[k], turned[k + 1]) for k in range(len(imag))]
    return (real[:whole] + mixed)[: 2 * lines // LANES]


def halves(stacked):
    half = stacked.shape[0] // 2
    return stacked[:half], stacked[half:]


def line_apply(stacked, table_ref, sign):
    mixed = jnp.dot(stacked.astype(BF16), table_ref[...], preferred_element_type=F32)
    width = table_ref.shape[1] // 2
    top, bottom = halves(mixed)
    return jnp.concatenate(
        [
            top[:, :width] - sign * bottom[:, width:],
            bottom[:, :width] + sign * top[:, width:],
        ],
        axis=0,
    )


def depth_apply(stacked, depth_ref):
    return jnp.dot(depth_ref[...], stacked.astype(BF16), preferred_element_type=F32)


def over_coils(value, coils):
    return jnp.concatenate([value] * coils, axis=0)


def coil_sum(value, coils):
    slots = value.shape[0] // coils
    total = value[:slots]
    for coil in range(1, coils):
        total = total + value[coil * slots : (coil + 1) * slots]
    return total


def spread(maps_real, maps_imag, real, imag, coils):
    real, imag = over_coils(real, coils), over_coils(imag, coils)
    return jnp.concatenate(
        [maps_real * real - maps_imag * imag, maps_real * imag + maps_imag * real], axis=0
    )


def collect(maps_real, maps_imag, images, coils):
    real, imag = halves(images)
    return (
        coil_sum(maps_real * real + maps_imag * imag, coils),
        coil_sum(maps_real * imag - maps_imag * real, coils),
    )


def masked_normal(images, table_ref, minus_ref, plus_ref, mask):
    spectrum = depth_apply(line_apply(images, table_ref, -1.0), minus_ref)
    return line_apply(depth_apply(spectrum * mask, plus_ref), table_ref, 1.0)


def write_rows(scratch, pitch, values, first=0):
    for index, value in enumerate(values):
        scratch[pl.ds(first + index, value.shape[0], stride=pitch), :] = value


def read_rows(scratch, pitch, first, count, rows):
    return [scratch[pl.ds(first + index, rows, stride=pitch), :] for index in range(count)]


def shifted(value, step):
    if step == 0:
        return value
    width = value.shape[1]
    return pltpu.roll(value, (-step) % width, 1)


def stack_shifted(value, order):
    return jnp.concatenate([shifted(value, step) for step in order], axis=0).astype(BF16)


def add_shifted(value, order, rows):
    total = None
    for index, step in enumerate(order):
        part = shifted(value[index * rows : (index + 1) * rows], step)
        total = part if total is None else total + part
    return total


def hidden_state(image, first_ref, bias_column):
    stack = stack_shifted(image, (-1, 0, 1))
    return (
        jnp.dot(first_ref[:, : stack.shape[0]], stack, preferred_element_type=F32) + bias_column
    )


def second_conv(hidden, second_ref, bias, rows, valid):
    mixed = jnp.dot(
        second_ref[...], jnp.where(valid, hidden, 0.0).astype(BF16), preferred_element_type=F32
    )
    total = add_shifted(mixed, (-1, 0, 1), 2 * rows)
    row = lax.broadcasted_iota(jnp.int32, total.shape, 0)
    total = total + jnp.where(row < rows, bias[0], bias[1])
    return jnp.where(valid[: 2 * rows], total, 0.0)


def pull_back(cotangent, slope, first_t_ref, second_t_ref, rows, valid):
    stack = stack_shifted(cotangent, (1, 0, -1))
    back = jnp.dot(second_t_ref[:, : stack.shape[0]], stack, preferred_element_type=F32)
    back = jnp.where(valid, back * slope, 0.0).astype(BF16)
    mixed = jnp.dot(first_t_ref[...], back, preferred_element_type=F32)
    total = add_shifted(mixed, (1, 0, -1), 2 * rows)
    return jnp.where(valid[: 2 * rows], total, 0.0)


def valid_lanes(rows, width, lines):
    return lane_index((rows, width)) < lines


def round_bf(value):
    return value.astype(BF16).astype(F32)


def pack_kernel(coils, rows, pitch, maps_ref, image_ref, out_ref, scratch):
    scratch[...] = jnp.zeros_like(scratch)
    count = maps_ref.shape[1] // LANES
    for coil in range(coils):
        value = maps_ref[coil * rows : (coil + 1) * rows, :].astype(F32)
        write_rows(scratch, pitch, lane_chunks(value), coil * count)
    write_rows(scratch, pitch, lane_chunks(image_ref[...].astype(F32)), coils * count)
    out_ref[...] = scratch[...].astype(BF16).reshape(out_ref.shape)


def begin_kernel(
    coils,
    lines,
    rows,
    kspace_ref,
    mask_ref,
    table_ref,
    plus_ref,
    taps_ref,
    repeat_ref,
    place_ref,
    offset_ref,
    images_ref,
    first_ref,
    first_t_ref,
    second_ref,
    second_t_ref,
    bias_ref,
):
    real, imag = split_complex(lane_chunks(kspace_ref[...].astype(F32)), lines)
    mask = over_coils(mask_ref[...], coils)
    measured = jnp.concatenate([real * mask, imag * mask], axis=0)
    images = line_apply(depth_apply(measured, plus_ref), table_ref, 1.0)
    images_ref[...] = images.astype(BF16)

    tall = jnp.dot(
        repeat_ref[...],
        taps_ref[...],
        precision=lax.Precision.HIGHEST,
        preferred_element_type=F32,
    )
    bias_ref[...] = tall
    wide = jnp.dot(tall.astype(BF16), place_ref[...], preferred_element_type=F32)
    offset = offset_ref[...]
    width = offset.shape[1]
    for cascade in range(CASCADES):
        for kind, straight, turned in ((0, first_ref, first_t_ref), (1, second_t_ref, second_ref)):
            total = jnp.zeros_like(offset)
            for tap in range(3):
                start = ((kind * CASCADES + cascade) * 3 + tap) * width
                wanted = float(tap if kind == 0 else 2 - tap)
                total = total + jnp.where(offset == wanted, wide[:, start : start + width], 0.0)
            straight[cascade] = total.astype(BF16)
            turned[cascade] = total.T[: 6 * rows].astype(BF16)


def rows_kernel(
    coils,
    slots,
    lines,
    pitch,
    sent_ref,
    images_ref,
    mask_ref,
    table_ref,
    minus_ref,
    plus_ref,
    out_ref,
    maps_ref,
    arrived,
    leaving,
):
    arrived[...] = sent_ref[...].astype(F32).reshape(arrived.shape)
    count = 2 * lines // LANES
    parts = [
        split_complex(read_rows(arrived, pitch, coil * count, count, slots), lines)
        for coil in range(coils)
    ]
    maps_real = jnp.concatenate([part[0] for part in parts], axis=0)
    maps_imag = jnp.concatenate([part[1] for part in parts], axis=0)
    maps_ref[...] = jnp.concatenate([maps_real, maps_imag], axis=0).astype(BF16)
    real, imag = split_complex(read_rows(arrived, pitch, coils * count, count, slots), lines)
    mask = over_coils(mask_ref[...], 2 * coils)
    images = spread(maps_real, maps_imag, real, imag, coils)
    images = masked_normal(images, table_ref, minus_ref, plus_ref, mask)
    turned = collect(maps_real, maps_imag, images, coils)
    begun = collect(maps_real, maps_imag, images_ref[...].astype(F32), coils)
    power = coil_sum(maps_real * maps_real + maps_imag * maps_imag, coils)
    leaving[...] = jnp.zeros_like(leaving)
    values = []
    for value in (*begun, *turned, power):
        values += lane_chunks(value)
    write_rows(leaving, out_ref.shape[2], values)
    message = leaving[...].astype(BF16).reshape(slots, *out_ref.shape[2:])
    for device in range(out_ref.shape[1]):
        out_ref[:, device] = message


def unpack_sum(sent_ref, scratch):
    total = sent_ref[:, 0].astype(F32)
    for device in range(1, sent_ref.shape[1]):
        total = total + sent_ref[:, device].astype(F32)
    scratch[...] = total.reshape(scratch.shape)


def read_pair(scratch, pitch, first, count, rows):
    real = jnp.concatenate(read_rows(scratch, pitch, first, count, rows), axis=1)
    imag = jnp.concatenate(read_rows(scratch, pitch, first + count, count, rows), axis=1)
    return jnp.concatenate([real, imag], axis=0)


def first_refine_kernel(
    lines, rows, bias_out_ref, sent_ref, first_ref, second_ref, bias_ref, out_ref, model_ref, arrived, leaving
):
    unpack_sum(sent_ref, arrived)
    width = padded(lines, LANES)
    count = width // LANES
    picture = round_bf(read_pair(arrived, sent_ref.shape[2], 0, count, rows))
    bias_at = 4 * 9 * CASCADES
    hidden = hidden_state(picture, first_ref.at[0], bias_ref[:, bias_at : bias_at + 1])
    valid = valid_lanes(hidden.shape[0], width, lines)
    hidden = hidden * jax.nn.sigmoid(hidden)
    bias = (bias_out_ref[0, 0], bias_out_ref[0, 1])
    model = second_conv(hidden, second_ref.at[0], bias, rows, valid)
    model_ref[...] = model.astype(BF16)
    leaving[...] = jnp.zeros_like(leaving)
    real, imag = halves(model)
    write_rows(leaving, out_ref.shape[1], lane_chunks(real) + lane_chunks(imag))
    out_ref[...] = leaving[...].astype(BF16).reshape(out_ref.shape)


def slots_kernel(
    lines,
    rows,
    weight_ref,
    bias_out_ref,
    sent_ref,
    model_ref,
    cotangent_ref,
    first_ref,
    first_t_ref,
    second_ref,
    second_t_ref,
    bias_ref,
    image_ref,
    spread_ref,
    arrived,
):
    unpack_sum(sent_ref, arrived)
    width = padded(lines, LANES)
    count = width // LANES
    pitch = sent_ref.shape[2]
    begun = read_pair(arrived, pitch, 0, count, rows)
    turned = read_pair(arrived, pitch, 2 * count, count, rows)
    power = jnp.concatenate(read_rows(arrived, pitch, 4 * count, count, rows), axis=1)
    power = jnp.concatenate([power, power], axis=0)
    cotangent = jnp.concatenate(
        split_complex(lane_chunks(cotangent_ref[...].astype(F32)), lines), axis=0
    )
    model = model_ref[...].astype(F32)
    bias_at = 4 * 9 * CASCADES
    weight = (weight_ref[0], weight_ref[1])

    share = [jnp.float32(1.0)]
    for cascade in range(CASCADES):
        share.append(share[cascade] - weight[cascade] * (share[cascade] - 1.0))

    def slopes(hidden):
        gate = jax.nn.sigmoid(hidden)
        return hidden * gate, gate * (1.0 + hidden * (1.0 - gate))

    hidden = hidden_state(round_bf(begun), first_ref.at[0], bias_ref[:, bias_at : bias_at + 1])
    valid = valid_lanes(hidden.shape[0], width, lines)
    unused, slope_first = slopes(hidden)
    picture = round_bf(share[1] * begun + power * model)
    hidden = hidden_state(picture, first_ref.at[1], bias_ref[:, bias_at + 1 : bias_at + 2])
    active, slope_second = slopes(hidden)
    bias = (bias_out_ref[1, 0], bias_out_ref[1, 1])
    later = round_bf(second_conv(active, second_ref.at[1], bias, rows, valid))
    image_ref[...] = share[2] * begun + power * (model + later)

    through = power * cotangent
    back_second = round_bf(
        pull_back(through, slope_second, first_t_ref.at[1], second_t_ref.at[1], rows, valid)
    )
    through = through - weight[1] * turned + power * back_second
    back_first = round_bf(
        pull_back(through, slope_first, first_t_ref.at[0], second_t_ref.at[0], rows, valid)
    )
    kept = (1.0 - weight[0], 1.0 - weight[1])
    of_cotangent = weight[1] + weight[0] * kept[1] + kept[0] * kept[1]
    of_second = weight[0] + kept[0]
    spread_ref[...] = of_cotangent * cotangent + of_second * back_second + back_first


def normal_kernel(
    coils,
    slots,
    sent_ref,
    maps_ref,
    spread_ref,
    mask_ref,
    table_ref,
    minus_ref,
    plus_ref,
    out_ref,
    arrived,
    leaving,
):
    arrived[...] = sent_ref[...].astype(F32).reshape(arrived.shape)
    count = maps_ref.shape[1] // LANES
    real, imag = halves(read_pair(arrived, sent_ref.shape[1], 0, count, slots))
    maps_real, maps_imag = halves(maps_ref[...].astype(F32))
    mask = over_coils(mask_ref[...], 2 * coils)
    images = spread(maps_real, maps_imag, real, imag, coils)
    images = masked_normal(images, table_ref, minus_ref, plus_ref, mask)
    leaving[...] = jnp.zeros_like(leaving)
    values = []
    for value in (*collect(maps_real, maps_imag, images, coils), *halves(spread_ref[...])):
        values += lane_chunks(value)
    write_rows(leaving, out_ref.shape[2], values)
    message = leaving[...].astype(BF16).reshape(slots, *out_ref.shape[2:])
    for device in range(out_ref.shape[1]):
        out_ref[:, device] = message


def end_kernel(
    coils,
    slots,
    lines,
    weight_ref,
    sent_ref,
    image_ref,
    maps_ref,
    mask_ref,
    table_ref,
    minus_ref,
    picture_ref,
    grad_ref,
    arrived,
):
    count = maps_ref.shape[1] // LANES
    pitch = sent_ref.shape[2]
    arrived[...] = sent_ref[:, 0].astype(F32).reshape(arrived.shape)
    real, imag = halves(read_pair(arrived, pitch, 2 * count, count, slots))
    maps_real, maps_imag = halves(maps_ref[...].astype(F32))
    images = spread(maps_real, maps_imag, real, imag, coils)
    spectrum = depth_apply(line_apply(images, table_ref, -1.0), minus_ref)
    spectrum = spectrum * over_coils(mask_ref[...], 2 * coils)
    for index, chunk in enumerate(join_complex(*halves(spectrum), lines)):
        grad_ref[:, index * LANES : (index + 1) * LANES] = chunk

    unpack_sum(sent_ref, arrived)
    turned = read_pair(arrived, pitch, 0, count, slots)
    picture = image_ref[...] - weight_ref[1] * turned
    for index, chunk in enumerate(join_complex(*halves(picture), lines)):
        picture_ref[:, index * LANES : (index + 1) * LANES] = chunk


def call(kernel, name, operands, scalars, outs, scratch, flops):
    spaces = [pltpu.SMEM] * scalars + [pltpu.VMEM] * (len(operands) - scalars)
    moved = sum(math.prod(item.shape) * item.dtype.itemsize for item in (*operands, *outs))
    return pl.pallas_call(
        kernel,
        name=name,
        out_shape=tuple(outs),
        in_specs=[pl.BlockSpec(memory_space=space) for space in spaces],
        out_specs=tuple(pl.BlockSpec(memory_space=pltpu.VMEM) for item in outs),
        scratch_shapes=[pltpu.VMEM(shape, F32) for shape in scratch],
        compiler_params=pltpu.CompilerParams(vmem_limit_bytes=VMEM_BYTES),
        cost_estimate=pl.CostEstimate(flops=flops, bytes_accessed=moved, transcendentals=0),
    )(*operands)


def body(
    kspace, coil_maps, sampling, dc_weight, kernel_in, bias_in, kernel_out, bias_out, cotangent
):
    coils, slots = kspace.shape[:2]
    rows, two_lines = coil_maps.shape[2:]
    lines = two_lines // 2
    channels = bias_in.shape[1]
    coil_devices = lax.axis_size("coil")
    width = padded(lines, LANES)
    count = width // LANES
    planes = coils * slots
    both = ("section", "coil")

    table = jnp.asarray(line_constant(lines))
    minus = jnp.asarray(depth_constant(coils, slots, VOLUMES, -1.0))
    plus = jnp.asarray(depth_constant(coils, slots, VOLUMES, 1.0))
    repeat, place, offset = (jnp.asarray(item) for item in conv_constants(rows, channels))
    mask = sampling.astype(F32).reshape(slots, lines)
    mask = jnp.pad(mask, ((0, 0), (0, width - lines)))
    taps = jnp.concatenate(
        [
            kernel_in.transpose(2, 0, 1, 3).reshape(channels, -1),
            kernel_out.transpose(3, 0, 1, 2).reshape(channels, -1),
            bias_in.T,
        ],
        axis=1,
    )
    taps = jnp.pad(taps, ((0, 0), (0, place.shape[0] - taps.shape[1])))

    def shape(*dims, kind=F32):
        return jax.ShapeDtypeStruct(dims, kind)

    line_flops = 2 * (2 * planes) * width * (2 * width)

    pitch = padded((coils + 1) * (two_lines // LANES), 16)
    (packed,) = call(
        functools.partial(pack_kernel, coils, rows, pitch),
        "pack_maps",
        (coil_maps.reshape(coils * rows, two_lines), cotangent.reshape(rows, two_lines)),
        0,
        [shape(rows, pitch, LANES, kind=BF16)],
        [(rows * pitch, LANES)],
        1000,
    )
    arrived = lax.all_to_all(packed, "section", 0, 0, tiled=True)

    tall, wide = channels * rows, offset.shape[1]
    images, first, first_t, second, second_t, bias = call(
        functools.partial(begin_kernel, coils, lines, rows),
        "measured_images",
        (kspace.reshape(planes, two_lines), mask, table, plus, taps, repeat, place, offset),
        0,
        [
            shape(2 * planes, width, kind=BF16),
            shape(CASCADES, tall, wide, kind=BF16),
            shape(CASCADES, 6 * rows, tall, kind=BF16),
            shape(CASCADES, 6 * rows, tall, kind=BF16),
            shape(CASCADES, tall, wide, kind=BF16),
            shape(tall, place.shape[0]),
        ],
        [],
        2 * line_flops,
    )

    depth_pitch = padded(5 * count, 16)
    partial, maps = call(
        functools.partial(rows_kernel, coils, slots, lines, pitch),
        "combine_rows",
        (arrived, images, mask, table, minus, plus),
        0,
        [
            shape(slots, coil_devices, depth_pitch, LANES, kind=BF16),
            shape(2 * planes, width, kind=BF16),
        ],
        [(slots * pitch, LANES), (slots * depth_pitch, LANES)],
        3 * line_flops,
    )
    partial = partial.reshape(slots * coil_devices, depth_pitch, LANES)
    partial = lax.all_to_all(partial, both, 0, 0, tiled=True)
    partial = partial.reshape(rows, coil_devices, depth_pitch, LANES)

    model_pitch = padded(2 * count, 8)
    moved, model = call(
        functools.partial(first_refine_kernel, lines, rows),
        "refine_first",
        (bias_out, partial, first, second, bias),
        1,
        [shape(rows, model_pitch, LANES, kind=BF16), shape(2 * rows, width, kind=BF16)],
        [(rows * depth_pitch, LANES), (rows * model_pitch, LANES)],
        4 * tall * wide * width,
    )
    moved = lax.all_to_all(moved, "section", 0, 0, tiled=True)

    image, pulled = call(
        functools.partial(slots_kernel, lines, rows),
        "refine_and_back",
        (
            dc_weight,
            bias_out,
            partial,
            model,
            cotangent.reshape(rows, two_lines),
            first,
            first_t,
            second,
            second_t,
            bias,
        ),
        2,
        [shape(2 * rows, width), shape(2 * rows, width)],
        [(rows * depth_pitch, LANES)],
        14 * tall * wide * width,
    )

    end_pitch = padded(4 * count, 16)
    (partial,) = call(
        functools.partial(normal_kernel, coils, slots),
        "masked_normal",
        (moved, maps, pulled, mask, table, minus, plus),
        0,
        [shape(slots, coil_devices, end_pitch, LANES, kind=BF16)],
        [(slots * model_pitch, LANES), (slots * end_pitch, LANES)],
        3 * line_flops,
    )
    partial = partial.reshape(slots * coil_devices, end_pitch, LANES)
    partial = lax.all_to_all(partial, both, 0, 0, tiled=True)
    partial = partial.reshape(rows, coil_devices, end_pitch, LANES)

    image, grad = call(
        functools.partial(end_kernel, coils, slots, lines),
        "outputs",
        (dc_weight, partial, image, maps, mask, table, minus),
        1,
        [shape(rows, two_lines), shape(planes, two_lines)],
        [(rows * end_pitch, LANES)],
        2 * line_flops,
    )
    return image.reshape(1, rows, two_lines), grad.reshape(coils, slots, 1, two_lines)


def solution(mesh):
    return jax.shard_map(
        body,
        mesh=mesh,
        in_specs=(
            P("coil", None, "section", None),
            P("coil", "section", None, None),
            P(),
            P(),
            P(),
            P(),
            P(),
            P(),
            P("section", None, None),
        ),
        out_specs=(P("section", None, None), P("coil", None, "section", None)),
        check_vma=False,
    )
```

time: 186 us -> 59.6 us (0.32)
  starting transfers between devices: 50.5 us -> 11.1 us
  waiting for transfers between devices: 39.2 us -> 7.6 us
  other arithmetic: 26.5 us -> 0.08 us
  matrix products: 21.7 us -> 0 us
  local copies, waits for them, and re-layouts: 20.2 us -> 8.06 us
  Pallas kernels: 0 us -> 10.1 us
  blocking collectives: 24.4 us -> 21.3 us
    all_to_all x11 -> x2, starting transfers between devices: 50.5 us -> 11.1 us  [the longest x1 7.52 us: body(): arrived = lax.all_to_all(packed, 'section', 0, 0, tiled=True)]
    all_to_all x11 -> x2, waiting for transfers between devices: 39.2 us -> 7.6 us  [the longest x1 3.94 us: body(): moved = lax.all_to_all(moved, 'section', 0, 0, tiled=True)]
    psum x3 -> x0, blocking collectives: 24.4 us -> none  [combine(): lax.psum(partial_sum.astype(jnp.bfloat16), 'coil').astype(jnp.float32)]
    dot_general x33 -> x0, matrix products: 21.7 us -> none  [the longest x10 9.03 us: line_transform(): jnp.dot(values.astype(jnp.bfloat16), matrix, preferred_element_type=jnp.f...]
    all_to_all x0 -> x2, blocking collectives: none -> 21.3 us  [body(): partial = lax.all_to_all(partial, both, 0, 0, tiled=True)]
    pallas_call x0 -> x7, Pallas kernels: none -> 10.1 us  [call(): pl.pallas_call(kernel, name=name, out_shape=tuple(outs), in_specs=[pl.Blo...]
    another operation x8 -> x0, other arithmetic: 7.01 us -> none
    unnamed x115 -> x36, local copies, waits for them, and re-layouts: 12.3 us -> 7.84 us
  transfers between devices with their start and end apart: 11 -> 2, of which waited for: 9 -> 2; matrix products, arithmetic and copies ran while one was open for 17% -> 1% of each run, Pallas kernels for 0% -> 5%
where the time goes in v1:
time: 59.6 us; the launch traced here: 59.1 us
  blocking collectives  21.3 us (36%)
  starting transfers between devices  11.1 us (19%)
  Pallas kernels  10.1 us (17%)
  local copies, waits for them, and re-layouts  8.06 us (14%)
  waiting for transfers between devices  7.6 us (13%)
  between operations  0.76 us (1%)
    all_to_all x2, blocking collectives, body(): partial = lax.all_to_all(partial, both, 0, 0, tiled=True)  21.3 us
    pallas_call x7, Pallas kernels, call(): pl.pallas_call(kernel, name=name, out_shape=tuple(outs), in_specs=[pl.Blo...  10.1 us
    unnamed x36, local copies, waits for them, and re-layouts  7.84 us
    all_to_all x1, starting transfers between devices, body(): arrived = lax.all_to_all(packed, 'section', 0, 0, tiled=True)  7.52 us
    all_to_all x1, waiting for transfers between devices, body(): moved = lax.all_to_all(moved, 'section', 0, 0, tiled=True)  3.94 us
    all_to_all x1, waiting for transfers between devices, body(): arrived = lax.all_to_all(packed, 'section', 0, 0, tiled=True)  3.65 us
    all_to_all x1, starting transfers between devices, body(): moved = lax.all_to_all(moved, 'section', 0, 0, tiled=True)  3.63 us
  transfers between devices with their start and end apart: 2, of which 2 were waited for; matrix products, arithmetic and copies ran while one was open for 1% of the time, Pallas kernels for 5%

profile of v1, /device:TPU:0, one launch (start us, length us, event | category | flops | bytes accessed | tf_op | source)
XLA Modules:
  0.0 59.1 jit_solution(4737204729699653986)
XLA Ops:
  0.6 0.0 copy-start
  0.6 0.0 copy-start.3
  0.7 1.0 %copy-done.3 = bf16[8,1,16,640]{3,2,1,0:T(8,128)(2,1)S(1)} copy-done((bf16[8,1,16,640]{3,2,1,0:T(8,128)(2,1)S(1)}, bf16[8,1,16,640]{3,2,1,0:T(8,128)(2,1)}, u32[]{:S(2)}) %copy-start.3) | copy-done | bytes 163864
  1.6 0.7 %copy-done.9 = bf16[1,16,640]{2,1,0:T(8,128)(2,1)S(1)} copy-done((bf16[1,16,640]{2,1,0:T(8,128)(2,1)S(1)}, bf16[1,16,640]{2,1,0:T(8,128)(2,1)}, u32[]{:S(2)}) %copy-start.9) | copy-done | bytes 20504
  2.4 0.8 %pack_maps.1 = bf16[16,48,128]{2,1,0:T(8,128)(2,1)} custom-call(bf16[128,640]{1,0:T(8,128)(2,1)S(1)} %bitcast.23, bf16[16,640]{1,0:T(8,128)(2,1)S(1)} %bitcast.26), custom_call_target="tpu_custom_call" | custom-call | flops 1000 | bytes 380928 | tf_op jit(solution)/shard_map/pack_maps/pallas_call | solution.py:478
  3.2 7.5 %all-to-all-start = ((bf16[16,48,128]{2,1,0:T(8,128)(2,1)}), bf16[16,48,128]{2,1,0:T(8,128)(2,1)S(1)}, u32[]{:S(2)}, u32[]{:S(2)}) async-start(bf16[16,48,128]{2,1,0:T(8,128)(2,1)} %pack_maps.1), calls=%async_computation | async-start | bytes 393216 | tf_op jit(solution)/shard_map/all_to_all | solution.py:534
  10.7 0.0 copy-done.16
  10.7 0.1 copy.21
  10.8 0.1 copy.22
  10.9 0.1 copy.23
  11.1 0.1 select_maximum_fusion.taps_ref
  11.1 0.0 copy-start.2
  11.2 0.9 %copy-done.2 = bf16[8,16,1,640]{3,1,2,0:T(8,128)(2,1)S(1)} copy-done((bf16[8,16,1,640]{3,1,2,0:T(8,128)(2,1)S(1)}, bf16[8,16,1,640]{3,1,2,0:T(8,128)(2,1)}, u32[]{:S(2)}) %copy-start.2) | copy-done | bytes 163864
  12.1 0.9 %copy-done.4 = f32[288,128]{1,0:T(8,128)S(1)} copy-done((f32[288,128]{1,0:T(8,128)S(1)}, f32[288,128]{1,0:T(8,128)}, u32[]{:S(2)}) %copy-start.4) | copy-done | bytes 147480
  13.0 0.9 %copy-done.5 = f32[288,18]{1,0:T(8,128)S(1)} copy-done((f32[288,18]{1,0:T(8,128)S(1)}, f32[288,18]{1,0:T(8,128)}, u32[]{:S(2)}) %copy-start.5) | copy-done | bytes 20760
  13.9 0.9 %copy-done.6 = bf16[256,256]{1,0:T(8,128)(2,1)S(1)} copy-done((bf16[256,256]{1,0:T(8,128)(2,1)S(1)}, bf16[256,256]{1,0:T(8,128)(2,1)}, u32[]{:S(2)}) %copy-start.6) | copy-done | bytes 131096
  14.8 1.3 %measured_images.1 = (bf16[256,384]{1,0:T(8,128)(2,1)S(1)}, bf16[2,288,128]{2,1,0:T(8,128)(2,1)S(1)}, bf16[2,96,288]{2,1,0:T(8,128)(2,1)S(1)}, bf16[2,96,288]{2,...) custom-call(bf16[128,640]{1,0:T(8,128)(2,1)S(1)} %bitcast.22, ...), custom_call_target="tpu_custom_call" | custom-call | flops 301989888 | bytes 2340096 | tf_op jit(solution)/shard_map/measured_images/pallas_call | solution.py:478
  16.0 3.7 %all-to-all-done.sent_ref = bf16[16,48,128]{2,1,0:T(8,128)(2,1)S(1)} async-done(((bf16[16,48,128]{2,1,0:T(8,128)(2,1)}), bf16[16,48,128]{2,1,0:T(8,128)(2,1)S(1)}, u32[]{:S(2)}, u32[]{:S(2)}) %all-to-all-start) | async-done | bytes 196640 | tf_op jit(solution)/shard_map/all_to_all | solution.py:534
  19.7 1.3 %combine_rows.1 = (bf16[16,2,16,128]{3,2,1,0:T(8,128)(2,1)S(1)}, bf16[256,384]{1,0:T(8,128)(2,1)S(1)}) custom-call(bf16[16,48,128]{2,1,0:T(8,128)(2,1)S(1)} %all-to-all-done.sent_ref, bf16[256,384]{1,0:T(8,128)(2,1)S(1)} %get-tuple-element.16.images_ref, f32[16,384]{1,0:T(8,128)S(1)} %pad.8.mask_ref, bf16[384,768]{1,0:T(8,128)(2,1)S(1)} %copy-done, ...), custom_call_target="tpu_custom_call" | custom-call | flops 452984832 | bytes 1597440 | tf_op jit(solution)/shard_map/combine_rows/pallas_call | solution.py:478
  21.0 11.0 %all_to_all.20 = bf16[32,16,128]{2,1,0:T(8,128)(2,1)S(1)} all-to-all(bf16[32,16,128]{2,1,0:T(8,128)(2,1)S(1)} %bitcast.24), channel_id=1, replica_groups=mesh['section'=16,'coil'=2] {'section','coil'}, dimensions={0} | all-to-all | bytes 262144 | tf_op jit(solution)/shard_map/all_to_all | solution.py:568
  32.0 0.7 %copy-done.11 = f32[2,2]{1,0:T(2,128)S(1)} copy-done((f32[2,2]{1,0:T(2,128)S(1)}, f32[2,2]{1,0:T(2,128)}, u32[]{:S(2)}) %copy-start.11) | copy-done | bytes 40
  32.7 1.7 %refine_first.1 = (bf16[16,8,128]{2,1,0:T(8,128)(2,1)}, bf16[32,384]{1,0:T(8,128)(2,1)S(1)}) custom-call(f32[2,2]{1,0:T(2,128)S(1)} %copy-done.11, bf16[16,2,16,128]{3,2,1,0:T(8,128)(2,1)S(1)} %bitcast.18, bf16[2,288,128]{2,1,0:T(8,128)(2,1)S(1)} %get-tuple-element.18.first_ref, bf16[2,96,288]{2,1,0:T(8,128)(2,1)S(1)} %get-tuple-element.19.second_ref, ...), custom_call_target="tpu_custom_call" | custom-call | flops 56623104 | bytes 593936 | tf_op jit(solution)/shard_map/refine_first/pallas_call | solution.py:478
  34.4 3.6 %all-to-all-start.2 = ((bf16[16,8,128]{2,1,0:T(8,128)(2,1)}), bf16[16,8,128]{2,1,0:T(8,128)(2,1)S(1)}, u32[]{:S(2)}, u32[]{:S(2)}) async-start(bf16[16,8,128]{2,1,0:T(8,128)(2,1)} %get-tuple-element.21), calls=%async_computation.2 | async-start | bytes 65536 | tf_op jit(solution)/shard_map/all_to_all | solution.py:581
  38.1 0.0 copy-start.12
  38.1 0.6 %copy-done.12 = f32[2]{0:T(128)S(1)} copy-done((f32[2]{0:T(128)S(1)}, f32[2]{0:T(128)}, u32[]{:S(2)}) %copy-start.12) | copy-done | bytes 32
  38.7 2.0 %refine_and_back.1 = (f32[32,384]{1,0:T(8,128)S(1)}, f32[32,384]{1,0:T(8,128)S(1)}) custom-call(f32[2]{0:T(128)S(1)} %copy-done.12, f32[2,2]{1,0:T(2,128)S(1)} %copy-done.11, bf16[16,2,16,128]{3,2,1,0:T(8,128)(2,1)S(1)} %bitcast.19, bf16[32,384]{1,0:T(8,128)(2,1)S(1)} %get-tuple-element.23.model_ref, bf16[16,640]{1,0:T(8,128)(2,1)S(1)} %bitcast.27, ...), custom_call_target="tpu_custom_call" | custom-call | flops 198180864 | bytes 938008 | tf_op jit(solution)/shard_map/refine_and_back/pallas_call | solution.py:478
  40.7 3.9 %all-to-all-done.2.sent_ref = bf16[16,8,128]{2,1,0:T(8,128)(2,1)S(1)} async-done(((bf16[16,8,128]{2,1,0:T(8,128)(2,1)}), bf16[16,8,128]{2,1,0:T(8,128)(2,1)S(1)}, u32[]{:S(2)}, u32[]{:S(2)}) %all-to-all-start.2) | async-done | bytes 32800 | tf_op jit(solution)/shard_map/all_to_all | solution.py:581
  44.7 0.0 copy-done.7
  44.7 1.1 %masked_normal.1 = bf16[16,2,16,128]{3,2,1,0:T(8,128)(2,1)S(1)} custom-call(bf16[16,8,128]{2,1,0:T(8,128)(2,1)S(1)} %all-to-all-done.2.sent_ref, bf16[256,384]{1,0:T(8,128)(2,1)S(1)} %get-tuple-element.22.maps_ref, f32[32,384]{1,0:T(8,128)S(1)} %get-tuple-element.26.spread_ref, f32[16,384]{1,0:T(8,128)S(1)} %pad.8.mask_ref, bf16[384,768]{1,0:T(8,128)(2,1)S(1)} %copy-done, ...), custom_call_target="tpu_custom_call" | custom-call | flops 452984832 | bytes 1286144 | tf_op jit(solution)/shard_map/masked_normal/pallas_call | solution.py:478
  45.8 10.3 %all_to_all.21 = bf16[32,16,128]{2,1,0:T(8,128)(2,1)S(1)} all-to-all(bf16[32,16,128]{2,1,0:T(8,128)(2,1)S(1)} %bitcast.25), channel_id=1, replica_groups=mesh['section'=16,'coil'=2] {'section','coil'}, dimensions={0} | all-to-all | bytes 262144 | tf_op jit(solution)/shard_map/all_to_all | solution.py:615
  56.1 1.9 %outputs.1 = (f32[16,640]{1,0:T(8,128)}, f32[128,640]{1,0:T(8,128)S(1)}) custom-call(f32[2]{0:T(128)S(1)} %copy-done.12, bf16[16,2,16,128]{3,2,1,0:T(8,128)(2,1)S(1)} %bitcast.20, f32[32,384]{1,0:T(8,128)S(1)} %get-tuple-element.27.image_ref, bf16[256,384]{1,0:T(8,128)(2,1)S(1)} %get-tuple-element.22.maps_ref, f32[16,384]{1,0:T(8,128)S(1)} %pad.8.mask_ref, ...), custom_call_target="tpu_custom_call" | custom-call | flops 301989888 | bytes 1490952 | tf_op jit(solution)/shard_map/outputs/pallas_call | solution.py:478
  58.0 1.1 %copy.24 = f32[8,16,1,640]{3,2,1,0:T(1,128)} copy(f32[8,16,1,640]{3,1,0,2:T(8,128)S(1)} %bitcast.21) | data formatting | bytes 655360
  (24 shorter events, 0.1 us)
Async XLA Ops:
  0.6 10.5 %copy-start = (bf16[384,768]{1,0:T(8,128)(2,1)S(1)}, bf16[384,768]{1,0:T(8,128)(2,1)}, u32[]{:S(2)}) copy-start(bf16[384,768]{1,0:T(8,128)(2,1)} %constant.15.clone.table_ref) | copy-start | bytes 1769476
  0.6 1.0 %copy-start.3 = (bf16[8,1,16,640]{3,2,1,0:T(8,128)(2,1)S(1)}, bf16[8,1,16,640]{3,2,1,0:T(8,128)(2,1)}, u32[]{:S(2)}) copy-start(bf16[8,1,16,640]{3,2,1,0:T(8,128)(2,1)} %param.16) | copy-start | bytes 491524
  1.6 0.7 %copy-start.9 = (bf16[1,16,640]{2,1,0:T(8,128)(2,1)S(1)}, bf16[1,16,640]{2,1,0:T(8,128)(2,1)}, u32[]{:S(2)}) copy-start(bf16[1,16,640]{2,1,0:T(8,128)(2,1)} %param.23) | copy-start | bytes 61444
  2.4 8.4 %copy-start.16 = (f32[2,18]{1,0:T(2,128)S(1)}, f32[2,18]{1,0:T(2,128)}, u32[]{:S(2)}) copy-start(f32[2,18]{1,0:T(2,128)} %param.20) | copy-start | bytes 436
  2.4 8.5 %copy-start.14 = (f32[2,9,18,2]{2,3,1,0:T(2,128)S(1)}, f32[2,9,18,2]{2,3,1,0:T(2,128)}, u32[]{:S(2)}) copy-start(f32[2,9,18,2]{2,3,1,0:T(2,128)} %param.19) | copy-start | bytes 7780
  2.4 8.6 %copy-start.15 = (f32[2,9,2,18]{3,2,1,0:T(2,128)S(1)}, f32[2,9,2,18]{3,2,1,0:T(2,128)}, u32[]{:S(2)}) copy-start(f32[2,9,2,18]{3,2,1,0:T(2,128)} %param.21) | copy-start | bytes 7780
  2.4 8.7 %copy-start.13 = (s32[2,8,320]{2,1,0:T(8,128)S(1)}, s32[2,8,320]{2,1,0:T(8,128)}, u32[]{:S(2)}) copy-start(s32[2,8,320]{2,1,0:T(8,128)} %param.17) | copy-start | bytes 61444
  3.2 8.0 %copy-start.1 = (bf16[128,1536]{1,0:T(8,128)(2,1)S(1)}, bf16[128,1536]{1,0:T(8,128)(2,1)}, u32[]{:S(2)}) copy-start(bf16[128,1536]{1,0:T(8,128)(2,1)} %constant.19.clone.place_ref) | copy-start | bytes 1179652
  3.2 16.5 %all-to-all-start = ((bf16[16,48,128]{2,1,0:T(8,128)(2,1)}), bf16[16,48,128]{2,1,0:T(8,128)(2,1)S(1)}, u32[]{:S(2)}, u32[]{:S(2)}) async-start(bf16[16,48,128]{2,1,0:T(8,128)(2,1)} %pack_maps.1), calls=%async_computation | async-start | bytes 393216 | tf_op jit(solution)/shard_map/all_to_all | solution.py:534
  11.1 0.9 %copy-start.2 = (bf16[8,16,1,640]{3,1,2,0:T(8,128)(2,1)S(1)}, bf16[8,16,1,640]{3,1,2,0:T(8,128)(2,1)}, u32[]{:S(2)}) copy-start(bf16[8,16,1,640]{3,1,2,0:T(8,128)(2,1)} %param.15) | copy-start | bytes 491524
  12.1 0.9 %copy-start.4 = (f32[288,128]{1,0:T(8,128)S(1)}, f32[288,128]{1,0:T(8,128)}, u32[]{:S(2)}) copy-start(f32[288,128]{1,0:T(8,128)} %constant.20.clone.offset_ref) | copy-start | bytes 442372
  13.0 0.9 %copy-start.5 = (f32[288,18]{1,0:T(8,128)S(1)}, f32[288,18]{1,0:T(8,128)}, u32[]{:S(2)}) copy-start(f32[288,18]{1,0:T(8,128)} %constant.18.clone.repeat_ref) | copy-start | bytes 62212
  13.9 0.9 %copy-start.6 = (bf16[256,256]{1,0:T(8,128)(2,1)S(1)}, bf16[256,256]{1,0:T(8,128)(2,1)}, u32[]{:S(2)}) copy-start(bf16[256,256]{1,0:T(8,128)(2,1)} %constant.17.clone.plus_ref) | copy-start | bytes 393220
  14.8 4.9 %copy-start.8 = (bf16[256,256]{1,0:T(8,128)(2,1)S(1)}, bf16[256,256]{1,0:T(8,128)(2,1)}, u32[]{:S(2)}) copy-start(bf16[256,256]{1,0:T(8,128)(2,1)} %constant.16.clone.minus_ref) | copy-start | bytes 393220
  32.0 0.7 %copy-start.11 = (f32[2,2]{1,0:T(2,128)S(1)}, f32[2,2]{1,0:T(2,128)}, u32[]{:S(2)}) copy-start(f32[2,2]{1,0:T(2,128)} %bias_out_ref.3) | copy-start | bytes 52
  34.4 3.7 %copy-start.10 = (bf16[1,16,640]{2,1,0:T(8,128)(2,1)S(1)}, bf16[1,16,640]{2,1,0:T(8,128)(2,1)}, u32[]{:S(2)}) copy-start(bf16[1,16,640]{2,1,0:T(8,128)(2,1)} %param.23) | copy-start | bytes 61444
  34.4 10.2 %all-to-all-start.2 = ((bf16[16,8,128]{2,1,0:T(8,128)(2,1)}), bf16[16,8,128]{2,1,0:T(8,128)(2,1)S(1)}, u32[]{:S(2)}, u32[]{:S(2)}) async-start(bf16[16,8,128]{2,1,0:T(8,128)(2,1)} %get-tuple-element.21), calls=%async_computation.2 | async-start | bytes 65536 | tf_op jit(solution)/shard_map/all_to_all | solution.py:581
  38.1 0.7 %copy-start.12 = (f32[2]{0:T(128)S(1)}, f32[2]{0:T(128)}, u32[]{:S(2)}) copy-start(f32[2]{0:T(128)} %weight_ref.3) | copy-start | bytes 28
  38.7 5.9 %copy-start.7 = (bf16[256,256]{1,0:T(8,128)(2,1)S(1)}, bf16[256,256]{1,0:T(8,128)(2,1)}, u32[]{:S(2)}) copy-start(bf16[256,256]{1,0:T(8,128)(2,1)} %constant.17.clone.plus_ref) | copy-start | bytes 393220

commit v2 on v1

--- a/solution.py
+++ b/solution.py
@@ -14,6 +14,7 @@
 VOLUMES = 2
 LANES = 128
 VMEM_BYTES = 48 * 1024 * 1024
+PACK_VMEM_BYTES = 60 * 1024 * 1024
 
 F32 = jnp.float32
 BF16 = jnp.bfloat16
@@ -51,7 +52,7 @@
     width = padded(groups * rows, LANES)
     repeat = np.kron(np.eye(channels), np.ones((rows, 1))).astype(np.float32)
     taps = CASCADES * 3
-    place = np.zeros((padded(2 * taps * groups + CASCADES, LANES), 2 * taps * width), np.float32)
+    place = np.zeros((padded(2 * taps * groups + 3 * CASCADES, LANES), 2 * taps * width), np.float32)
     for kind in range(2):
         for tap in range(taps):
             for group in range(groups):
@@ -186,14 +187,12 @@
     )
 
 
-def second_conv(hidden, second_ref, bias, rows, valid):
+def second_conv(hidden, second_ref, bias_column, rows, valid):
     mixed = jnp.dot(
         second_ref[...], jnp.where(valid, hidden, 0.0).astype(BF16), preferred_element_type=F32
     )
     total = add_shifted(mixed, (-1, 0, 1), 2 * rows)
-    row = lax.broadcasted_iota(jnp.int32, total.shape, 0)
-    total = total + jnp.where(row < rows, bias[0], bias[1])
-    return jnp.where(valid[: 2 * rows], total, 0.0)
+    return jnp.where(valid[: 2 * rows], total + bias_column, 0.0)
 
 
 def pull_back(cotangent, slope, first_t_ref, second_t_ref, rows, valid):
@@ -207,6 +206,11 @@
 
 def valid_lanes(rows, width, lines):
     return lane_index((rows, width)) < lines
+
+
+def column(columns_ref, place, rows):
+    at = 4 * 9 * CASCADES + place
+    return columns_ref[:rows, at : at + 1]
 
 
 def round_bf(value):
@@ -240,7 +244,7 @@
     first_t_ref,
     second_ref,
     second_t_ref,
-    bias_ref,
+    columns_ref,
 ):
     real, imag = split_complex(lane_chunks(kspace_ref[...].astype(F32)), lines)
     mask = over_coils(mask_ref[...], coils)
@@ -254,7 +258,7 @@
         precision=lax.Precision.HIGHEST,
         preferred_element_type=F32,
     )
-    bias_ref[...] = tall
+    columns_ref[...] = tall
     wide = jnp.dot(tall.astype(BF16), place_ref[...], preferred_element_type=F32)
     offset = offset_ref[...]
     width = offset.shape[1]
@@ -325,17 +329,16 @@
 
 
 def first_refine_kernel(
-    lines, rows, bias_out_ref, sent_ref, first_ref, second_ref, bias_ref, out_ref, model_ref, arrived, leaving
+    lines, rows, sent_ref, first_ref, second_ref, columns_ref, out_ref, model_ref, arrived, leaving
 ):
     unpack_sum(sent_ref, arrived)
     width = padded(lines, LANES)
     count = width // LANES
     picture = round_bf(read_pair(arrived, sent_ref.shape[2], 0, count, rows))
-    bias_at = 4 * 9 * CASCADES
-    hidden = hidden_state(picture, first_ref.at[0], bias_ref[:, bias_at : bias_at + 1])
+    hidden = hidden_state(picture, first_ref.at[0], column(columns_ref, 0, first_ref.shape[1]))
     valid = valid_lanes(hidden.shape[0], width, lines)
     hidden = hidden * jax.nn.sigmoid(hidden)
-    bias = (bias_out_ref[0, 0], bias_out_ref[0, 1])
+    bias = column(columns_ref, 2 * CASCADES, 2 * rows)
     model = second_conv(hidden, second_ref.at[0], bias, rows, valid)
     model_ref[...] = model.astype(BF16)
     leaving[...] = jnp.zeros_like(leaving)
@@ -347,8 +350,6 @@
 def slots_kernel(
     lines,
     rows,
-    weight_ref,
-    bias_out_ref,
     sent_ref,
     model_ref,
     cotangent_ref,
@@ -356,7 +357,7 @@
     first_t_ref,
     second_ref,
     second_t_ref,
-    bias_ref,
+    columns_ref,
     image_ref,
     spread_ref,
     arrived,
@@ -373,10 +374,10 @@
         split_complex(lane_chunks(cotangent_ref[...].astype(F32)), lines), axis=0
     )
     model = model_ref[...].astype(F32)
-    bias_at = 4 * 9 * CASCADES
-    weight = (weight_ref[0], weight_ref[1])
-
-    share = [jnp.float32(1.0)]
+    tall = first_ref.shape[1]
+    weight = [column(columns_ref, CASCADES + cascade, 2 * rows) for cascade in range(CASCADES)]
+
+    share = [jnp.ones_like(weight[0])]
     for cascade in range(CASCADES):
         share.append(share[cascade] - weight[cascade] * (share[cascade] - 1.0))
 
@@ -384,13 +385,13 @@
         gate = jax.nn.sigmoid(hidden)
         return hidden * gate, gate * (1.0 + hidden * (1.0 - gate))
 
-    hidden = hidden_state(round_bf(begun), first_ref.at[0], bias_ref[:, bias_at : bias_at + 1])
+    hidden = hidden_state(round_bf(begun), first_ref.at[0], column(columns_ref, 0, tall))
     valid = valid_lanes(hidden.shape[0], width, lines)
     unused, slope_first = slopes(hidden)
     picture = round_bf(share[1] * begun + power * model)
-    hidden = hidden_state(picture, first_ref.at[1], bias_ref[:, bias_at + 1 : bias_at + 2])
+    hidden = hidden_state(picture, first_ref.at[1], column(columns_ref, 1, tall))
     active, slope_second = slopes(hidden)
-    bias = (bias_out_ref[1, 0], bias_out_ref[1, 1])
+    bias = column(columns_ref, 2 * CASCADES + 1, 2 * rows)
     later = round_bf(second_conv(active, second_ref.at[1], bias, rows, valid))
     image_ref[...] = share[2] * begun + power * (model + later)
 
@@ -443,7 +444,7 @@
     coils,
     slots,
     lines,
-    weight_ref,
+    columns_ref,
     sent_ref,
     image_ref,
     maps_ref,
@@ -462,27 +463,26 @@
     images = spread(maps_real, maps_imag, real, imag, coils)
     spectrum = depth_apply(line_apply(images, table_ref, -1.0), minus_ref)
     spectrum = spectrum * over_coils(mask_ref[...], 2 * coils)
-    for index, chunk in enumerate(join_complex(*halves(spectrum), lines)):
-        grad_ref[:, index * LANES : (index + 1) * LANES] = chunk
+    chunks = join_complex(*halves(spectrum), lines)
+    write_rows(grad_ref, len(chunks), chunks)
 
     unpack_sum(sent_ref, arrived)
     turned = read_pair(arrived, pitch, 0, count, slots)
-    picture = image_ref[...] - weight_ref[1] * turned
+    picture = image_ref[...] - column(columns_ref, CASCADES + 1, turned.shape[0]) * turned
     for index, chunk in enumerate(join_complex(*halves(picture), lines)):
         picture_ref[:, index * LANES : (index + 1) * LANES] = chunk
 
 
-def call(kernel, name, operands, scalars, outs, scratch, flops):
-    spaces = [pltpu.SMEM] * scalars + [pltpu.VMEM] * (len(operands) - scalars)
+def call(kernel, name, operands, outs, scratch, flops, vmem_bytes=VMEM_BYTES):
     moved = sum(math.prod(item.shape) * item.dtype.itemsize for item in (*operands, *outs))
     return pl.pallas_call(
         kernel,
         name=name,
         out_shape=tuple(outs),
-        in_specs=[pl.BlockSpec(memory_space=space) for space in spaces],
+        in_specs=[pl.BlockSpec(memory_space=pltpu.VMEM) for item in operands],
         out_specs=tuple(pl.BlockSpec(memory_space=pltpu.VMEM) for item in outs),
         scratch_shapes=[pltpu.VMEM(shape, F32) for shape in scratch],
-        compiler_params=pltpu.CompilerParams(vmem_limit_bytes=VMEM_BYTES),
+        compiler_params=pltpu.CompilerParams(vmem_limit_bytes=vmem_bytes),
         cost_estimate=pl.CostEstimate(flops=flops, bytes_accessed=moved, transcendentals=0),
     )(*operands)
 
@@ -511,6 +511,8 @@
             kernel_in.transpose(2, 0, 1, 3).reshape(channels, -1),
             kernel_out.transpose(3, 0, 1, 2).reshape(channels, -1),
             bias_in.T,
+            jnp.broadcast_to(dc_weight[None, :], (channels, CASCADES)),
+            jnp.pad(bias_out.T, ((0, channels - bias_out.shape[1]), (0, 0))),
         ],
         axis=1,
     )
@@ -526,19 +528,18 @@
         functools.partial(pack_kernel, coils, rows, pitch),
         "pack_maps",
         (coil_maps.reshape(coils * rows, two_lines), cotangent.reshape(rows, two_lines)),
-        0,
         [shape(rows, pitch, LANES, kind=BF16)],
         [(rows * pitch, LANES)],
         1000,
+        PACK_VMEM_BYTES,
     )
     arrived = lax.all_to_all(packed, "section", 0, 0, tiled=True)
 
     tall, wide = channels * rows, offset.shape[1]
-    images, first, first_t, second, second_t, bias = call(
+    images, first, first_t, second, second_t, columns = call(
         functools.partial(begin_kernel, coils, lines, rows),
         "measured_images",
         (kspace.reshape(planes, two_lines), mask, table, plus, taps, repeat, place, offset),
-        0,
         [
             shape(2 * planes, width, kind=BF16),
             shape(CASCADES, tall, wide, kind=BF16),
@@ -556,7 +557,6 @@
         functools.partial(rows_kernel, coils, slots, lines, pitch),
         "combine_rows",
         (arrived, images, mask, table, minus, plus),
-        0,
         [
             shape(slots, coil_devices, depth_pitch, LANES, kind=BF16),
             shape(2 * planes, width, kind=BF16),
@@ -572,8 +572,7 @@
     moved, model = call(
         functools.partial(first_refine_kernel, lines, rows),
         "refine_first",
-        (bias_out, partial, first, second, bias),
-        1,
+        (partial, first, second, columns),
         [shape(rows, model_pitch, LANES, kind=BF16), shape(2 * rows, width, kind=BF16)],
         [(rows * depth_pitch, LANES), (rows * model_pitch, LANES)],
         4 * tall * wide * width,
@@ -584,8 +583,6 @@
         functools.partial(slots_kernel, lines, rows),
         "refine_and_back",
         (
-            dc_weight,
-            bias_out,
             partial,
             model,
             cotangent.reshape(rows, two_lines),
@@ -593,9 +590,8 @@
             first_t,
             second,
             second_t,
-            bias,
+            columns,
         ),
-        2,
         [shape(2 * rows, width), shape(2 * rows, width)],
         [(rows * depth_pitch, LANES)],
         14 * tall * wide * width,
@@ -606,7 +602,6 @@
         functools.partial(normal_kernel, coils, slots),
         "masked_normal",
         (moved, maps, pulled, mask, table, minus, plus),
-        0,
         [shape(slots, coil_devices, end_pitch, LANES, kind=BF16)],
         [(slots * model_pitch, LANES), (slots * end_pitch, LANES)],
         3 * line_flops,
@@ -618,9 +613,8 @@
     image, grad = call(
         functools.partial(end_kernel, coils, slots, lines),
         "outputs",
-        (dc_weight, partial, image, maps, mask, table, minus),
-        1,
-        [shape(rows, two_lines), shape(planes, two_lines)],
+        (columns, partial, image, maps, mask, table, minus),
+        [shape(rows, two_lines), shape(planes * (two_lines // LANES), LANES)],
         [(rows * end_pitch, LANES)],
         2 * line_flops,
     )

time: 59.6 us -> 56.7 us (0.951)
  local copies, waits for them, and re-layouts: 8.06 us -> 4.72 us
    unnamed x36 -> x28, local copies, waits for them, and re-layouts: 7.84 us -> 2.96 us
    all_to_all x1, waiting for transfers between devices: 3.94 us -> 5.11 us  [body(): moved = lax.all_to_all(moved, 'section', 0, 0, tiled=True)]
    reshape x2, local copies, waits for them, and re-layouts: 0.11 us -> 0.83 us  [body(): kernel_in.transpose(2, 0, 1, 3).reshape(channels, -1)]
    reshape x2, local copies, waits for them, and re-layouts: 0.11 us -> 0.83 us  [body(): kernel_out.transpose(3, 0, 1, 2).reshape(channels, -1)]
    all_to_all x1, waiting for transfers between devices: 3.65 us -> 2.94 us  [body(): arrived = lax.all_to_all(packed, 'section', 0, 0, tiled=True)]
  transfers between devices with their start and end apart: 2 -> 2, of which waited for: 2 -> 2; matrix products, arithmetic and copies ran while one was open for 1% -> 3% of each run, Pallas kernels for 5% -> 5%
where the time goes in v2:
time: 56.7 us; the launch traced here: 56.2 us
  blocking collectives  21.7 us (38%)
  starting transfers between devices  11.1 us (20%)
  Pallas kernels  9.67 us (17%)
  waiting for transfers between devices  8.05 us (14%)
  local copies, waits for them, and re-layouts  4.72 us (8%)
  between operations  0.82 us (1%)
    all_to_all x2, blocking collectives, body(): partial = lax.all_to_all(partial, both, 0, 0, tiled=True)  21.7 us
    pallas_call x7, Pallas kernels, call(): pl.pallas_call(kernel, name=name, out_shape=tuple(outs), in_specs=[pl.Blo...  9.67 us
    all_to_all x1, starting transfers between devices, body(): arrived = lax.all_to_all(packed, 'section', 0, 0, tiled=True)  7.52 us
    all_to_all x1, waiting for transfers between devices, body(): moved = lax.all_to_all(moved, 'section', 0, 0, tiled=True)  5.11 us
    all_to_all x1, starting transfers between devices, body(): moved = lax.all_to_all(moved, 'section', 0, 0, tiled=True)  3.63 us
    unnamed x28, local copies, waits for them, and re-layouts  2.96 us
    all_to_all x1, waiting for transfers between devices, body(): arrived = lax.all_to_all(packed, 'section', 0, 0, tiled=True)  2.94 us
  transfers between devices with their start and end apart: 2, of which 2 were waited for; matrix products, arithmetic and copies ran while one was open for 3% of the time, Pallas kernels for 5%

profile of v2, /device:TPU:0, one launch (start us, length us, event | category | flops | bytes accessed | tf_op | source)
XLA Modules:
  0.0 56.2 jit_solution(7242481582373646577)
XLA Ops:
  0.6 0.0 copy-start
  0.6 0.0 copy-start.10
  0.7 0.0 copy-start.11
  0.7 0.0 copy-start.12
  0.7 1.8 %pack_maps.1 = bf16[16,48,128]{2,1,0:T(8,128)(2,1)} custom-call(bf16[128,640]{1,0:T(8,128)(2,1)} %bitcast.27, bf16[16,640]{1,0:T(8,128)(2,1)} %bitcast.25), custom_call_target="tpu_custom_call" | custom-call | flops 1000 | bytes 380928 | tf_op jit(solution)/shard_map/pack_maps/pallas_call | solution.py:478
  2.5 7.5 %all-to-all-start = ((bf16[16,48,128]{2,1,0:T(8,128)(2,1)}), bf16[16,48,128]{2,1,0:T(8,128)(2,1)S(1)}, u32[]{:S(2)}, u32[]{:S(2)}) async-start(bf16[16,48,128]{2,1,0:T(8,128)(2,1)} %pack_maps.1), calls=%async_computation | async-start | bytes 393216 | tf_op jit(solution)/shard_map/all_to_all | solution.py:536
  10.0 0.1 copy.23
  10.1 0.0 copy-done.11
  10.1 0.1 copy.22
  10.2 0.7 %reshape.44 = f32[18,36]{0,1:T(8,128)S(1)} reshape(f32[18,2,9,2]{0,3,2,1:T(2,128)} %bitcast.29) | data formatting | bytes 5184 | tf_op jit(solution)/shard_map/reshape | solution.py:511
  10.9 0.0 copy-start.2
  11.0 0.1 copy.24
  11.0 0.7 %reshape.45 = f32[18,36]{0,1:T(8,128)S(1)} reshape(f32[18,2,9,2]{0,3,2,1:T(2,128)} %bitcast.30) | data formatting | bytes 5184 | tf_op jit(solution)/shard_map/reshape | solution.py:512
  11.8 0.1 copy.25
  11.9 0.1 concatenate.3
  12.0 0.0 copy-done
  12.1 0.0 copy-start.3
  12.1 0.9 %copy-done.3 = f32[288,128]{1,0:T(8,128)S(1)} copy-done((f32[288,128]{1,0:T(8,128)S(1)}, f32[288,128]{1,0:T(8,128)}, u32[]{:S(2)}) %copy-start.3) | copy-done | bytes 147480
  13.0 0.9 %copy-done.4 = f32[288,18]{1,0:T(8,128)S(1)} copy-done((f32[288,18]{1,0:T(8,128)S(1)}, f32[288,18]{1,0:T(8,128)}, u32[]{:S(2)}) %copy-start.4) | copy-done | bytes 20760
  13.9 0.9 %copy-done.6 = bf16[256,256]{1,0:T(8,128)(2,1)S(1)} copy-done((bf16[256,256]{1,0:T(8,128)(2,1)S(1)}, bf16[256,256]{1,0:T(8,128)(2,1)}, u32[]{:S(2)}) %copy-start.6) | copy-done | bytes 131096
  14.8 1.3 %measured_images.1 = (bf16[256,384]{1,0:T(8,128)(2,1)S(1)}, bf16[2,288,128]{2,1,0:T(8,128)(2,1)S(1)}, bf16[2,96,288]{2,1,0:T(8,128)(2,1)S(1)}, bf16[2,96,288]{2,...) custom-call(bf16[128,640]{1,0:T(8,128)(2,1)S(1)} %bitcast.22, ...), custom_call_target="tpu_custom_call" | custom-call | flops 301989888 | bytes 2340096 | tf_op jit(solution)/shard_map/measured_images/pallas_call | solution.py:478
  16.1 2.9 %all-to-all-done.sent_ref = bf16[16,48,128]{2,1,0:T(8,128)(2,1)S(1)} async-done(((bf16[16,48,128]{2,1,0:T(8,128)(2,1)}), bf16[16,48,128]{2,1,0:T(8,128)(2,1)S(1)}, u32[]{:S(2)}, u32[]{:S(2)}) %all-to-all-start) | async-done | bytes 196640 | tf_op jit(solution)/shard_map/all_to_all | solution.py:536
  19.0 1.3 %combine_rows.1 = (bf16[16,2,16,128]{3,2,1,0:T(8,128)(2,1)S(1)}, bf16[256,384]{1,0:T(8,128)(2,1)S(1)}) custom-call(bf16[16,48,128]{2,1,0:T(8,128)(2,1)S(1)} %all-to-all-done.sent_ref, bf16[256,384]{1,0:T(8,128)(2,1)S(1)} %get-tuple-element.17.images_ref, f32[16,384]{1,0:T(8,128)S(1)} %pad.12.mask_ref, bf16[384,768]{1,0:T(8,128)(2,1)S(1)} %copy-done, ...), custom_call_target="tpu_custom_call" | custom-call | flops 452984832 | bytes 1597440 | tf_op jit(solution)/shard_map/combine_rows/pallas_call | solution.py:478
  20.3 11.4 %all_to_all.20 = bf16[32,16,128]{2,1,0:T(8,128)(2,1)S(1)} all-to-all(bf16[32,16,128]{2,1,0:T(8,128)(2,1)S(1)} %bitcast.23), channel_id=1, replica_groups=mesh['section'=16,'coil'=2] {'section','coil'}, dimensions={0} | all-to-all | bytes 262144 | tf_op jit(solution)/shard_map/all_to_all | solution.py:568
  31.7 1.2 %refine_first.1 = (bf16[16,8,128]{2,1,0:T(8,128)(2,1)}, bf16[32,384]{1,0:T(8,128)(2,1)S(1)}) custom-call(bf16[16,2,16,128]{3,2,1,0:T(8,128)(2,1)S(1)} %bitcast.19, bf16[2,288,128]{2,1,0:T(8,128)(2,1)S(1)} %get-tuple-element.19.first_ref, bf16[2,96,288]{2,1,0:T(8,128)(2,1)S(1)} %get-tuple-element.20.second_ref, f32[288,128]{1,0:T(8,128)S(1)} %get-tuple-element.16.columns_ref), custom_call_target="tpu_custom_call" | custom-call | flops 56623104 | bytes 593920 | tf_op jit(solution)/shard_map/refine_first/pallas_call | solution.py:478
  32.9 3.6 %all-to-all-start.2 = ((bf16[16,8,128]{2,1,0:T(8,128)(2,1)}), bf16[16,8,128]{2,1,0:T(8,128)(2,1)S(1)}, u32[]{:S(2)}, u32[]{:S(2)}) async-start(bf16[16,8,128]{2,1,0:T(8,128)(2,1)} %get-tuple-element.21), calls=%async_computation.2 | async-start | bytes 65536 | tf_op jit(solution)/shard_map/all_to_all | solution.py:580
  36.6 0.0 copy-start.7
  36.6 1.5 %refine_and_back.1 = (f32[32,384]{1,0:T(8,128)S(1)}, f32[32,384]{1,0:T(8,128)S(1)}) custom-call(bf16[16,2,16,128]{3,2,1,0:T(8,128)(2,1)S(1)} %bitcast.20, bf16[32,384]{1,0:T(8,128)(2,1)S(1)} %get-tuple-element.23.model_ref, bf16[16,640]{1,0:T(8,128)(2,1)S(1)} %bitcast.26, bf16[2,288,128]{2,1,0:T(8,128)(2,1)S(1)} %get-tuple-element.19.first_ref, ...), custom_call_target="tpu_custom_call" | custom-call | flops 198180864 | bytes 937984 | tf_op jit(solution)/shard_map/refine_and_back/pallas_call | solution.py:478
  38.1 5.1 %all-to-all-done.2.sent_ref = bf16[16,8,128]{2,1,0:T(8,128)(2,1)S(1)} async-done(((bf16[16,8,128]{2,1,0:T(8,128)(2,1)}), bf16[16,8,128]{2,1,0:T(8,128)(2,1)S(1)}, u32[]{:S(2)}, u32[]{:S(2)}) %all-to-all-start.2) | async-done | bytes 32800 | tf_op jit(solution)/shard_map/all_to_all | solution.py:580
  43.2 1.1 %masked_normal.1 = bf16[16,2,16,128]{3,2,1,0:T(8,128)(2,1)S(1)} custom-call(bf16[16,8,128]{2,1,0:T(8,128)(2,1)S(1)} %all-to-all-done.2.sent_ref, bf16[256,384]{1,0:T(8,128)(2,1)S(1)} %get-tuple-element.22.maps_ref, f32[32,384]{1,0:T(8,128)S(1)} %get-tuple-element.26.spread_ref, f32[16,384]{1,0:T(8,128)S(1)} %pad.12.mask_ref, bf16[384,768]{1,0:T(8,128)(2,1)S(1)} %copy-done, ...), custom_call_target="tpu_custom_call" | custom-call | flops 452984832 | bytes 1286144 | tf_op jit(solution)/shard_map/masked_normal/pallas_call | solution.py:478
  44.3 10.3 %all_to_all.21 = bf16[32,16,128]{2,1,0:T(8,128)(2,1)S(1)} all-to-all(bf16[32,16,128]{2,1,0:T(8,128)(2,1)S(1)} %bitcast.24), channel_id=1, replica_groups=mesh['section'=16,'coil'=2] {'section','coil'}, dimensions={0} | all-to-all | bytes 262144 | tf_op jit(solution)/shard_map/all_to_all | solution.py:610
  54.6 1.6 %outputs.1 = (f32[16,640]{1,0:T(8,128)}, f32[640,128]{1,0:T(8,128)}) custom-call(f32[288,128]{1,0:T(8,128)S(1)} %get-tuple-element.16.columns_ref, bf16[16,2,16,128]{3,2,1,0:T(8,128)(2,1)S(1)} %bitcast.21, f32[32,384]{1,0:T(8,128)S(1)} %get-tuple-element.27.image_ref, bf16[256,384]{1,0:T(8,128)(2,1)S(1)} %get-tuple-element.22.maps_ref, ...), custom_call_target="tpu_custom_call" | custom-call | flops 301989888 | bytes 1638400 | tf_op jit(solution)/shard_map/outputs/pallas_call | solution.py:478
  (19 shorter events, 0.1 us)
Async XLA Ops:
  0.6 11.4 %copy-start = (bf16[384,768]{1,0:T(8,128)(2,1)S(1)}, bf16[384,768]{1,0:T(8,128)(2,1)}, u32[]{:S(2)}) copy-start(bf16[384,768]{1,0:T(8,128)(2,1)} %constant.15.clone.table_ref) | copy-start | bytes 1769476
  0.6 9.4 %copy-start.10 = (f32[2,2]{1,0:T(2,128)S(1)}, f32[2,2]{1,0:T(2,128)}, u32[]{:S(2)}) copy-start(f32[2,2]{1,0:T(2,128)} %param.22) | copy-start | bytes 52
  0.7 9.4 %copy-start.11 = (f32[2,18]{1,0:T(2,128)S(1)}, f32[2,18]{1,0:T(2,128)}, u32[]{:S(2)}) copy-start(f32[2,18]{1,0:T(2,128)} %param.20) | copy-start | bytes 436
  0.7 11.2 %copy-start.12 = (f32[2]{0:T(128)S(1)}, f32[2]{0:T(128)}, u32[]{:S(2)}) copy-start(f32[2]{0:T(128)} %param.18) | copy-start | bytes 28
  2.5 9.6 %copy-start.1 = (bf16[128,1536]{1,0:T(8,128)(2,1)S(1)}, bf16[128,1536]{1,0:T(8,128)(2,1)}, u32[]{:S(2)}) copy-start(bf16[128,1536]{1,0:T(8,128)(2,1)} %constant.19.clone.place_ref) | copy-start | bytes 1179652
  2.5 16.5 %all-to-all-start = ((bf16[16,48,128]{2,1,0:T(8,128)(2,1)}), bf16[16,48,128]{2,1,0:T(8,128)(2,1)S(1)}, u32[]{:S(2)}, u32[]{:S(2)}) async-start(bf16[16,48,128]{2,1,0:T(8,128)(2,1)} %pack_maps.1), calls=%async_computation | async-start | bytes 393216 | tf_op jit(solution)/shard_map/all_to_all | solution.py:536
  10.2 1.8 %copy-start.9 = (s32[2,8,320]{2,1,0:T(8,128)S(1)}, s32[2,8,320]{2,1,0:T(8,128)}, u32[]{:S(2)}) copy-start(s32[2,8,320]{2,1,0:T(8,128)} %param.17) | copy-start | bytes 61444
  10.9 1.1 %copy-start.2 = (bf16[8,16,1,640]{3,1,2,0:T(8,128)(2,1)S(1)}, bf16[8,16,1,640]{3,1,2,0:T(8,128)(2,1)}, u32[]{:S(2)}) copy-start(bf16[8,16,1,640]{3,1,2,0:T(8,128)(2,1)} %param.15) | copy-start | bytes 491524
  12.1 0.9 %copy-start.3 = (f32[288,128]{1,0:T(8,128)S(1)}, f32[288,128]{1,0:T(8,128)}, u32[]{:S(2)}) copy-start(f32[288,128]{1,0:T(8,128)} %constant.20.clone.offset_ref) | copy-start | bytes 442372
  13.0 0.9 %copy-start.4 = (f32[288,18]{1,0:T(8,128)S(1)}, f32[288,18]{1,0:T(8,128)}, u32[]{:S(2)}) copy-start(f32[288,18]{1,0:T(8,128)} %constant.18.clone.repeat_ref) | copy-start | bytes 62212
  13.9 0.9 %copy-start.6 = (bf16[256,256]{1,0:T(8,128)(2,1)S(1)}, bf16[256,256]{1,0:T(8,128)(2,1)}, u32[]{:S(2)}) copy-start(bf16[256,256]{1,0:T(8,128)(2,1)} %constant.17.clone.plus_ref) | copy-start | bytes 393220
  14.8 4.2 %copy-start.5 = (bf16[256,256]{1,0:T(8,128)(2,1)S(1)}, bf16[256,256]{1,0:T(8,128)(2,1)}, u32[]{:S(2)}) copy-start(bf16[256,256]{1,0:T(8,128)(2,1)} %constant.16.clone.minus_ref) | copy-start | bytes 393220
  32.9 3.6 %copy-start.8 = (bf16[1,16,640]{2,1,0:T(8,128)(2,1)S(1)}, bf16[1,16,640]{2,1,0:T(8,128)(2,1)}, u32[]{:S(2)}) copy-start(bf16[1,16,640]{2,1,0:T(8,128)(2,1)} %param.23) | copy-start | bytes 61444
  32.9 10.2 %all-to-all-start.2 = ((bf16[16,8,128]{2,1,0:T(8,128)(2,1)}), bf16[16,8,128]{2,1,0:T(8,128)(2,1)S(1)}, u32[]{:S(2)}, u32[]{:S(2)}) async-start(bf16[16,8,128]{2,1,0:T(8,128)(2,1)} %get-tuple-element.21), calls=%async_computation.2 | async-start | bytes 65536 | tf_op jit(solution)/shard_map/all_to_all | solution.py:580
  36.6 6.6 %copy-start.7 = (bf16[256,256]{1,0:T(8,128)(2,1)S(1)}, bf16[256,256]{1,0:T(8,128)(2,1)}, u32[]{:S(2)}) copy-start(bf16[256,256]{1,0:T(8,128)(2,1)} %constant.17.clone.plus_ref) | copy-start | bytes 393220

commit v3 on v2

--- a/solution.py
+++ b/solution.py
@@ -14,7 +14,7 @@
 VOLUMES = 2
 LANES = 128
 VMEM_BYTES = 48 * 1024 * 1024
-PACK_VMEM_BYTES = 60 * 1024 * 1024
+LARGE_VMEM_BYTES = 60 * 1024 * 1024
 
 F32 = jnp.float32
 BF16 = jnp.bfloat16
@@ -51,6 +51,7 @@
     groups = 6
     width = padded(groups * rows, LANES)
     repeat = np.kron(np.eye(channels), np.ones((rows, 1))).astype(np.float32)
+    repeat = np.pad(repeat, ((0, 0), (0, padded(channels, LANES) - channels)))
     taps = CASCADES * 3
     place = np.zeros((padded(2 * taps * groups + 3 * CASCADES, LANES), 2 * taps * width), np.float32)
     for kind in range(2):
@@ -132,19 +133,39 @@
     return total
 
 
-def spread(maps_real, maps_imag, real, imag, coils):
-    real, imag = over_coils(real, coils), over_coils(imag, coils)
+def over_rows(parts, coils):
+    return jnp.concatenate([part for part in parts for coil in range(coils)], axis=0)
+
+
+def spread(maps_real, maps_imag, real, imag):
     return jnp.concatenate(
         [maps_real * real - maps_imag * imag, maps_real * imag + maps_imag * real], axis=0
     )
 
 
-def collect(maps_real, maps_imag, images, coils):
+def collect(maps_real, maps_imag, images):
     real, imag = halves(images)
-    return (
-        coil_sum(maps_real * real + maps_imag * imag, coils),
-        coil_sum(maps_real * imag - maps_imag * real, coils),
-    )
+    return maps_real * real + maps_imag * imag, maps_real * imag - maps_imag * real
+
+
+def blocks(value, count):
+    size = value.shape[0] // count
+    return [value[index * size : (index + 1) * size] for index in range(count)]
+
+
+def row_sums(value, rows, coils):
+    return [coil_sum(part, coils) for part in blocks(value, rows)]
+
+
+def pick(parts, index):
+    chosen = parts[0]
+    for place in range(1, len(parts)):
+        chosen = jnp.where(index == place, parts[place], chosen)
+    return chosen
+
+
+def own_volume(depth):
+    return lax.div(lax.axis_index("section"), jnp.int32(depth))
 
 
 def masked_normal(images, table_ref, minus_ref, plus_ref, mask):
@@ -217,44 +238,77 @@
     return value.astype(BF16).astype(F32)
 
 
-def pack_kernel(coils, rows, pitch, maps_ref, image_ref, out_ref, scratch):
+def pack_kernel(coils, depth, pitch, maps_ref, image_ref, out_ref, scratch):
+    rows = image_ref.shape[0]
+    count = maps_ref.shape[1] // LANES
     scratch[...] = jnp.zeros_like(scratch)
-    count = maps_ref.shape[1] // LANES
-    for coil in range(coils):
-        value = maps_ref[coil * rows : (coil + 1) * rows, :].astype(F32)
-        write_rows(scratch, pitch, lane_chunks(value), coil * count)
-    write_rows(scratch, pitch, lane_chunks(image_ref[...].astype(F32)), coils * count)
+    image = image_ref[...].astype(F32)
+    for coil in range(coils + 1):
+        value = maps_ref[coil * rows : (coil + 1) * rows, :].astype(F32) if coil < coils else image
+        for place, part in enumerate(blocks(value, rows // depth)):
+            first = (place * (coils + 1) + coil) * count
+            write_rows(scratch, pitch, lane_chunks(part), first)
     out_ref[...] = scratch[...].astype(BF16).reshape(out_ref.shape)
 
 
-def begin_kernel(
-    coils,
-    lines,
+def images_kernel(coils, lines, volumes, mask_ref, table_ref, plus_ref, *refs):
+    depth = mask_ref.shape[0] // volumes
+    volume = own_volume(depth)
+    arrivals = []
+    for ref in refs[:volumes]:
+        parts = blocks(ref[...].astype(F32), coils * volumes)
+        arrivals.append(
+            jnp.concatenate(
+                [pick(parts[coil * volumes : (coil + 1) * volumes], volume) for coil in range(coils)],
+                axis=0,
+            )
+        )
+    ordered = []
+    for place in range(volumes):
+        step = lax.rem(volume - place + volumes, jnp.int32(volumes))
+        ordered.append(pick(arrivals, step))
+    kspace = jnp.concatenate(ordered, axis=0)
+    mask = over_coils(pick(blocks(mask_ref[...], volumes), volume), volumes * coils)
+    real, imag = split_complex(lane_chunks(kspace), lines)
+    measured = jnp.concatenate([real * mask, imag * mask], axis=0)
+    images = line_apply(depth_apply(measured, plus_ref), table_ref, 1.0)
+    refs[volumes][...] = images.astype(BF16)
+
+
+def taps_kernel(
     rows,
-    kspace_ref,
-    mask_ref,
-    table_ref,
-    plus_ref,
-    taps_ref,
+    weight_ref,
+    kernel_in_ref,
+    kernel_out_ref,
+    bias_in_ref,
+    bias_out_ref,
     repeat_ref,
     place_ref,
     offset_ref,
-    images_ref,
     first_ref,
     first_t_ref,
     second_ref,
     second_t_ref,
     columns_ref,
+    taps,
 ):
-    real, imag = split_complex(lane_chunks(kspace_ref[...].astype(F32)), lines)
-    mask = over_coils(mask_ref[...], coils)
-    measured = jnp.concatenate([real * mask, imag * mask], axis=0)
-    images = line_apply(depth_apply(measured, plus_ref), table_ref, 1.0)
-    images_ref[...] = images.astype(BF16)
-
-    tall = jnp.dot(
+    taps[...] = jnp.zeros_like(taps)
+    channels = kernel_in_ref.shape[2]
+    at = 0
+    for ref in (kernel_in_ref, kernel_out_ref):
+        for index in range(ref.shape[0]):
+            taps[at : at + 2, :channels] = ref[index]
+            at += 2
+    taps[at : at + CASCADES, :channels] = bias_in_ref[...]
+    at += CASCADES
+    for cascade in range(CASCADES):
+        taps[at : at + 1, :] = jnp.full((1, taps.shape[1]), weight_ref[cascade], F32)
+        at += 1
+    taps[at : at + CASCADES, : bias_out_ref.shape[1]] = bias_out_ref[...]
+    tall = lax.dot_general(
         repeat_ref[...],
-        taps_ref[...],
+        taps[...],
+        (((1,), (1,)), ((), ())),
         precision=lax.Precision.HIGHEST,
         preferred_element_type=F32,
     )
@@ -275,9 +329,8 @@
 
 def rows_kernel(
     coils,
-    slots,
     lines,
-    pitch,
+    volumes,
     sent_ref,
     images_ref,
     mask_ref,
@@ -286,31 +339,46 @@
     plus_ref,
     out_ref,
     maps_ref,
-    arrived,
-    leaving,
+    *refs,
 ):
+    handed, (arrived, leaving) = refs[: volumes - 1], refs[volumes - 1 :]
+    depth, pitch = sent_ref.shape[:2]
+    volume = own_volume(depth)
     arrived[...] = sent_ref[...].astype(F32).reshape(arrived.shape)
     count = 2 * lines // LANES
-    parts = [
-        split_complex(read_rows(arrived, pitch, coil * count, count, slots), lines)
-        for coil in range(coils)
-    ]
+    parts, reals, imags = [], [], []
+    for place in range(volumes):
+        first = place * (coils + 1) * count
+        for coil in range(coils):
+            chunks = read_rows(arrived, pitch, first + coil * count, count, depth)
+            parts.append(split_complex(chunks, lines))
+        chunks = read_rows(arrived, pitch, first + coils * count, count, depth)
+        real, imag = split_complex(chunks, lines)
+        reals.append(real)
+        imags.append(imag)
     maps_real = jnp.concatenate([part[0] for part in parts], axis=0)
     maps_imag = jnp.concatenate([part[1] for part in parts], axis=0)
     maps_ref[...] = jnp.concatenate([maps_real, maps_imag], axis=0).astype(BF16)
-    real, imag = split_complex(read_rows(arrived, pitch, coils * count, count, slots), lines)
-    mask = over_coils(mask_ref[...], 2 * coils)
-    images = spread(maps_real, maps_imag, real, imag, coils)
+    real_parts, imag_parts = blocks(maps_real, volumes), blocks(maps_imag, volumes)
+    for step, ref in enumerate(handed, 1):
+        place = lax.rem(volume + step, jnp.int32(volumes))
+        both = [pick(real_parts, place), pick(imag_parts, place)]
+        ref[...] = jnp.concatenate(both, axis=0).astype(BF16)
+
+    mask = over_coils(pick(blocks(mask_ref[...], volumes), volume), 2 * volumes * coils)
+    images = spread(maps_real, maps_imag, over_rows(reals, coils), over_rows(imags, coils))
     images = masked_normal(images, table_ref, minus_ref, plus_ref, mask)
-    turned = collect(maps_real, maps_imag, images, coils)
-    begun = collect(maps_real, maps_imag, images_ref[...].astype(F32), coils)
-    power = coil_sum(maps_real * maps_real + maps_imag * maps_imag, coils)
+    found = [
+        *collect(maps_real, maps_imag, images_ref[...].astype(F32)),
+        *collect(maps_real, maps_imag, images),
+        maps_real * maps_real + maps_imag * maps_imag,
+    ]
     leaving[...] = jnp.zeros_like(leaving)
-    values = []
-    for value in (*begun, *turned, power):
-        values += lane_chunks(value)
-    write_rows(leaving, out_ref.shape[2], values)
-    message = leaving[...].astype(BF16).reshape(slots, *out_ref.shape[2:])
+    sums = [row_sums(value, volumes, coils) for value in found]
+    for place in range(volumes):
+        chunks = [chunk for value in sums for chunk in lane_chunks(value[place])]
+        write_rows(leaving, out_ref.shape[2], chunks, place * len(chunks))
+    message = leaving[...].astype(BF16).reshape(depth, *out_ref.shape[2:])
     for device in range(out_ref.shape[1]):
         out_ref[:, device] = message
 
@@ -322,19 +390,41 @@
     scratch[...] = total.reshape(scratch.shape)
 
 
-def read_pair(scratch, pitch, first, count, rows):
-    real = jnp.concatenate(read_rows(scratch, pitch, first, count, rows), axis=1)
-    imag = jnp.concatenate(read_rows(scratch, pitch, first + count, count, rows), axis=1)
+def read_image(scratch, pitch, first, count, depth):
+    return jnp.concatenate(read_rows(scratch, pitch, first, count, depth), axis=1)
+
+
+def read_places(scratch, pitch, first, period, count, depth, volumes):
+    parts = [
+        read_image(scratch, pitch, first + place * period, count, depth) for place in range(volumes)
+    ]
+    return jnp.concatenate(parts, axis=0)
+
+
+def read_complex(scratch, pitch, first, period, count, depth, volumes):
+    real = read_places(scratch, pitch, first, period, count, depth, volumes)
+    imag = read_places(scratch, pitch, first + count, period, count, depth, volumes)
     return jnp.concatenate([real, imag], axis=0)
 
 
 def first_refine_kernel(
-    lines, rows, sent_ref, first_ref, second_ref, columns_ref, out_ref, model_ref, arrived, leaving
+    lines,
+    volumes,
+    sent_ref,
+    first_ref,
+    second_ref,
+    columns_ref,
+    out_ref,
+    model_ref,
+    arrived,
+    leaving,
 ):
     unpack_sum(sent_ref, arrived)
+    depth, pitch = sent_ref.shape[0], sent_ref.shape[2]
+    rows = depth * volumes
     width = padded(lines, LANES)
     count = width // LANES
-    picture = round_bf(read_pair(arrived, sent_ref.shape[2], 0, count, rows))
+    picture = round_bf(read_complex(arrived, pitch, 0, 5 * count, count, depth, volumes))
     hidden = hidden_state(picture, first_ref.at[0], column(columns_ref, 0, first_ref.shape[1]))
     valid = valid_lanes(hidden.shape[0], width, lines)
     hidden = hidden * jax.nn.sigmoid(hidden)
@@ -343,13 +433,15 @@
     model_ref[...] = model.astype(BF16)
     leaving[...] = jnp.zeros_like(leaving)
     real, imag = halves(model)
-    write_rows(leaving, out_ref.shape[1], lane_chunks(real) + lane_chunks(imag))
+    for place, pair in enumerate(zip(blocks(real, volumes), blocks(imag, volumes))):
+        chunks = lane_chunks(pair[0]) + lane_chunks(pair[1])
+        write_rows(leaving, out_ref.shape[1], chunks, place * len(chunks))
     out_ref[...] = leaving[...].astype(BF16).reshape(out_ref.shape)
 
 
 def slots_kernel(
     lines,
-    rows,
+    volumes,
     sent_ref,
     model_ref,
     cotangent_ref,
@@ -363,12 +455,13 @@
     arrived,
 ):
     unpack_sum(sent_ref, arrived)
+    depth, pitch = sent_ref.shape[0], sent_ref.shape[2]
+    rows = depth * volumes
     width = padded(lines, LANES)
     count = width // LANES
-    pitch = sent_ref.shape[2]
-    begun = read_pair(arrived, pitch, 0, count, rows)
-    turned = read_pair(arrived, pitch, 2 * count, count, rows)
-    power = jnp.concatenate(read_rows(arrived, pitch, 4 * count, count, rows), axis=1)
+    begun = read_complex(arrived, pitch, 0, 5 * count, count, depth, volumes)
+    turned = read_complex(arrived, pitch, 2 * count, 5 * count, count, depth, volumes)
+    power = read_places(arrived, pitch, 4 * count, 5 * count, count, depth, volumes)
     power = jnp.concatenate([power, power], axis=0)
     cotangent = jnp.concatenate(
         split_complex(lane_chunks(cotangent_ref[...].astype(F32)), lines), axis=0
@@ -411,7 +504,8 @@
 
 def normal_kernel(
     coils,
-    slots,
+    lines,
+    volumes,
     sent_ref,
     maps_ref,
     spread_ref,
@@ -424,62 +518,97 @@
     leaving,
 ):
     arrived[...] = sent_ref[...].astype(F32).reshape(arrived.shape)
+    depth, pitch = sent_ref.shape[:2]
+    volume = own_volume(depth)
     count = maps_ref.shape[1] // LANES
-    real, imag = halves(read_pair(arrived, sent_ref.shape[1], 0, count, slots))
+    firsts = [place * 2 * count for place in range(volumes)]
+    reals = [read_image(arrived, pitch, first, count, depth) for first in firsts]
+    imags = [read_image(arrived, pitch, first + count, count, depth) for first in firsts]
     maps_real, maps_imag = halves(maps_ref[...].astype(F32))
-    mask = over_coils(mask_ref[...], 2 * coils)
-    images = spread(maps_real, maps_imag, real, imag, coils)
+    mask = over_coils(pick(blocks(mask_ref[...], volumes), volume), 2 * volumes * coils)
+    images = spread(maps_real, maps_imag, over_rows(reals, coils), over_rows(imags, coils))
     images = masked_normal(images, table_ref, minus_ref, plus_ref, mask)
+    found = [row_sums(value, volumes, coils) for value in collect(maps_real, maps_imag, images)]
     leaving[...] = jnp.zeros_like(leaving)
-    values = []
-    for value in (*collect(maps_real, maps_imag, images, coils), *halves(spread_ref[...])):
-        values += lane_chunks(value)
-    write_rows(leaving, out_ref.shape[2], values)
-    message = leaving[...].astype(BF16).reshape(slots, *out_ref.shape[2:])
+    pitch = out_ref.shape[2]
+    first = 0
+    for place in range(volumes):
+        chunks = join_complex(found[0][place], found[1][place], lines)
+        for target in range(volumes):
+            kept = [jnp.where(volume == target, chunk, 0.0) for chunk in chunks]
+            write_rows(leaving, pitch, kept, target * depth * pitch + first)
+        first += len(chunks)
+    write_rows(leaving, pitch, join_complex(*halves(spread_ref[...]), lines), first)
+    message = leaving[...].astype(BF16).reshape(out_ref.shape[0], *out_ref.shape[2:])
     for device in range(out_ref.shape[1]):
         out_ref[:, device] = message
 
 
 def end_kernel(
     coils,
-    slots,
     lines,
+    volumes,
     columns_ref,
     sent_ref,
     image_ref,
-    maps_ref,
     mask_ref,
     table_ref,
     minus_ref,
-    picture_ref,
-    grad_ref,
-    arrived,
+    maps_ref,
+    *refs,
 ):
-    count = maps_ref.shape[1] // LANES
-    pitch = sent_ref.shape[2]
+    handed, (picture_ref, grad_ref, arrived) = refs[: volumes - 1], refs[volumes - 1 :]
+    slots, pitch = sent_ref.shape[0], sent_ref.shape[2]
+    depth = slots // volumes
+    volume = own_volume(depth)
+    count = 2 * lines // LANES
+    own = maps_ref[...].astype(F32)
+    sources = [[pick(blocks(part, volumes), volume) for part in halves(own)]]
+    sources += [halves(ref[...].astype(F32)) for ref in handed]
+    maps = []
+    for part in range(2):
+        ordered = []
+        for place in range(volumes):
+            step = lax.rem(volume - place + volumes, jnp.int32(volumes))
+            ordered.append(blocks(pick([source[part] for source in sources], step), coils))
+        maps.append(
+            jnp.concatenate([ordered[v][coil] for coil in range(coils) for v in range(volumes)], 0)
+        )
     arrived[...] = sent_ref[:, 0].astype(F32).reshape(arrived.shape)
-    real, imag = halves(read_pair(arrived, pitch, 2 * count, count, slots))
-    maps_real, maps_imag = halves(maps_ref[...].astype(F32))
-    images = spread(maps_real, maps_imag, real, imag, coils)
+    chunks = read_rows(arrived, pitch, volumes * count, count, slots)
+    real, imag = split_complex(chunks, lines)
+    images = spread(*maps, over_coils(real, coils), over_coils(imag, coils))
     spectrum = depth_apply(line_apply(images, table_ref, -1.0), minus_ref)
     spectrum = spectrum * over_coils(mask_ref[...], 2 * coils)
     chunks = join_complex(*halves(spectrum), lines)
     write_rows(grad_ref, len(chunks), chunks)
 
     unpack_sum(sent_ref, arrived)
-    turned = read_pair(arrived, pitch, 0, count, slots)
-    picture = image_ref[...] - column(columns_ref, CASCADES + 1, turned.shape[0]) * turned
+    picture = image_ref[...]
+    scale = column(columns_ref, CASCADES + 1, picture.shape[0])
+    parts = [[], []]
+    size = depth * pitch
+    total = arrived[:size]
+    for other in range(1, volumes):
+        total = total + arrived[other * size : (other + 1) * size]
+    arrived[:size] = total
+    for place in range(volumes):
+        chunks = read_rows(arrived, pitch, place * count, count, depth)
+        for part, value in zip(parts, split_complex(chunks, lines)):
+            part.append(value)
+    picture = picture - scale * jnp.concatenate(parts[0] + parts[1], axis=0)
     for index, chunk in enumerate(join_complex(*halves(picture), lines)):
         picture_ref[:, index * LANES : (index + 1) * LANES] = chunk
 
 
-def call(kernel, name, operands, outs, scratch, flops, vmem_bytes=VMEM_BYTES):
+def call(kernel, name, operands, outs, scratch, flops, vmem_bytes=VMEM_BYTES, scalars=0):
+    spaces = [pltpu.SMEM] * scalars + [pltpu.VMEM] * (len(operands) - scalars)
     moved = sum(math.prod(item.shape) * item.dtype.itemsize for item in (*operands, *outs))
     return pl.pallas_call(
         kernel,
         name=name,
         out_shape=tuple(outs),
-        in_specs=[pl.BlockSpec(memory_space=pltpu.VMEM) for item in operands],
+        in_specs=[pl.BlockSpec(memory_space=space) for space in spaces],
         out_specs=tuple(pl.BlockSpec(memory_space=pltpu.VMEM) for item in outs),
         scratch_shapes=[pltpu.VMEM(shape, F32) for shape in scratch],
         compiler_params=pltpu.CompilerParams(vmem_limit_bytes=vmem_bytes),
@@ -494,93 +623,116 @@
     rows, two_lines = coil_maps.shape[2:]
     lines = two_lines // 2
     channels = bias_in.shape[1]
-    coil_devices = lax.axis_size("coil")
+    coil_devices, sections = lax.axis_size("coil"), lax.axis_size("section")
+    volumes = VOLUMES
+    depth = slots // volumes
     width = padded(lines, LANES)
-    count = width // LANES
+    count, whole_count = width // LANES, two_lines // LANES
     planes = coils * slots
     both = ("section", "coil")
+    near = [[group * depth + t for t in range(depth)] for group in range(volumes)]
+    span = depth * coil_devices
+    near_both = [[group * span + t for t in range(span)] for group in range(volumes)]
+
+    def from_group(value, step):
+        shift = step * depth
+        return lax.ppermute(value, "section", [(s, (s + shift) % sections) for s in range(sections)])
+
+    def exchange(value, axes, groups):
+        return lax.all_to_all(value, axes, 0, 0, tiled=True, axis_index_groups=groups)
 
     table = jnp.asarray(line_constant(lines))
-    minus = jnp.asarray(depth_constant(coils, slots, VOLUMES, -1.0))
-    plus = jnp.asarray(depth_constant(coils, slots, VOLUMES, 1.0))
+    minus = jnp.asarray(depth_constant(coils, slots, volumes, -1.0))
+    plus = jnp.asarray(depth_constant(coils, slots, volumes, 1.0))
     repeat, place, offset = (jnp.asarray(item) for item in conv_constants(rows, channels))
     mask = sampling.astype(F32).reshape(slots, lines)
     mask = jnp.pad(mask, ((0, 0), (0, width - lines)))
-    taps = jnp.concatenate(
-        [
-            kernel_in.transpose(2, 0, 1, 3).reshape(channels, -1),
-            kernel_out.transpose(3, 0, 1, 2).reshape(channels, -1),
-            bias_in.T,
-            jnp.broadcast_to(dc_weight[None, :], (channels, CASCADES)),
-            jnp.pad(bias_out.T, ((0, channels - bias_out.shape[1]), (0, 0))),
-        ],
-        axis=1,
-    )
-    taps = jnp.pad(taps, ((0, 0), (0, place.shape[0] - taps.shape[1])))
 
     def shape(*dims, kind=F32):
         return jax.ShapeDtypeStruct(dims, kind)
 
     line_flops = 2 * (2 * planes) * width * (2 * width)
 
-    pitch = padded((coils + 1) * (two_lines // LANES), 16)
+    pitch = padded(volumes * (coils + 1) * whole_count, 16)
     (packed,) = call(
-        functools.partial(pack_kernel, coils, rows, pitch),
+        functools.partial(pack_kernel, coils, depth, pitch),
         "pack_maps",
         (coil_maps.reshape(coils * rows, two_lines), cotangent.reshape(rows, two_lines)),
-        [shape(rows, pitch, LANES, kind=BF16)],
-        [(rows * pitch, LANES)],
+        [shape(depth, pitch, LANES, kind=BF16)],
+        [(depth * pitch, LANES)],
         1000,
-        PACK_VMEM_BYTES,
-    )
-    arrived = lax.all_to_all(packed, "section", 0, 0, tiled=True)
-
+        LARGE_VMEM_BYTES,
+    )
+    samples = kspace.reshape(planes, two_lines)
+    arrivals = [samples] + [from_group(samples, step) for step in range(1, volumes)]
+    arrived = exchange(packed, "section", near)
+
+    (images,) = call(
+        functools.partial(images_kernel, coils, lines, volumes),
+        "measured_images",
+        (mask, table, plus, *arrivals),
+        [shape(2 * planes, width, kind=BF16)],
+        [],
+        2 * line_flops,
+    )
+
+    depth_pitch = padded(volumes * 5 * count, 16)
+    partial, maps, *handed = call(
+        functools.partial(rows_kernel, coils, lines, volumes),
+        "combine_rows",
+        (arrived, images, mask, table, minus, plus),
+        [
+            shape(depth, coil_devices, depth_pitch, LANES, kind=BF16),
+            shape(2 * planes, width, kind=BF16),
+        ]
+        + [shape(2 * planes // volumes, width, kind=BF16)] * (volumes - 1),
+        [(depth * pitch, LANES), (depth * depth_pitch, LANES)],
+        3 * line_flops,
+    )
+    kernel_in, kernel_out, partial = lax.optimization_barrier((kernel_in, kernel_out, partial))
     tall, wide = channels * rows, offset.shape[1]
-    images, first, first_t, second, second_t, columns = call(
-        functools.partial(begin_kernel, coils, lines, rows),
-        "measured_images",
-        (kspace.reshape(planes, two_lines), mask, table, plus, taps, repeat, place, offset),
+    first, first_t, second, second_t, columns = call(
+        functools.partial(taps_kernel, rows),
+        "lay_out_taps",
+        (
+            dc_weight,
+            kernel_in.transpose(0, 1, 3, 2).reshape(-1, 2, channels),
+            kernel_out.reshape(-1, 2, channels),
+            bias_in,
+            bias_out,
+            repeat,
+            place,
+            offset,
+        ),
         [
-            shape(2 * planes, width, kind=BF16),
             shape(CASCADES, tall, wide, kind=BF16),
             shape(CASCADES, 6 * rows, tall, kind=BF16),
             shape(CASCADES, 6 * rows, tall, kind=BF16),
             shape(CASCADES, tall, wide, kind=BF16),
             shape(tall, place.shape[0]),
         ],
-        [],
-        2 * line_flops,
-    )
-
-    depth_pitch = padded(5 * count, 16)
-    partial, maps = call(
-        functools.partial(rows_kernel, coils, slots, lines, pitch),
-        "combine_rows",
-        (arrived, images, mask, table, minus, plus),
-        [
-            shape(slots, coil_devices, depth_pitch, LANES, kind=BF16),
-            shape(2 * planes, width, kind=BF16),
-        ],
-        [(slots * pitch, LANES), (slots * depth_pitch, LANES)],
-        3 * line_flops,
-    )
-    partial = partial.reshape(slots * coil_devices, depth_pitch, LANES)
-    partial = lax.all_to_all(partial, both, 0, 0, tiled=True)
-    partial = partial.reshape(rows, coil_devices, depth_pitch, LANES)
-
-    model_pitch = padded(2 * count, 8)
+        [(place.shape[0], repeat.shape[1])],
+        2 * tall * place.shape[0] * place.shape[1],
+        LARGE_VMEM_BYTES,
+        1,
+    )
+    partial = exchange(partial.reshape(-1, depth_pitch, LANES), both, near_both)
+    partial = partial.reshape(depth, coil_devices, depth_pitch, LANES)
+    handed = [from_group(value, step) for step, value in enumerate(handed, 1)]
+
+    model_pitch = padded(volumes * 2 * count, 16)
     moved, model = call(
-        functools.partial(first_refine_kernel, lines, rows),
+        functools.partial(first_refine_kernel, lines, volumes),
         "refine_first",
         (partial, first, second, columns),
-        [shape(rows, model_pitch, LANES, kind=BF16), shape(2 * rows, width, kind=BF16)],
-        [(rows * depth_pitch, LANES), (rows * model_pitch, LANES)],
+        [shape(depth, model_pitch, LANES, kind=BF16), shape(2 * rows, width, kind=BF16)],
+        [(depth * depth_pitch, LANES), (depth * model_pitch, LANES)],
         4 * tall * wide * width,
     )
-    moved = lax.all_to_all(moved, "section", 0, 0, tiled=True)
+    moved = exchange(moved, "section", near)
 
     image, pulled = call(
-        functools.partial(slots_kernel, lines, rows),
+        functools.partial(slots_kernel, lines, volumes),
         "refine_and_back",
         (
             partial,
@@ -593,29 +745,28 @@
             columns,
         ),
         [shape(2 * rows, width), shape(2 * rows, width)],
-        [(rows * depth_pitch, LANES)],
+        [(depth * depth_pitch, LANES)],
         14 * tall * wide * width,
     )
 
-    end_pitch = padded(4 * count, 16)
+    end_pitch = padded((volumes + 1) * whole_count, 16)
     (partial,) = call(
-        functools.partial(normal_kernel, coils, slots),
+        functools.partial(normal_kernel, coils, lines, volumes),
         "masked_normal",
         (moved, maps, pulled, mask, table, minus, plus),
         [shape(slots, coil_devices, end_pitch, LANES, kind=BF16)],
-        [(slots * model_pitch, LANES), (slots * end_pitch, LANES)],
+        [(depth * model_pitch, LANES), (slots * end_pitch, LANES)],
         3 * line_flops,
     )
-    partial = partial.reshape(slots * coil_devices, end_pitch, LANES)
-    partial = lax.all_to_all(partial, both, 0, 0, tiled=True)
-    partial = partial.reshape(rows, coil_devices, end_pitch, LANES)
+    partial = exchange(partial.reshape(-1, end_pitch, LANES), both, None)
+    partial = partial.reshape(slots, coil_devices, end_pitch, LANES)
 
     image, grad = call(
-        functools.partial(end_kernel, coils, slots, lines),
+        functools.partial(end_kernel, coils, lines, volumes),
         "outputs",
-        (columns, partial, image, maps, mask, table, minus),
-        [shape(rows, two_lines), shape(planes * (two_lines // LANES), LANES)],
-        [(rows * end_pitch, LANES)],
+        (columns, partial, image, mask, table, minus, maps, *handed),
+        [shape(rows, two_lines), shape(planes * whole_count, LANES)],
+        [(slots * end_pitch, LANES)],
         2 * line_flops,
     )
     return image.reshape(1, rows, two_lines), grad.reshape(coils, slots, 1, two_lines)

time: 56.7 us -> 62.7 us (1.11)
  blocking collectives: 21.7 us -> 0 us
  waiting for transfers between devices: 8.05 us -> 21.2 us
  starting transfers between devices: 11.1 us -> 22.1 us
  Pallas kernels: 9.67 us -> 13.6 us
  local copies, waits for them, and re-layouts: 4.72 us -> 3.68 us
  other arithmetic: 0.01 us -> 0.74 us
    all_to_all x2 -> x0, blocking collectives: 21.7 us -> none  [body(): partial = lax.all_to_all(partial, both, 0, 0, tiled=True)]
    ppermute x0 -> x2, waiting for transfers between devices: none -> 15.7 us  [from_group(): lax.ppermute(value, 'section', [(s, (s + shift) % sections) for s in rang...]
    all_to_all x2 -> x4, starting transfers between devices: 11.1 us -> 16.7 us  [exchange(): lax.all_to_all(value, axes, 0, 0, tiled=True, axis_index_groups=groups)]
    ppermute x0 -> x2, starting transfers between devices: none -> 5.39 us  [from_group(): lax.ppermute(value, 'section', [(s, (s + shift) % sections) for s in rang...]
    pallas_call x7 -> x8, Pallas kernels: 9.67 us -> 13.6 us  [call(): pl.pallas_call(kernel, name=name, out_shape=tuple(outs), in_specs=[pl.Blo...]
    all_to_all x2 -> x4, waiting for transfers between devices: 8.05 us -> 5.5 us  [exchange(): lax.all_to_all(value, axes, 0, 0, tiled=True, axis_index_groups=groups)]
    reshape x4 -> x0, local copies, waits for them, and re-layouts: 1.66 us -> none  [the longest x2 0.83 us: body(): kernel_in.transpose(2, 0, 1, 3).reshape(channels, -1)]
    reshape x1, other arithmetic: 0.01 us -> 0.74 us  [body(): mask = sampling.astype(F32).reshape(slots, lines)]
  transfers between devices with their start and end apart: 2 -> 6, of which waited for: 2 -> 4; matrix products, arithmetic and copies ran while one was open for 3% -> 1% of each run, Pallas kernels for 5% -> 8%
where the time goes in v3:
time: 62.7 us; the launch traced here: 62.1 us
  starting transfers between devices  22.1 us (35%)
  waiting for transfers between devices  21.2 us (34%)
  Pallas kernels  13.6 us (22%)
  local copies, waits for them, and re-layouts  3.68 us (6%)
  between operations  0.76 us (1%)
  other arithmetic  0.74 us (1%)
    all_to_all x4, starting transfers between devices, exchange(): lax.all_to_all(value, axes, 0, 0, tiled=True, axis_index_groups=groups)  16.7 us
    ppermute x2, waiting for transfers between devices, from_group(): lax.ppermute(value, 'section', [(s, (s + shift) % sections) for s in rang...  15.7 us
    pallas_call x8, Pallas kernels, call(): pl.pallas_call(kernel, name=name, out_shape=tuple(outs), in_specs=[pl.Blo...  13.6 us
    all_to_all x4, waiting for transfers between devices, exchange(): lax.all_to_all(value, axes, 0, 0, tiled=True, axis_index_groups=groups)  5.5 us
    ppermute x2, starting transfers between devices, from_group(): lax.ppermute(value, 'section', [(s, (s + shift) % sections) for s in rang...  5.39 us
    unnamed x26, local copies, waits for them, and re-layouts  3.67 us
  transfers between devices with their start and end apart: 6, of which 4 were waited for; matrix products, arithmetic and copies ran while one was open for 1% of the time, Pallas kernels for 8%

profile of v3, /device:TPU:0, one launch (start us, length us, event | category | flops | bytes accessed | tf_op | source)
XLA Modules:
  0.0 62.1 jit_solution(9214578408936300463)
XLA Ops:
  0.6 0.0 copy-start
  0.6 1.9 %pack_maps.1 = bf16[8,96,128]{2,1,0:T(8,128)(2,1)} custom-call(bf16[128,640]{1,0:T(8,128)(2,1)} %bitcast.22, bf16[16,640]{1,0:T(8,128)(2,1)} %bitcast.20), custom_call_target="tpu_custom_call" | custom-call | flops 1000 | bytes 380928 | tf_op jit(solution)/shard_map/pack_maps/pallas_call | solution.py:607
  2.6 5.4 %all-to-all-start = ((bf16[8,96,128]{2,1,0:T(8,128)(2,1)}), bf16[8,96,128]{2,1,0:T(8,128)(2,1)S(1)}, u32[]{:S(2)}, u32[]{:S(2)}) async-start(bf16[8,96,128]{2,1,0:T(8,128)(2,1)} %pack_maps.1), calls=%async_computation | async-start | bytes 393216 | tf_op jit(solution)/shard_map/all_to_all | solution.py:642
  7.9 2.7 %collective-permute-start = (bf16[128,640]{1,0:T(8,128)(2,1)S(1)}, bf16[128,640]{1,0:T(8,128)(2,1)S(1)}, u32[]{:S(2)}, u32[]{:S(2)}) collective-permute-start(bf16[128,640]{1,0:T(8,128)(2,1)S(1)} %bitcast.18), channel_id=1, source_target_pairs={{0,16},{2,18},{4,20},{6,22},{8,24},{10,26},{12,28},{14,30},{16,0},... | collective-permute-start | bytes 491528 | tf_op jit(solution)/shard_map/ppermute | solution.py:639
  10.6 0.7 %convert_bitcast_fusion = f32[16,320]{1,0:T(8,128)S(1)} fusion(s32[2,8,320]{2,1,0:T(8,128)} %param.17), kind=kLoop, calls=%fused_computation | loop fusion | flops 5120 | bytes 40960 | tf_op jit(solution)/shard_map/reshape | solution.py:648
  11.4 7.7 %collective-permute-done.refs_1_ = bf16[128,640]{1,0:T(8,128)(2,1)S(1)} collective-permute-done((bf16[128,640]{1,0:T(8,128)(2,1)S(1)}, bf16[128,640]{1,0:T(8,128)(2,1)S(1)}, u32[]{:S(2)}, u32[]{:S(2)}) %collective-permute-start) | collective-permute-done | bytes 163872 | tf_op jit(solution)/shard_map/ppermute | solution.py:639
  19.0 0.6 measured_images.1.images_ref
  19.6 0.0 all-to-all-done.sent_ref
  19.7 2.1 %combine_rows.1 = (bf16[8,2,32,128]{3,2,1,0:T(8,128)(2,1)}, bf16[256,384]{1,0:T(8,128)(2,1)S(1)}, bf16[128,384]{1,0:T(8,128)(2,1)S(1)}) custom-call(bf16[8,96,128]{2,1,0:T(8,128)(2,1)S(1)} %all-to-all-done.sent_ref, bf16[256,384]{1,0:T(8,128)(2,1)S(1)} %measured_images.1.images_ref, f32[16,384]{1,0:T(8,128)S(1)} %pad.4.mask_ref, ...), custom_call_target="tpu_custom_call" | custom-call | flops 452984832 | bytes 1695744 | tf_op jit(solution)/shard_map/combine_rows/pallas_call | solution.py:607
  21.8 4.0 %all-to-all-start.1 = ((bf16[16,32,128]{2,1,0:T(8,128)(2,1)}), bf16[16,32,128]{2,1,0:T(8,128)(2,1)S(1)}, u32[]{:S(2)}, u32[]{:S(2)}) async-start(bf16[16,32,128]{2,1,0:T(8,128)(2,1)} %bitcast.7), calls=%async_computation.1 | async-start | bytes 262144 | tf_op jit(solution)/shard_map/all_to_all | solution.py:642
  25.8 2.8 %lay_out_taps.1 = (bf16[2,288,128]{2,1,0:T(8,128)(2,1)}, bf16[2,96,288]{2,1,0:T(8,128)(2,1)}, bf16[2,96,288]{2,1,0:T(8,128)(2,1)}, bf16[2,288,128]{2,1,0:T(8,128)(2,1)}, f32[288,128]{1,0:T(8,128)}) custom-call(f32[2]{0:T(128)} %weight_ref.1, f32[18,2,18]{2,1,0:T(2,128)} %bitcast.23, f32[18,2,18]{2,1,0:T(2,128)} %bitcast.24, f32[2,18]{1,0:T(2,128)} %bias_in_ref.1, ...), custom_call_target="tpu_custom_call" | custom-call | flops 113246208 | bytes 1357032 | tf_op jit(solution)/shard_map/lay_out_taps/pallas_call | solution.py:607
  28.6 3.2 %all-to-all-done.1 = bf16[16,32,128]{2,1,0:T(8,128)(2,1)S(1)} async-done(((bf16[16,32,128]{2,1,0:T(8,128)(2,1)}), bf16[16,32,128]{2,1,0:T(8,128)(2,1)S(1)}, u32[]{:S(2)}, u32[]{:S(2)}) %all-to-all-start.1) | async-done | bytes 131104 | tf_op jit(solution)/shard_map/all_to_all | solution.py:642
  31.9 0.9 %copy-done.1 = f32[288,128]{1,0:T(8,128)S(1)} copy-done((f32[288,128]{1,0:T(8,128)S(1)}, f32[288,128]{1,0:T(8,128)}, u32[]{:S(2)}) %copy-start.1) | copy-done | bytes 147480
  32.8 0.9 %copy-done.3 = bf16[2,288,128]{2,1,0:T(8,128)(2,1)S(1)} copy-done((bf16[2,288,128]{2,1,0:T(8,128)(2,1)S(1)}, bf16[2,288,128]{2,1,0:T(8,128)(2,1)}, u32[]{:S(2)}) %copy-start.3) | copy-done | bytes 147480
  33.7 0.9 %copy-done.5 = bf16[2,96,288]{2,1,0:T(8,128)(2,1)S(1)} copy-done((bf16[2,96,288]{2,1,0:T(8,128)(2,1)S(1)}, bf16[2,96,288]{2,1,0:T(8,128)(2,1)}, u32[]{:S(2)}) %copy-start.5) | copy-done | bytes 110616
  34.6 1.2 %refine_first.1 = (bf16[8,16,128]{2,1,0:T(8,128)(2,1)}, bf16[32,384]{1,0:T(8,128)(2,1)S(1)}) custom-call(bf16[8,2,32,128]{3,2,1,0:T(8,128)(2,1)S(1)} %bitcast.15, bf16[2,288,128]{2,1,0:T(8,128)(2,1)S(1)} %copy-done.3, bf16[2,96,288]{2,1,0:T(8,128)(2,1)S(1)} %copy-done.5, f32[288,128]{1,0:T(8,128)S(1)} %copy-done.1), custom_call_target="tpu_custom_call" | custom-call | flops 56623104 | bytes 593920 | tf_op jit(solution)/shard_map/refine_first/pallas_call | solution.py:607
  35.8 3.5 %all-to-all-start.2 = ((bf16[8,16,128]{2,1,0:T(8,128)(2,1)}), bf16[8,16,128]{2,1,0:T(8,128)(2,1)S(1)}, u32[]{:S(2)}, u32[]{:S(2)}) async-start(bf16[8,16,128]{2,1,0:T(8,128)(2,1)} %get-tuple-element.26), calls=%async_computation.2 | async-start | bytes 65536 | tf_op jit(solution)/shard_map/all_to_all | solution.py:642
  39.3 0.0 copy-done.2
  39.3 0.0 copy-done.4
  39.3 0.0 copy-done.6
  39.4 0.0 copy-done.8
  39.4 0.0 copy-done.12
  39.4 0.0 copy-start.9
  39.4 0.9 %copy-done.9 = bf16[2,288,128]{2,1,0:T(8,128)(2,1)S(1)} copy-done((bf16[2,288,128]{2,1,0:T(8,128)(2,1)S(1)}, bf16[2,288,128]{2,1,0:T(8,128)(2,1)}, u32[]{:S(2)}) %copy-start.9) | copy-done | bytes 147480
  40.3 1.5 %refine_and_back.1 = (f32[32,384]{1,0:T(8,128)S(1)}, f32[32,384]{1,0:T(8,128)S(1)}) custom-call(bf16[8,2,32,128]{3,2,1,0:T(8,128)(2,1)S(1)} %bitcast.16, bf16[32,384]{1,0:T(8,128)(2,1)S(1)} %get-tuple-element.28.model_ref, bf16[16,640]{1,0:T(8,128)(2,1)S(1)} %bitcast.21, bf16[2,288,128]{2,1,0:T(8,128)(2,1)S(1)} %copy-done.4, ...), custom_call_target="tpu_custom_call" | custom-call | flops 198180864 | bytes 937984 | tf_op jit(solution)/shard_map/refine_and_back/pallas_call | solution.py:607
  41.8 2.3 %all-to-all-done.2.sent_ref = bf16[8,16,128]{2,1,0:T(8,128)(2,1)S(1)} async-done(((bf16[8,16,128]{2,1,0:T(8,128)(2,1)}), bf16[8,16,128]{2,1,0:T(8,128)(2,1)S(1)}, u32[]{:S(2)}, u32[]{:S(2)}) %all-to-all-start.2) | async-done | bytes 32800 | tf_op jit(solution)/shard_map/all_to_all | solution.py:642
  44.0 1.8 %masked_normal.1 = bf16[16,2,16,128]{3,2,1,0:T(8,128)(2,1)} custom-call(bf16[8,16,128]{2,1,0:T(8,128)(2,1)S(1)} %all-to-all-done.2.sent_ref, bf16[256,384]{1,0:T(8,128)(2,1)S(1)} %get-tuple-element.27.maps_ref, f32[32,384]{1,0:T(8,128)S(1)} %get-tuple-element.31.spread_ref, f32[16,384]{1,0:T(8,128)S(1)} %pad.4.mask_ref, bf16[384,768]{1,0:T(8,128)(2,1)S(1)} %copy-done, ...), custom_call_target="tpu_custom_call" | custom-call | flops 452984832 | bytes 1286144 | tf_op jit(solution)/shard_map/masked_normal/pallas_call | solution.py:607
  45.8 3.8 %all-to-all-start.3 = ((bf16[32,16,128]{2,1,0:T(8,128)(2,1)}), bf16[32,16,128]{2,1,0:T(8,128)(2,1)S(1)}, u32[]{:S(2)}, u32[]{:S(2)}) async-start(bf16[32,16,128]{2,1,0:T(8,128)(2,1)} %bitcast.9), calls=%async_computation.3 | async-start | bytes 262144 | tf_op jit(solution)/shard_map/all_to_all | solution.py:642
  49.7 2.7 %collective-permute-start.1 = (bf16[128,384]{1,0:T(8,128)(2,1)S(1)}, bf16[128,384]{1,0:T(8,128)(2,1)S(1)}, u32[]{:S(2)}, u32[]{:S(2)}) collective-permute-start(bf16[128,384]{1,0:T(8,128)(2,1)S(1)} %get-tuple-element.33), channel_id=1, source_target_pairs={{0,16},{2,18},{4,20},{6,22},{8,24},{10,26},{12,28},{14,30},{16,0},... | collective-permute-start | bytes 294920 | tf_op jit(solution)/shard_map/ppermute | solution.py:639
  52.4 8.0 %collective-permute-done.1.refs_0_ = bf16[128,384]{1,0:T(8,128)(2,1)S(1)} collective-permute-done((bf16[128,384]{1,0:T(8,128)(2,1)S(1)}, bf16[128,384]{1,0:T(8,128)(2,1)S(1)}, u32[]{:S(2)}, u32[]{:S(2)}) %collective-permute-start.1) | collective-permute-done | bytes 98336 | tf_op jit(solution)/shard_map/ppermute | solution.py:639
  60.5 0.0 all-to-all-done.3
  60.5 1.6 %outputs.1 = (f32[16,640]{1,0:T(8,128)}, f32[640,128]{1,0:T(8,128)}) custom-call(f32[288,128]{1,0:T(8,128)S(1)} %copy-done.2, bf16[16,2,16,128]{3,2,1,0:T(8,128)(2,1)S(1)} %bitcast.17, f32[32,384]{1,0:T(8,128)S(1)} %get-tuple-element.32.image_ref, f32[16,384]{1,0:T(8,128)S(1)} %pad.4.mask_ref, bf16[384,768]{1,0:T(8,128)(2,1)S(1)} %copy-done, ...), custom_call_target="tpu_custom_call" | custom-call | flops 301989888 | bytes 1736704 | tf_op jit(solution)/shard_map/outputs/pallas_call | solution.py:607
  (16 shorter events, 0.0 us)
Async XLA Ops:
  0.6 18.4 %copy-start = (bf16[384,768]{1,0:T(8,128)(2,1)S(1)}, bf16[384,768]{1,0:T(8,128)(2,1)}, u32[]{:S(2)}) copy-start(bf16[384,768]{1,0:T(8,128)(2,1)} %constant.15.clone.table_ref) | copy-start | bytes 1769476
  2.6 5.4 %copy-start.7 = (bf16[8,16,1,640]{3,1,2,0:T(8,128)(2,1)S(1)}, bf16[8,16,1,640]{3,1,2,0:T(8,128)(2,1)}, u32[]{:S(2)}) copy-start(bf16[8,16,1,640]{3,1,2,0:T(8,128)(2,1)} %param.15) | copy-start | bytes 491524
  2.6 16.5 %copy-start.10 = (bf16[256,256]{1,0:T(8,128)(2,1)S(1)}, bf16[256,256]{1,0:T(8,128)(2,1)}, u32[]{:S(2)}) copy-start(bf16[256,256]{1,0:T(8,128)(2,1)} %constant.17.clone.plus_ref) | copy-start | bytes 393220
  2.6 17.1 %all-to-all-start = ((bf16[8,96,128]{2,1,0:T(8,128)(2,1)}), bf16[8,96,128]{2,1,0:T(8,128)(2,1)S(1)}, u32[]{:S(2)}, u32[]{:S(2)}) async-start(bf16[8,96,128]{2,1,0:T(8,128)(2,1)} %pack_maps.1), calls=%async_computation | async-start | bytes 393216 | tf_op jit(solution)/shard_map/all_to_all | solution.py:642
  7.9 11.1 %collective-permute-start = (bf16[128,640]{1,0:T(8,128)(2,1)S(1)}, bf16[128,640]{1,0:T(8,128)(2,1)S(1)}, u32[]{:S(2)}, u32[]{:S(2)}) collective-permute-start(bf16[128,640]{1,0:T(8,128)(2,1)S(1)} %bitcast.18), channel_id=1, source_target_pairs={{0,16},{2,18},{4,20},{6,22},{8,24},{10,26},{12,28},{14,30},{16,0},... | collective-permute-start | bytes 491528 | tf_op jit(solution)/shard_map/ppermute | solution.py:639
  11.4 8.3 %copy-start.11 = (bf16[256,256]{1,0:T(8,128)(2,1)S(1)}, bf16[256,256]{1,0:T(8,128)(2,1)}, u32[]{:S(2)}) copy-start(bf16[256,256]{1,0:T(8,128)(2,1)} %constant.16.clone.minus_ref) | copy-start | bytes 393220
  21.8 10.1 %all-to-all-start.1 = ((bf16[16,32,128]{2,1,0:T(8,128)(2,1)}), bf16[16,32,128]{2,1,0:T(8,128)(2,1)S(1)}, u32[]{:S(2)}, u32[]{:S(2)}) async-start(bf16[16,32,128]{2,1,0:T(8,128)(2,1)} %bitcast.7), calls=%async_computation.1 | async-start | bytes 262144 | tf_op jit(solution)/shard_map/all_to_all | solution.py:642
  31.9 0.9 %copy-start.1 = (f32[288,128]{1,0:T(8,128)S(1)}, f32[288,128]{1,0:T(8,128)}, u32[]{:S(2)}) copy-start(f32[288,128]{1,0:T(8,128)} %get-tuple-element.22.columns_ref) | copy-start | bytes 442372
  32.8 0.9 %copy-start.3 = (bf16[2,288,128]{2,1,0:T(8,128)(2,1)S(1)}, bf16[2,288,128]{2,1,0:T(8,128)(2,1)}, u32[]{:S(2)}) copy-start(bf16[2,288,128]{2,1,0:T(8,128)(2,1)} %get-tuple-element.24.first_ref) | copy-start | bytes 442372
  33.7 0.9 %copy-start.5 = (bf16[2,96,288]{2,1,0:T(8,128)(2,1)S(1)}, bf16[2,96,288]{2,1,0:T(8,128)(2,1)}, u32[]{:S(2)}) copy-start(bf16[2,96,288]{2,1,0:T(8,128)(2,1)} %get-tuple-element.25.second_ref) | copy-start | bytes 331780
  34.6 4.7 %copy-start.2 = (f32[288,128]{1,0:T(8,128)S(1)}, f32[288,128]{1,0:T(8,128)}, u32[]{:S(2)}) copy-start(f32[288,128]{1,0:T(8,128)} %get-tuple-element.22.columns_ref) | copy-start | bytes 442372
  34.6 4.7 %copy-start.4 = (bf16[2,288,128]{2,1,0:T(8,128)(2,1)S(1)}, bf16[2,288,128]{2,1,0:T(8,128)(2,1)}, u32[]{:S(2)}) copy-start(bf16[2,288,128]{2,1,0:T(8,128)(2,1)} %get-tuple-element.24.first_ref) | copy-start | bytes 442372
  34.6 4.7 %copy-start.6 = (bf16[2,96,288]{2,1,0:T(8,128)(2,1)S(1)}, bf16[2,96,288]{2,1,0:T(8,128)(2,1)}, u32[]{:S(2)}) copy-start(bf16[2,96,288]{2,1,0:T(8,128)(2,1)} %get-tuple-element.25.second_ref) | copy-start | bytes 331780
  34.6 4.7 %copy-start.8 = (bf16[2,96,288]{2,1,0:T(8,128)(2,1)S(1)}, bf16[2,96,288]{2,1,0:T(8,128)(2,1)}, u32[]{:S(2)}) copy-start(bf16[2,96,288]{2,1,0:T(8,128)(2,1)} %get-tuple-element.29.first_t_ref) | copy-start | bytes 331780
  35.8 3.5 %copy-start.12 = (bf16[1,16,640]{2,1,0:T(8,128)(2,1)S(1)}, bf16[1,16,640]{2,1,0:T(8,128)(2,1)}, u32[]{:S(2)}) copy-start(bf16[1,16,640]{2,1,0:T(8,128)(2,1)} %param.23) | copy-start | bytes 61444
  35.8 8.2 %all-to-all-start.2 = ((bf16[8,16,128]{2,1,0:T(8,128)(2,1)}), bf16[8,16,128]{2,1,0:T(8,128)(2,1)S(1)}, u32[]{:S(2)}, u32[]{:S(2)}) async-start(bf16[8,16,128]{2,1,0:T(8,128)(2,1)} %get-tuple-element.26), calls=%async_computation.2 | async-start | bytes 65536 | tf_op jit(solution)/shard_map/all_to_all | solution.py:642
  39.4 0.9 %copy-start.9 = (bf16[2,288,128]{2,1,0:T(8,128)(2,1)S(1)}, bf16[2,288,128]{2,1,0:T(8,128)(2,1)}, u32[]{:S(2)}) copy-start(bf16[2,288,128]{2,1,0:T(8,128)(2,1)} %get-tuple-element.30.second_t_ref) | copy-start | bytes 442372
  45.8 14.6 %all-to-all-start.3 = ((bf16[32,16,128]{2,1,0:T(8,128)(2,1)}), bf16[32,16,128]{2,1,0:T(8,128)(2,1)S(1)}, u32[]{:S(2)}, u32[]{:S(2)}) async-start(bf16[32,16,128]{2,1,0:T(8,128)(2,1)} %bitcast.9), calls=%async_computation.3 | async-start | bytes 262144 | tf_op jit(solution)/shard_map/all_to_all | solution.py:642
  49.7 10.8 %collective-permute-start.1 = (bf16[128,384]{1,0:T(8,128)(2,1)S(1)}, bf16[128,384]{1,0:T(8,128)(2,1)S(1)}, u32[]{:S(2)}, u32[]{:S(2)}) collective-permute-start(bf16[128,384]{1,0:T(8,128)(2,1)S(1)} %get-tuple-element.33), channel_id=1, source_target_pairs={{0,16},{2,18},{4,20},{6,22},{8,24},{10,26},{12,28},{14,30},{16,0},... | collective-permute-start | bytes 294920 | tf_op jit(solution)/shard_map/ppermute | solution.py:639

commit v4 on v3

--- a/solution.py
+++ b/solution.py
@@ -238,14 +238,27 @@
     return value.astype(BF16).astype(F32)
 
 
-def pack_kernel(coils, depth, pitch, maps_ref, image_ref, out_ref, scratch):
+def choose_volume(value, coils, volumes, volume):
+    parts = blocks(value, coils * volumes)
+    chosen = [pick(parts[coil * volumes : (coil + 1) * volumes], volume) for coil in range(coils)]
+    return jnp.concatenate(chosen, axis=0)
+
+
+def pack_kernel(coils, volumes, pitch, kspace_ref, maps_ref, image_ref, out_ref, *refs):
+    handed, (scratch,) = refs[:-1], refs[-1:]
     rows = image_ref.shape[0]
+    depth = rows // volumes
+    volume = own_volume(depth)
+    kspace = kspace_ref[...].astype(F32)
+    for step, ref in enumerate(handed):
+        other = lax.rem(volume + step, jnp.int32(volumes))
+        ref[...] = choose_volume(kspace, coils, volumes, other).astype(BF16)
     count = maps_ref.shape[1] // LANES
     scratch[...] = jnp.zeros_like(scratch)
     image = image_ref[...].astype(F32)
     for coil in range(coils + 1):
         value = maps_ref[coil * rows : (coil + 1) * rows, :].astype(F32) if coil < coils else image
-        for place, part in enumerate(blocks(value, rows // depth)):
+        for place, part in enumerate(blocks(value, volumes)):
             first = (place * (coils + 1) + coil) * count
             write_rows(scratch, pitch, lane_chunks(part), first)
     out_ref[...] = scratch[...].astype(BF16).reshape(out_ref.shape)
@@ -254,15 +267,7 @@
 def images_kernel(coils, lines, volumes, mask_ref, table_ref, plus_ref, *refs):
     depth = mask_ref.shape[0] // volumes
     volume = own_volume(depth)
-    arrivals = []
-    for ref in refs[:volumes]:
-        parts = blocks(ref[...].astype(F32), coils * volumes)
-        arrivals.append(
-            jnp.concatenate(
-                [pick(parts[coil * volumes : (coil + 1) * volumes], volume) for coil in range(coils)],
-                axis=0,
-            )
-        )
+    arrivals = [ref[...].astype(F32) for ref in refs[:volumes]]
     ordered = []
     for place in range(volumes):
         step = lax.rem(volume - place + volumes, jnp.int32(volumes))
@@ -277,7 +282,9 @@
 
 def taps_kernel(
     rows,
+    volumes,
     weight_ref,
+    maps_ref,
     kernel_in_ref,
     kernel_out_ref,
     bias_in_ref,
@@ -290,8 +297,15 @@
     second_ref,
     second_t_ref,
     columns_ref,
-    taps,
+    *refs,
 ):
+    handed, (taps,) = refs[:-1], refs[-1:]
+    volume = own_volume(rows // volumes)
+    maps = blocks(maps_ref[...].astype(F32), 2 * volumes)
+    for step, ref in enumerate(handed, 1):
+        place = lax.rem(volume + step, jnp.int32(volumes))
+        both = [pick(maps[:volumes], place), pick(maps[volumes:], place)]
+        ref[...] = jnp.concatenate(both, axis=0).astype(BF16)
     taps[...] = jnp.zeros_like(taps)
     channels = kernel_in_ref.shape[2]
     at = 0
@@ -339,9 +353,9 @@
     plus_ref,
     out_ref,
     maps_ref,
-    *refs,
+    arrived,
+    leaving,
 ):
-    handed, (arrived, leaving) = refs[: volumes - 1], refs[volumes - 1 :]
     depth, pitch = sent_ref.shape[:2]
     volume = own_volume(depth)
     arrived[...] = sent_ref[...].astype(F32).reshape(arrived.shape)
@@ -359,11 +373,6 @@
     maps_real = jnp.concatenate([part[0] for part in parts], axis=0)
     maps_imag = jnp.concatenate([part[1] for part in parts], axis=0)
     maps_ref[...] = jnp.concatenate([maps_real, maps_imag], axis=0).astype(BF16)
-    real_parts, imag_parts = blocks(maps_real, volumes), blocks(maps_imag, volumes)
-    for step, ref in enumerate(handed, 1):
-        place = lax.rem(volume + step, jnp.int32(volumes))
-        both = [pick(real_parts, place), pick(imag_parts, place)]
-        ref[...] = jnp.concatenate(both, axis=0).astype(BF16)
 
     mask = over_coils(pick(blocks(mask_ref[...], volumes), volume), 2 * volumes * coils)
     images = spread(maps_real, maps_imag, over_rows(reals, coils), over_rows(imags, coils))
@@ -654,17 +663,22 @@
     line_flops = 2 * (2 * planes) * width * (2 * width)
 
     pitch = padded(volumes * (coils + 1) * whole_count, 16)
-    (packed,) = call(
-        functools.partial(pack_kernel, coils, depth, pitch),
+    packed, *samples = call(
+        functools.partial(pack_kernel, coils, volumes, pitch),
         "pack_maps",
-        (coil_maps.reshape(coils * rows, two_lines), cotangent.reshape(rows, two_lines)),
-        [shape(depth, pitch, LANES, kind=BF16)],
+        (
+            kspace.reshape(planes, two_lines),
+            coil_maps.reshape(coils * rows, two_lines),
+            cotangent.reshape(rows, two_lines),
+        ),
+        [shape(depth, pitch, LANES, kind=BF16)]
+        + [shape(coils * depth, two_lines, kind=BF16)] * volumes,
         [(depth * pitch, LANES)],
         1000,
         LARGE_VMEM_BYTES,
     )
-    samples = kspace.reshape(planes, two_lines)
-    arrivals = [samples] + [from_group(samples, step) for step in range(1, volumes)]
+    arrivals = samples[:1]
+    arrivals += [from_group(value, step) for step, value in enumerate(samples[1:], 1)]
     arrived = exchange(packed, "section", near)
 
     (images,) = call(
@@ -677,25 +691,25 @@
     )
 
     depth_pitch = padded(volumes * 5 * count, 16)
-    partial, maps, *handed = call(
+    partial, maps = call(
         functools.partial(rows_kernel, coils, lines, volumes),
         "combine_rows",
         (arrived, images, mask, table, minus, plus),
         [
             shape(depth, coil_devices, depth_pitch, LANES, kind=BF16),
             shape(2 * planes, width, kind=BF16),
-        ]
-        + [shape(2 * planes // volumes, width, kind=BF16)] * (volumes - 1),
+        ],
         [(depth * pitch, LANES), (depth * depth_pitch, LANES)],
         3 * line_flops,
     )
     kernel_in, kernel_out, partial = lax.optimization_barrier((kernel_in, kernel_out, partial))
     tall, wide = channels * rows, offset.shape[1]
-    first, first_t, second, second_t, columns = call(
-        functools.partial(taps_kernel, rows),
+    first, first_t, second, second_t, columns, *handed = call(
+        functools.partial(taps_kernel, rows, volumes),
         "lay_out_taps",
         (
             dc_weight,
+            maps,
             kernel_in.transpose(0, 1, 3, 2).reshape(-1, 2, channels),
             kernel_out.reshape(-1, 2, channels),
             bias_in,
@@ -710,11 +724,11 @@
             shape(CASCADES, 6 * rows, tall, kind=BF16),
             shape(CASCADES, tall, wide, kind=BF16),
             shape(tall, place.shape[0]),
-        ],
+        ]
+        + [shape(2 * planes // volumes, width, kind=BF16)] * (volumes - 1),
         [(place.shape[0], repeat.shape[1])],
         2 * tall * place.shape[0] * place.shape[1],
-        LARGE_VMEM_BYTES,
-        1,
+        scalars=1,
     )
     partial = exchange(partial.reshape(-1, depth_pitch, LANES), both, near_both)
     partial = partial.reshape(depth, coil_devices, depth_pitch, LANES)
@@ -749,6 +763,7 @@
         14 * tall * wide * width,
     )
 
+    moved, *handed = lax.optimization_barrier((moved, *handed))
     end_pitch = padded((volumes + 1) * whole_count, 16)
     (partial,) = call(
         functools.partial(normal_kernel, coils, lines, volumes),

time: 62.7 us -> 54 us (0.86)
  waiting for transfers between devices: 21.2 us -> 8.78 us
  blocking collectives: 0 us -> 11.2 us
  local copies, waits for them, and re-layouts: 3.68 us -> 0.67 us
  Pallas kernels: 13.6 us -> 11.7 us
  starting transfers between devices: 22.1 us -> 20.4 us
  other arithmetic: 0.74 us -> 0.01 us
    ppermute x2, waiting for transfers between devices: 15.7 us -> 3.4 us  [from_group(): lax.ppermute(value, 'section', [(s, (s + shift) % sections) for s in rang...]
    all_to_all x0 -> x1, blocking collectives: none -> 11.2 us  [exchange(): lax.all_to_all(value, axes, 0, 0, tiled=True, axis_index_groups=groups)]
    unnamed x26 -> x28, local copies, waits for them, and re-layouts: 3.67 us -> 0.66 us
    pallas_call x8, Pallas kernels: 13.6 us -> 11.7 us  [call(): pl.pallas_call(kernel, name=name, out_shape=tuple(outs), in_specs=[pl.Blo...]
    all_to_all x4 -> x3, starting transfers between devices: 16.7 us -> 15.4 us  [exchange(): lax.all_to_all(value, axes, 0, 0, tiled=True, axis_index_groups=groups)]
    reshape x1, other arithmetic: 0.74 us -> 0.01 us  [body(): mask = sampling.astype(F32).reshape(slots, lines)]
    all_to_all x4 -> x3, waiting for transfers between devices: 5.5 us -> 5.38 us  [exchange(): lax.all_to_all(value, axes, 0, 0, tiled=True, axis_index_groups=groups)]
  transfers between devices with their start and end apart: 6 -> 5, of which waited for: 4 -> 4; matrix products, arithmetic and copies ran while one was open for 1% -> 0% of each run, Pallas kernels for 8% -> 9%
where the time goes in v4:
time: 54 us; the launch traced here: 53.5 us
  starting transfers between devices  20.4 us (38%)
  Pallas kernels  11.7 us (22%)
  blocking collectives  11.2 us (21%)
  waiting for transfers between devices  8.78 us (16%)
  between operations  0.79 us (1%)
  local copies, waits for them, and re-layouts  0.67 us (1%)
    all_to_all x3, starting transfers between devices, exchange(): lax.all_to_all(value, axes, 0, 0, tiled=True, axis_index_groups=groups)  15.4 us
    pallas_call x8, Pallas kernels, call(): pl.pallas_call(kernel, name=name, out_shape=tuple(outs), in_specs=[pl.Blo...  11.7 us
    all_to_all x1, blocking collectives, exchange(): lax.all_to_all(value, axes, 0, 0, tiled=True, axis_index_groups=groups)  11.2 us
    all_to_all x3, waiting for transfers between devices, exchange(): lax.all_to_all(value, axes, 0, 0, tiled=True, axis_index_groups=groups)  5.38 us
    ppermute x2, starting transfers between devices, from_group(): lax.ppermute(value, 'section', [(s, (s + shift) % sections) for s in rang...  5.02 us
    ppermute x2, waiting for transfers between devices, from_group(): lax.ppermute(value, 'section', [(s, (s + shift) % sections) for s in rang...  3.4 us
  transfers between devices with their start and end apart: 5, of which 4 were waited for; matrix products, arithmetic and copies ran while one was open for 0% of the time, Pallas kernels for 9%

profile of v4, /device:TPU:0, one launch (start us, length us, event | category | flops | bytes accessed | tf_op | source)
XLA Modules:
  0.0 53.5 jit_solution(8370169259891757774)
XLA Ops:
  0.6 0.0 copy-start
  0.6 2.0 %pack_maps.1 = (bf16[8,96,128]{2,1,0:T(8,128)(2,1)}, bf16[64,640]{1,0:T(8,128)(2,1)}, bf16[64,640]{1,0:T(8,128)(2,1)}) custom-call(bf16[128,640]{1,0:T(8,128)(2,1)} %bitcast.23, bf16[128,640]{1,0:T(8,128)(2,1)} %bitcast.24, bf16[16,640]{1,0:T(8,128)(2,1)} %bitcast.19), custom_call_target="tpu_custom_call" | custom-call | flops 1000 | bytes 708608 | tf_op jit(solution)/shard_map/pack_maps/pallas_call | solution.py:616
  2.7 5.4 %all-to-all-start = ((bf16[8,96,128]{2,1,0:T(8,128)(2,1)}), bf16[8,96,128]{2,1,0:T(8,128)(2,1)S(1)}, u32[]{:S(2)}, u32[]{:S(2)}) async-start(bf16[8,96,128]{2,1,0:T(8,128)(2,1)} %get-tuple-element.24), calls=%async_computation | async-start | bytes 393216 | tf_op jit(solution)/shard_map/all_to_all | solution.py:651
  8.1 2.7 %collective-permute-start = (bf16[64,640]{1,0:T(8,128)(2,1)}, bf16[64,640]{1,0:T(8,128)(2,1)S(1)}, u32[]{:S(2)}, u32[]{:S(2)}) collective-permute-start(bf16[64,640]{1,0:T(8,128)(2,1)} %get-tuple-element.26), channel_id=1, source_target_pairs={{0,16},{2,18},{4,20},{6,22},{8,24},{10,26},{12,28},{14,30},{16,0},... | collective-permute-start | bytes 245768 | tf_op jit(solution)/shard_map/ppermute | solution.py:648
  10.7 0.0 copy-done.13
  10.8 3.4 %collective-permute-done.refs_1_ = bf16[64,640]{1,0:T(8,128)(2,1)S(1)} collective-permute-done((bf16[64,640]{1,0:T(8,128)(2,1)}, bf16[64,640]{1,0:T(8,128)(2,1)S(1)}, u32[]{:S(2)}, u32[]{:S(2)}) %collective-permute-start) | collective-permute-done | bytes 81952 | tf_op jit(solution)/shard_map/ppermute | solution.py:648
  14.2 0.0 copy-start.4
  14.2 0.6 %measured_images.1.images_ref = bf16[256,384]{1,0:T(8,128)(2,1)S(1)} custom-call(f32[16,384]{1,0:T(8,128)S(1)} %pad.4.mask_ref, bf16[384,768]{1,0:T(8,128)(2,1)S(1)} %copy-done, bf16[256,256]{1,0:T(8,128)(2,1)S(1)} %copy-done.12, bf16[64,640]{1,0:T(8,128)(2,1)S(1)} %copy-done.11, bf16[64,640]{1,0:T(8,128)(2,1)S(1)} %collective-permute-done.refs_1_), custom_call_target="tpu_custom_call" | custom-call | flops 301989888 | bytes 1105920 | tf_op jit(solution)/shard_map/measured_images/pallas_call | solution.py:616
  14.8 0.7 %all-to-all-done.sent_ref = bf16[8,96,128]{2,1,0:T(8,128)(2,1)S(1)} async-done(((bf16[8,96,128]{2,1,0:T(8,128)(2,1)}), bf16[8,96,128]{2,1,0:T(8,128)(2,1)S(1)}, u32[]{:S(2)}, u32[]{:S(2)}) %all-to-all-start) | async-done | bytes 196640 | tf_op jit(solution)/shard_map/all_to_all | solution.py:651
  15.5 0.0 copy-done.4
  15.5 2.1 %combine_rows.1 = (bf16[8,2,32,128]{3,2,1,0:T(8,128)(2,1)}, bf16[256,384]{1,0:T(8,128)(2,1)S(1)}) custom-call(bf16[8,96,128]{2,1,0:T(8,128)(2,1)S(1)} %all-to-all-done.sent_ref, bf16[256,384]{1,0:T(8,128)(2,1)S(1)} %measured_images.1.images_ref, f32[16,384]{1,0:T(8,128)S(1)} %pad.4.mask_ref, bf16[384,768]{1,0:T(8,128)(2,1)S(1)} %copy-done, ...), custom_call_target="tpu_custom_call" | custom-call | flops 452984832 | bytes 1597440 | tf_op jit(solution)/shard_map/combine_rows/pallas_call | solution.py:616
  17.6 6.5 %all-to-all-start.1 = ((bf16[16,32,128]{2,1,0:T(8,128)(2,1)}), bf16[16,32,128]{2,1,0:T(8,128)(2,1)S(1)}, u32[]{:S(2)}, u32[]{:S(2)}) async-start(bf16[16,32,128]{2,1,0:T(8,128)(2,1)} %bitcast.7), calls=%async_computation.1 | async-start | bytes 262144 | tf_op jit(solution)/shard_map/all_to_all | solution.py:651
  24.1 0.0 copy-start.8
  24.1 0.0 copy-start.10
  24.2 0.0 copy-done.1
  24.2 0.0 copy-done.3
  24.2 0.0 copy-done.2
  24.2 0.0 copy-done.6
  24.2 0.0 copy-done.7
  24.2 0.0 copy-done.9
  24.2 0.6 %copy-done.8 = f32[2,18]{1,0:T(2,128)S(1)} copy-done((f32[2,18]{1,0:T(2,128)S(1)}, f32[2,18]{1,0:T(2,128)}, u32[]{:S(2)}) %copy-start.8) | copy-done | bytes 168
  24.8 1.5 %lay_out_taps.1 = (bf16[2,288,128]{2,1,0:T(8,128)(2,1)S(1)}, bf16[2,96,288]{2,1,0:T(8,128)(2,1)S(1)}, bf16[2,96,288]{2,1,0:T(8,128)(2,1)S(1)}, bf16[2,288,128]{2...) custom-call(f32[2]{0:T(128)S(1)} %copy-done.10, ...), custom_call_target="tpu_custom_call" | custom-call | flops 113246208 | bytes 1651944 | tf_op jit(solution)/shard_map/lay_out_taps/pallas_call | solution.py:616
  26.3 2.4 %collective-permute-start.1 = (bf16[128,384]{1,0:T(8,128)(2,1)S(1)}, bf16[128,384]{1,0:T(8,128)(2,1)S(1)}, u32[]{:S(2)}, u32[]{:S(2)}) collective-permute-start(bf16[128,384]{1,0:T(8,128)(2,1)S(1)} %get-tuple-element.36), channel_id=1, source_target_pairs={{0,16},{2,18},{4,20},{6,22},{8,24},{10,26},{12,28},{14,30},{16,0},... | collective-permute-start | bytes 294920 | tf_op jit(solution)/shard_map/ppermute | solution.py:648
  28.7 1.5 %all-to-all-done.1 = bf16[16,32,128]{2,1,0:T(8,128)(2,1)S(1)} async-done(((bf16[16,32,128]{2,1,0:T(8,128)(2,1)}), bf16[16,32,128]{2,1,0:T(8,128)(2,1)S(1)}, u32[]{:S(2)}, u32[]{:S(2)}) %all-to-all-start.1) | async-done | bytes 131104 | tf_op jit(solution)/shard_map/all_to_all | solution.py:651
  30.2 1.2 %refine_first.1 = (bf16[8,16,128]{2,1,0:T(8,128)(2,1)}, bf16[32,384]{1,0:T(8,128)(2,1)S(1)}) custom-call(bf16[8,2,32,128]{3,2,1,0:T(8,128)(2,1)S(1)} %bitcast.15, bf16[2,288,128]{2,1,0:T(8,128)(2,1)S(1)} %get-tuple-element.33.first_ref, bf16[2,96,288]{2,1,0:T(8,128)(2,1)S(1)} %get-tuple-element.34.second_ref, f32[288,128]{1,0:T(8,128)S(1)} %get-tuple-element.31.columns_ref), custom_call_target="tpu_custom_call" | custom-call | flops 56623104 | bytes 593920 | tf_op jit(solution)/shard_map/refine_first/pallas_call | solution.py:616
  31.4 3.5 %all-to-all-start.2 = ((bf16[8,16,128]{2,1,0:T(8,128)(2,1)}), bf16[8,16,128]{2,1,0:T(8,128)(2,1)S(1)}, u32[]{:S(2)}, u32[]{:S(2)}) async-start(bf16[8,16,128]{2,1,0:T(8,128)(2,1)} %get-tuple-element.35), calls=%async_computation.2 | async-start | bytes 65536 | tf_op jit(solution)/shard_map/all_to_all | solution.py:651
  34.9 1.5 %refine_and_back.1 = (f32[32,384]{1,0:T(8,128)S(1)}, f32[32,384]{1,0:T(8,128)S(1)}) custom-call(bf16[8,2,32,128]{3,2,1,0:T(8,128)(2,1)S(1)} %bitcast.16, bf16[32,384]{1,0:T(8,128)(2,1)S(1)} %get-tuple-element.38.model_ref, bf16[16,640]{1,0:T(8,128)(2,1)S(1)} %bitcast.20, bf16[2,288,128]{2,1,0:T(8,128)(2,1)S(1)} %get-tuple-element.33.first_ref, ...), custom_call_target="tpu_custom_call" | custom-call | flops 198180864 | bytes 937984 | tf_op jit(solution)/shard_map/refine_and_back/pallas_call | solution.py:616
  36.4 0.0 collective-permute-done.1.refs_0_
  36.4 3.2 %all-to-all-done.2.sent_ref = bf16[8,16,128]{2,1,0:T(8,128)(2,1)S(1)} async-done(((bf16[8,16,128]{2,1,0:T(8,128)(2,1)}), bf16[8,16,128]{2,1,0:T(8,128)(2,1)S(1)}, u32[]{:S(2)}, u32[]{:S(2)}) %all-to-all-start.2) | async-done | bytes 32800 | tf_op jit(solution)/shard_map/all_to_all | solution.py:651
  39.6 1.2 %masked_normal.1 = bf16[16,2,16,128]{3,2,1,0:T(8,128)(2,1)S(1)} custom-call(bf16[8,16,128]{2,1,0:T(8,128)(2,1)S(1)} %all-to-all-done.2.sent_ref, bf16[256,384]{1,0:T(8,128)(2,1)S(1)} %get-tuple-element.27.maps_ref, f32[32,384]{1,0:T(8,128)S(1)} %get-tuple-element.41.spread_ref, f32[16,384]{1,0:T(8,128)S(1)} %pad.4.mask_ref, bf16[384,768]{1,0:T(8,128)(2,1)S(1)} %copy-done, ...), custom_call_target="tpu_custom_call" | custom-call | flops 452984832 | bytes 1286144 | tf_op jit(solution)/shard_map/masked_normal/pallas_call | solution.py:616
  40.8 11.2 %all_to_all.20 = bf16[32,16,128]{2,1,0:T(8,128)(2,1)S(1)} all-to-all(bf16[32,16,128]{2,1,0:T(8,128)(2,1)S(1)} %bitcast.18), channel_id=1, replica_groups=mesh['section'=16,'coil'=2] {'section','coil'}, dimensions={0} | all-to-all | bytes 262144 | tf_op jit(solution)/shard_map/all_to_all | solution.py:651
  52.0 1.6 %outputs.1 = (f32[16,640]{1,0:T(8,128)}, f32[640,128]{1,0:T(8,128)}) custom-call(f32[288,128]{1,0:T(8,128)S(1)} %get-tuple-element.31.columns_ref, bf16[16,2,16,128]{3,2,1,0:T(8,128)(2,1)S(1)} %bitcast.17, f32[32,384]{1,0:T(8,128)S(1)} %get-tuple-element.42.image_ref, f32[16,384]{1,0:T(8,128)S(1)} %pad.4.mask_ref, bf16[384,768]{1,0:T(8,128)(2,1)S(1)} %copy-done, ...), custom_call_target="tpu_custom_call" | custom-call | flops 301989888 | bytes 1736704 | tf_op jit(solution)/shard_map/outputs/pallas_call | solution.py:616
  (17 shorter events, 0.0 us)
Async XLA Ops:
  0.6 13.5 %copy-start = (bf16[384,768]{1,0:T(8,128)(2,1)S(1)}, bf16[384,768]{1,0:T(8,128)(2,1)}, u32[]{:S(2)}) copy-start(bf16[384,768]{1,0:T(8,128)(2,1)} %constant.15.clone.table_ref) | copy-start | bytes 1769476
  2.7 8.1 %copy-start.13 = (s32[2,8,320]{2,1,0:T(8,128)S(1)}, s32[2,8,320]{2,1,0:T(8,128)}, u32[]{:S(2)}) copy-start(s32[2,8,320]{2,1,0:T(8,128)} %param.17) | copy-start | bytes 61444
  2.7 11.5 %copy-start.12 = (bf16[256,256]{1,0:T(8,128)(2,1)S(1)}, bf16[256,256]{1,0:T(8,128)(2,1)}, u32[]{:S(2)}) copy-start(bf16[256,256]{1,0:T(8,128)(2,1)} %constant.17.clone.plus_ref) | copy-start | bytes 393220
  2.7 12.8 %all-to-all-start = ((bf16[8,96,128]{2,1,0:T(8,128)(2,1)}), bf16[8,96,128]{2,1,0:T(8,128)(2,1)S(1)}, u32[]{:S(2)}, u32[]{:S(2)}) async-start(bf16[8,96,128]{2,1,0:T(8,128)(2,1)} %get-tuple-element.24), calls=%async_computation | async-start | bytes 393216 | tf_op jit(solution)/shard_map/all_to_all | solution.py:651
  8.1 6.1 %copy-start.11 = (bf16[64,640]{1,0:T(8,128)(2,1)S(1)}, bf16[64,640]{1,0:T(8,128)(2,1)}, u32[]{:S(2)}) copy-start(bf16[64,640]{1,0:T(8,128)(2,1)} %get-tuple-element.25.refs_0_) | copy-start | bytes 245764
  8.1 6.1 %collective-permute-start = (bf16[64,640]{1,0:T(8,128)(2,1)}, bf16[64,640]{1,0:T(8,128)(2,1)S(1)}, u32[]{:S(2)}, u32[]{:S(2)}) collective-permute-start(bf16[64,640]{1,0:T(8,128)(2,1)} %get-tuple-element.26), channel_id=1, source_target_pairs={{0,16},{2,18},{4,20},{6,22},{8,24},{10,26},{12,28},{14,30},{16,0},... | collective-permute-start | bytes 245768 | tf_op jit(solution)/shard_map/ppermute | solution.py:648
  14.2 1.3 %copy-start.4 = (bf16[256,256]{1,0:T(8,128)(2,1)S(1)}, bf16[256,256]{1,0:T(8,128)(2,1)}, u32[]{:S(2)}) copy-start(bf16[256,256]{1,0:T(8,128)(2,1)} %constant.16.clone.minus_ref) | copy-start | bytes 393220
  15.5 8.7 %copy-start.1 = (bf16[128,1536]{1,0:T(8,128)(2,1)S(1)}, bf16[128,1536]{1,0:T(8,128)(2,1)}, u32[]{:S(2)}) copy-start(bf16[128,1536]{1,0:T(8,128)(2,1)} %constant.19.clone.place_ref) | copy-start | bytes 1179652
  15.5 8.7 %copy-start.3 = (f32[288,128]{1,0:T(8,128)S(1)}, f32[288,128]{1,0:T(8,128)}, u32[]{:S(2)}) copy-start(f32[288,128]{1,0:T(8,128)} %constant.18.clone.repeat_ref) | copy-start | bytes 442372
  17.6 6.6 %copy-start.2 = (f32[288,128]{1,0:T(8,128)S(1)}, f32[288,128]{1,0:T(8,128)}, u32[]{:S(2)}) copy-start(f32[288,128]{1,0:T(8,128)} %constant.20.clone.offset_ref) | copy-start | bytes 442372
  17.6 6.6 %copy-start.6 = (f32[2,9,18,2]{2,3,1,0:T(2,128)S(1)}, f32[2,9,18,2]{2,3,1,0:T(2,128)}, u32[]{:S(2)}) copy-start(f32[2,9,18,2]{2,3,1,0:T(2,128)} %param.19) | copy-start | bytes 7780
  17.6 6.6 %copy-start.7 = (f32[2,9,2,18]{3,2,1,0:T(2,128)S(1)}, f32[2,9,2,18]{3,2,1,0:T(2,128)}, u32[]{:S(2)}) copy-start(f32[2,9,2,18]{3,2,1,0:T(2,128)} %param.21) | copy-start | bytes 7780
  17.6 6.6 %copy-start.9 = (f32[2,2]{1,0:T(2,128)S(1)}, f32[2,2]{1,0:T(2,128)}, u32[]{:S(2)}) copy-start(f32[2,2]{1,0:T(2,128)} %bias_out_ref.1) | copy-start | bytes 52
  17.6 12.6 %all-to-all-start.1 = ((bf16[16,32,128]{2,1,0:T(8,128)(2,1)}), bf16[16,32,128]{2,1,0:T(8,128)(2,1)S(1)}, u32[]{:S(2)}, u32[]{:S(2)}) async-start(bf16[16,32,128]{2,1,0:T(8,128)(2,1)} %bitcast.7), calls=%async_computation.1 | async-start | bytes 262144 | tf_op jit(solution)/shard_map/all_to_all | solution.py:651
  24.1 0.7 %copy-start.8 = (f32[2,18]{1,0:T(2,128)S(1)}, f32[2,18]{1,0:T(2,128)}, u32[]{:S(2)}) copy-start(f32[2,18]{1,0:T(2,128)} %bias_in_ref.1) | copy-start | bytes 436
  24.1 0.7 %copy-start.10 = (f32[2]{0:T(128)S(1)}, f32[2]{0:T(128)}, u32[]{:S(2)}) copy-start(f32[2]{0:T(128)} %weight_ref.1) | copy-start | bytes 28
  26.3 10.0 %collective-permute-start.1 = (bf16[128,384]{1,0:T(8,128)(2,1)S(1)}, bf16[128,384]{1,0:T(8,128)(2,1)S(1)}, u32[]{:S(2)}, u32[]{:S(2)}) collective-permute-start(bf16[128,384]{1,0:T(8,128)(2,1)S(1)} %get-tuple-element.36), channel_id=1, source_target_pairs={{0,16},{2,18},{4,20},{6,22},{8,24},{10,26},{12,28},{14,30},{16,0},... | collective-permute-start | bytes 294920 | tf_op jit(solution)/shard_map/ppermute | solution.py:648
  31.4 3.5 %copy-start.5 = (bf16[1,16,640]{2,1,0:T(8,128)(2,1)S(1)}, bf16[1,16,640]{2,1,0:T(8,128)(2,1)}, u32[]{:S(2)}) copy-start(bf16[1,16,640]{2,1,0:T(8,128)(2,1)} %param.23) | copy-start | bytes 61444
  31.4 8.2 %all-to-all-start.2 = ((bf16[8,16,128]{2,1,0:T(8,128)(2,1)}), bf16[8,16,128]{2,1,0:T(8,128)(2,1)S(1)}, u32[]{:S(2)}, u32[]{:S(2)}) async-start(bf16[8,16,128]{2,1,0:T(8,128)(2,1)} %get-tuple-element.35), calls=%async_computation.2 | async-start | bytes 65536 | tf_op jit(solution)/shard_map/all_to_all | solution.py:651

commit v5 on v4

--- a/solution.py
+++ b/solution.py
@@ -250,7 +250,7 @@
     depth = rows // volumes
     volume = own_volume(depth)
     kspace = kspace_ref[...].astype(F32)
-    for step, ref in enumerate(handed):
+    for step, ref in enumerate(handed, 1):
         other = lax.rem(volume + step, jnp.int32(volumes))
         ref[...] = choose_volume(kspace, coils, volumes, other).astype(BF16)
     count = maps_ref.shape[1] // LANES
@@ -264,27 +264,9 @@
     out_ref[...] = scratch[...].astype(BF16).reshape(out_ref.shape)
 
 
-def images_kernel(coils, lines, volumes, mask_ref, table_ref, plus_ref, *refs):
-    depth = mask_ref.shape[0] // volumes
-    volume = own_volume(depth)
-    arrivals = [ref[...].astype(F32) for ref in refs[:volumes]]
-    ordered = []
-    for place in range(volumes):
-        step = lax.rem(volume - place + volumes, jnp.int32(volumes))
-        ordered.append(pick(arrivals, step))
-    kspace = jnp.concatenate(ordered, axis=0)
-    mask = over_coils(pick(blocks(mask_ref[...], volumes), volume), volumes * coils)
-    real, imag = split_complex(lane_chunks(kspace), lines)
-    measured = jnp.concatenate([real * mask, imag * mask], axis=0)
-    images = line_apply(depth_apply(measured, plus_ref), table_ref, 1.0)
-    refs[volumes][...] = images.astype(BF16)
-
-
 def taps_kernel(
     rows,
-    volumes,
     weight_ref,
-    maps_ref,
     kernel_in_ref,
     kernel_out_ref,
     bias_in_ref,
@@ -297,15 +279,8 @@
     second_ref,
     second_t_ref,
     columns_ref,
-    *refs,
+    taps,
 ):
-    handed, (taps,) = refs[:-1], refs[-1:]
-    volume = own_volume(rows // volumes)
-    maps = blocks(maps_ref[...].astype(F32), 2 * volumes)
-    for step, ref in enumerate(handed, 1):
-        place = lax.rem(volume + step, jnp.int32(volumes))
-        both = [pick(maps[:volumes], place), pick(maps[volumes:], place)]
-        ref[...] = jnp.concatenate(both, axis=0).astype(BF16)
     taps[...] = jnp.zeros_like(taps)
     channels = kernel_in_ref.shape[2]
     at = 0
@@ -341,21 +316,29 @@
             turned[cascade] = total.T[: 6 * rows].astype(BF16)
 
 
+def write_sums(scratch, pitch, first, values, volumes, coils):
+    sums = [row_sums(value, volumes, coils) for value in values]
+    period = pitch // volumes
+    for place in range(volumes):
+        chunks = [chunk for value in sums for chunk in lane_chunks(value[place])]
+        write_rows(scratch, pitch, chunks, place * period + first)
+
+
 def rows_kernel(
     coils,
     lines,
     volumes,
+    sums_pitch,
     sent_ref,
-    images_ref,
     mask_ref,
     table_ref,
     minus_ref,
     plus_ref,
-    out_ref,
     maps_ref,
-    arrived,
-    leaving,
+    sums_ref,
+    *refs,
 ):
+    handed, (arrived,) = refs[:-1], refs[-1:]
     depth, pitch = sent_ref.shape[:2]
     volume = own_volume(depth)
     arrived[...] = sent_ref[...].astype(F32).reshape(arrived.shape)
@@ -373,20 +356,50 @@
     maps_real = jnp.concatenate([part[0] for part in parts], axis=0)
     maps_imag = jnp.concatenate([part[1] for part in parts], axis=0)
     maps_ref[...] = jnp.concatenate([maps_real, maps_imag], axis=0).astype(BF16)
-
+    real_parts, imag_parts = blocks(maps_real, volumes), blocks(maps_imag, volumes)
+    for step, ref in enumerate(handed, 1):
+        place = lax.rem(volume + step, jnp.int32(volumes))
+        both = [pick(real_parts, place), pick(imag_parts, place)]
+        ref[...] = jnp.concatenate(both, axis=0).astype(BF16)
     mask = over_coils(pick(blocks(mask_ref[...], volumes), volume), 2 * volumes * coils)
     images = spread(maps_real, maps_imag, over_rows(reals, coils), over_rows(imags, coils))
     images = masked_normal(images, table_ref, minus_ref, plus_ref, mask)
-    found = [
-        *collect(maps_real, maps_imag, images_ref[...].astype(F32)),
-        *collect(maps_real, maps_imag, images),
-        maps_real * maps_real + maps_imag * maps_imag,
-    ]
-    leaving[...] = jnp.zeros_like(leaving)
-    sums = [row_sums(value, volumes, coils) for value in found]
+    sums_ref[...] = jnp.zeros_like(sums_ref)
+    power = maps_real * maps_real + maps_imag * maps_imag
+    found = [*collect(maps_real, maps_imag, images), power]
+    first = 2 * maps_ref.shape[1] // LANES
+    write_sums(sums_ref, sums_pitch, first, found, volumes, coils)
+
+
+def measured_kernel(
+    coils,
+    lines,
+    volumes,
+    kspace_ref,
+    mask_ref,
+    table_ref,
+    plus_ref,
+    maps_ref,
+    sums_ref,
+    *refs,
+):
+    arrival_refs, (out_ref, leaving) = refs[: volumes - 1], refs[volumes - 1 :]
+    depth, pitch = out_ref.shape[0], out_ref.shape[2]
+    volume = own_volume(depth)
+    arrivals = [choose_volume(kspace_ref[...].astype(F32), coils, volumes, volume)]
+    arrivals += [ref[...].astype(F32) for ref in arrival_refs]
+    ordered = []
     for place in range(volumes):
-        chunks = [chunk for value in sums for chunk in lane_chunks(value[place])]
-        write_rows(leaving, out_ref.shape[2], chunks, place * len(chunks))
+        step = lax.rem(volume - place + volumes, jnp.int32(volumes))
+        ordered.append(pick(arrivals, step))
+    mask = over_coils(pick(blocks(mask_ref[...], volumes), volume), volumes * coils)
+    real, imag = split_complex(lane_chunks(jnp.concatenate(ordered, axis=0)), lines)
+    measured = jnp.concatenate([real * mask, imag * mask], axis=0)
+    images = line_apply(depth_apply(measured, plus_ref), table_ref, 1.0)
+    maps_real, maps_imag = halves(maps_ref[...].astype(F32))
+    leaving[...] = sums_ref[...]
+    found = collect(maps_real, maps_imag, round_bf(images))
+    write_sums(leaving, pitch, 0, found, volumes, coils)
     message = leaving[...].astype(BF16).reshape(depth, *out_ref.shape[2:])
     for device in range(out_ref.shape[1]):
         out_ref[:, device] = message
@@ -433,7 +446,7 @@
     rows = depth * volumes
     width = padded(lines, LANES)
     count = width // LANES
-    picture = round_bf(read_complex(arrived, pitch, 0, 5 * count, count, depth, volumes))
+    picture = round_bf(read_complex(arrived, pitch, 0, pitch // volumes, count, depth, volumes))
     hidden = hidden_state(picture, first_ref.at[0], column(columns_ref, 0, first_ref.shape[1]))
     valid = valid_lanes(hidden.shape[0], width, lines)
     hidden = hidden * jax.nn.sigmoid(hidden)
@@ -468,9 +481,9 @@
     rows = depth * volumes
     width = padded(lines, LANES)
     count = width // LANES
-    begun = read_complex(arrived, pitch, 0, 5 * count, count, depth, volumes)
-    turned = read_complex(arrived, pitch, 2 * count, 5 * count, count, depth, volumes)
-    power = read_places(arrived, pitch, 4 * count, 5 * count, count, depth, volumes)
+    begun = read_complex(arrived, pitch, 0, pitch // volumes, count, depth, volumes)
+    turned = read_complex(arrived, pitch, 2 * count, pitch // volumes, count, depth, volumes)
+    power = read_places(arrived, pitch, 4 * count, pitch // volumes, count, depth, volumes)
     power = jnp.concatenate([power, power], axis=0)
     cotangent = jnp.concatenate(
         split_complex(lane_chunks(cotangent_ref[...].astype(F32)), lines), axis=0
@@ -672,44 +685,20 @@
             cotangent.reshape(rows, two_lines),
         ),
         [shape(depth, pitch, LANES, kind=BF16)]
-        + [shape(coils * depth, two_lines, kind=BF16)] * volumes,
+        + [shape(coils * depth, two_lines, kind=BF16)] * (volumes - 1),
         [(depth * pitch, LANES)],
         1000,
         LARGE_VMEM_BYTES,
     )
-    arrivals = samples[:1]
-    arrivals += [from_group(value, step) for step, value in enumerate(samples[1:], 1)]
+    samples = [from_group(value, step) for step, value in enumerate(samples, 1)]
     arrived = exchange(packed, "section", near)
 
-    (images,) = call(
-        functools.partial(images_kernel, coils, lines, volumes),
-        "measured_images",
-        (mask, table, plus, *arrivals),
-        [shape(2 * planes, width, kind=BF16)],
-        [],
-        2 * line_flops,
-    )
-
-    depth_pitch = padded(volumes * 5 * count, 16)
-    partial, maps = call(
-        functools.partial(rows_kernel, coils, lines, volumes),
-        "combine_rows",
-        (arrived, images, mask, table, minus, plus),
-        [
-            shape(depth, coil_devices, depth_pitch, LANES, kind=BF16),
-            shape(2 * planes, width, kind=BF16),
-        ],
-        [(depth * pitch, LANES), (depth * depth_pitch, LANES)],
-        3 * line_flops,
-    )
-    kernel_in, kernel_out, partial = lax.optimization_barrier((kernel_in, kernel_out, partial))
     tall, wide = channels * rows, offset.shape[1]
-    first, first_t, second, second_t, columns, *handed = call(
-        functools.partial(taps_kernel, rows, volumes),
+    first, first_t, second, second_t, columns = call(
+        functools.partial(taps_kernel, rows),
         "lay_out_taps",
         (
             dc_weight,
-            maps,
             kernel_in.transpose(0, 1, 3, 2).reshape(-1, 2, channels),
             kernel_out.reshape(-1, 2, channels),
             bias_in,
@@ -724,15 +713,34 @@
             shape(CASCADES, 6 * rows, tall, kind=BF16),
             shape(CASCADES, tall, wide, kind=BF16),
             shape(tall, place.shape[0]),
-        ]
-        + [shape(2 * planes // volumes, width, kind=BF16)] * (volumes - 1),
+        ],
         [(place.shape[0], repeat.shape[1])],
         2 * tall * place.shape[0] * place.shape[1],
         scalars=1,
     )
+    arrived, columns = lax.optimization_barrier((arrived, columns))
+
+    depth_pitch = padded(volumes * 5 * count, 16 * volumes)
+    maps, sums, *handed = call(
+        functools.partial(rows_kernel, coils, lines, volumes, depth_pitch),
+        "combine_rows",
+        (arrived, mask, table, minus, plus),
+        [shape(2 * planes, width, kind=BF16), shape(depth * depth_pitch, LANES)]
+        + [shape(2 * planes // volumes, width, kind=BF16)] * (volumes - 1),
+        [(depth * pitch, LANES)],
+        3 * line_flops,
+    )
+    (partial,) = call(
+        functools.partial(measured_kernel, coils, lines, volumes),
+        "combine_measured",
+        (kspace.reshape(planes, two_lines), mask, table, plus, maps, sums, *samples),
+        [shape(depth, coil_devices, depth_pitch, LANES, kind=BF16)],
+        [(depth * depth_pitch, LANES)],
+        2 * line_flops,
+    )
+    handed = [from_group(value, step) for step, value in enumerate(handed, 1)]
     partial = exchange(partial.reshape(-1, depth_pitch, LANES), both, near_both)
     partial = partial.reshape(depth, coil_devices, depth_pitch, LANES)
-    handed = [from_group(value, step) for step, value in enumerate(handed, 1)]
 
     model_pitch = padded(volumes * 2 * count, 16)
     moved, model = call(

time: 54 us -> 53.2 us (0.985)
  starting transfers between devices: 20.4 us -> 17.9 us
  local copies, waits for them, and re-layouts: 0.67 us -> 2.06 us
  blocking collectives: 11.2 us -> 10.3 us
  other arithmetic: 0.01 us -> 0.74 us
    all_to_all x3, waiting for transfers between devices: 5.38 us -> 9.16 us  [exchange(): lax.all_to_all(value, axes, 0, 0, tiled=True, axis_index_groups=groups)]
    ppermute x2, waiting for transfers between devices: 3.4 us -> 0.01 us  [from_group(): lax.ppermute(value, 'section', [(s, (s + shift) % sections) for s in rang...]
    all_to_all x3, starting transfers between devices: 15.4 us -> 13.6 us  [exchange(): lax.all_to_all(value, axes, 0, 0, tiled=True, axis_index_groups=groups)]
    unnamed x28 -> x26, local copies, waits for them, and re-layouts: 0.66 us -> 2.05 us
    all_to_all x1, blocking collectives: 11.2 us -> 10.3 us  [exchange(): lax.all_to_all(value, axes, 0, 0, tiled=True, axis_index_groups=groups)]
    reshape x1, other arithmetic: 0.01 us -> 0.74 us  [body(): mask = sampling.astype(F32).reshape(slots, lines)]
    ppermute x2, starting transfers between devices: 5.02 us -> 4.29 us  [from_group(): lax.ppermute(value, 'section', [(s, (s + shift) % sections) for s in rang...]
  transfers between devices with their start and end apart: 5 -> 5, of which waited for: 4 -> 3; matrix products, arithmetic and copies ran while one was open for 0% -> 1% of each run, Pallas kernels for 9% -> 10%
where the time goes in v5:
time: 53.2 us; the launch traced here: 52.6 us
  starting transfers between devices  17.9 us (34%)
  Pallas kernels  11.6 us (22%)
  blocking collectives  10.3 us (19%)
  waiting for transfers between devices  9.17 us (17%)
  local copies, waits for them, and re-layouts  2.06 us (4%)
  between operations  0.8 us (2%)
  other arithmetic  0.74 us (1%)
    all_to_all x3, starting transfers between devices, exchange(): lax.all_to_all(value, axes, 0, 0, tiled=True, axis_index_groups=groups)  13.6 us
    pallas_call x8, Pallas kernels, call(): pl.pallas_call(kernel, name=name, out_shape=tuple(outs), in_specs=[pl.Blo...  11.6 us
    all_to_all x1, blocking collectives, exchange(): lax.all_to_all(value, axes, 0, 0, tiled=True, axis_index_groups=groups)  10.3 us
    all_to_all x3, waiting for transfers between devices, exchange(): lax.all_to_all(value, axes, 0, 0, tiled=True, axis_index_groups=groups)  9.16 us
    ppermute x2, starting transfers between devices, from_group(): lax.ppermute(value, 'section', [(s, (s + shift) % sections) for s in rang...  4.29 us
    unnamed x26, local copies, waits for them, and re-layouts  2.05 us
  transfers between devices with their start and end apart: 5, of which 3 were waited for; matrix products, arithmetic and copies ran while one was open for 1% of the time, Pallas kernels for 10%

profile of v5, /device:TPU:0, one launch (start us, length us, event | category | flops | bytes accessed | tf_op | source)
XLA Modules:
  0.0 52.6 jit_solution(1961116554757795869)
XLA Ops:
  0.6 0.0 copy-start.2
  0.6 0.0 copy-start.8
  0.7 0.0 copy-start.9
  0.7 2.0 %pack_maps.1 = (bf16[8,96,128]{2,1,0:T(8,128)(2,1)}, bf16[64,640]{1,0:T(8,128)(2,1)}) custom-call(bf16[128,640]{1,0:T(8,128)(2,1)} %bitcast.17, bf16[128,640]{1,0:T(8,128)(2,1)} %bitcast.25, bf16[16,640]{1,0:T(8,128)(2,1)} %bitcast.21), custom_call_target="tpu_custom_call" | custom-call | flops 1000 | bytes 626688 | tf_op jit(solution)/shard_map/pack_maps/pallas_call | solution.py:629
  2.7 5.4 %all-to-all-start = ((bf16[8,96,128]{2,1,0:T(8,128)(2,1)}), bf16[8,96,128]{2,1,0:T(8,128)(2,1)S(1)}, u32[]{:S(2)}, u32[]{:S(2)}) async-start(bf16[8,96,128]{2,1,0:T(8,128)(2,1)} %get-tuple-element.22), calls=%async_computation | async-start | bytes 393216 | tf_op jit(solution)/shard_map/all_to_all | solution.py:664
  8.1 2.6 %collective-permute-start = (bf16[64,640]{1,0:T(8,128)(2,1)}, bf16[64,640]{1,0:T(8,128)(2,1)S(1)}, u32[]{:S(2)}, u32[]{:S(2)}) collective-permute-start(bf16[64,640]{1,0:T(8,128)(2,1)} %get-tuple-element.28), channel_id=1, source_target_pairs={{0,16},{2,18},{4,20},{6,22},{8,24},{10,26},{12,28},{14,30},{16,0},... | collective-permute-start | bytes 245768 | tf_op jit(solution)/shard_map/ppermute | solution.py:661
  10.7 0.7 %convert_bitcast_fusion = f32[16,320]{1,0:T(8,128)S(1)} fusion(s32[2,8,320]{2,1,0:T(8,128)} %param.17), kind=kLoop, calls=%fused_computation | loop fusion | flops 5120 | bytes 40960 | tf_op jit(solution)/shard_map/reshape | solution.py:670
  11.4 0.0 copy-done.2
  11.4 0.0 copy-done.8
  11.5 0.0 copy-start.10
  11.5 0.7 %copy-done.10 = f32[2,18]{1,0:T(2,128)S(1)} copy-done((f32[2,18]{1,0:T(2,128)S(1)}, f32[2,18]{1,0:T(2,128)}, u32[]{:S(2)}) %copy-start.10) | copy-done | bytes 168
  12.1 0.7 %copy-done.11 = f32[2,2]{1,0:T(2,128)S(1)} copy-done((f32[2,2]{1,0:T(2,128)S(1)}, f32[2,2]{1,0:T(2,128)}, u32[]{:S(2)}) %copy-start.11) | copy-done | bytes 40
  12.8 0.7 %copy-done.12 = f32[2]{0:T(128)S(1)} copy-done((f32[2]{0:T(128)S(1)}, f32[2]{0:T(128)}, u32[]{:S(2)}) %copy-start.12) | copy-done | bytes 32
  13.5 1.5 %lay_out_taps.1 = (bf16[2,288,128]{2,1,0:T(8,128)(2,1)S(1)}, bf16[2,96,288]{2,1,0:T(8,128)(2,1)S(1)}, bf16[2,96,288]{2,1,0:T(8,128)(2,1)S(1)}, bf16[2,288,128]{2,1,0:T(8,128)(2,1)S(1)}, f32[288,128]{1,0:T(8,128)S(1)}) custom-call(f32[2]{0:T(128)S(1)} %copy-done.12, f32[18,2,18]{2,1,0:T(2,128)S(1)} %bitcast.23, f32[18,2,18]{2,1,0:T(2,128)S(1)} %bitcast.24, ...), custom_call_target="tpu_custom_call" | custom-call | flops 113246208 | bytes 1357032 | tf_op jit(solution)/shard_map/lay_out_taps/pallas_call | solution.py:629
  15.0 0.5 all-to-all-done.sent_ref
  15.5 0.0 copy-done.6
  15.5 0.0 copy-start.1
  15.5 1.3 %combine_rows.1 = (bf16[256,384]{1,0:T(8,128)(2,1)S(1)}, f32[256,128]{1,0:T(8,128)S(1)}, bf16[128,384]{1,0:T(8,128)(2,1)S(1)}) custom-call(bf16[8,96,128]{2,1,0:T(8,128)(2,1)S(1)} %all-to-all-done.sent_ref, f32[16,384]{1,0:T(8,128)S(1)} %pad.4.mask_ref, bf16[384,768]{1,0:T(8,128)(2,1)S(1)} %copy-done, bf16[256,256]{1,0:T(8,128)(2,1)S(1)} %copy-done.5, ...), custom_call_target="tpu_custom_call" | custom-call | flops 452984832 | bytes 1499136 | tf_op jit(solution)/shard_map/combine_rows/pallas_call | solution.py:629
  16.8 0.0 collective-permute-done.refs_0_
  16.9 1.3 %combine_measured.1 = bf16[8,2,32,128]{3,2,1,0:T(8,128)(2,1)} custom-call(bf16[128,640]{1,0:T(8,128)(2,1)S(1)} %bitcast.18, f32[16,384]{1,0:T(8,128)S(1)} %pad.4.mask_ref, bf16[384,768]{1,0:T(8,128)(2,1)S(1)} %copy-done, bf16[256,256]{1,0:T(8,128)(2,1)S(1)} %copy-done.6, bf16[256,384]{1,0:T(8,128)(2,1)S(1)} %get-tuple-element.26.maps_ref, ...), custom_call_target="tpu_custom_call" | custom-call | flops 301989888 | bytes 1449984 | tf_op jit(solution)/shard_map/combine_measured/pallas_call | solution.py:629
  18.2 4.8 %all-to-all-start.1 = ((bf16[16,32,128]{2,1,0:T(8,128)(2,1)}), bf16[16,32,128]{2,1,0:T(8,128)(2,1)S(1)}, u32[]{:S(2)}, u32[]{:S(2)}) async-start(bf16[16,32,128]{2,1,0:T(8,128)(2,1)} %bitcast.7), calls=%async_computation.1 | async-start | bytes 262144 | tf_op jit(solution)/shard_map/all_to_all | solution.py:664
  23.0 1.7 %collective-permute-start.1 = (bf16[128,384]{1,0:T(8,128)(2,1)S(1)}, bf16[128,384]{1,0:T(8,128)(2,1)S(1)}, u32[]{:S(2)}, u32[]{:S(2)}) collective-permute-start(bf16[128,384]{1,0:T(8,128)(2,1)S(1)} %get-tuple-element.32), channel_id=1, source_target_pairs={{0,16},{2,18},{4,20},{6,22},{8,24},{10,26},{12,28},{14,30},{16,0},... | collective-permute-start | bytes 294920 | tf_op jit(solution)/shard_map/ppermute | solution.py:661
  24.7 5.5 %all-to-all-done.1 = bf16[16,32,128]{2,1,0:T(8,128)(2,1)S(1)} async-done(((bf16[16,32,128]{2,1,0:T(8,128)(2,1)}), bf16[16,32,128]{2,1,0:T(8,128)(2,1)S(1)}, u32[]{:S(2)}, u32[]{:S(2)}) %all-to-all-start.1) | async-done | bytes 131104 | tf_op jit(solution)/shard_map/all_to_all | solution.py:664
  30.1 1.2 %refine_first.1 = (bf16[8,16,128]{2,1,0:T(8,128)(2,1)}, bf16[32,384]{1,0:T(8,128)(2,1)S(1)}) custom-call(bf16[8,2,32,128]{3,2,1,0:T(8,128)(2,1)S(1)} %bitcast.15, bf16[2,288,128]{2,1,0:T(8,128)(2,1)S(1)} %get-tuple-element.29.first_ref, bf16[2,96,288]{2,1,0:T(8,128)(2,1)S(1)} %get-tuple-element.30.second_ref, f32[288,128]{1,0:T(8,128)S(1)} %get-tuple-element.24.columns_ref), custom_call_target="tpu_custom_call" | custom-call | flops 56623104 | bytes 593920 | tf_op jit(solution)/shard_map/refine_first/pallas_call | solution.py:629
  31.3 3.5 %all-to-all-start.2 = ((bf16[8,16,128]{2,1,0:T(8,128)(2,1)}), bf16[8,16,128]{2,1,0:T(8,128)(2,1)S(1)}, u32[]{:S(2)}, u32[]{:S(2)}) async-start(bf16[8,16,128]{2,1,0:T(8,128)(2,1)} %get-tuple-element.31), calls=%async_computation.2 | async-start | bytes 65536 | tf_op jit(solution)/shard_map/all_to_all | solution.py:664
  34.8 0.0 copy-done.7
  34.8 1.5 %refine_and_back.1 = (f32[32,384]{1,0:T(8,128)S(1)}, f32[32,384]{1,0:T(8,128)S(1)}) custom-call(bf16[8,2,32,128]{3,2,1,0:T(8,128)(2,1)S(1)} %bitcast.16, bf16[32,384]{1,0:T(8,128)(2,1)S(1)} %get-tuple-element.34.model_ref, bf16[16,640]{1,0:T(8,128)(2,1)S(1)} %bitcast.22, bf16[2,288,128]{2,1,0:T(8,128)(2,1)S(1)} %get-tuple-element.29.first_ref, ...), custom_call_target="tpu_custom_call" | custom-call | flops 198180864 | bytes 937984 | tf_op jit(solution)/shard_map/refine_and_back/pallas_call | solution.py:629
  36.3 0.0 collective-permute-done.1.refs_0_
  36.3 3.2 %all-to-all-done.2.sent_ref = bf16[8,16,128]{2,1,0:T(8,128)(2,1)S(1)} async-done(((bf16[8,16,128]{2,1,0:T(8,128)(2,1)}), bf16[8,16,128]{2,1,0:T(8,128)(2,1)S(1)}, u32[]{:S(2)}, u32[]{:S(2)}) %all-to-all-start.2) | async-done | bytes 32800 | tf_op jit(solution)/shard_map/all_to_all | solution.py:664
  39.5 1.2 %masked_normal.1 = bf16[16,2,16,128]{3,2,1,0:T(8,128)(2,1)S(1)} custom-call(bf16[8,16,128]{2,1,0:T(8,128)(2,1)S(1)} %all-to-all-done.2.sent_ref, bf16[256,384]{1,0:T(8,128)(2,1)S(1)} %get-tuple-element.26.maps_ref, f32[32,384]{1,0:T(8,128)S(1)} %get-tuple-element.37.spread_ref, f32[16,384]{1,0:T(8,128)S(1)} %pad.4.mask_ref, bf16[384,768]{1,0:T(8,128)(2,1)S(1)} %copy-done, ...), custom_call_target="tpu_custom_call" | custom-call | flops 452984832 | bytes 1286144 | tf_op jit(solution)/shard_map/masked_normal/pallas_call | solution.py:629
  40.7 10.3 %all_to_all.20 = bf16[32,16,128]{2,1,0:T(8,128)(2,1)S(1)} all-to-all(bf16[32,16,128]{2,1,0:T(8,128)(2,1)S(1)} %bitcast.20), channel_id=1, replica_groups=mesh['section'=16,'coil'=2] {'section','coil'}, dimensions={0} | all-to-all | bytes 262144 | tf_op jit(solution)/shard_map/all_to_all | solution.py:664
  51.0 1.6 %outputs.1 = (f32[16,640]{1,0:T(8,128)}, f32[640,128]{1,0:T(8,128)}) custom-call(f32[288,128]{1,0:T(8,128)S(1)} %get-tuple-element.24.columns_ref, bf16[16,2,16,128]{3,2,1,0:T(8,128)(2,1)S(1)} %bitcast.19, f32[32,384]{1,0:T(8,128)S(1)} %get-tuple-element.38.image_ref, f32[16,384]{1,0:T(8,128)S(1)} %pad.4.mask_ref, bf16[384,768]{1,0:T(8,128)(2,1)S(1)} %copy-done, ...), custom_call_target="tpu_custom_call" | custom-call | flops 301989888 | bytes 1736704 | tf_op jit(solution)/shard_map/outputs/pallas_call | solution.py:629
  (15 shorter events, 0.0 us)
Async XLA Ops:
  0.6 10.8 %copy-start.2 = (bf16[128,1536]{1,0:T(8,128)(2,1)S(1)}, bf16[128,1536]{1,0:T(8,128)(2,1)}, u32[]{:S(2)}) copy-start(bf16[128,1536]{1,0:T(8,128)(2,1)} %constant.19.clone.place_ref) | copy-start | bytes 1179652
  0.6 10.8 %copy-start.8 = (f32[2,9,18,2]{2,3,1,0:T(2,128)S(1)}, f32[2,9,18,2]{2,3,1,0:T(2,128)}, u32[]{:S(2)}) copy-start(f32[2,9,18,2]{2,3,1,0:T(2,128)} %param.19) | copy-start | bytes 7780
  0.7 10.8 %copy-start.9 = (f32[2,9,2,18]{3,2,1,0:T(2,128)S(1)}, f32[2,9,2,18]{3,2,1,0:T(2,128)}, u32[]{:S(2)}) copy-start(f32[2,9,2,18]{3,2,1,0:T(2,128)} %param.21) | copy-start | bytes 7780
  2.7 8.8 %copy-start.3 = (f32[288,128]{1,0:T(8,128)S(1)}, f32[288,128]{1,0:T(8,128)}, u32[]{:S(2)}) copy-start(f32[288,128]{1,0:T(8,128)} %constant.20.clone.offset_ref) | copy-start | bytes 442372
  2.7 8.8 %copy-start.4 = (f32[288,128]{1,0:T(8,128)S(1)}, f32[288,128]{1,0:T(8,128)}, u32[]{:S(2)}) copy-start(f32[288,128]{1,0:T(8,128)} %constant.18.clone.repeat_ref) | copy-start | bytes 442372
  2.7 12.8 %copy-start = (bf16[384,768]{1,0:T(8,128)(2,1)S(1)}, bf16[384,768]{1,0:T(8,128)(2,1)}, u32[]{:S(2)}) copy-start(bf16[384,768]{1,0:T(8,128)(2,1)} %constant.15.clone.table_ref) | copy-start | bytes 1769476
  2.7 12.8 %all-to-all-start = ((bf16[8,96,128]{2,1,0:T(8,128)(2,1)}), bf16[8,96,128]{2,1,0:T(8,128)(2,1)S(1)}, u32[]{:S(2)}, u32[]{:S(2)}) async-start(bf16[8,96,128]{2,1,0:T(8,128)(2,1)} %get-tuple-element.22), calls=%async_computation | async-start | bytes 393216 | tf_op jit(solution)/shard_map/all_to_all | solution.py:664
  8.1 8.8 %collective-permute-start = (bf16[64,640]{1,0:T(8,128)(2,1)}, bf16[64,640]{1,0:T(8,128)(2,1)S(1)}, u32[]{:S(2)}, u32[]{:S(2)}) collective-permute-start(bf16[64,640]{1,0:T(8,128)(2,1)} %get-tuple-element.28), channel_id=1, source_target_pairs={{0,16},{2,18},{4,20},{6,22},{8,24},{10,26},{12,28},{14,30},{16,0},... | collective-permute-start | bytes 245768 | tf_op jit(solution)/shard_map/ppermute | solution.py:661
  11.5 0.7 %copy-start.10 = (f32[2,18]{1,0:T(2,128)S(1)}, f32[2,18]{1,0:T(2,128)}, u32[]{:S(2)}) copy-start(f32[2,18]{1,0:T(2,128)} %bias_in_ref.1) | copy-start | bytes 436
  12.1 0.7 %copy-start.11 = (f32[2,2]{1,0:T(2,128)S(1)}, f32[2,2]{1,0:T(2,128)}, u32[]{:S(2)}) copy-start(f32[2,2]{1,0:T(2,128)} %bias_out_ref.1) | copy-start | bytes 52
  12.8 0.7 %copy-start.12 = (f32[2]{0:T(128)S(1)}, f32[2]{0:T(128)}, u32[]{:S(2)}) copy-start(f32[2]{0:T(128)} %weight_ref.1) | copy-start | bytes 28
  13.5 2.0 %copy-start.5 = (bf16[256,256]{1,0:T(8,128)(2,1)S(1)}, bf16[256,256]{1,0:T(8,128)(2,1)}, u32[]{:S(2)}) copy-start(bf16[256,256]{1,0:T(8,128)(2,1)} %constant.16.clone.minus_ref) | copy-start | bytes 393220
  13.5 2.0 %copy-start.6 = (bf16[256,256]{1,0:T(8,128)(2,1)S(1)}, bf16[256,256]{1,0:T(8,128)(2,1)}, u32[]{:S(2)}) copy-start(bf16[256,256]{1,0:T(8,128)(2,1)} %constant.17.clone.plus_ref) | copy-start | bytes 393220
  15.5 1.4 %copy-start.1 = (bf16[8,16,1,640]{3,1,2,0:T(8,128)(2,1)S(1)}, bf16[8,16,1,640]{3,1,2,0:T(8,128)(2,1)}, u32[]{:S(2)}) copy-start(bf16[8,16,1,640]{3,1,2,0:T(8,128)(2,1)} %param.15) | copy-start | bytes 491524
  18.2 11.9 %all-to-all-start.1 = ((bf16[16,32,128]{2,1,0:T(8,128)(2,1)}), bf16[16,32,128]{2,1,0:T(8,128)(2,1)S(1)}, u32[]{:S(2)}, u32[]{:S(2)}) async-start(bf16[16,32,128]{2,1,0:T(8,128)(2,1)} %bitcast.7), calls=%async_computation.1 | async-start | bytes 262144 | tf_op jit(solution)/shard_map/all_to_all | solution.py:664
  23.0 13.4 %collective-permute-start.1 = (bf16[128,384]{1,0:T(8,128)(2,1)S(1)}, bf16[128,384]{1,0:T(8,128)(2,1)S(1)}, u32[]{:S(2)}, u32[]{:S(2)}) collective-permute-start(bf16[128,384]{1,0:T(8,128)(2,1)S(1)} %get-tuple-element.32), channel_id=1, source_target_pairs={{0,16},{2,18},{4,20},{6,22},{8,24},{10,26},{12,28},{14,30},{16,0},... | collective-permute-start | bytes 294920 | tf_op jit(solution)/shard_map/ppermute | solution.py:661
  31.3 3.5 %copy-start.7 = (bf16[1,16,640]{2,1,0:T(8,128)(2,1)S(1)}, bf16[1,16,640]{2,1,0:T(8,128)(2,1)}, u32[]{:S(2)}) copy-start(bf16[1,16,640]{2,1,0:T(8,128)(2,1)} %param.23) | copy-start | bytes 61444
  31.3 8.2 %all-to-all-start.2 = ((bf16[8,16,128]{2,1,0:T(8,128)(2,1)}), bf16[8,16,128]{2,1,0:T(8,128)(2,1)S(1)}, u32[]{:S(2)}, u32[]{:S(2)}) async-start(bf16[8,16,128]{2,1,0:T(8,128)(2,1)} %get-tuple-element.31), calls=%async_computation.2 | async-start | bytes 65536 | tf_op jit(solution)/shard_map/all_to_all | solution.py:664

commit v6 on v5

--- a/solution.py
+++ b/solution.py
@@ -14,6 +14,7 @@
 VOLUMES = 2
 LANES = 128
 VMEM_BYTES = 48 * 1024 * 1024
+FAR_PARTS = 3
 LARGE_VMEM_BYTES = 60 * 1024 * 1024
 
 F32 = jnp.float32
@@ -223,6 +224,11 @@
     mixed = jnp.dot(first_t_ref[...], back, preferred_element_type=F32)
     total = add_shifted(mixed, (1, 0, -1), 2 * rows)
     return jnp.where(valid[: 2 * rows], total, 0.0)
+
+
+def read_mask(sampling_ref, width):
+    mask = sampling_ref[...].astype(F32)
+    return jnp.pad(mask, ((0, 0), (0, width - mask.shape[1])))
 
 
 def valid_lanes(rows, width, lines):
@@ -316,31 +322,56 @@
             turned[cascade] = total.T[: 6 * rows].astype(BF16)
 
 
-def write_sums(scratch, pitch, first, values, volumes, coils):
-    sums = [row_sums(value, volumes, coils) for value in values]
-    period = pitch // volumes
-    for place in range(volumes):
-        chunks = [chunk for value in sums for chunk in lane_chunks(value[place])]
-        write_rows(scratch, pitch, chunks, place * period + first)
+def line_images(kspace, mask, lines, table_ref, plus_ref):
+    real, imag = split_complex(lane_chunks(kspace), lines)
+    measured = jnp.concatenate([real * mask, imag * mask], axis=0)
+    return line_apply(depth_apply(measured, plus_ref), table_ref, 1.0)
+
+
+def far_kernel(coils, lines, volumes, kspace_ref, mask_ref, table_ref, plus_ref, out_ref):
+    parts = blocks(read_mask(mask_ref, table_ref.shape[0]), volumes)
+    mask = pick(parts, own_volume(parts[0].shape[0]))
+    mask = over_coils(mask, coils)
+    images = line_images(kspace_ref[...].astype(F32), mask, lines, table_ref, plus_ref)
+    out_ref[: images.shape[0]] = images
+    if out_ref.shape[0] > images.shape[0]:
+        out_ref[images.shape[0] :] = jnp.zeros_like(out_ref[images.shape[0] :])
+
+
+def own_kernel(coils, lines, volumes, kspace_ref, mask_ref, table_ref, plus_ref, out_ref):
+    parts = blocks(read_mask(mask_ref, table_ref.shape[0]), volumes)
+    volume = own_volume(parts[0].shape[0])
+    kspace = choose_volume(kspace_ref[...].astype(F32), coils, volumes, volume)
+    mask = over_coils(pick(parts, volume), coils)
+    out_ref[...] = line_images(kspace, mask, lines, table_ref, plus_ref)
 
 
 def rows_kernel(
     coils,
     lines,
     volumes,
-    sums_pitch,
     sent_ref,
     mask_ref,
     table_ref,
     minus_ref,
     plus_ref,
-    maps_ref,
-    sums_ref,
     *refs,
 ):
-    handed, (arrived,) = refs[:-1], refs[-1:]
+    arrival_refs, refs = refs[:volumes], refs[volumes:]
+    (out_ref, maps_ref), handed, (arrived, leaving) = refs[:2], refs[2:-2], refs[-2:]
     depth, pitch = sent_ref.shape[:2]
     volume = own_volume(depth)
+    mask = pick(blocks(read_mask(mask_ref, table_ref.shape[0]), volumes), volume)
+    mask = over_coils(mask, volumes * coils)
+
+    arrivals = [halves(ref[: 2 * coils * depth]) for ref in arrival_refs]
+    measured = []
+    for part in range(2):
+        for place in range(volumes):
+            step = lax.rem(volume - place + volumes, jnp.int32(volumes))
+            measured.append(pick([arrival[part] for arrival in arrivals], step))
+    measured = jnp.concatenate(measured, axis=0)
+
     arrived[...] = sent_ref[...].astype(F32).reshape(arrived.shape)
     count = 2 * lines // LANES
     parts, reals, imags = [], [], []
@@ -361,45 +392,21 @@
         place = lax.rem(volume + step, jnp.int32(volumes))
         both = [pick(real_parts, place), pick(imag_parts, place)]
         ref[...] = jnp.concatenate(both, axis=0).astype(BF16)
-    mask = over_coils(pick(blocks(mask_ref[...], volumes), volume), 2 * volumes * coils)
+
     images = spread(maps_real, maps_imag, over_rows(reals, coils), over_rows(imags, coils))
+    mask = jnp.concatenate([mask, mask], axis=0)
     images = masked_normal(images, table_ref, minus_ref, plus_ref, mask)
-    sums_ref[...] = jnp.zeros_like(sums_ref)
-    power = maps_real * maps_real + maps_imag * maps_imag
-    found = [*collect(maps_real, maps_imag, images), power]
-    first = 2 * maps_ref.shape[1] // LANES
-    write_sums(sums_ref, sums_pitch, first, found, volumes, coils)
-
-
-def measured_kernel(
-    coils,
-    lines,
-    volumes,
-    kspace_ref,
-    mask_ref,
-    table_ref,
-    plus_ref,
-    maps_ref,
-    sums_ref,
-    *refs,
-):
-    arrival_refs, (out_ref, leaving) = refs[: volumes - 1], refs[volumes - 1 :]
-    depth, pitch = out_ref.shape[0], out_ref.shape[2]
-    volume = own_volume(depth)
-    arrivals = [choose_volume(kspace_ref[...].astype(F32), coils, volumes, volume)]
-    arrivals += [ref[...].astype(F32) for ref in arrival_refs]
-    ordered = []
+    found = [
+        *collect(maps_real, maps_imag, round_bf(measured)),
+        *collect(maps_real, maps_imag, images),
+        maps_real * maps_real + maps_imag * maps_imag,
+    ]
+    leaving[...] = jnp.zeros_like(leaving)
+    sums = [row_sums(value, volumes, coils) for value in found]
+    pitch = out_ref.shape[2]
     for place in range(volumes):
-        step = lax.rem(volume - place + volumes, jnp.int32(volumes))
-        ordered.append(pick(arrivals, step))
-    mask = over_coils(pick(blocks(mask_ref[...], volumes), volume), volumes * coils)
-    real, imag = split_complex(lane_chunks(jnp.concatenate(ordered, axis=0)), lines)
-    measured = jnp.concatenate([real * mask, imag * mask], axis=0)
-    images = line_apply(depth_apply(measured, plus_ref), table_ref, 1.0)
-    maps_real, maps_imag = halves(maps_ref[...].astype(F32))
-    leaving[...] = sums_ref[...]
-    found = collect(maps_real, maps_imag, round_bf(images))
-    write_sums(leaving, pitch, 0, found, volumes, coils)
+        chunks = [chunk for value in sums for chunk in lane_chunks(value[place])]
+        write_rows(leaving, pitch, chunks, place * (pitch // volumes))
     message = leaving[...].astype(BF16).reshape(depth, *out_ref.shape[2:])
     for device in range(out_ref.shape[1]):
         out_ref[:, device] = message
@@ -547,7 +554,7 @@
     reals = [read_image(arrived, pitch, first, count, depth) for first in firsts]
     imags = [read_image(arrived, pitch, first + count, count, depth) for first in firsts]
     maps_real, maps_imag = halves(maps_ref[...].astype(F32))
-    mask = over_coils(pick(blocks(mask_ref[...], volumes), volume), 2 * volumes * coils)
+    mask = over_coils(pick(blocks(read_mask(mask_ref, table_ref.shape[0]), volumes), volume), 2 * volumes * coils)
     images = spread(maps_real, maps_imag, over_rows(reals, coils), over_rows(imags, coils))
     images = masked_normal(images, table_ref, minus_ref, plus_ref, mask)
     found = [row_sums(value, volumes, coils) for value in collect(maps_real, maps_imag, images)]
@@ -601,7 +608,7 @@
     real, imag = split_complex(chunks, lines)
     images = spread(*maps, over_coils(real, coils), over_coils(imag, coils))
     spectrum = depth_apply(line_apply(images, table_ref, -1.0), minus_ref)
-    spectrum = spectrum * over_coils(mask_ref[...], 2 * coils)
+    spectrum = spectrum * over_coils(read_mask(mask_ref, table_ref.shape[0]), 2 * coils)
     chunks = join_complex(*halves(spectrum), lines)
     write_rows(grad_ref, len(chunks), chunks)
 
@@ -656,9 +663,12 @@
     span = depth * coil_devices
     near_both = [[group * span + t for t in range(span)] for group in range(volumes)]
 
-    def from_group(value, step):
-        shift = step * depth
-        return lax.ppermute(value, "section", [(s, (s + shift) % sections) for s in range(sections)])
+    def from_group(value, step, core=0):
+        pairs = [(s, ((s + step * depth) % sections) ^ core) for s in range(sections)]
+        return lax.ppermute(value, "section", pairs)
+
+    def between_cores(value):
+        return lax.ppermute(value, "section", [(s, s ^ 1) for s in range(sections)])
 
     def exchange(value, axes, groups):
         return lax.all_to_all(value, axes, 0, 0, tiled=True, axis_index_groups=groups)
@@ -666,9 +676,9 @@
     table = jnp.asarray(line_constant(lines))
     minus = jnp.asarray(depth_constant(coils, slots, volumes, -1.0))
     plus = jnp.asarray(depth_constant(coils, slots, volumes, 1.0))
+    near_plus = jnp.asarray(depth_constant(coils, depth, 1, 1.0))
     repeat, place, offset = (jnp.asarray(item) for item in conv_constants(rows, channels))
-    mask = sampling.astype(F32).reshape(slots, lines)
-    mask = jnp.pad(mask, ((0, 0), (0, width - lines)))
+    mask = sampling.reshape(slots, lines)
 
     def shape(*dims, kind=F32):
         return jax.ShapeDtypeStruct(dims, kind)
@@ -690,9 +700,7 @@
         1000,
         LARGE_VMEM_BYTES,
     )
-    samples = [from_group(value, step) for step, value in enumerate(samples, 1)]
-    arrived = exchange(packed, "section", near)
-
+    samples = [from_group(value, step, 1) for step, value in enumerate(samples, 1)]
     tall, wide = channels * rows, offset.shape[1]
     first, first_t, second, second_t, columns = call(
         functools.partial(taps_kernel, rows),
@@ -718,27 +726,43 @@
         2 * tall * place.shape[0] * place.shape[1],
         scalars=1,
     )
-    arrived, columns = lax.optimization_barrier((arrived, columns))
+    *samples, columns = lax.optimization_barrier((*samples, columns))
+    (own,) = call(
+        functools.partial(own_kernel, coils, lines, volumes),
+        "own_images",
+        (kspace.reshape(planes, two_lines), mask, table, near_plus),
+        [shape(2 * coils * depth, width)],
+        [],
+        line_flops,
+    )
+    images = [own]
+    for value in samples:
+        (image,) = call(
+            functools.partial(far_kernel, coils, lines, volumes),
+            "far_images",
+            (value, mask, table, near_plus),
+            [shape(FAR_PARTS * coils * depth, width)],
+            [],
+            line_flops,
+        )
+        images.append(between_cores(image))
+    arrived = exchange(packed, "section", near)
 
     depth_pitch = padded(volumes * 5 * count, 16 * volumes)
-    maps, sums, *handed = call(
-        functools.partial(rows_kernel, coils, lines, volumes, depth_pitch),
+    partial, maps, *handed = call(
+        functools.partial(rows_kernel, coils, lines, volumes),
         "combine_rows",
-        (arrived, mask, table, minus, plus),
-        [shape(2 * planes, width, kind=BF16), shape(depth * depth_pitch, LANES)]
+        (arrived, mask, table, minus, plus, *images),
+        [
+            shape(depth, coil_devices, depth_pitch, LANES, kind=BF16),
+            shape(2 * planes, width, kind=BF16),
+        ]
         + [shape(2 * planes // volumes, width, kind=BF16)] * (volumes - 1),
-        [(depth * pitch, LANES)],
-        3 * line_flops,
-    )
-    (partial,) = call(
-        functools.partial(measured_kernel, coils, lines, volumes),
-        "combine_measured",
-        (kspace.reshape(planes, two_lines), mask, table, plus, maps, sums, *samples),
-        [shape(depth, coil_devices, depth_pitch, LANES, kind=BF16)],
-        [(depth * depth_pitch, LANES)],
-        2 * line_flops,
+        [(depth * pitch, LANES), (depth * depth_pitch, LANES)],
+        4 * line_flops,
     )
     handed = [from_group(value, step) for step, value in enumerate(handed, 1)]
+
     partial = exchange(partial.reshape(-1, depth_pitch, LANES), both, near_both)
     partial = partial.reshape(depth, coil_devices, depth_pitch, LANES)
 

time: 53.2 us -> 52 us (0.977)
  waiting for transfers between devices: 9.17 us -> 11.2 us
  local copies, waits for them, and re-layouts: 2.06 us -> 0.08 us
  starting transfers between devices: 17.9 us -> 17.1 us
  other arithmetic: 0.74 us -> 0 us
    all_to_all x3, starting transfers between devices: 13.6 us -> 11.1 us  [exchange(): lax.all_to_all(value, axes, 0, 0, tiled=True, axis_index_groups=groups)]
    all_to_all x3, waiting for transfers between devices: 9.16 us -> 11.2 us  [exchange(): lax.all_to_all(value, axes, 0, 0, tiled=True, axis_index_groups=groups)]
    unnamed x26 -> x30, local copies, waits for them, and re-layouts: 2.05 us -> 0.08 us
    ppermute x2 -> x3, starting transfers between devices: 4.29 us -> 5.99 us  [the longest x2 5.43 us: from_group(): return lax.ppermute(value, 'section', pairs)]
    reshape x1 -> x0, other arithmetic: 0.74 us -> none  [body(): mask = sampling.astype(F32).reshape(slots, lines)]
    pallas_call x8 -> x9, Pallas kernels: 11.6 us -> 12 us  [call(): pl.pallas_call(kernel, name=name, out_shape=tuple(outs), in_specs=[pl.Blo...]
  transfers between devices with their start and end apart: 5 -> 6, of which waited for: 3 -> 3; matrix products, arithmetic and copies ran while one was open for 1% -> 0% of each run, Pallas kernels for 10% -> 10%
where the time goes in v6:
time: 52 us; the launch traced here: 51.5 us
  starting transfers between devices  17.1 us (33%)
  Pallas kernels  12 us (23%)
  waiting for transfers between devices  11.2 us (22%)
  blocking collectives  10.3 us (20%)
  between operations  0.91 us (2%)
    pallas_call x9, Pallas kernels, call(): pl.pallas_call(kernel, name=name, out_shape=tuple(outs), in_specs=[pl.Blo...  12 us
    all_to_all x3, waiting for transfers between devices, exchange(): lax.all_to_all(value, axes, 0, 0, tiled=True, axis_index_groups=groups)  11.2 us
    all_to_all x3, starting transfers between devices, exchange(): lax.all_to_all(value, axes, 0, 0, tiled=True, axis_index_groups=groups)  11.1 us
    all_to_all x1, blocking collectives, exchange(): lax.all_to_all(value, axes, 0, 0, tiled=True, axis_index_groups=groups)  10.3 us
    ppermute x2, starting transfers between devices, from_group(): return lax.ppermute(value, 'section', pairs)  5.43 us
  transfers between devices with their start and end apart: 6, of which 3 were waited for; matrix products, arithmetic and copies ran while one was open for 0% of the time, Pallas kernels for 10%

profile of v6, /device:TPU:0, one launch (start us, length us, event | category | flops | bytes accessed | tf_op | source)
XLA Modules:
  0.0 51.5 jit_solution(10007361558659010013)
XLA Ops:
  0.6 0.0 copy-start.2
  0.6 0.0 copy-start.4
  0.7 0.0 copy-start.5
  0.7 0.0 copy-start.9
  0.7 0.0 copy-start.10
  0.7 2.0 %pack_maps.1 = (bf16[8,96,128]{2,1,0:T(8,128)(2,1)}, bf16[64,640]{1,0:T(8,128)(2,1)}) custom-call(bf16[128,640]{1,0:T(8,128)(2,1)} %bitcast.16, bf16[128,640]{1,0:T(8,128)(2,1)} %bitcast.29, bf16[16,640]{1,0:T(8,128)(2,1)} %bitcast.25), custom_call_target="tpu_custom_call" | custom-call | flops 1000 | bytes 626688 | tf_op jit(solution)/shard_map/pack_maps/pallas_call | solution.py:636
  2.7 3.5 %collective-permute-start = (bf16[64,640]{1,0:T(8,128)(2,1)}, bf16[64,640]{1,0:T(8,128)(2,1)S(1)}, u32[]{:S(2)}, u32[]{:S(2)}) collective-permute-start(bf16[64,640]{1,0:T(8,128)(2,1)} %get-tuple-element.22), channel_id=1, source_target_pairs={{0,18},{2,16},{4,22},{6,20},{8,26},{10,24},{12,30},{14,28},{16,2},... | collective-permute-start | bytes 245768 | tf_op jit(solution)/shard_map/ppermute | solution.py:668
  6.2 4.1 %all-to-all-start = ((bf16[8,96,128]{2,1,0:T(8,128)(2,1)}), bf16[8,96,128]{2,1,0:T(8,128)(2,1)S(1)}, u32[]{:S(2)}, u32[]{:S(2)}) async-start(bf16[8,96,128]{2,1,0:T(8,128)(2,1)} %get-tuple-element.25), calls=%async_computation | async-start | bytes 393216 | tf_op jit(solution)/shard_map/all_to_all | solution.py:674
  10.4 0.0 copy-start.3
  10.4 0.0 copy-start.6
  10.4 1.5 %lay_out_taps.1 = (bf16[2,288,128]{2,1,0:T(8,128)(2,1)S(1)}, bf16[2,96,288]{2,1,0:T(8,128)(2,1)S(1)}, bf16[2,96,288]{2,1,0:T(8,128)(2,1)S(1)}, bf16[2,288,128]{2,1,0:T(8,128)(2,1)S(1)}, f32[288,128]{1,0:T(8,128)S(1)}) custom-call(f32[2]{0:T(128)S(1)} %copy-done.13, f32[18,2,18]{2,1,0:T(2,128)S(1)} %bitcast.27, f32[18,2,18]{2,1,0:T(2,128)S(1)} %bitcast.28, ...), custom_call_target="tpu_custom_call" | custom-call | flops 113246208 | bytes 1357032 | tf_op jit(solution)/shard_map/lay_out_taps/pallas_call | solution.py:636
  11.9 0.0 collective-permute-done.kspace_ref
  11.9 0.0 copy-start.1
  12.0 0.4 far_images.1
  12.4 0.0 copy-start.7
  12.4 0.0 copy-start.14
  12.4 0.6 %collective-permute-start.1 = (f32[192,384]{1,0:T(8,128)S(1)}, f32[192,384]{1,0:T(8,128)S(1)}, u32[]{:S(2)}, u32[]{:S(2)}) collective-permute-start(f32[192,384]{1,0:T(8,128)S(1)} %far_images.1), channel_id=1, source_target_pairs={{0,2},{2,0},{4,6},{6,4},{8,10},{10,8},{12,14},{14,12},{16,18},{18,... | collective-permute-start | bytes 884744 | tf_op jit(solution)/shard_map/ppermute | solution.py:671
  13.0 0.5 own_images.1.refs_0_
  13.5 2.5 %all-to-all-done.sent_ref = bf16[8,96,128]{2,1,0:T(8,128)(2,1)S(1)} async-done(((bf16[8,96,128]{2,1,0:T(8,128)(2,1)}), bf16[8,96,128]{2,1,0:T(8,128)(2,1)S(1)}, u32[]{:S(2)}, u32[]{:S(2)}) %all-to-all-start) | async-done | bytes 196640 | tf_op jit(solution)/shard_map/all_to_all | solution.py:674
  15.9 0.0 collective-permute-done.1.refs_1_
  16.0 2.1 %combine_rows.1 = (bf16[8,2,32,128]{3,2,1,0:T(8,128)(2,1)}, bf16[256,384]{1,0:T(8,128)(2,1)S(1)}, bf16[128,384]{1,0:T(8,128)(2,1)S(1)}) custom-call(bf16[8,96,128]{2,1,0:T(8,128)(2,1)S(1)} %all-to-all-done.sent_ref, s32[16,320]{1,0:T(8,128)S(1)} %bitcast.21, bf16[384,768]{1,0:T(8,128)(2,1)S(1)} %copy-done, bf16[256,256]{1,0:T(8,128)(2,1)S(1)} %copy-done.7, ...), custom_call_target="tpu_custom_call" | custom-call | flops 603979776 | bytes 1986560 | tf_op jit(solution)/shard_map/combine_rows/pallas_call | solution.py:636
  18.1 3.5 %all-to-all-start.1 = ((bf16[16,32,128]{2,1,0:T(8,128)(2,1)}), bf16[16,32,128]{2,1,0:T(8,128)(2,1)S(1)}, u32[]{:S(2)}, u32[]{:S(2)}) async-start(bf16[16,32,128]{2,1,0:T(8,128)(2,1)} %bitcast.7), calls=%async_computation.1 | async-start | bytes 262144 | tf_op jit(solution)/shard_map/all_to_all | solution.py:674
  21.6 1.9 %collective-permute-start.2 = (bf16[128,384]{1,0:T(8,128)(2,1)S(1)}, bf16[128,384]{1,0:T(8,128)(2,1)S(1)}, u32[]{:S(2)}, u32[]{:S(2)}) collective-permute-start(bf16[128,384]{1,0:T(8,128)(2,1)S(1)} %get-tuple-element.31), channel_id=1, source_target_pairs={{0,16},{2,18},{4,20},{6,22},{8,24},{10,26},{12,28},{14,30},{16,0},... | collective-permute-start | bytes 294920 | tf_op jit(solution)/shard_map/ppermute | solution.py:668
  23.6 5.5 %all-to-all-done.1 = bf16[16,32,128]{2,1,0:T(8,128)(2,1)S(1)} async-done(((bf16[16,32,128]{2,1,0:T(8,128)(2,1)}), bf16[16,32,128]{2,1,0:T(8,128)(2,1)S(1)}, u32[]{:S(2)}, u32[]{:S(2)}) %all-to-all-start.1) | async-done | bytes 131104 | tf_op jit(solution)/shard_map/all_to_all | solution.py:674
  29.1 1.2 %refine_first.1 = (bf16[8,16,128]{2,1,0:T(8,128)(2,1)}, bf16[32,384]{1,0:T(8,128)(2,1)S(1)}) custom-call(bf16[8,2,32,128]{3,2,1,0:T(8,128)(2,1)S(1)} %bitcast.14, bf16[2,288,128]{2,1,0:T(8,128)(2,1)S(1)} %get-tuple-element.28.first_ref, bf16[2,96,288]{2,1,0:T(8,128)(2,1)S(1)} %get-tuple-element.29.second_ref, f32[288,128]{1,0:T(8,128)S(1)} %get-tuple-element.24.columns_ref), custom_call_target="tpu_custom_call" | custom-call | flops 56623104 | bytes 593920 | tf_op jit(solution)/shard_map/refine_first/pallas_call | solution.py:636
  30.3 3.5 %all-to-all-start.2 = ((bf16[8,16,128]{2,1,0:T(8,128)(2,1)}), bf16[8,16,128]{2,1,0:T(8,128)(2,1)S(1)}, u32[]{:S(2)}, u32[]{:S(2)}) async-start(bf16[8,16,128]{2,1,0:T(8,128)(2,1)} %get-tuple-element.30), calls=%async_computation.2 | async-start | bytes 65536 | tf_op jit(solution)/shard_map/all_to_all | solution.py:674
  33.8 1.5 %refine_and_back.1 = (f32[32,384]{1,0:T(8,128)S(1)}, f32[32,384]{1,0:T(8,128)S(1)}) custom-call(bf16[8,2,32,128]{3,2,1,0:T(8,128)(2,1)S(1)} %bitcast.15, bf16[32,384]{1,0:T(8,128)(2,1)S(1)} %get-tuple-element.34.model_ref, bf16[16,640]{1,0:T(8,128)(2,1)S(1)} %bitcast.26, bf16[2,288,128]{2,1,0:T(8,128)(2,1)S(1)} %get-tuple-element.28.first_ref, ...), custom_call_target="tpu_custom_call" | custom-call | flops 198180864 | bytes 937984 | tf_op jit(solution)/shard_map/refine_and_back/pallas_call | solution.py:636
  35.2 0.0 collective-permute-done.2.refs_0_
  35.2 3.2 %all-to-all-done.2.sent_ref = bf16[8,16,128]{2,1,0:T(8,128)(2,1)S(1)} async-done(((bf16[8,16,128]{2,1,0:T(8,128)(2,1)}), bf16[8,16,128]{2,1,0:T(8,128)(2,1)S(1)}, u32[]{:S(2)}, u32[]{:S(2)}) %all-to-all-start.2) | async-done | bytes 32800 | tf_op jit(solution)/shard_map/all_to_all | solution.py:674
  38.4 1.2 %masked_normal.1 = bf16[16,2,16,128]{3,2,1,0:T(8,128)(2,1)S(1)} custom-call(bf16[8,16,128]{2,1,0:T(8,128)(2,1)S(1)} %all-to-all-done.2.sent_ref, bf16[256,384]{1,0:T(8,128)(2,1)S(1)} %get-tuple-element.33.maps_ref, f32[32,384]{1,0:T(8,128)S(1)} %get-tuple-element.37.spread_ref, s32[16,320]{1,0:T(8,128)S(1)} %bitcast.22, bf16[384,768]{1,0:T(8,128)(2,1)S(1)} %copy-done, ...), custom_call_target="tpu_custom_call" | custom-call | flops 452984832 | bytes 1282048 | tf_op jit(solution)/shard_map/masked_normal/pallas_call | solution.py:636
  39.6 10.3 %all_to_all.20 = bf16[32,16,128]{2,1,0:T(8,128)(2,1)S(1)} all-to-all(bf16[32,16,128]{2,1,0:T(8,128)(2,1)S(1)} %bitcast.24), channel_id=1, replica_groups=mesh['section'=16,'coil'=2] {'section','coil'}, dimensions={0} | all-to-all | bytes 262144 | tf_op jit(solution)/shard_map/all_to_all | solution.py:674
  49.9 1.6 %outputs.1 = (f32[16,640]{1,0:T(8,128)}, f32[640,128]{1,0:T(8,128)}) custom-call(f32[288,128]{1,0:T(8,128)S(1)} %get-tuple-element.24.columns_ref, bf16[16,2,16,128]{3,2,1,0:T(8,128)(2,1)S(1)} %bitcast.18, f32[32,384]{1,0:T(8,128)S(1)} %get-tuple-element.38.image_ref, s32[16,320]{1,0:T(8,128)S(1)} %bitcast.23, bf16[384,768]{1,0:T(8,128)(2,1)S(1)} %copy-done, ...), custom_call_target="tpu_custom_call" | custom-call | flops 301989888 | bytes 1732608 | tf_op jit(solution)/shard_map/outputs/pallas_call | solution.py:636
  (20 shorter events, 0.0 us)
Async XLA Ops:
  0.6 9.7 %copy-start.2 = (bf16[128,1536]{1,0:T(8,128)(2,1)S(1)}, bf16[128,1536]{1,0:T(8,128)(2,1)}, u32[]{:S(2)}) copy-start(bf16[128,1536]{1,0:T(8,128)(2,1)} %constant.19.clone.place_ref) | copy-start | bytes 1179652
  0.6 9.7 %copy-start.4 = (f32[288,128]{1,0:T(8,128)S(1)}, f32[288,128]{1,0:T(8,128)}, u32[]{:S(2)}) copy-start(f32[288,128]{1,0:T(8,128)} %constant.20.clone.offset_ref) | copy-start | bytes 442372
  0.7 9.7 %copy-start.5 = (f32[288,128]{1,0:T(8,128)S(1)}, f32[288,128]{1,0:T(8,128)}, u32[]{:S(2)}) copy-start(f32[288,128]{1,0:T(8,128)} %constant.18.clone.repeat_ref) | copy-start | bytes 442372
  0.7 9.7 %copy-start.9 = (f32[2,9,18,2]{2,3,1,0:T(2,128)S(1)}, f32[2,9,18,2]{2,3,1,0:T(2,128)}, u32[]{:S(2)}) copy-start(f32[2,9,18,2]{2,3,1,0:T(2,128)} %param.20) | copy-start | bytes 7780
  0.7 9.7 %copy-start.10 = (f32[2,9,2,18]{3,2,1,0:T(2,128)S(1)}, f32[2,9,2,18]{3,2,1,0:T(2,128)}, u32[]{:S(2)}) copy-start(f32[2,9,2,18]{3,2,1,0:T(2,128)} %param.22) | copy-start | bytes 7780
  0.7 9.7 %copy-start.11 = (f32[2,18]{1,0:T(2,128)S(1)}, f32[2,18]{1,0:T(2,128)}, u32[]{:S(2)}) copy-start(f32[2,18]{1,0:T(2,128)} %bias_in_ref.1) | copy-start | bytes 436
  0.7 9.7 %copy-start.12 = (f32[2,2]{1,0:T(2,128)S(1)}, f32[2,2]{1,0:T(2,128)}, u32[]{:S(2)}) copy-start(f32[2,2]{1,0:T(2,128)} %bias_out_ref.1) | copy-start | bytes 52
  0.7 9.7 %copy-start.13 = (f32[2]{0:T(128)S(1)}, f32[2]{0:T(128)}, u32[]{:S(2)}) copy-start(f32[2]{0:T(128)} %weight_ref.1) | copy-start | bytes 28
  2.7 9.2 %copy-start = (bf16[384,768]{1,0:T(8,128)(2,1)S(1)}, bf16[384,768]{1,0:T(8,128)(2,1)}, u32[]{:S(2)}) copy-start(bf16[384,768]{1,0:T(8,128)(2,1)} %constant.14.clone.table_ref) | copy-start | bytes 1769476
  2.7 9.2 %collective-permute-start = (bf16[64,640]{1,0:T(8,128)(2,1)}, bf16[64,640]{1,0:T(8,128)(2,1)S(1)}, u32[]{:S(2)}, u32[]{:S(2)}) collective-permute-start(bf16[64,640]{1,0:T(8,128)(2,1)} %get-tuple-element.22), channel_id=1, source_target_pairs={{0,18},{2,16},{4,22},{6,20},{8,26},{10,24},{12,30},{14,28},{16,2},... | collective-permute-start | bytes 245768 | tf_op jit(solution)/shard_map/ppermute | solution.py:668
  6.2 9.7 %all-to-all-start = ((bf16[8,96,128]{2,1,0:T(8,128)(2,1)}), bf16[8,96,128]{2,1,0:T(8,128)(2,1)S(1)}, u32[]{:S(2)}, u32[]{:S(2)}) async-start(bf16[8,96,128]{2,1,0:T(8,128)(2,1)} %get-tuple-element.25), calls=%async_computation | async-start | bytes 393216 | tf_op jit(solution)/shard_map/all_to_all | solution.py:674
  10.4 1.6 %copy-start.3 = (s32[2,8,320]{2,1,0:T(8,128)S(1)}, s32[2,8,320]{2,1,0:T(8,128)}, u32[]{:S(2)}) copy-start(s32[2,8,320]{2,1,0:T(8,128)} %param.18) | copy-start | bytes 61444
  10.4 1.6 %copy-start.6 = (bf16[128,128]{1,0:T(8,128)(2,1)S(1)}, bf16[128,128]{1,0:T(8,128)(2,1)}, u32[]{:S(2)}) copy-start(bf16[128,128]{1,0:T(8,128)(2,1)} %constant.17.clone.plus_ref) | copy-start | bytes 98308
  11.9 1.1 %copy-start.1 = (bf16[8,16,1,640]{3,1,2,0:T(8,128)(2,1)S(1)}, bf16[8,16,1,640]{3,1,2,0:T(8,128)(2,1)}, u32[]{:S(2)}) copy-start(bf16[8,16,1,640]{3,1,2,0:T(8,128)(2,1)} %param.16) | copy-start | bytes 491524
  12.4 3.5 %copy-start.7 = (bf16[256,256]{1,0:T(8,128)(2,1)S(1)}, bf16[256,256]{1,0:T(8,128)(2,1)}, u32[]{:S(2)}) copy-start(bf16[256,256]{1,0:T(8,128)(2,1)} %constant.15.clone.minus_ref) | copy-start | bytes 393220
  12.4 3.5 %copy-start.14 = (bf16[256,256]{1,0:T(8,128)(2,1)S(1)}, bf16[256,256]{1,0:T(8,128)(2,1)}, u32[]{:S(2)}) copy-start(bf16[256,256]{1,0:T(8,128)(2,1)} %constant.16.clone.plus_ref) | copy-start | bytes 393220
  12.4 3.5 %collective-permute-start.1 = (f32[192,384]{1,0:T(8,128)S(1)}, f32[192,384]{1,0:T(8,128)S(1)}, u32[]{:S(2)}, u32[]{:S(2)}) collective-permute-start(f32[192,384]{1,0:T(8,128)S(1)} %far_images.1), channel_id=1, source_target_pairs={{0,2},{2,0},{4,6},{6,4},{8,10},{10,8},{12,14},{14,12},{16,18},{18,... | collective-permute-start | bytes 884744 | tf_op jit(solution)/shard_map/ppermute | solution.py:671
  18.1 11.0 %all-to-all-start.1 = ((bf16[16,32,128]{2,1,0:T(8,128)(2,1)}), bf16[16,32,128]{2,1,0:T(8,128)(2,1)S(1)}, u32[]{:S(2)}, u32[]{:S(2)}) async-start(bf16[16,32,128]{2,1,0:T(8,128)(2,1)} %bitcast.7), calls=%async_computation.1 | async-start | bytes 262144 | tf_op jit(solution)/shard_map/all_to_all | solution.py:674
  21.6 13.6 %collective-permute-start.2 = (bf16[128,384]{1,0:T(8,128)(2,1)S(1)}, bf16[128,384]{1,0:T(8,128)(2,1)S(1)}, u32[]{:S(2)}, u32[]{:S(2)}) collective-permute-start(bf16[128,384]{1,0:T(8,128)(2,1)S(1)} %get-tuple-element.31), channel_id=1, source_target_pairs={{0,16},{2,18},{4,20},{6,22},{8,24},{10,26},{12,28},{14,30},{16,0},... | collective-permute-start | bytes 294920 | tf_op jit(solution)/shard_map/ppermute | solution.py:668
  30.3 3.5 %copy-start.8 = (bf16[1,16,640]{2,1,0:T(8,128)(2,1)S(1)}, bf16[1,16,640]{2,1,0:T(8,128)(2,1)}, u32[]{:S(2)}) copy-start(bf16[1,16,640]{2,1,0:T(8,128)(2,1)} %param.24) | copy-start | bytes 61444
  30.3 8.2 %all-to-all-start.2 = ((bf16[8,16,128]{2,1,0:T(8,128)(2,1)}), bf16[8,16,128]{2,1,0:T(8,128)(2,1)S(1)}, u32[]{:S(2)}, u32[]{:S(2)}) async-start(bf16[8,16,128]{2,1,0:T(8,128)(2,1)} %get-tuple-element.30), calls=%async_computation.2 | async-start | bytes 65536 | tf_op jit(solution)/shard_map/all_to_all | solution.py:674

commit v7 on v6

--- a/solution.py
+++ b/solution.py
@@ -358,7 +358,7 @@
     *refs,
 ):
     arrival_refs, refs = refs[:volumes], refs[volumes:]
-    (out_ref, maps_ref), handed, (arrived, leaving) = refs[:2], refs[2:-2], refs[-2:]
+    out_ref, maps_ref, arrived, leaving = refs
     depth, pitch = sent_ref.shape[:2]
     volume = own_volume(depth)
     mask = pick(blocks(read_mask(mask_ref, table_ref.shape[0]), volumes), volume)
@@ -387,11 +387,6 @@
     maps_real = jnp.concatenate([part[0] for part in parts], axis=0)
     maps_imag = jnp.concatenate([part[1] for part in parts], axis=0)
     maps_ref[...] = jnp.concatenate([maps_real, maps_imag], axis=0).astype(BF16)
-    real_parts, imag_parts = blocks(maps_real, volumes), blocks(maps_imag, volumes)
-    for step, ref in enumerate(handed, 1):
-        place = lax.rem(volume + step, jnp.int32(volumes))
-        both = [pick(real_parts, place), pick(imag_parts, place)]
-        ref[...] = jnp.concatenate(both, axis=0).astype(BF16)
 
     images = spread(maps_real, maps_imag, over_rows(reals, coils), over_rows(imags, coils))
     mask = jnp.concatenate([mask, mask], axis=0)
@@ -436,52 +431,20 @@
     return jnp.concatenate([real, imag], axis=0)
 
 
-def first_refine_kernel(
+def refine_kernel(
     lines,
     volumes,
     sent_ref,
-    first_ref,
-    second_ref,
-    columns_ref,
-    out_ref,
-    model_ref,
-    arrived,
-    leaving,
-):
-    unpack_sum(sent_ref, arrived)
-    depth, pitch = sent_ref.shape[0], sent_ref.shape[2]
-    rows = depth * volumes
-    width = padded(lines, LANES)
-    count = width // LANES
-    picture = round_bf(read_complex(arrived, pitch, 0, pitch // volumes, count, depth, volumes))
-    hidden = hidden_state(picture, first_ref.at[0], column(columns_ref, 0, first_ref.shape[1]))
-    valid = valid_lanes(hidden.shape[0], width, lines)
-    hidden = hidden * jax.nn.sigmoid(hidden)
-    bias = column(columns_ref, 2 * CASCADES, 2 * rows)
-    model = second_conv(hidden, second_ref.at[0], bias, rows, valid)
-    model_ref[...] = model.astype(BF16)
-    leaving[...] = jnp.zeros_like(leaving)
-    real, imag = halves(model)
-    for place, pair in enumerate(zip(blocks(real, volumes), blocks(imag, volumes))):
-        chunks = lane_chunks(pair[0]) + lane_chunks(pair[1])
-        write_rows(leaving, out_ref.shape[1], chunks, place * len(chunks))
-    out_ref[...] = leaving[...].astype(BF16).reshape(out_ref.shape)
-
-
-def slots_kernel(
-    lines,
-    volumes,
-    sent_ref,
-    model_ref,
     cotangent_ref,
     first_ref,
     first_t_ref,
     second_ref,
     second_t_ref,
     columns_ref,
+    out_ref,
     image_ref,
-    spread_ref,
     arrived,
+    leaving,
 ):
     unpack_sum(sent_ref, arrived)
     depth, pitch = sent_ref.shape[0], sent_ref.shape[2]
@@ -495,9 +458,9 @@
     cotangent = jnp.concatenate(
         split_complex(lane_chunks(cotangent_ref[...].astype(F32)), lines), axis=0
     )
-    model = model_ref[...].astype(F32)
     tall = first_ref.shape[1]
     weight = [column(columns_ref, CASCADES + cascade, 2 * rows) for cascade in range(CASCADES)]
+    bias = [column(columns_ref, 2 * CASCADES + cascade, 2 * rows) for cascade in range(CASCADES)]
 
     share = [jnp.ones_like(weight[0])]
     for cascade in range(CASCADES):
@@ -509,12 +472,12 @@
 
     hidden = hidden_state(round_bf(begun), first_ref.at[0], column(columns_ref, 0, tall))
     valid = valid_lanes(hidden.shape[0], width, lines)
-    unused, slope_first = slopes(hidden)
+    active, slope_first = slopes(hidden)
+    model = round_bf(second_conv(active, second_ref.at[0], bias[0], rows, valid))
     picture = round_bf(share[1] * begun + power * model)
     hidden = hidden_state(picture, first_ref.at[1], column(columns_ref, 1, tall))
     active, slope_second = slopes(hidden)
-    bias = column(columns_ref, 2 * CASCADES + 1, 2 * rows)
-    later = round_bf(second_conv(active, second_ref.at[1], bias, rows, valid))
+    later = round_bf(second_conv(active, second_ref.at[1], bias[1], rows, valid))
     image_ref[...] = share[2] * begun + power * (model + later)
 
     through = power * cotangent
@@ -528,7 +491,13 @@
     kept = (1.0 - weight[0], 1.0 - weight[1])
     of_cotangent = weight[1] + weight[0] * kept[1] + kept[0] * kept[1]
     of_second = weight[0] + kept[0]
-    spread_ref[...] = of_cotangent * cotangent + of_second * back_second + back_first
+    pulled = of_cotangent * cotangent + of_second * back_second + back_first
+    leaving[...] = jnp.zeros_like(leaving)
+    parts = [blocks(part, volumes) for value in (model, pulled) for part in halves(value)]
+    for place in range(volumes):
+        chunks = [chunk for part in parts for chunk in lane_chunks(part[place])]
+        write_rows(leaving, out_ref.shape[1], chunks, place * len(chunks))
+    out_ref[...] = leaving[...].astype(BF16).reshape(out_ref.shape)
 
 
 def normal_kernel(
@@ -537,40 +506,52 @@
     volumes,
     sent_ref,
     maps_ref,
-    spread_ref,
     mask_ref,
     table_ref,
     minus_ref,
     plus_ref,
     out_ref,
-    arrived,
-    leaving,
+    *refs,
 ):
+    pulled_refs, (arrived, leaving) = refs[:volumes], refs[volumes:]
     arrived[...] = sent_ref[...].astype(F32).reshape(arrived.shape)
     depth, pitch = sent_ref.shape[:2]
     volume = own_volume(depth)
     count = maps_ref.shape[1] // LANES
-    firsts = [place * 2 * count for place in range(volumes)]
-    reals = [read_image(arrived, pitch, first, count, depth) for first in firsts]
-    imags = [read_image(arrived, pitch, first + count, count, depth) for first in firsts]
+    fields = [
+        [
+            read_image(arrived, pitch, (place * 4 + field) * count, count, depth)
+            for place in range(volumes)
+        ]
+        for field in range(4)
+    ]
+    reals, imags = fields[:2]
     maps_real, maps_imag = halves(maps_ref[...].astype(F32))
+    parts = [blocks(maps_real, volumes), blocks(maps_imag, volumes), *fields[2:]]
+    for step, ref in enumerate(pulled_refs):
+        place = lax.rem(volume + step, jnp.int32(volumes))
+        chosen = [pick(part, place) for part in parts]
+        ref[...] = jnp.concatenate(chosen, axis=0).astype(BF16)
     mask = over_coils(pick(blocks(read_mask(mask_ref, table_ref.shape[0]), volumes), volume), 2 * volumes * coils)
     images = spread(maps_real, maps_imag, over_rows(reals, coils), over_rows(imags, coils))
     images = masked_normal(images, table_ref, minus_ref, plus_ref, mask)
     found = [row_sums(value, volumes, coils) for value in collect(maps_real, maps_imag, images)]
     leaving[...] = jnp.zeros_like(leaving)
-    pitch = out_ref.shape[2]
-    first = 0
     for place in range(volumes):
         chunks = join_complex(found[0][place], found[1][place], lines)
-        for target in range(volumes):
-            kept = [jnp.where(volume == target, chunk, 0.0) for chunk in chunks]
-            write_rows(leaving, pitch, kept, target * depth * pitch + first)
-        first += len(chunks)
-    write_rows(leaving, pitch, join_complex(*halves(spread_ref[...]), lines), first)
-    message = leaving[...].astype(BF16).reshape(out_ref.shape[0], *out_ref.shape[2:])
+        write_rows(leaving, out_ref.shape[2], chunks, place * len(chunks))
+    message = leaving[...].astype(BF16).reshape(depth, *out_ref.shape[2:])
     for device in range(out_ref.shape[1]):
         out_ref[:, device] = message
+
+
+def from_volumes(refs, volume, parts, volumes):
+    sources = [blocks(ref, parts) for ref in refs]
+    ordered = []
+    for place in range(volumes):
+        step = lax.rem(volume - place + volumes, jnp.int32(volumes))
+        ordered.append([pick([source[part] for source in sources], step) for part in range(parts)])
+    return ordered
 
 
 def end_kernel(
@@ -583,29 +564,22 @@
     mask_ref,
     table_ref,
     minus_ref,
-    maps_ref,
     *refs,
 ):
-    handed, (picture_ref, grad_ref, arrived) = refs[: volumes - 1], refs[volumes - 1 :]
-    slots, pitch = sent_ref.shape[0], sent_ref.shape[2]
-    depth = slots // volumes
+    handed = [ref[...].astype(F32) for ref in refs[:volumes]]
+    picture_ref, grad_ref, arrived = refs[volumes:]
+    depth, pitch = sent_ref.shape[0], sent_ref.shape[2]
     volume = own_volume(depth)
     count = 2 * lines // LANES
-    own = maps_ref[...].astype(F32)
-    sources = [[pick(blocks(part, volumes), volume) for part in halves(own)]]
-    sources += [halves(ref[...].astype(F32)) for ref in handed]
-    maps = []
-    for part in range(2):
-        ordered = []
-        for place in range(volumes):
-            step = lax.rem(volume - place + volumes, jnp.int32(volumes))
-            ordered.append(blocks(pick([source[part] for source in sources], step), coils))
-        maps.append(
-            jnp.concatenate([ordered[v][coil] for coil in range(coils) for v in range(volumes)], 0)
-        )
-    arrived[...] = sent_ref[:, 0].astype(F32).reshape(arrived.shape)
-    chunks = read_rows(arrived, pitch, volumes * count, count, slots)
-    real, imag = split_complex(chunks, lines)
+    planes = coils * depth
+    maps = [value[: 2 * planes] for value in handed]
+    maps = from_volumes(maps, volume, 2 * coils, volumes)
+    maps = [
+        jnp.concatenate([maps[v][first + coil] for coil in range(coils) for v in range(volumes)], 0)
+        for first in (0, coils)
+    ]
+    pulled = from_volumes([value[2 * planes :] for value in handed], volume, 2, volumes)
+    real, imag = [jnp.concatenate([part[field] for part in pulled], 0) for field in range(2)]
     images = spread(*maps, over_coils(real, coils), over_coils(imag, coils))
     spectrum = depth_apply(line_apply(images, table_ref, -1.0), minus_ref)
     spectrum = spectrum * over_coils(read_mask(mask_ref, table_ref.shape[0]), 2 * coils)
@@ -613,18 +587,13 @@
     write_rows(grad_ref, len(chunks), chunks)
 
     unpack_sum(sent_ref, arrived)
-    picture = image_ref[...]
-    scale = column(columns_ref, CASCADES + 1, picture.shape[0])
     parts = [[], []]
-    size = depth * pitch
-    total = arrived[:size]
-    for other in range(1, volumes):
-        total = total + arrived[other * size : (other + 1) * size]
-    arrived[:size] = total
     for place in range(volumes):
         chunks = read_rows(arrived, pitch, place * count, count, depth)
         for part, value in zip(parts, split_complex(chunks, lines)):
             part.append(value)
+    picture = image_ref[...]
+    scale = column(columns_ref, CASCADES + 1, picture.shape[0])
     picture = picture - scale * jnp.concatenate(parts[0] + parts[1], axis=0)
     for index, chunk in enumerate(join_complex(*halves(picture), lines)):
         picture_ref[:, index * LANES : (index + 1) * LANES] = chunk
@@ -749,40 +718,27 @@
     arrived = exchange(packed, "section", near)
 
     depth_pitch = padded(volumes * 5 * count, 16 * volumes)
-    partial, maps, *handed = call(
+    partial, maps = call(
         functools.partial(rows_kernel, coils, lines, volumes),
         "combine_rows",
         (arrived, mask, table, minus, plus, *images),
         [
             shape(depth, coil_devices, depth_pitch, LANES, kind=BF16),
             shape(2 * planes, width, kind=BF16),
-        ]
-        + [shape(2 * planes // volumes, width, kind=BF16)] * (volumes - 1),
+        ],
         [(depth * pitch, LANES), (depth * depth_pitch, LANES)],
         4 * line_flops,
     )
-    handed = [from_group(value, step) for step, value in enumerate(handed, 1)]
 
     partial = exchange(partial.reshape(-1, depth_pitch, LANES), both, near_both)
     partial = partial.reshape(depth, coil_devices, depth_pitch, LANES)
 
-    model_pitch = padded(volumes * 2 * count, 16)
-    moved, model = call(
-        functools.partial(first_refine_kernel, lines, volumes),
-        "refine_first",
-        (partial, first, second, columns),
-        [shape(depth, model_pitch, LANES, kind=BF16), shape(2 * rows, width, kind=BF16)],
-        [(depth * depth_pitch, LANES), (depth * model_pitch, LANES)],
-        4 * tall * wide * width,
-    )
-    moved = exchange(moved, "section", near)
-
-    image, pulled = call(
-        functools.partial(slots_kernel, lines, volumes),
+    model_pitch = padded(volumes * 4 * count, 8)
+    moved, image = call(
+        functools.partial(refine_kernel, lines, volumes),
         "refine_and_back",
         (
             partial,
-            model,
             cotangent.reshape(rows, two_lines),
             first,
             first_t,
@@ -790,30 +746,34 @@
             second_t,
             columns,
         ),
-        [shape(2 * rows, width), shape(2 * rows, width)],
-        [(depth * depth_pitch, LANES)],
+        [shape(depth, model_pitch, LANES, kind=BF16), shape(2 * rows, width)],
+        [(depth * depth_pitch, LANES), (depth * model_pitch, LANES)],
         14 * tall * wide * width,
     )
-
-    moved, *handed = lax.optimization_barrier((moved, *handed))
-    end_pitch = padded((volumes + 1) * whole_count, 16)
-    (partial,) = call(
+    moved = exchange(moved, "section", near)
+
+    end_pitch = padded(volumes * whole_count, 16)
+    partial, *handed = call(
         functools.partial(normal_kernel, coils, lines, volumes),
         "masked_normal",
-        (moved, maps, pulled, mask, table, minus, plus),
-        [shape(slots, coil_devices, end_pitch, LANES, kind=BF16)],
-        [(depth * model_pitch, LANES), (slots * end_pitch, LANES)],
+        (moved, maps, mask, table, minus, plus),
+        [shape(depth, coil_devices, end_pitch, LANES, kind=BF16)]
+        + [shape(2 * planes // volumes + 2 * depth, width, kind=BF16)] * volumes,
+        [(depth * model_pitch, LANES), (depth * end_pitch, LANES)],
         3 * line_flops,
     )
-    partial = exchange(partial.reshape(-1, end_pitch, LANES), both, None)
-    partial = partial.reshape(slots, coil_devices, end_pitch, LANES)
+    partial = exchange(partial.reshape(-1, end_pitch, LANES), both, near_both)
+    partial = partial.reshape(depth, coil_devices, end_pitch, LANES)
+    handed[1:] = [
+        between_cores(from_group(value, step, 1)) for step, value in enumerate(handed[1:], 1)
+    ]
 
     image, grad = call(
         functools.partial(end_kernel, coils, lines, volumes),
         "outputs",
-        (columns, partial, image, mask, table, minus, maps, *handed),
+        (columns, partial, image, mask, table, minus, *handed),
         [shape(rows, two_lines), shape(planes * whole_count, LANES)],
-        [(slots * end_pitch, LANES)],
+        [(depth * end_pitch, LANES)],
         2 * line_flops,
     )
     return image.reshape(1, rows, two_lines), grad.reshape(coils, slots, 1, two_lines)

time: 52 us -> 50.1 us (0.963)
  blocking collectives: 10.3 us -> 16.5 us
  starting transfers between devices: 17.1 us -> 12.9 us
  waiting for transfers between devices: 11.2 us -> 8.15 us
  Pallas kernels: 12 us -> 11.1 us
    all_to_all x3 -> x2, waiting for transfers between devices: 11.2 us -> 4.33 us  [exchange(): lax.all_to_all(value, axes, 0, 0, tiled=True, axis_index_groups=groups)]
    all_to_all x1 -> x2, blocking collectives: 10.3 us -> 16.5 us  [exchange(): lax.all_to_all(value, axes, 0, 0, tiled=True, axis_index_groups=groups)]
    ppermute x2, waiting for transfers between devices: 0.01 us -> 3.81 us  [from_group(): return lax.ppermute(value, 'section', pairs)]
    all_to_all x3 -> x2, starting transfers between devices: 11.1 us -> 7.59 us  [exchange(): lax.all_to_all(value, axes, 0, 0, tiled=True, axis_index_groups=groups)]
    pallas_call x9 -> x8, Pallas kernels: 12 us -> 11.1 us  [call(): pl.pallas_call(kernel, name=name, out_shape=tuple(outs), in_specs=[pl.Blo...]
    ppermute x2, starting transfers between devices: 5.43 us -> 4.78 us  [from_group(): return lax.ppermute(value, 'section', pairs)]
  transfers between devices with their start and end apart: 6 -> 6, of which waited for: 3 -> 3; matrix products, arithmetic and copies ran while one was open for 0% -> 0% of each run, Pallas kernels for 10% -> 5%
where the time goes in v7:
time: 50.1 us; the launch traced here: 49.7 us
  blocking collectives  16.5 us (33%)
  starting transfers between devices  12.9 us (26%)
  Pallas kernels  11.1 us (22%)
  waiting for transfers between devices  8.15 us (16%)
  between operations  0.89 us (2%)
    all_to_all x2, blocking collectives, exchange(): lax.all_to_all(value, axes, 0, 0, tiled=True, axis_index_groups=groups)  16.5 us
    pallas_call x8, Pallas kernels, call(): pl.pallas_call(kernel, name=name, out_shape=tuple(outs), in_specs=[pl.Blo...  11.1 us
    all_to_all x2, starting transfers between devices, exchange(): lax.all_to_all(value, axes, 0, 0, tiled=True, axis_index_groups=groups)  7.59 us
    ppermute x2, starting transfers between devices, from_group(): return lax.ppermute(value, 'section', pairs)  4.78 us
    all_to_all x2, waiting for transfers between devices, exchange(): lax.all_to_all(value, axes, 0, 0, tiled=True, axis_index_groups=groups)  4.33 us
    ppermute x2, waiting for transfers between devices, from_group(): return lax.ppermute(value, 'section', pairs)  3.81 us
  transfers between devices with their start and end apart: 6, of which 3 were waited for; matrix products, arithmetic and copies ran while one was open for 0% of the time, Pallas kernels for 5%

profile of v7, /device:TPU:0, one launch (start us, length us, event | category | flops | bytes accessed | tf_op | source)
XLA Modules:
  0.0 49.7 jit_solution(15598561280338294188)
XLA Ops:
  0.6 0.0 copy-start.2
  0.6 0.0 copy-start.4
  0.7 0.0 copy-start.5
  0.7 2.0 %pack_maps.1 = (bf16[8,96,128]{2,1,0:T(8,128)(2,1)}, bf16[64,640]{1,0:T(8,128)(2,1)}) custom-call(bf16[128,640]{1,0:T(8,128)(2,1)} %bitcast.14, bf16[128,640]{1,0:T(8,128)(2,1)} %bitcast.28, bf16[16,640]{1,0:T(8,128)(2,1)} %bitcast.24), custom_call_target="tpu_custom_call" | custom-call | flops 1000 | bytes 626688 | tf_op jit(solution)/shard_map/pack_maps/pallas_call | solution.py:605
  2.7 3.5 %collective-permute-start = (bf16[64,640]{1,0:T(8,128)(2,1)}, bf16[64,640]{1,0:T(8,128)(2,1)S(1)}, u32[]{:S(2)}, u32[]{:S(2)}) collective-permute-start(bf16[64,640]{1,0:T(8,128)(2,1)} %get-tuple-element.20), channel_id=1, source_target_pairs={{0,18},{2,16},{4,22},{6,20},{8,26},{10,24},{12,30},{14,28},{16,2},... | collective-permute-start | bytes 245768 | tf_op jit(solution)/shard_map/ppermute | solution.py:637
  6.2 4.1 %all-to-all-start = ((bf16[8,96,128]{2,1,0:T(8,128)(2,1)}), bf16[8,96,128]{2,1,0:T(8,128)(2,1)S(1)}, u32[]{:S(2)}, u32[]{:S(2)}) async-start(bf16[8,96,128]{2,1,0:T(8,128)(2,1)} %get-tuple-element.23), calls=%async_computation | async-start | bytes 393216 | tf_op jit(solution)/shard_map/all_to_all | solution.py:643
  10.4 0.0 copy-start.3
  10.4 0.0 copy-start.7
  10.4 1.5 %lay_out_taps.1 = (bf16[2,288,128]{2,1,0:T(8,128)(2,1)S(1)}, bf16[2,96,288]{2,1,0:T(8,128)(2,1)S(1)}, bf16[2,96,288]{2,1,0:T(8,128)(2,1)S(1)}, bf16[2,288,128]{2,1,0:T(8,128)(2,1)S(1)}, f32[288,128]{1,0:T(8,128)S(1)}) custom-call(f32[2]{0:T(128)S(1)} %copy-done.13, f32[18,2,18]{2,1,0:T(2,128)S(1)} %bitcast.26, f32[18,2,18]{2,1,0:T(2,128)S(1)} %bitcast.27, ...), custom_call_target="tpu_custom_call" | custom-call | flops 113246208 | bytes 1357032 | tf_op jit(solution)/shard_map/lay_out_taps/pallas_call | solution.py:605
  11.9 0.0 collective-permute-done.kspace_ref
  11.9 0.0 copy-start.1
  12.0 0.4 far_images.1
  12.4 0.0 copy-start.6
  12.4 0.0 copy-start.14
  12.4 0.6 %collective-permute-start.1 = (f32[192,384]{1,0:T(8,128)S(1)}, f32[192,384]{1,0:T(8,128)S(1)}, u32[]{:S(2)}, u32[]{:S(2)}) collective-permute-start(f32[192,384]{1,0:T(8,128)S(1)} %far_images.1), channel_id=1, source_target_pairs={{0,2},{2,0},{4,6},{6,4},{8,10},{10,8},{12,14},{14,12},{16,18},{18,... | collective-permute-start | bytes 884744 | tf_op jit(solution)/shard_map/ppermute | solution.py:640
  13.0 0.4 own_images.1.refs_0_
  13.5 2.5 %all-to-all-done.sent_ref = bf16[8,96,128]{2,1,0:T(8,128)(2,1)S(1)} async-done(((bf16[8,96,128]{2,1,0:T(8,128)(2,1)}), bf16[8,96,128]{2,1,0:T(8,128)(2,1)S(1)}, u32[]{:S(2)}, u32[]{:S(2)}) %all-to-all-start) | async-done | bytes 196640 | tf_op jit(solution)/shard_map/all_to_all | solution.py:643
  15.9 0.0 collective-permute-done.1.refs_1_
  16.0 1.4 %combine_rows.1 = (bf16[8,2,32,128]{3,2,1,0:T(8,128)(2,1)S(1)}, bf16[256,384]{1,0:T(8,128)(2,1)S(1)}) custom-call(bf16[8,96,128]{2,1,0:T(8,128)(2,1)S(1)} %all-to-all-done.sent_ref, s32[16,320]{1,0:T(8,128)S(1)} %bitcast.20, bf16[384,768]{1,0:T(8,128)(2,1)S(1)} %copy-done, bf16[256,256]{1,0:T(8,128)(2,1)S(1)} %copy-done.6, bf16[256,256]{1,0:T(8,128)(2,1)S(1)} %copy-done.14, ...), custom_call_target="tpu_custom_call" | custom-call | flops 603979776 | bytes 1888256 | tf_op jit(solution)/shard_map/combine_rows/pallas_call | solution.py:605
  17.4 0.0 copy-start.8
  17.4 9.3 %all_to_all.20 = bf16[16,32,128]{2,1,0:T(8,128)(2,1)S(1)} all-to-all(bf16[16,32,128]{2,1,0:T(8,128)(2,1)S(1)} %bitcast.23), channel_id=1, replica_groups={{0,1,2,3,4,5,6,7,8,9,10,11,12,13,14,15},{16,17,18,19,20,21,22,23,24,25,..., dimensions={0} | all-to-all | bytes 262144 | tf_op jit(solution)/shard_map/all_to_all | solution.py:643
  26.8 0.0 copy-done.8
  26.8 1.9 %refine_and_back.1 = (bf16[8,24,128]{2,1,0:T(8,128)(2,1)S(1)}, f32[32,384]{1,0:T(8,128)S(1)}) custom-call(bf16[8,2,32,128]{3,2,1,0:T(8,128)(2,1)S(1)} %bitcast.16, bf16[16,640]{1,0:T(8,128)(2,1)S(1)} %bitcast.25, bf16[2,288,128]{2,1,0:T(8,128)(2,1)S(1)} %get-tuple-element.26.first_ref, bf16[2,96,288]{2,1,0:T(8,128)(2,1)S(1)} %get-tuple-element.27.first_t_ref, ...), custom_call_target="tpu_custom_call" | custom-call | flops 198180864 | bytes 913408 | tf_op jit(solution)/shard_map/refine_and_back/pallas_call | solution.py:605
  28.7 7.2 %all_to_all.21.sent_ref = bf16[8,24,128]{2,1,0:T(8,128)(2,1)S(1)} all-to-all(bf16[8,24,128]{2,1,0:T(8,128)(2,1)S(1)} %get-tuple-element.30), channel_id=1, replica_groups={{0,2,4,6,8,10,12,14},{16,18,20,22,24,26,28,30},{1,3,5,7,9,11,13,15},{17..., dimensions={0} | all-to-all | bytes 98304 | tf_op jit(solution)/shard_map/all_to_all | solution.py:643
  35.8 1.8 %masked_normal.1 = (bf16[8,2,16,128]{3,2,1,0:T(8,128)(2,1)}, bf16[144,384]{1,0:T(8,128)(2,1)S(1)}, bf16[144,384]{1,0:T(8,128)(2,1)S(1)}) custom-call(bf16[8,24,128]{2,1,0:T(8,128)(2,1)S(1)} %all_to_all.21.sent_ref, bf16[256,384]{1,0:T(8,128)(2,1)S(1)} %get-tuple-element.31.maps_ref, s32[16,320]{1,0:T(8,128)S(1)} %bitcast.21, bf16[384,768]{1,0:T(8,128)(2,1)S(1)} %copy-done, ...), custom_call_target="tpu_custom_call" | custom-call | flops 452984832 | bytes 1404928 | tf_op jit(solution)/shard_map/masked_normal/pallas_call | solution.py:605
  37.7 1.3 %collective-permute-start.2 = (bf16[144,384]{1,0:T(8,128)(2,1)S(1)}, bf16[144,384]{1,0:T(8,128)(2,1)S(1)}, u32[]{:S(2)}, u32[]{:S(2)}) collective-permute-start(bf16[144,384]{1,0:T(8,128)(2,1)S(1)} %get-tuple-element.35), channel_id=1, source_target_pairs={{0,18},{2,16},{4,22},{6,20},{8,26},{10,24},{12,30},{14,28},{16,2},... | collective-permute-start | bytes 331784 | tf_op jit(solution)/shard_map/ppermute | solution.py:637
  39.0 3.5 %all-to-all-start.3 = ((bf16[16,16,128]{2,1,0:T(8,128)(2,1)}), bf16[16,16,128]{2,1,0:T(8,128)(2,1)S(1)}, u32[]{:S(2)}, u32[]{:S(2)}) async-start(bf16[16,16,128]{2,1,0:T(8,128)(2,1)} %bitcast.9), calls=%async_computation.3 | async-start | bytes 131072 | tf_op jit(solution)/shard_map/all_to_all | solution.py:643
  42.5 3.8 %collective-permute-done.2 = bf16[144,384]{1,0:T(8,128)(2,1)S(1)} collective-permute-done((bf16[144,384]{1,0:T(8,128)(2,1)S(1)}, bf16[144,384]{1,0:T(8,128)(2,1)S(1)}, u32[]{:S(2)}, u32[]{:S(2)}) %collective-permute-start.2) | collective-permute-done | bytes 110624 | tf_op jit(solution)/shard_map/ppermute | solution.py:637
  46.3 0.0 collective-permute-start.3
  46.3 1.8 %all-to-all-done.3 = bf16[16,16,128]{2,1,0:T(8,128)(2,1)S(1)} async-done(((bf16[16,16,128]{2,1,0:T(8,128)(2,1)}), bf16[16,16,128]{2,1,0:T(8,128)(2,1)S(1)}, u32[]{:S(2)}, u32[]{:S(2)}) %all-to-all-start.3) | async-done | bytes 65568 | tf_op jit(solution)/shard_map/all_to_all | solution.py:643
  48.1 0.0 collective-permute-done.3.refs_1_
  48.1 1.5 %outputs.1 = (f32[16,640]{1,0:T(8,128)}, f32[640,128]{1,0:T(8,128)}) custom-call(f32[288,128]{1,0:T(8,128)S(1)} %get-tuple-element.22.columns_ref, bf16[8,2,16,128]{3,2,1,0:T(8,128)(2,1)S(1)} %bitcast.17, f32[32,384]{1,0:T(8,128)S(1)} %get-tuple-element.33.image_ref, s32[16,320]{1,0:T(8,128)S(1)} %bitcast.22, bf16[384,768]{1,0:T(8,128)(2,1)S(1)} %copy-done, ...), custom_call_target="tpu_custom_call" | custom-call | flops 301989888 | bytes 1593344 | tf_op jit(solution)/shard_map/outputs/pallas_call | solution.py:605
  (20 shorter events, 0.0 us)
Async XLA Ops:
  0.6 9.7 %copy-start.2 = (bf16[128,1536]{1,0:T(8,128)(2,1)S(1)}, bf16[128,1536]{1,0:T(8,128)(2,1)}, u32[]{:S(2)}) copy-start(bf16[128,1536]{1,0:T(8,128)(2,1)} %constant.19.clone.place_ref) | copy-start | bytes 1179652
  0.6 9.7 %copy-start.4 = (f32[288,128]{1,0:T(8,128)S(1)}, f32[288,128]{1,0:T(8,128)}, u32[]{:S(2)}) copy-start(f32[288,128]{1,0:T(8,128)} %constant.20.clone.offset_ref) | copy-start | bytes 442372
  0.7 9.7 %copy-start.5 = (f32[288,128]{1,0:T(8,128)S(1)}, f32[288,128]{1,0:T(8,128)}, u32[]{:S(2)}) copy-start(f32[288,128]{1,0:T(8,128)} %constant.18.clone.repeat_ref) | copy-start | bytes 442372
  0.7 9.7 %copy-start.9 = (f32[2,9,18,2]{2,3,1,0:T(2,128)S(1)}, f32[2,9,18,2]{2,3,1,0:T(2,128)}, u32[]{:S(2)}) copy-start(f32[2,9,18,2]{2,3,1,0:T(2,128)} %param.20) | copy-start | bytes 7780
  0.7 9.7 %copy-start.10 = (f32[2,9,2,18]{3,2,1,0:T(2,128)S(1)}, f32[2,9,2,18]{3,2,1,0:T(2,128)}, u32[]{:S(2)}) copy-start(f32[2,9,2,18]{3,2,1,0:T(2,128)} %param.22) | copy-start | bytes 7780
  0.7 9.7 %copy-start.11 = (f32[2,18]{1,0:T(2,128)S(1)}, f32[2,18]{1,0:T(2,128)}, u32[]{:S(2)}) copy-start(f32[2,18]{1,0:T(2,128)} %bias_in_ref.1) | copy-start | bytes 436
  0.7 9.7 %copy-start.12 = (f32[2,2]{1,0:T(2,128)S(1)}, f32[2,2]{1,0:T(2,128)}, u32[]{:S(2)}) copy-start(f32[2,2]{1,0:T(2,128)} %bias_out_ref.1) | copy-start | bytes 52
  0.7 9.7 %copy-start.13 = (f32[2]{0:T(128)S(1)}, f32[2]{0:T(128)}, u32[]{:S(2)}) copy-start(f32[2]{0:T(128)} %weight_ref.1) | copy-start | bytes 28
  2.7 9.2 %copy-start = (bf16[384,768]{1,0:T(8,128)(2,1)S(1)}, bf16[384,768]{1,0:T(8,128)(2,1)}, u32[]{:S(2)}) copy-start(bf16[384,768]{1,0:T(8,128)(2,1)} %constant.14.clone.table_ref) | copy-start | bytes 1769476
  2.7 9.2 %collective-permute-start = (bf16[64,640]{1,0:T(8,128)(2,1)}, bf16[64,640]{1,0:T(8,128)(2,1)S(1)}, u32[]{:S(2)}, u32[]{:S(2)}) collective-permute-start(bf16[64,640]{1,0:T(8,128)(2,1)} %get-tuple-element.20), channel_id=1, source_target_pairs={{0,18},{2,16},{4,22},{6,20},{8,26},{10,24},{12,30},{14,28},{16,2},... | collective-permute-start | bytes 245768 | tf_op jit(solution)/shard_map/ppermute | solution.py:637
  6.2 9.7 %all-to-all-start = ((bf16[8,96,128]{2,1,0:T(8,128)(2,1)}), bf16[8,96,128]{2,1,0:T(8,128)(2,1)S(1)}, u32[]{:S(2)}, u32[]{:S(2)}) async-start(bf16[8,96,128]{2,1,0:T(8,128)(2,1)} %get-tuple-element.23), calls=%async_computation | async-start | bytes 393216 | tf_op jit(solution)/shard_map/all_to_all | solution.py:643
  10.4 1.6 %copy-start.3 = (s32[2,8,320]{2,1,0:T(8,128)S(1)}, s32[2,8,320]{2,1,0:T(8,128)}, u32[]{:S(2)}) copy-start(s32[2,8,320]{2,1,0:T(8,128)} %param.18) | copy-start | bytes 61444
  10.4 1.6 %copy-start.7 = (bf16[128,128]{1,0:T(8,128)(2,1)S(1)}, bf16[128,128]{1,0:T(8,128)(2,1)}, u32[]{:S(2)}) copy-start(bf16[128,128]{1,0:T(8,128)(2,1)} %constant.17.clone.plus_ref) | copy-start | bytes 98308
  11.9 1.1 %copy-start.1 = (bf16[8,16,1,640]{3,1,2,0:T(8,128)(2,1)S(1)}, bf16[8,16,1,640]{3,1,2,0:T(8,128)(2,1)}, u32[]{:S(2)}) copy-start(bf16[8,16,1,640]{3,1,2,0:T(8,128)(2,1)} %param.16) | copy-start | bytes 491524
  12.4 3.5 %copy-start.6 = (bf16[256,256]{1,0:T(8,128)(2,1)S(1)}, bf16[256,256]{1,0:T(8,128)(2,1)}, u32[]{:S(2)}) copy-start(bf16[256,256]{1,0:T(8,128)(2,1)} %constant.15.clone.minus_ref) | copy-start | bytes 393220
  12.4 3.5 %copy-start.14 = (bf16[256,256]{1,0:T(8,128)(2,1)S(1)}, bf16[256,256]{1,0:T(8,128)(2,1)}, u32[]{:S(2)}) copy-start(bf16[256,256]{1,0:T(8,128)(2,1)} %constant.16.clone.plus_ref) | copy-start | bytes 393220
  12.4 3.5 %collective-permute-start.1 = (f32[192,384]{1,0:T(8,128)S(1)}, f32[192,384]{1,0:T(8,128)S(1)}, u32[]{:S(2)}, u32[]{:S(2)}) collective-permute-start(f32[192,384]{1,0:T(8,128)S(1)} %far_images.1), channel_id=1, source_target_pairs={{0,2},{2,0},{4,6},{6,4},{8,10},{10,8},{12,14},{14,12},{16,18},{18,... | collective-permute-start | bytes 884744 | tf_op jit(solution)/shard_map/ppermute | solution.py:640
  17.4 9.3 %copy-start.8 = (bf16[1,16,640]{2,1,0:T(8,128)(2,1)S(1)}, bf16[1,16,640]{2,1,0:T(8,128)(2,1)}, u32[]{:S(2)}) copy-start(bf16[1,16,640]{2,1,0:T(8,128)(2,1)} %param.24) | copy-start | bytes 61444
  37.7 8.6 %collective-permute-start.2 = (bf16[144,384]{1,0:T(8,128)(2,1)S(1)}, bf16[144,384]{1,0:T(8,128)(2,1)S(1)}, u32[]{:S(2)}, u32[]{:S(2)}) collective-permute-start(bf16[144,384]{1,0:T(8,128)(2,1)S(1)} %get-tuple-element.35), channel_id=1, source_target_pairs={{0,18},{2,16},{4,22},{6,20},{8,26},{10,24},{12,30},{14,28},{16,2},... | collective-permute-start | bytes 331784 | tf_op jit(solution)/shard_map/ppermute | solution.py:637
  39.0 9.2 %all-to-all-start.3 = ((bf16[16,16,128]{2,1,0:T(8,128)(2,1)}), bf16[16,16,128]{2,1,0:T(8,128)(2,1)S(1)}, u32[]{:S(2)}, u32[]{:S(2)}) async-start(bf16[16,16,128]{2,1,0:T(8,128)(2,1)} %bitcast.9), calls=%async_computation.3 | async-start | bytes 131072 | tf_op jit(solution)/shard_map/all_to_all | solution.py:643
  46.3 1.8 %collective-permute-start.3 = (bf16[144,384]{1,0:T(8,128)(2,1)S(1)}, bf16[144,384]{1,0:T(8,128)(2,1)S(1)}, u32[]{:S(2)}, u32[]{:S(2)}) collective-permute-start(bf16[144,384]{1,0:T(8,128)(2,1)S(1)} %collective-permute-done.2), channel_id=1, source_target_pairs={{0,2},{2,0},{4,6},{6,4},{8,10},{10,8},{12,14},{14,12},{16,18},{18,... | collective-permute-start | bytes 331784 | tf_op jit(solution)/shard_map/ppermute | solution.py:640

commit v8 on v7

--- a/solution.py
+++ b/solution.py
@@ -500,6 +500,26 @@
     out_ref[...] = leaving[...].astype(BF16).reshape(out_ref.shape)
 
 
+def hand_kernel(volumes, sent_ref, maps_ref, *refs):
+    outs, (arrived,) = refs[:-1], refs[-1:]
+    arrived[...] = sent_ref[...].astype(F32).reshape(arrived.shape)
+    depth, pitch = sent_ref.shape[:2]
+    volume = own_volume(depth)
+    count = maps_ref.shape[1] // LANES
+    parts = [blocks(part, volumes) for part in halves(maps_ref[...].astype(F32))]
+    for field in (2, 3):
+        parts.append(
+            [
+                read_image(arrived, pitch, (place * 4 + field) * count, count, depth)
+                for place in range(volumes)
+            ]
+        )
+    for step, ref in enumerate(outs):
+        place = lax.rem(volume + step, jnp.int32(volumes))
+        chosen = [pick(part, place) for part in parts]
+        ref[...] = jnp.concatenate(chosen, axis=0).astype(BF16)
+
+
 def normal_kernel(
     coils,
     lines,
@@ -511,9 +531,9 @@
     minus_ref,
     plus_ref,
     out_ref,
-    *refs,
+    arrived,
+    leaving,
 ):
-    pulled_refs, (arrived, leaving) = refs[:volumes], refs[volumes:]
     arrived[...] = sent_ref[...].astype(F32).reshape(arrived.shape)
     depth, pitch = sent_ref.shape[:2]
     volume = own_volume(depth)
@@ -523,15 +543,10 @@
             read_image(arrived, pitch, (place * 4 + field) * count, count, depth)
             for place in range(volumes)
         ]
-        for field in range(4)
+        for field in range(2)
     ]
-    reals, imags = fields[:2]
+    reals, imags = fields
     maps_real, maps_imag = halves(maps_ref[...].astype(F32))
-    parts = [blocks(maps_real, volumes), blocks(maps_imag, volumes), *fields[2:]]
-    for step, ref in enumerate(pulled_refs):
-        place = lax.rem(volume + step, jnp.int32(volumes))
-        chosen = [pick(part, place) for part in parts]
-        ref[...] = jnp.concatenate(chosen, axis=0).astype(BF16)
     mask = over_coils(pick(blocks(read_mask(mask_ref, table_ref.shape[0]), volumes), volume), 2 * volumes * coils)
     images = spread(maps_real, maps_imag, over_rows(reals, coils), over_rows(imags, coils))
     images = masked_normal(images, table_ref, minus_ref, plus_ref, mask)
@@ -554,23 +569,18 @@
     return ordered
 
 
-def end_kernel(
+def grad_kernel(
     coils,
     lines,
     volumes,
-    columns_ref,
-    sent_ref,
-    image_ref,
     mask_ref,
     table_ref,
     minus_ref,
     *refs,
 ):
-    handed = [ref[...].astype(F32) for ref in refs[:volumes]]
-    picture_ref, grad_ref, arrived = refs[volumes:]
-    depth, pitch = sent_ref.shape[0], sent_ref.shape[2]
+    handed, (grad_ref,) = [ref[...].astype(F32) for ref in refs[:volumes]], refs[volumes:]
+    depth = mask_ref.shape[0] // volumes
     volume = own_volume(depth)
-    count = 2 * lines // LANES
     planes = coils * depth
     maps = [value[: 2 * planes] for value in handed]
     maps = from_volumes(maps, volume, 2 * coils, volumes)
@@ -586,6 +596,10 @@
     chunks = join_complex(*halves(spectrum), lines)
     write_rows(grad_ref, len(chunks), chunks)
 
+
+def picture_kernel(lines, volumes, columns_ref, sent_ref, image_ref, picture_ref, arrived):
+    depth, pitch = sent_ref.shape[0], sent_ref.shape[2]
+    count = 2 * lines // LANES
     unpack_sum(sent_ref, arrived)
     parts = [[], []]
     for place in range(volumes):
@@ -753,28 +767,45 @@
     moved = exchange(moved, "section", near)
 
     end_pitch = padded(volumes * whole_count, 16)
-    partial, *handed = call(
+    handed = call(
+        functools.partial(hand_kernel, volumes),
+        "hand_on",
+        (moved, maps),
+        [shape(2 * planes // volumes + 2 * depth, width, kind=BF16)] * volumes,
+        [(depth * model_pitch, LANES)],
+        1000,
+    )
+    handed = list(handed)
+    (partial,) = call(
         functools.partial(normal_kernel, coils, lines, volumes),
         "masked_normal",
         (moved, maps, mask, table, minus, plus),
-        [shape(depth, coil_devices, end_pitch, LANES, kind=BF16)]
-        + [shape(2 * planes // volumes + 2 * depth, width, kind=BF16)] * volumes,
+        [shape(depth, coil_devices, end_pitch, LANES, kind=BF16)],
         [(depth * model_pitch, LANES), (depth * end_pitch, LANES)],
         3 * line_flops,
     )
     partial = exchange(partial.reshape(-1, end_pitch, LANES), both, near_both)
     partial = partial.reshape(depth, coil_devices, end_pitch, LANES)
     handed[1:] = [
-        between_cores(from_group(value, step, 1)) for step, value in enumerate(handed[1:], 1)
+        from_group(value, step) for step, value in enumerate(handed[1:], 1)
     ]
 
-    image, grad = call(
-        functools.partial(end_kernel, coils, lines, volumes),
-        "outputs",
-        (columns, partial, image, mask, table, minus, *handed),
-        [shape(rows, two_lines), shape(planes * whole_count, LANES)],
+    (grad,) = call(
+        functools.partial(grad_kernel, coils, lines, volumes),
+        "grad_kspace",
+        (mask, table, minus, *handed),
+        [shape(planes * whole_count, LANES)],
+        [],
+        line_flops,
+    )
+    partial, grad = lax.optimization_barrier((partial, grad))
+    (image,) = call(
+        functools.partial(picture_kernel, lines, volumes),
+        "image_out",
+        (columns, partial, image),
+        [shape(rows, two_lines)],
         [(depth * end_pitch, LANES)],
-        2 * line_flops,
+        1000,
     )
     return image.reshape(1, rows, two_lines), grad.reshape(coils, slots, 1, two_lines)
 

time: 50.1 us -> 50.1 us (level)
  waiting for transfers between devices: 8.15 us -> 6.62 us
  Pallas kernels: 11.1 us -> 11.9 us
  starting transfers between devices: 12.9 us -> 13.6 us
    ppermute x2, waiting for transfers between devices: 3.81 us -> 0.74 us  [from_group(): return lax.ppermute(value, 'section', pairs)]
    all_to_all x2, waiting for transfers between devices: 4.33 us -> 5.88 us  [exchange(): lax.all_to_all(value, axes, 0, 0, tiled=True, axis_index_groups=groups)]
    pallas_call x8 -> x10, Pallas kernels: 11.1 us -> 11.9 us  [call(): pl.pallas_call(kernel, name=name, out_shape=tuple(outs), in_specs=[pl.Blo...]
    ppermute x2, starting transfers between devices: 4.78 us -> 5.49 us  [from_group(): return lax.ppermute(value, 'section', pairs)]
  transfers between devices with their start and end apart: 6 -> 5, of which waited for: 3 -> 3; matrix products, arithmetic and copies ran while one was open for 0% -> 0% of each run, Pallas kernels for 5% -> 11%
where the time goes in v8:
time: 50.1 us; the launch traced here: 49.7 us
  blocking collectives  16.5 us (33%)
  starting transfers between devices  13.6 us (27%)
  Pallas kernels  11.9 us (24%)
  waiting for transfers between devices  6.62 us (13%)
  between operations  0.89 us (2%)
    all_to_all x2, blocking collectives, exchange(): lax.all_to_all(value, axes, 0, 0, tiled=True, axis_index_groups=groups)  16.5 us
    pallas_call x10, Pallas kernels, call(): pl.pallas_call(kernel, name=name, out_shape=tuple(outs), in_specs=[pl.Blo...  11.9 us
    all_to_all x2, starting transfers between devices, exchange(): lax.all_to_all(value, axes, 0, 0, tiled=True, axis_index_groups=groups)  7.59 us
    all_to_all x2, waiting for transfers between devices, exchange(): lax.all_to_all(value, axes, 0, 0, tiled=True, axis_index_groups=groups)  5.88 us
    ppermute x2, starting transfers between devices, from_group(): return lax.ppermute(value, 'section', pairs)  5.49 us
  transfers between devices with their start and end apart: 5, of which 3 were waited for; matrix products, arithmetic and copies ran while one was open for 0% of the time, Pallas kernels for 11%

profile of v8, /device:TPU:0, one launch (start us, length us, event | category | flops | bytes accessed | tf_op | source)
XLA Modules:
  0.0 49.7 jit_solution(354053372423886305)
XLA Ops:
  0.6 0.0 copy-start.2
  0.6 0.0 copy-start.4
  0.7 0.0 copy-start.5
  0.7 2.0 %pack_maps.1 = (bf16[8,96,128]{2,1,0:T(8,128)(2,1)}, bf16[64,640]{1,0:T(8,128)(2,1)}) custom-call(bf16[128,640]{1,0:T(8,128)(2,1)} %bitcast.14, bf16[128,640]{1,0:T(8,128)(2,1)} %bitcast.29, bf16[16,640]{1,0:T(8,128)(2,1)} %bitcast.24), custom_call_target="tpu_custom_call" | custom-call | flops 1000 | bytes 626688 | tf_op jit(solution)/shard_map/pack_maps/pallas_call | solution.py:619
  2.7 3.5 %collective-permute-start = (bf16[64,640]{1,0:T(8,128)(2,1)}, bf16[64,640]{1,0:T(8,128)(2,1)S(1)}, u32[]{:S(2)}, u32[]{:S(2)}) collective-permute-start(bf16[64,640]{1,0:T(8,128)(2,1)} %get-tuple-element.19), channel_id=1, source_target_pairs={{0,18},{2,16},{4,22},{6,20},{8,26},{10,24},{12,30},{14,28},{16,2},... | collective-permute-start | bytes 245768 | tf_op jit(solution)/shard_map/ppermute | solution.py:651
  6.2 4.1 %all-to-all-start = ((bf16[8,96,128]{2,1,0:T(8,128)(2,1)}), bf16[8,96,128]{2,1,0:T(8,128)(2,1)S(1)}, u32[]{:S(2)}, u32[]{:S(2)}) async-start(bf16[8,96,128]{2,1,0:T(8,128)(2,1)} %get-tuple-element.22), calls=%async_computation | async-start | bytes 393216 | tf_op jit(solution)/shard_map/all_to_all | solution.py:657
  10.4 0.0 copy-start.3
  10.4 0.0 copy-start.7
  10.4 1.5 %lay_out_taps.1 = (bf16[2,288,128]{2,1,0:T(8,128)(2,1)S(1)}, bf16[2,96,288]{2,1,0:T(8,128)(2,1)S(1)}, bf16[2,96,288]{2,1,0:T(8,128)(2,1)S(1)}, bf16[2,288,128]{2,1,0:T(8,128)(2,1)S(1)}, f32[288,128]{1,0:T(8,128)S(1)}) custom-call(f32[2]{0:T(128)S(1)} %copy-done.13, f32[18,2,18]{2,1,0:T(2,128)S(1)} %bitcast.26, f32[18,2,18]{2,1,0:T(2,128)S(1)} %bitcast.27, ...), custom_call_target="tpu_custom_call" | custom-call | flops 113246208 | bytes 1357032 | tf_op jit(solution)/shard_map/lay_out_taps/pallas_call | solution.py:619
  11.9 0.0 collective-permute-done.kspace_ref
  11.9 0.0 copy-start.1
  12.0 0.4 far_images.1
  12.4 0.0 copy-start.6
  12.4 0.0 copy-start.14
  12.4 0.6 %collective-permute-start.1 = (f32[192,384]{1,0:T(8,128)S(1)}, f32[192,384]{1,0:T(8,128)S(1)}, u32[]{:S(2)}, u32[]{:S(2)}) collective-permute-start(f32[192,384]{1,0:T(8,128)S(1)} %far_images.1), channel_id=1, source_target_pairs={{0,2},{2,0},{4,6},{6,4},{8,10},{10,8},{12,14},{14,12},{16,18},{18,... | collective-permute-start | bytes 884744 | tf_op jit(solution)/shard_map/ppermute | solution.py:654
  13.0 0.4 own_images.1.refs_0_
  13.5 2.5 %all-to-all-done.sent_ref = bf16[8,96,128]{2,1,0:T(8,128)(2,1)S(1)} async-done(((bf16[8,96,128]{2,1,0:T(8,128)(2,1)}), bf16[8,96,128]{2,1,0:T(8,128)(2,1)S(1)}, u32[]{:S(2)}, u32[]{:S(2)}) %all-to-all-start) | async-done | bytes 196640 | tf_op jit(solution)/shard_map/all_to_all | solution.py:657
  15.9 0.0 collective-permute-done.1.refs_1_
  16.0 0.0 copy-done.14
  16.0 1.4 %combine_rows.1 = (bf16[8,2,32,128]{3,2,1,0:T(8,128)(2,1)S(1)}, bf16[256,384]{1,0:T(8,128)(2,1)S(1)}) custom-call(bf16[8,96,128]{2,1,0:T(8,128)(2,1)S(1)} %all-to-all-done.sent_ref, s32[16,320]{1,0:T(8,128)S(1)} %bitcast.20, bf16[384,768]{1,0:T(8,128)(2,1)S(1)} %copy-done, bf16[256,256]{1,0:T(8,128)(2,1)S(1)} %copy-done.6, bf16[256,256]{1,0:T(8,128)(2,1)S(1)} %copy-done.14, ...), custom_call_target="tpu_custom_call" | custom-call | flops 603979776 | bytes 1888256 | tf_op jit(solution)/shard_map/combine_rows/pallas_call | solution.py:619
  17.4 0.0 copy-start.8
  17.4 9.3 %all_to_all.20 = bf16[16,32,128]{2,1,0:T(8,128)(2,1)S(1)} all-to-all(bf16[16,32,128]{2,1,0:T(8,128)(2,1)S(1)} %bitcast.23), channel_id=1, replica_groups={{0,1,2,3,4,5,6,7,8,9,10,11,12,13,14,15},{16,17,18,19,20,21,22,23,24,25,..., dimensions={0} | all-to-all | bytes 262144 | tf_op jit(solution)/shard_map/all_to_all | solution.py:657
  26.8 1.9 %refine_and_back.1 = (bf16[8,24,128]{2,1,0:T(8,128)(2,1)S(1)}, f32[32,384]{1,0:T(8,128)S(1)}) custom-call(bf16[8,2,32,128]{3,2,1,0:T(8,128)(2,1)S(1)} %bitcast.16, bf16[16,640]{1,0:T(8,128)(2,1)S(1)} %bitcast.25, bf16[2,288,128]{2,1,0:T(8,128)(2,1)S(1)} %get-tuple-element.25.first_ref, bf16[2,96,288]{2,1,0:T(8,128)(2,1)S(1)} %get-tuple-element.26.first_t_ref, ...), custom_call_target="tpu_custom_call" | custom-call | flops 198180864 | bytes 913408 | tf_op jit(solution)/shard_map/refine_and_back/pallas_call | solution.py:619
  28.7 7.2 %all_to_all.21.sent_ref = bf16[8,24,128]{2,1,0:T(8,128)(2,1)S(1)} all-to-all(bf16[8,24,128]{2,1,0:T(8,128)(2,1)S(1)} %get-tuple-element.29), channel_id=1, replica_groups={{0,2,4,6,8,10,12,14},{16,18,20,22,24,26,28,30},{1,3,5,7,9,11,13,15},{17..., dimensions={0} | all-to-all | bytes 98304 | tf_op jit(solution)/shard_map/all_to_all | solution.py:657
  35.8 0.1 hand_on.1
  35.9 2.0 %collective-permute-start.2 = (bf16[144,384]{1,0:T(8,128)(2,1)S(1)}, bf16[144,384]{1,0:T(8,128)(2,1)S(1)}, u32[]{:S(2)}, u32[]{:S(2)}) collective-permute-start(bf16[144,384]{1,0:T(8,128)(2,1)S(1)} %get-tuple-element.32), channel_id=1, source_target_pairs={{0,16},{2,18},{4,20},{6,22},{8,24},{10,26},{12,28},{14,30},{16,0},... | collective-permute-start | bytes 331784 | tf_op jit(solution)/shard_map/ppermute | solution.py:651
  37.9 1.8 %masked_normal.1 = bf16[8,2,16,128]{3,2,1,0:T(8,128)(2,1)} custom-call(bf16[8,24,128]{2,1,0:T(8,128)(2,1)S(1)} %all_to_all.21.sent_ref, bf16[256,384]{1,0:T(8,128)(2,1)S(1)} %get-tuple-element.30.maps_ref, s32[16,320]{1,0:T(8,128)S(1)} %bitcast.21, bf16[384,768]{1,0:T(8,128)(2,1)S(1)} %copy-done, bf16[256,256]{1,0:T(8,128)(2,1)S(1)} %copy-done.6, ...), custom_call_target="tpu_custom_call" | custom-call | flops 452984832 | bytes 1183744 | tf_op jit(solution)/shard_map/masked_normal/pallas_call | solution.py:619
  39.7 3.5 %all-to-all-start.3 = ((bf16[16,16,128]{2,1,0:T(8,128)(2,1)}), bf16[16,16,128]{2,1,0:T(8,128)(2,1)S(1)}, u32[]{:S(2)}, u32[]{:S(2)}) async-start(bf16[16,16,128]{2,1,0:T(8,128)(2,1)} %bitcast.9), calls=%async_computation.3 | async-start | bytes 131072 | tf_op jit(solution)/shard_map/all_to_all | solution.py:657
  43.2 0.7 %collective-permute-done.2.refs_1_ = bf16[144,384]{1,0:T(8,128)(2,1)S(1)} collective-permute-done((bf16[144,384]{1,0:T(8,128)(2,1)S(1)}, bf16[144,384]{1,0:T(8,128)(2,1)S(1)}, u32[]{:S(2)}, u32[]{:S(2)}) %collective-permute-start.2) | collective-permute-done | bytes 110624 | tf_op jit(solution)/shard_map/ppermute | solution.py:651
  44.0 1.5 %grad_kspace.1 = f32[640,128]{1,0:T(8,128)} custom-call(s32[16,320]{1,0:T(8,128)S(1)} %bitcast.22, bf16[384,768]{1,0:T(8,128)(2,1)S(1)} %copy-done, bf16[256,256]{1,0:T(8,128)(2,1)S(1)} %copy-done.6, bf16[144,384]{1,0:T(8,128)(2,1)S(1)} %get-tuple-element.31.refs_0_, bf16[144,384]{1,0:T(8,128)(2,1)S(1)} %collective-permute-done.2.refs_1_), custom_call_target="tpu_custom_call" | custom-call | flops 150994944 | bytes 1290240 | tf_op jit(solution)/shard_map/grad_kspace/pallas_call | solution.py:619
  45.5 3.4 %all-to-all-done.3 = bf16[16,16,128]{2,1,0:T(8,128)(2,1)S(1)} async-done(((bf16[16,16,128]{2,1,0:T(8,128)(2,1)}), bf16[16,16,128]{2,1,0:T(8,128)(2,1)S(1)}, u32[]{:S(2)}, u32[]{:S(2)}) %all-to-all-start.3) | async-done | bytes 65568 | tf_op jit(solution)/shard_map/all_to_all | solution.py:657
  48.9 0.8 %image_out.1 = f32[16,640]{1,0:T(8,128)} custom-call(f32[288,128]{1,0:T(8,128)S(1)} %get-tuple-element.21.columns_ref, bf16[8,2,16,128]{3,2,1,0:T(8,128)(2,1)S(1)} %bitcast.17, f32[32,384]{1,0:T(8,128)S(1)} %get-tuple-element.34.image_ref), custom_call_target="tpu_custom_call" | custom-call | flops 1000 | bytes 303104 | tf_op jit(solution)/shard_map/image_out/pallas_call | solution.py:619
  (20 shorter events, 0.0 us)
Async XLA Ops:
  0.6 9.7 %copy-start.2 = (bf16[128,1536]{1,0:T(8,128)(2,1)S(1)}, bf16[128,1536]{1,0:T(8,128)(2,1)}, u32[]{:S(2)}) copy-start(bf16[128,1536]{1,0:T(8,128)(2,1)} %constant.19.clone.place_ref) | copy-start | bytes 1179652
  0.6 9.7 %copy-start.4 = (f32[288,128]{1,0:T(8,128)S(1)}, f32[288,128]{1,0:T(8,128)}, u32[]{:S(2)}) copy-start(f32[288,128]{1,0:T(8,128)} %constant.20.clone.offset_ref) | copy-start | bytes 442372
  0.7 9.7 %copy-start.5 = (f32[288,128]{1,0:T(8,128)S(1)}, f32[288,128]{1,0:T(8,128)}, u32[]{:S(2)}) copy-start(f32[288,128]{1,0:T(8,128)} %constant.18.clone.repeat_ref) | copy-start | bytes 442372
  0.7 9.7 %copy-start.9 = (f32[2,9,18,2]{2,3,1,0:T(2,128)S(1)}, f32[2,9,18,2]{2,3,1,0:T(2,128)}, u32[]{:S(2)}) copy-start(f32[2,9,18,2]{2,3,1,0:T(2,128)} %param.20) | copy-start | bytes 7780
  0.7 9.7 %copy-start.10 = (f32[2,9,2,18]{3,2,1,0:T(2,128)S(1)}, f32[2,9,2,18]{3,2,1,0:T(2,128)}, u32[]{:S(2)}) copy-start(f32[2,9,2,18]{3,2,1,0:T(2,128)} %param.22) | copy-start | bytes 7780
  0.7 9.7 %copy-start.11 = (f32[2,18]{1,0:T(2,128)S(1)}, f32[2,18]{1,0:T(2,128)}, u32[]{:S(2)}) copy-start(f32[2,18]{1,0:T(2,128)} %bias_in_ref.1) | copy-start | bytes 436
  0.7 9.7 %copy-start.12 = (f32[2,2]{1,0:T(2,128)S(1)}, f32[2,2]{1,0:T(2,128)}, u32[]{:S(2)}) copy-start(f32[2,2]{1,0:T(2,128)} %bias_out_ref.1) | copy-start | bytes 52
  0.7 9.7 %copy-start.13 = (f32[2]{0:T(128)S(1)}, f32[2]{0:T(128)}, u32[]{:S(2)}) copy-start(f32[2]{0:T(128)} %weight_ref.1) | copy-start | bytes 28
  2.7 9.2 %copy-start = (bf16[384,768]{1,0:T(8,128)(2,1)S(1)}, bf16[384,768]{1,0:T(8,128)(2,1)}, u32[]{:S(2)}) copy-start(bf16[384,768]{1,0:T(8,128)(2,1)} %constant.14.clone.table_ref) | copy-start | bytes 1769476
  2.7 9.2 %collective-permute-start = (bf16[64,640]{1,0:T(8,128)(2,1)}, bf16[64,640]{1,0:T(8,128)(2,1)S(1)}, u32[]{:S(2)}, u32[]{:S(2)}) collective-permute-start(bf16[64,640]{1,0:T(8,128)(2,1)} %get-tuple-element.19), channel_id=1, source_target_pairs={{0,18},{2,16},{4,22},{6,20},{8,26},{10,24},{12,30},{14,28},{16,2},... | collective-permute-start | bytes 245768 | tf_op jit(solution)/shard_map/ppermute | solution.py:651
  6.2 9.7 %all-to-all-start = ((bf16[8,96,128]{2,1,0:T(8,128)(2,1)}), bf16[8,96,128]{2,1,0:T(8,128)(2,1)S(1)}, u32[]{:S(2)}, u32[]{:S(2)}) async-start(bf16[8,96,128]{2,1,0:T(8,128)(2,1)} %get-tuple-element.22), calls=%async_computation | async-start | bytes 393216 | tf_op jit(solution)/shard_map/all_to_all | solution.py:657
  10.4 1.6 %copy-start.3 = (s32[2,8,320]{2,1,0:T(8,128)S(1)}, s32[2,8,320]{2,1,0:T(8,128)}, u32[]{:S(2)}) copy-start(s32[2,8,320]{2,1,0:T(8,128)} %param.18) | copy-start | bytes 61444
  10.4 1.6 %copy-start.7 = (bf16[128,128]{1,0:T(8,128)(2,1)S(1)}, bf16[128,128]{1,0:T(8,128)(2,1)}, u32[]{:S(2)}) copy-start(bf16[128,128]{1,0:T(8,128)(2,1)} %constant.17.clone.plus_ref) | copy-start | bytes 98308
  11.9 1.1 %copy-start.1 = (bf16[8,16,1,640]{3,1,2,0:T(8,128)(2,1)S(1)}, bf16[8,16,1,640]{3,1,2,0:T(8,128)(2,1)}, u32[]{:S(2)}) copy-start(bf16[8,16,1,640]{3,1,2,0:T(8,128)(2,1)} %param.16) | copy-start | bytes 491524
  12.4 3.5 %copy-start.6 = (bf16[256,256]{1,0:T(8,128)(2,1)S(1)}, bf16[256,256]{1,0:T(8,128)(2,1)}, u32[]{:S(2)}) copy-start(bf16[256,256]{1,0:T(8,128)(2,1)} %constant.15.clone.minus_ref) | copy-start | bytes 393220
  12.4 3.5 %copy-start.14 = (bf16[256,256]{1,0:T(8,128)(2,1)S(1)}, bf16[256,256]{1,0:T(8,128)(2,1)}, u32[]{:S(2)}) copy-start(bf16[256,256]{1,0:T(8,128)(2,1)} %constant.16.clone.plus_ref) | copy-start | bytes 393220
  12.4 3.5 %collective-permute-start.1 = (f32[192,384]{1,0:T(8,128)S(1)}, f32[192,384]{1,0:T(8,128)S(1)}, u32[]{:S(2)}, u32[]{:S(2)}) collective-permute-start(f32[192,384]{1,0:T(8,128)S(1)} %far_images.1), channel_id=1, source_target_pairs={{0,2},{2,0},{4,6},{6,4},{8,10},{10,8},{12,14},{14,12},{16,18},{18,... | collective-permute-start | bytes 884744 | tf_op jit(solution)/shard_map/ppermute | solution.py:654
  17.4 9.3 %copy-start.8 = (bf16[1,16,640]{2,1,0:T(8,128)(2,1)S(1)}, bf16[1,16,640]{2,1,0:T(8,128)(2,1)}, u32[]{:S(2)}) copy-start(bf16[1,16,640]{2,1,0:T(8,128)(2,1)} %param.24) | copy-start | bytes 61444
  35.9 8.1 %collective-permute-start.2 = (bf16[144,384]{1,0:T(8,128)(2,1)S(1)}, bf16[144,384]{1,0:T(8,128)(2,1)S(1)}, u32[]{:S(2)}, u32[]{:S(2)}) collective-permute-start(bf16[144,384]{1,0:T(8,128)(2,1)S(1)} %get-tuple-element.32), channel_id=1, source_target_pairs={{0,16},{2,18},{4,20},{6,22},{8,24},{10,26},{12,28},{14,30},{16,0},... | collective-permute-start | bytes 331784 | tf_op jit(solution)/shard_map/ppermute | solution.py:651
  39.7 9.2 %all-to-all-start.3 = ((bf16[16,16,128]{2,1,0:T(8,128)(2,1)}), bf16[16,16,128]{2,1,0:T(8,128)(2,1)S(1)}, u32[]{:S(2)}, u32[]{:S(2)}) async-start(bf16[16,16,128]{2,1,0:T(8,128)(2,1)} %bitcast.9), calls=%async_computation.3 | async-start | bytes 131072 | tf_op jit(solution)/shard_map/all_to_all | solution.py:657

commit v9 on v8

--- a/solution.py
+++ b/solution.py
@@ -15,6 +15,7 @@
 LANES = 128
 VMEM_BYTES = 48 * 1024 * 1024
 FAR_PARTS = 3
+HAND_PLANES = 6
 LARGE_VMEM_BYTES = 60 * 1024 * 1024
 
 F32 = jnp.float32
@@ -517,7 +518,9 @@
     for step, ref in enumerate(outs):
         place = lax.rem(volume + step, jnp.int32(volumes))
         chosen = [pick(part, place) for part in parts]
-        ref[...] = jnp.concatenate(chosen, axis=0).astype(BF16)
+        ref[...] = jnp.zeros_like(ref)
+        chosen = jnp.concatenate(chosen, axis=0).astype(BF16)
+        ref[: chosen.shape[0]] = chosen
 
 
 def normal_kernel(
@@ -588,7 +591,8 @@
         jnp.concatenate([maps[v][first + coil] for coil in range(coils) for v in range(volumes)], 0)
         for first in (0, coils)
     ]
-    pulled = from_volumes([value[2 * planes :] for value in handed], volume, 2, volumes)
+    pulled = [value[2 * planes : 2 * planes + 2 * depth] for value in handed]
+    pulled = from_volumes(pulled, volume, 2, volumes)
     real, imag = [jnp.concatenate([part[field] for part in pulled], 0) for field in range(2)]
     images = spread(*maps, over_coils(real, coils), over_coils(imag, coils))
     spectrum = depth_apply(line_apply(images, table_ref, -1.0), minus_ref)
@@ -611,6 +615,23 @@
     picture = picture - scale * jnp.concatenate(parts[0] + parts[1], axis=0)
     for index, chunk in enumerate(join_complex(*halves(picture), lines)):
         picture_ref[:, index * LANES : (index + 1) * LANES] = chunk
+
+
+def end_kernel(
+    coils,
+    lines,
+    volumes,
+    columns_ref,
+    sent_ref,
+    image_ref,
+    mask_ref,
+    table_ref,
+    minus_ref,
+    *refs,
+):
+    handed, (picture_ref, grad_ref, arrived) = refs[:volumes], refs[volumes:]
+    grad_kernel(coils, lines, volumes, mask_ref, table_ref, minus_ref, *handed, grad_ref)
+    picture_kernel(lines, volumes, columns_ref, sent_ref, image_ref, picture_ref, arrived)
 
 
 def call(kernel, name, operands, outs, scratch, flops, vmem_bytes=VMEM_BYTES, scalars=0):
@@ -771,7 +792,7 @@
         functools.partial(hand_kernel, volumes),
         "hand_on",
         (moved, maps),
-        [shape(2 * planes // volumes + 2 * depth, width, kind=BF16)] * volumes,
+        [shape(2 * planes // volumes + HAND_PLANES * depth, width, kind=BF16)] * volumes,
         [(depth * model_pitch, LANES)],
         1000,
     )
@@ -790,22 +811,13 @@
         from_group(value, step) for step, value in enumerate(handed[1:], 1)
     ]
 
-    (grad,) = call(
-        functools.partial(grad_kernel, coils, lines, volumes),
-        "grad_kspace",
-        (mask, table, minus, *handed),
-        [shape(planes * whole_count, LANES)],
-        [],
-        line_flops,
-    )
-    partial, grad = lax.optimization_barrier((partial, grad))
-    (image,) = call(
-        functools.partial(picture_kernel, lines, volumes),
-        "image_out",
-        (columns, partial, image),
-        [shape(rows, two_lines)],
+    image, grad = call(
+        functools.partial(end_kernel, coils, lines, volumes),
+        "outputs",
+        (columns, partial, image, mask, table, minus, *handed),
+        [shape(rows, two_lines), shape(planes * whole_count, LANES)],
         [(depth * end_pitch, LANES)],
-        1000,
+        2 * line_flops,
     )
     return image.reshape(1, rows, two_lines), grad.reshape(coils, slots, 1, two_lines)
 

time: 50.1 us -> 49.3 us (0.984)
  blocking collectives: 16.5 us -> 24.8 us
  waiting for transfers between devices: 6.62 us -> 2.5 us
  starting transfers between devices: 13.6 us -> 10.1 us
  Pallas kernels: 11.9 us -> 10.5 us
    all_to_all x2 -> x3, blocking collectives: 16.5 us -> 24.8 us  [exchange(): lax.all_to_all(value, axes, 0, 0, tiled=True, axis_index_groups=groups)]
    all_to_all x2 -> x1, starting transfers between devices: 7.59 us -> 4.09 us  [exchange(): lax.all_to_all(value, axes, 0, 0, tiled=True, axis_index_groups=groups)]
    all_to_all x2 -> x1, waiting for transfers between devices: 5.88 us -> 2.5 us  [exchange(): lax.all_to_all(value, axes, 0, 0, tiled=True, axis_index_groups=groups)]
    pallas_call x10 -> x9, Pallas kernels: 11.9 us -> 10.5 us  [call(): pl.pallas_call(kernel, name=name, out_shape=tuple(outs), in_specs=[pl.Blo...]
    ppermute x2, waiting for transfers between devices: 0.74 us -> 0.01 us  [from_group(): return lax.ppermute(value, 'section', pairs)]
  transfers between devices with their start and end apart: 5 -> 4, of which waited for: 3 -> 1; matrix products, arithmetic and copies ran while one was open for 0% -> 0% of each run, Pallas kernels for 11% -> 7%
where the time goes in v9:
time: 49.3 us; the launch traced here: 48.9 us
  blocking collectives  24.8 us (50%)
  Pallas kernels  10.5 us (21%)
  starting transfers between devices  10.1 us (20%)
  waiting for transfers between devices  2.5 us (5%)
  between operations  0.88 us (2%)
    all_to_all x3, blocking collectives, exchange(): lax.all_to_all(value, axes, 0, 0, tiled=True, axis_index_groups=groups)  24.8 us
    pallas_call x9, Pallas kernels, call(): pl.pallas_call(kernel, name=name, out_shape=tuple(outs), in_specs=[pl.Blo...  10.5 us
    ppermute x2, starting transfers between devices, from_group(): return lax.ppermute(value, 'section', pairs)  5.49 us
    all_to_all x1, starting transfers between devices, exchange(): lax.all_to_all(value, axes, 0, 0, tiled=True, axis_index_groups=groups)  4.09 us
    all_to_all x1, waiting for transfers between devices, exchange(): lax.all_to_all(value, axes, 0, 0, tiled=True, axis_index_groups=groups)  2.5 us
  transfers between devices with their start and end apart: 4, of which 1 were waited for; matrix products, arithmetic and copies ran while one was open for 0% of the time, Pallas kernels for 7%

profile of v9, /device:TPU:0, one launch (start us, length us, event | category | flops | bytes accessed | tf_op | source)
XLA Modules:
  0.0 48.9 jit_solution(15407177296292944266)
XLA Ops:
  0.6 0.0 copy-start.2
  0.6 0.0 copy-start.4
  0.7 0.0 copy-start.5
  0.7 0.0 copy-start.9
  0.7 0.0 copy-start.10
  0.7 2.0 %pack_maps.1 = (bf16[8,96,128]{2,1,0:T(8,128)(2,1)}, bf16[64,640]{1,0:T(8,128)(2,1)}) custom-call(bf16[128,640]{1,0:T(8,128)(2,1)} %bitcast.14, bf16[128,640]{1,0:T(8,128)(2,1)} %bitcast.29, bf16[16,640]{1,0:T(8,128)(2,1)} %bitcast.24), custom_call_target="tpu_custom_call" | custom-call | flops 1000 | bytes 626688 | tf_op jit(solution)/shard_map/pack_maps/pallas_call | solution.py:640
  2.7 3.5 %collective-permute-start = (bf16[64,640]{1,0:T(8,128)(2,1)}, bf16[64,640]{1,0:T(8,128)(2,1)S(1)}, u32[]{:S(2)}, u32[]{:S(2)}) collective-permute-start(bf16[64,640]{1,0:T(8,128)(2,1)} %get-tuple-element.19), channel_id=1, source_target_pairs={{0,18},{2,16},{4,22},{6,20},{8,26},{10,24},{12,30},{14,28},{16,2},... | collective-permute-start | bytes 245768 | tf_op jit(solution)/shard_map/ppermute | solution.py:672
  6.2 4.1 %all-to-all-start = ((bf16[8,96,128]{2,1,0:T(8,128)(2,1)}), bf16[8,96,128]{2,1,0:T(8,128)(2,1)S(1)}, u32[]{:S(2)}, u32[]{:S(2)}) async-start(bf16[8,96,128]{2,1,0:T(8,128)(2,1)} %get-tuple-element.22), calls=%async_computation | async-start | bytes 393216 | tf_op jit(solution)/shard_map/all_to_all | solution.py:678
  10.4 0.0 copy-start.3
  10.4 0.0 copy-start.7
  10.4 1.5 %lay_out_taps.1 = (bf16[2,288,128]{2,1,0:T(8,128)(2,1)S(1)}, bf16[2,96,288]{2,1,0:T(8,128)(2,1)S(1)}, bf16[2,96,288]{2,1,0:T(8,128)(2,1)S(1)}, bf16[2,288,128]{2,1,0:T(8,128)(2,1)S(1)}, f32[288,128]{1,0:T(8,128)S(1)}) custom-call(f32[2]{0:T(128)S(1)} %copy-done.13, f32[18,2,18]{2,1,0:T(2,128)S(1)} %bitcast.27, f32[18,2,18]{2,1,0:T(2,128)S(1)} %bitcast.28, ...), custom_call_target="tpu_custom_call" | custom-call | flops 113246208 | bytes 1357032 | tf_op jit(solution)/shard_map/lay_out_taps/pallas_call | solution.py:640
  11.9 0.0 collective-permute-done.kspace_ref
  11.9 0.0 copy-start.1
  12.0 0.4 far_images.1
  12.4 0.0 copy-start.6
  12.4 0.0 copy-start.14
  12.4 0.6 %collective-permute-start.1 = (f32[192,384]{1,0:T(8,128)S(1)}, f32[192,384]{1,0:T(8,128)S(1)}, u32[]{:S(2)}, u32[]{:S(2)}) collective-permute-start(f32[192,384]{1,0:T(8,128)S(1)} %far_images.1), channel_id=1, source_target_pairs={{0,2},{2,0},{4,6},{6,4},{8,10},{10,8},{12,14},{14,12},{16,18},{18,... | collective-permute-start | bytes 884744 | tf_op jit(solution)/shard_map/ppermute | solution.py:675
  13.0 0.4 own_images.1.refs_0_
  13.5 2.5 %all-to-all-done.sent_ref = bf16[8,96,128]{2,1,0:T(8,128)(2,1)S(1)} async-done(((bf16[8,96,128]{2,1,0:T(8,128)(2,1)}), bf16[8,96,128]{2,1,0:T(8,128)(2,1)S(1)}, u32[]{:S(2)}, u32[]{:S(2)}) %all-to-all-start) | async-done | bytes 196640 | tf_op jit(solution)/shard_map/all_to_all | solution.py:678
  15.9 0.0 collective-permute-done.1.refs_1_
  16.0 1.4 %combine_rows.1 = (bf16[8,2,32,128]{3,2,1,0:T(8,128)(2,1)S(1)}, bf16[256,384]{1,0:T(8,128)(2,1)S(1)}) custom-call(bf16[8,96,128]{2,1,0:T(8,128)(2,1)S(1)} %all-to-all-done.sent_ref, s32[16,320]{1,0:T(8,128)S(1)} %bitcast.20, bf16[384,768]{1,0:T(8,128)(2,1)S(1)} %copy-done, bf16[256,256]{1,0:T(8,128)(2,1)S(1)} %copy-done.6, bf16[256,256]{1,0:T(8,128)(2,1)S(1)} %copy-done.14, ...), custom_call_target="tpu_custom_call" | custom-call | flops 603979776 | bytes 1888256 | tf_op jit(solution)/shard_map/combine_rows/pallas_call | solution.py:640
  17.4 0.0 copy-start.8
  17.4 9.3 %all_to_all.20 = bf16[16,32,128]{2,1,0:T(8,128)(2,1)S(1)} all-to-all(bf16[16,32,128]{2,1,0:T(8,128)(2,1)S(1)} %bitcast.23), channel_id=1, replica_groups={{0,1,2,3,4,5,6,7,8,9,10,11,12,13,14,15},{16,17,18,19,20,21,22,23,24,25,..., dimensions={0} | all-to-all | bytes 262144 | tf_op jit(solution)/shard_map/all_to_all | solution.py:678
  26.8 0.0 copy-done.8
  26.8 1.9 %refine_and_back.1 = (bf16[8,24,128]{2,1,0:T(8,128)(2,1)S(1)}, f32[32,384]{1,0:T(8,128)S(1)}) custom-call(bf16[8,2,32,128]{3,2,1,0:T(8,128)(2,1)S(1)} %bitcast.16, bf16[16,640]{1,0:T(8,128)(2,1)S(1)} %bitcast.25, bf16[2,288,128]{2,1,0:T(8,128)(2,1)S(1)} %get-tuple-element.25.first_ref, bf16[2,96,288]{2,1,0:T(8,128)(2,1)S(1)} %get-tuple-element.26.first_t_ref, ...), custom_call_target="tpu_custom_call" | custom-call | flops 198180864 | bytes 913408 | tf_op jit(solution)/shard_map/refine_and_back/pallas_call | solution.py:640
  28.7 7.2 %all_to_all.21.sent_ref = bf16[8,24,128]{2,1,0:T(8,128)(2,1)S(1)} all-to-all(bf16[8,24,128]{2,1,0:T(8,128)(2,1)S(1)} %get-tuple-element.29), channel_id=1, replica_groups={{0,2,4,6,8,10,12,14},{16,18,20,22,24,26,28,30},{1,3,5,7,9,11,13,15},{17..., dimensions={0} | all-to-all | bytes 98304 | tf_op jit(solution)/shard_map/all_to_all | solution.py:678
  35.8 0.1 hand_on.1
  35.9 2.0 %collective-permute-start.2 = (bf16[176,384]{1,0:T(8,128)(2,1)S(1)}, bf16[176,384]{1,0:T(8,128)(2,1)S(1)}, u32[]{:S(2)}, u32[]{:S(2)}) collective-permute-start(bf16[176,384]{1,0:T(8,128)(2,1)S(1)} %get-tuple-element.33), channel_id=1, source_target_pairs={{0,16},{2,18},{4,20},{6,22},{8,24},{10,26},{12,28},{14,30},{16,0},... | collective-permute-start | bytes 405512 | tf_op jit(solution)/shard_map/ppermute | solution.py:672
  38.0 1.2 %masked_normal.1 = bf16[8,2,16,128]{3,2,1,0:T(8,128)(2,1)S(1)} custom-call(bf16[8,24,128]{2,1,0:T(8,128)(2,1)S(1)} %all_to_all.21.sent_ref, bf16[256,384]{1,0:T(8,128)(2,1)S(1)} %get-tuple-element.30.maps_ref, s32[16,320]{1,0:T(8,128)S(1)} %bitcast.21, bf16[384,768]{1,0:T(8,128)(2,1)S(1)} %copy-done, bf16[256,256]{1,0:T(8,128)(2,1)S(1)} %copy-done.6, ...), custom_call_target="tpu_custom_call" | custom-call | flops 452984832 | bytes 1183744 | tf_op jit(solution)/shard_map/masked_normal/pallas_call | solution.py:640
  39.1 8.3 %all_to_all.22 = bf16[16,16,128]{2,1,0:T(8,128)(2,1)S(1)} all-to-all(bf16[16,16,128]{2,1,0:T(8,128)(2,1)S(1)} %bitcast.26), channel_id=1, replica_groups={{0,1,2,3,4,5,6,7,8,9,10,11,12,13,14,15},{16,17,18,19,20,21,22,23,24,25,..., dimensions={0} | all-to-all | bytes 131072 | tf_op jit(solution)/shard_map/all_to_all | solution.py:678
  47.4 0.0 collective-permute-done.2.refs_1_
  47.4 1.5 %outputs.1 = (f32[16,640]{1,0:T(8,128)}, f32[640,128]{1,0:T(8,128)}) custom-call(f32[288,128]{1,0:T(8,128)S(1)} %get-tuple-element.21.columns_ref, bf16[8,2,16,128]{3,2,1,0:T(8,128)(2,1)S(1)} %bitcast.17, f32[32,384]{1,0:T(8,128)S(1)} %get-tuple-element.31.image_ref, s32[16,320]{1,0:T(8,128)S(1)} %bitcast.22, bf16[384,768]{1,0:T(8,128)(2,1)S(1)} %copy-done, ...), custom_call_target="tpu_custom_call" | custom-call | flops 301989888 | bytes 1642496 | tf_op jit(solution)/shard_map/outputs/pallas_call | solution.py:640
  (18 shorter events, 0.0 us)
Async XLA Ops:
  0.6 9.7 %copy-start.2 = (bf16[128,1536]{1,0:T(8,128)(2,1)S(1)}, bf16[128,1536]{1,0:T(8,128)(2,1)}, u32[]{:S(2)}) copy-start(bf16[128,1536]{1,0:T(8,128)(2,1)} %constant.19.clone.place_ref) | copy-start | bytes 1179652
  0.6 9.7 %copy-start.4 = (f32[288,128]{1,0:T(8,128)S(1)}, f32[288,128]{1,0:T(8,128)}, u32[]{:S(2)}) copy-start(f32[288,128]{1,0:T(8,128)} %constant.20.clone.offset_ref) | copy-start | bytes 442372
  0.7 9.7 %copy-start.5 = (f32[288,128]{1,0:T(8,128)S(1)}, f32[288,128]{1,0:T(8,128)}, u32[]{:S(2)}) copy-start(f32[288,128]{1,0:T(8,128)} %constant.18.clone.repeat_ref) | copy-start | bytes 442372
  0.7 9.7 %copy-start.9 = (f32[2,9,18,2]{2,3,1,0:T(2,128)S(1)}, f32[2,9,18,2]{2,3,1,0:T(2,128)}, u32[]{:S(2)}) copy-start(f32[2,9,18,2]{2,3,1,0:T(2,128)} %param.20) | copy-start | bytes 7780
  0.7 9.7 %copy-start.10 = (f32[2,9,2,18]{3,2,1,0:T(2,128)S(1)}, f32[2,9,2,18]{3,2,1,0:T(2,128)}, u32[]{:S(2)}) copy-start(f32[2,9,2,18]{3,2,1,0:T(2,128)} %param.22) | copy-start | bytes 7780
  0.7 9.7 %copy-start.11 = (f32[2,18]{1,0:T(2,128)S(1)}, f32[2,18]{1,0:T(2,128)}, u32[]{:S(2)}) copy-start(f32[2,18]{1,0:T(2,128)} %bias_in_ref.1) | copy-start | bytes 436
  0.7 9.7 %copy-start.12 = (f32[2,2]{1,0:T(2,128)S(1)}, f32[2,2]{1,0:T(2,128)}, u32[]{:S(2)}) copy-start(f32[2,2]{1,0:T(2,128)} %bias_out_ref.1) | copy-start | bytes 52
  0.7 9.7 %copy-start.13 = (f32[2]{0:T(128)S(1)}, f32[2]{0:T(128)}, u32[]{:S(2)}) copy-start(f32[2]{0:T(128)} %weight_ref.1) | copy-start | bytes 28
  2.7 9.2 %copy-start = (bf16[384,768]{1,0:T(8,128)(2,1)S(1)}, bf16[384,768]{1,0:T(8,128)(2,1)}, u32[]{:S(2)}) copy-start(bf16[384,768]{1,0:T(8,128)(2,1)} %constant.14.clone.table_ref) | copy-start | bytes 1769476
  2.7 9.2 %collective-permute-start = (bf16[64,640]{1,0:T(8,128)(2,1)}, bf16[64,640]{1,0:T(8,128)(2,1)S(1)}, u32[]{:S(2)}, u32[]{:S(2)}) collective-permute-start(bf16[64,640]{1,0:T(8,128)(2,1)} %get-tuple-element.19), channel_id=1, source_target_pairs={{0,18},{2,16},{4,22},{6,20},{8,26},{10,24},{12,30},{14,28},{16,2},... | collective-permute-start | bytes 245768 | tf_op jit(solution)/shard_map/ppermute | solution.py:672
  6.2 9.7 %all-to-all-start = ((bf16[8,96,128]{2,1,0:T(8,128)(2,1)}), bf16[8,96,128]{2,1,0:T(8,128)(2,1)S(1)}, u32[]{:S(2)}, u32[]{:S(2)}) async-start(bf16[8,96,128]{2,1,0:T(8,128)(2,1)} %get-tuple-element.22), calls=%async_computation | async-start | bytes 393216 | tf_op jit(solution)/shard_map/all_to_all | solution.py:678
  10.4 1.6 %copy-start.3 = (s32[2,8,320]{2,1,0:T(8,128)S(1)}, s32[2,8,320]{2,1,0:T(8,128)}, u32[]{:S(2)}) copy-start(s32[2,8,320]{2,1,0:T(8,128)} %param.18) | copy-start | bytes 61444
  10.4 1.6 %copy-start.7 = (bf16[128,128]{1,0:T(8,128)(2,1)S(1)}, bf16[128,128]{1,0:T(8,128)(2,1)}, u32[]{:S(2)}) copy-start(bf16[128,128]{1,0:T(8,128)(2,1)} %constant.17.clone.plus_ref) | copy-start | bytes 98308
  11.9 1.1 %copy-start.1 = (bf16[8,16,1,640]{3,1,2,0:T(8,128)(2,1)S(1)}, bf16[8,16,1,640]{3,1,2,0:T(8,128)(2,1)}, u32[]{:S(2)}) copy-start(bf16[8,16,1,640]{3,1,2,0:T(8,128)(2,1)} %param.16) | copy-start | bytes 491524
  12.4 3.5 %copy-start.6 = (bf16[256,256]{1,0:T(8,128)(2,1)S(1)}, bf16[256,256]{1,0:T(8,128)(2,1)}, u32[]{:S(2)}) copy-start(bf16[256,256]{1,0:T(8,128)(2,1)} %constant.15.clone.minus_ref) | copy-start | bytes 393220
  12.4 3.5 %copy-start.14 = (bf16[256,256]{1,0:T(8,128)(2,1)S(1)}, bf16[256,256]{1,0:T(8,128)(2,1)}, u32[]{:S(2)}) copy-start(bf16[256,256]{1,0:T(8,128)(2,1)} %constant.16.clone.plus_ref) | copy-start | bytes 393220
  12.4 3.5 %collective-permute-start.1 = (f32[192,384]{1,0:T(8,128)S(1)}, f32[192,384]{1,0:T(8,128)S(1)}, u32[]{:S(2)}, u32[]{:S(2)}) collective-permute-start(f32[192,384]{1,0:T(8,128)S(1)} %far_images.1), channel_id=1, source_target_pairs={{0,2},{2,0},{4,6},{6,4},{8,10},{10,8},{12,14},{14,12},{16,18},{18,... | collective-permute-start | bytes 884744 | tf_op jit(solution)/shard_map/ppermute | solution.py:675
  17.4 9.3 %copy-start.8 = (bf16[1,16,640]{2,1,0:T(8,128)(2,1)S(1)}, bf16[1,16,640]{2,1,0:T(8,128)(2,1)}, u32[]{:S(2)}) copy-start(bf16[1,16,640]{2,1,0:T(8,128)(2,1)} %param.24) | copy-start | bytes 61444
  35.9 11.4 %collective-permute-start.2 = (bf16[176,384]{1,0:T(8,128)(2,1)S(1)}, bf16[176,384]{1,0:T(8,128)(2,1)S(1)}, u32[]{:S(2)}, u32[]{:S(2)}) collective-permute-start(bf16[176,384]{1,0:T(8,128)(2,1)S(1)} %get-tuple-element.33), channel_id=1, source_target_pairs={{0,16},{2,18},{4,20},{6,22},{8,24},{10,26},{12,28},{14,30},{16,0},... | collective-permute-start | bytes 405512 | tf_op jit(solution)/shard_map/ppermute | solution.py:672

commit v10 on v9

--- a/solution.py
+++ b/solution.py
@@ -15,7 +15,6 @@
 LANES = 128
 VMEM_BYTES = 48 * 1024 * 1024
 FAR_PARTS = 3
-HAND_PLANES = 6
 LARGE_VMEM_BYTES = 60 * 1024 * 1024
 
 F32 = jnp.float32
@@ -184,6 +183,23 @@
     return [scratch[pl.ds(first + index, rows, stride=pitch), :] for index in range(count)]
 
 
+def put_messages(out_ref, scratch, places):
+    pitch = scratch.shape[0] // len(places)
+    for member, spots in enumerate(places):
+        message = scratch[member * pitch : member * pitch + out_ref.shape[1]].astype(BF16)
+        for spot in spots:
+            out_ref[spot] = message
+
+
+def take_messages(scratch, sent_ref, places):
+    pitch = scratch.shape[0] // len(places)
+    for member, spots in enumerate(places):
+        total = sent_ref[spots[0]].astype(F32)
+        for spot in spots[1:]:
+            total = total + sent_ref[spot].astype(F32)
+        scratch[member * pitch : member * pitch + sent_ref.shape[1]] = total
+
+
 def shifted(value, step):
     if step == 0:
         return value
@@ -251,7 +267,7 @@
     return jnp.concatenate(chosen, axis=0)
 
 
-def pack_kernel(coils, volumes, pitch, kspace_ref, maps_ref, image_ref, out_ref, *refs):
+def pack_kernel(coils, volumes, pitch, places, kspace_ref, maps_ref, image_ref, out_ref, *refs):
     handed, (scratch,) = refs[:-1], refs[-1:]
     rows = image_ref.shape[0]
     depth = rows // volumes
@@ -268,7 +284,7 @@
         for place, part in enumerate(blocks(value, volumes)):
             first = (place * (coils + 1) + coil) * count
             write_rows(scratch, pitch, lane_chunks(part), first)
-    out_ref[...] = scratch[...].astype(BF16).reshape(out_ref.shape)
+    put_messages(out_ref, scratch, places)
 
 
 def taps_kernel(
@@ -351,6 +367,8 @@
     coils,
     lines,
     volumes,
+    from_places,
+    to_places,
     sent_ref,
     mask_ref,
     table_ref,
@@ -373,7 +391,7 @@
             measured.append(pick([arrival[part] for arrival in arrivals], step))
     measured = jnp.concatenate(measured, axis=0)
 
-    arrived[...] = sent_ref[...].astype(F32).reshape(arrived.shape)
+    take_messages(arrived, sent_ref, from_places)
     count = 2 * lines // LANES
     parts, reals, imags = [], [], []
     for place in range(volumes):
@@ -399,20 +417,11 @@
     ]
     leaving[...] = jnp.zeros_like(leaving)
     sums = [row_sums(value, volumes, coils) for value in found]
-    pitch = out_ref.shape[2]
+    pitch = out_ref.shape[1]
     for place in range(volumes):
         chunks = [chunk for value in sums for chunk in lane_chunks(value[place])]
         write_rows(leaving, pitch, chunks, place * (pitch // volumes))
-    message = leaving[...].astype(BF16).reshape(depth, *out_ref.shape[2:])
-    for device in range(out_ref.shape[1]):
-        out_ref[:, device] = message
-
-
-def unpack_sum(sent_ref, scratch):
-    total = sent_ref[:, 0].astype(F32)
-    for device in range(1, sent_ref.shape[1]):
-        total = total + sent_ref[:, device].astype(F32)
-    scratch[...] = total.reshape(scratch.shape)
+    put_messages(out_ref, leaving, to_places)
 
 
 def read_image(scratch, pitch, first, count, depth):
@@ -435,6 +444,8 @@
 def refine_kernel(
     lines,
     volumes,
+    from_places,
+    to_places,
     sent_ref,
     cotangent_ref,
     first_ref,
@@ -447,8 +458,8 @@
     arrived,
     leaving,
 ):
-    unpack_sum(sent_ref, arrived)
-    depth, pitch = sent_ref.shape[0], sent_ref.shape[2]
+    take_messages(arrived, sent_ref, from_places)
+    depth, pitch = len(from_places), sent_ref.shape[1]
     rows = depth * volumes
     width = padded(lines, LANES)
     count = width // LANES
@@ -498,35 +509,36 @@
     for place in range(volumes):
         chunks = [chunk for part in parts for chunk in lane_chunks(part[place])]
         write_rows(leaving, out_ref.shape[1], chunks, place * len(chunks))
-    out_ref[...] = leaving[...].astype(BF16).reshape(out_ref.shape)
-
-
-def hand_kernel(volumes, sent_ref, maps_ref, *refs):
+    put_messages(out_ref, leaving, to_places)
+
+
+def hand_kernel(lines, volumes, from_places, sent_ref, maps_ref, *refs):
     outs, (arrived,) = refs[:-1], refs[-1:]
-    arrived[...] = sent_ref[...].astype(F32).reshape(arrived.shape)
+    take_messages(arrived, sent_ref, from_places)
     depth, pitch = sent_ref.shape[:2]
     volume = own_volume(depth)
     count = maps_ref.shape[1] // LANES
-    parts = [blocks(part, volumes) for part in halves(maps_ref[...].astype(F32))]
-    for field in (2, 3):
-        parts.append(
-            [
-                read_image(arrived, pitch, (place * 4 + field) * count, count, depth)
-                for place in range(volumes)
-            ]
-        )
+    maps = [blocks(part, volumes) for part in halves(maps_ref[...].astype(F32))]
+    pulled = [
+        [
+            read_image(arrived, pitch, (place * 4 + field) * count, count, depth)
+            for place in range(volumes)
+        ]
+        for field in (2, 3)
+    ]
     for step, ref in enumerate(outs):
         place = lax.rem(volume + step, jnp.int32(volumes))
-        chosen = [pick(part, place) for part in parts]
-        ref[...] = jnp.zeros_like(ref)
-        chosen = jnp.concatenate(chosen, axis=0).astype(BF16)
-        ref[: chosen.shape[0]] = chosen
+        chosen = [jnp.concatenate([pick(a, place), pick(b, place)]) for a, b in zip(maps, pulled)]
+        for index, chunk in enumerate(join_complex(*chosen, lines)):
+            ref[:, index * LANES : (index + 1) * LANES] = chunk.astype(BF16)
 
 
 def normal_kernel(
     coils,
     lines,
     volumes,
+    from_places,
+    to_places,
     sent_ref,
     maps_ref,
     mask_ref,
@@ -537,7 +549,7 @@
     arrived,
     leaving,
 ):
-    arrived[...] = sent_ref[...].astype(F32).reshape(arrived.shape)
+    take_messages(arrived, sent_ref, from_places)
     depth, pitch = sent_ref.shape[:2]
     volume = own_volume(depth)
     count = maps_ref.shape[1] // LANES
@@ -557,10 +569,8 @@
     leaving[...] = jnp.zeros_like(leaving)
     for place in range(volumes):
         chunks = join_complex(found[0][place], found[1][place], lines)
-        write_rows(leaving, out_ref.shape[2], chunks, place * len(chunks))
-    message = leaving[...].astype(BF16).reshape(depth, *out_ref.shape[2:])
-    for device in range(out_ref.shape[1]):
-        out_ref[:, device] = message
+        write_rows(leaving, leaving.shape[0] // depth, chunks, place * len(chunks))
+    put_messages(out_ref, leaving, to_places)
 
 
 def from_volumes(refs, volume, parts, volumes):
@@ -581,19 +591,18 @@
     minus_ref,
     *refs,
 ):
-    handed, (grad_ref,) = [ref[...].astype(F32) for ref in refs[:volumes]], refs[volumes:]
+    handed, (grad_ref,) = refs[:volumes], refs[volumes:]
     depth = mask_ref.shape[0] // volumes
     volume = own_volume(depth)
-    planes = coils * depth
-    maps = [value[: 2 * planes] for value in handed]
-    maps = from_volumes(maps, volume, 2 * coils, volumes)
-    maps = [
-        jnp.concatenate([maps[v][first + coil] for coil in range(coils) for v in range(volumes)], 0)
-        for first in (0, coils)
-    ]
-    pulled = [value[2 * planes : 2 * planes + 2 * depth] for value in handed]
-    pulled = from_volumes(pulled, volume, 2, volumes)
-    real, imag = [jnp.concatenate([part[field] for part in pulled], 0) for field in range(2)]
+    handed = [split_complex(lane_chunks(ref[...].astype(F32)), lines) for ref in handed]
+    handed = [jnp.concatenate(parts, axis=0) for parts in handed]
+    found = from_volumes(handed, volume, 2 * (coils + 1), volumes)
+    maps, pulled = [], []
+    for first in (0, coils + 1):
+        parts = [found[v][first + coil] for coil in range(coils) for v in range(volumes)]
+        maps.append(jnp.concatenate(parts, axis=0))
+        pulled.append(jnp.concatenate([found[v][first + coils] for v in range(volumes)], axis=0))
+    real, imag = pulled
     images = spread(*maps, over_coils(real, coils), over_coils(imag, coils))
     spectrum = depth_apply(line_apply(images, table_ref, -1.0), minus_ref)
     spectrum = spectrum * over_coils(read_mask(mask_ref, table_ref.shape[0]), 2 * coils)
@@ -601,10 +610,11 @@
     write_rows(grad_ref, len(chunks), chunks)
 
 
-def picture_kernel(lines, volumes, columns_ref, sent_ref, image_ref, picture_ref, arrived):
-    depth, pitch = sent_ref.shape[0], sent_ref.shape[2]
+def picture_kernel(lines, volumes, from_places, columns_ref, sent_ref, image_ref, picture_ref, arrived):
+    depth = len(from_places)
+    pitch = arrived.shape[0] // depth
     count = 2 * lines // LANES
-    unpack_sum(sent_ref, arrived)
+    take_messages(arrived, sent_ref, from_places)
     parts = [[], []]
     for place in range(volumes):
         chunks = read_rows(arrived, pitch, place * count, count, depth)
@@ -621,6 +631,7 @@
     coils,
     lines,
     volumes,
+    from_places,
     columns_ref,
     sent_ref,
     image_ref,
@@ -631,7 +642,9 @@
 ):
     handed, (picture_ref, grad_ref, arrived) = refs[:volumes], refs[volumes:]
     grad_kernel(coils, lines, volumes, mask_ref, table_ref, minus_ref, *handed, grad_ref)
-    picture_kernel(lines, volumes, columns_ref, sent_ref, image_ref, picture_ref, arrived)
+    picture_kernel(
+        lines, volumes, from_places, columns_ref, sent_ref, image_ref, picture_ref, arrived
+    )
 
 
 def call(kernel, name, operands, outs, scratch, flops, vmem_bytes=VMEM_BYTES, scalars=0):
@@ -663,9 +676,16 @@
     count, whole_count = width // LANES, two_lines // LANES
     planes = coils * slots
     both = ("section", "coil")
-    near = [[group * depth + t for t in range(depth)] for group in range(volumes)]
     span = depth * coil_devices
-    near_both = [[group * span + t for t in range(span)] for group in range(volumes)]
+    near_order = [depth - 1] + list(range(depth - 1))
+    both_order = list(range(span))[::-1]
+    near = [[group * depth + member for member in near_order] for group in range(volumes)]
+    near_both = [[group * span + member for member in both_order] for group in range(volumes)]
+    near_places = [[near_order.index(member)] for member in range(depth)]
+    both_places = [
+        [both_order.index(member * coil_devices + coil) for coil in range(coil_devices)]
+        for member in range(depth)
+    ]
 
     def from_group(value, step, core=0):
         pairs = [(s, ((s + step * depth) % sections) ^ core) for s in range(sections)]
@@ -691,7 +711,7 @@
 
     pitch = padded(volumes * (coils + 1) * whole_count, 16)
     packed, *samples = call(
-        functools.partial(pack_kernel, coils, volumes, pitch),
+        functools.partial(pack_kernel, coils, volumes, pitch, near_places),
         "pack_maps",
         (
             kspace.reshape(planes, two_lines),
@@ -754,23 +774,22 @@
 
     depth_pitch = padded(volumes * 5 * count, 16 * volumes)
     partial, maps = call(
-        functools.partial(rows_kernel, coils, lines, volumes),
+        functools.partial(rows_kernel, coils, lines, volumes, near_places, both_places),
         "combine_rows",
         (arrived, mask, table, minus, plus, *images),
         [
-            shape(depth, coil_devices, depth_pitch, LANES, kind=BF16),
+            shape(span, depth_pitch, LANES, kind=BF16),
             shape(2 * planes, width, kind=BF16),
         ],
         [(depth * pitch, LANES), (depth * depth_pitch, LANES)],
         4 * line_flops,
     )
 
-    partial = exchange(partial.reshape(-1, depth_pitch, LANES), both, near_both)
-    partial = partial.reshape(depth, coil_devices, depth_pitch, LANES)
+    partial = exchange(partial, both, near_both)
 
     model_pitch = padded(volumes * 4 * count, 8)
     moved, image = call(
-        functools.partial(refine_kernel, lines, volumes),
+        functools.partial(refine_kernel, lines, volumes, both_places, near_places),
         "refine_and_back",
         (
             partial,
@@ -787,32 +806,32 @@
     )
     moved = exchange(moved, "section", near)
 
-    end_pitch = padded(volumes * whole_count, 16)
+    end_lines = volumes * whole_count
+    end_pitch = padded(end_lines, 16)
     handed = call(
-        functools.partial(hand_kernel, volumes),
+        functools.partial(hand_kernel, lines, volumes, near_places),
         "hand_on",
         (moved, maps),
-        [shape(2 * planes // volumes + HAND_PLANES * depth, width, kind=BF16)] * volumes,
+        [shape((coils + 1) * depth, two_lines, kind=BF16)] * volumes,
         [(depth * model_pitch, LANES)],
         1000,
     )
     handed = list(handed)
     (partial,) = call(
-        functools.partial(normal_kernel, coils, lines, volumes),
+        functools.partial(normal_kernel, coils, lines, volumes, near_places, both_places),
         "masked_normal",
         (moved, maps, mask, table, minus, plus),
-        [shape(depth, coil_devices, end_pitch, LANES, kind=BF16)],
+        [shape(span, end_lines, LANES, kind=BF16)],
         [(depth * model_pitch, LANES), (depth * end_pitch, LANES)],
         3 * line_flops,
     )
-    partial = exchange(partial.reshape(-1, end_pitch, LANES), both, near_both)
-    partial = partial.reshape(depth, coil_devices, end_pitch, LANES)
+    partial = exchange(partial, both, near_both)
     handed[1:] = [
         from_group(value, step) for step, value in enumerate(handed[1:], 1)
     ]
 
     image, grad = call(
-        functools.partial(end_kernel, coils, lines, volumes),
+        functools.partial(end_kernel, coils, lines, volumes, both_places),
         "outputs",
         (columns, partial, image, mask, table, minus, *handed),
         [shape(rows, two_lines), shape(planes * whole_count, LANES)],

time: 49.3 us -> 46.1 us (0.935)
  blocking collectives: 24.8 us -> 21.9 us
  waiting for transfers between devices: 2.5 us -> 0.89 us
  starting transfers between devices: 10.1 us -> 11.2 us
    all_to_all x3, blocking collectives: 24.8 us -> 21.9 us  [exchange(): lax.all_to_all(value, axes, 0, 0, tiled=True, axis_index_groups=groups)]
    all_to_all x1, starting transfers between devices: 4.09 us -> 6.11 us  [exchange(): lax.all_to_all(value, axes, 0, 0, tiled=True, axis_index_groups=groups)]
    all_to_all x1, waiting for transfers between devices: 2.5 us -> 0.89 us  [exchange(): lax.all_to_all(value, axes, 0, 0, tiled=True, axis_index_groups=groups)]
    ppermute x2, starting transfers between devices: 5.49 us -> 4.84 us  [from_group(): return lax.ppermute(value, 'section', pairs)]
  transfers between devices with their start and end apart: 4 -> 4, of which waited for: 1 -> 1; matrix products, arithmetic and copies ran while one was open for 0% -> 0% of each run, Pallas kernels for 7% -> 8%
where the time goes in v10:
time: 46.1 us; the launch traced here: 45.7 us
  blocking collectives  21.9 us (48%)
  starting transfers between devices  11.2 us (24%)
  Pallas kernels  10.6 us (23%)
  waiting for transfers between devices  0.89 us (2%)
  between operations  0.88 us (2%)
    all_to_all x3, blocking collectives, exchange(): lax.all_to_all(value, axes, 0, 0, tiled=True, axis_index_groups=groups)  21.9 us
    pallas_call x9, Pallas kernels, call(): pl.pallas_call(kernel, name=name, out_shape=tuple(outs), in_specs=[pl.Blo...  10.6 us
    all_to_all x1, starting transfers between devices, exchange(): lax.all_to_all(value, axes, 0, 0, tiled=True, axis_index_groups=groups)  6.11 us
    ppermute x2, starting transfers between devices, from_group(): return lax.ppermute(value, 'section', pairs)  4.84 us
  transfers between devices with their start and end apart: 4, of which 1 were waited for; matrix products, arithmetic and copies ran while one was open for 0% of the time, Pallas kernels for 8%

profile of v10, /device:TPU:0, one launch (start us, length us, event | category | flops | bytes accessed | tf_op | source)
XLA Modules:
  0.0 45.7 jit_solution(4715607085041792285)
XLA Ops:
  0.6 0.0 copy-start.2
  0.6 0.0 copy-start.4
  0.7 0.0 copy-start.5
  0.7 0.0 copy-start.9
  0.7 0.0 copy-start.10
  0.7 2.0 %pack_maps.1 = (bf16[8,96,128]{2,1,0:T(8,128)(2,1)}, bf16[64,640]{1,0:T(8,128)(2,1)}) custom-call(bf16[128,640]{1,0:T(8,128)(2,1)} %bitcast.10, bf16[128,640]{1,0:T(8,128)(2,1)} %bitcast.21, bf16[16,640]{1,0:T(8,128)(2,1)} %bitcast.17), custom_call_target="tpu_custom_call" | custom-call | flops 1000 | bytes 626688 | tf_op jit(solution)/shard_map/pack_maps/pallas_call | solution.py:653
  2.7 3.5 %collective-permute-start = (bf16[64,640]{1,0:T(8,128)(2,1)}, bf16[64,640]{1,0:T(8,128)(2,1)S(1)}, u32[]{:S(2)}, u32[]{:S(2)}) collective-permute-start(bf16[64,640]{1,0:T(8,128)(2,1)} %get-tuple-element.19), channel_id=1, source_target_pairs={{0,18},{2,16},{4,22},{6,20},{8,26},{10,24},{12,30},{14,28},{16,2},... | collective-permute-start | bytes 245768 | tf_op jit(solution)/shard_map/ppermute | solution.py:692
  6.2 6.1 %all-to-all-start = ((bf16[8,96,128]{2,1,0:T(8,128)(2,1)}), bf16[8,96,128]{2,1,0:T(8,128)(2,1)S(1)}, u32[]{:S(2)}, u32[]{:S(2)}) async-start(bf16[8,96,128]{2,1,0:T(8,128)(2,1)} %get-tuple-element.22), calls=%async_computation | async-start | bytes 393216 | tf_op jit(solution)/shard_map/all_to_all | solution.py:698
  12.4 0.0 copy-start.3
  12.4 0.0 copy-start.7
  12.4 1.5 %lay_out_taps.1 = (bf16[2,288,128]{2,1,0:T(8,128)(2,1)S(1)}, bf16[2,96,288]{2,1,0:T(8,128)(2,1)S(1)}, bf16[2,96,288]{2,1,0:T(8,128)(2,1)S(1)}, bf16[2,288,128]{2,1,0:T(8,128)(2,1)S(1)}, f32[288,128]{1,0:T(8,128)S(1)}) custom-call(f32[2]{0:T(128)S(1)} %copy-done.13, f32[18,2,18]{2,1,0:T(2,128)S(1)} %bitcast.19, f32[18,2,18]{2,1,0:T(2,128)S(1)} %bitcast.20, ...), custom_call_target="tpu_custom_call" | custom-call | flops 113246208 | bytes 1357032 | tf_op jit(solution)/shard_map/lay_out_taps/pallas_call | solution.py:653
  13.9 0.0 collective-permute-done.kspace_ref
  14.0 0.0 copy-start.1
  14.0 0.4 far_images.1
  14.4 0.0 copy-start.6
  14.4 0.0 copy-start.14
  14.4 0.2 collective-permute-start.1
  14.7 0.2 copy-done.1
  14.9 0.4 own_images.1.refs_0_
  15.3 0.9 %all-to-all-done.sent_ref = bf16[8,96,128]{2,1,0:T(8,128)(2,1)S(1)} async-done(((bf16[8,96,128]{2,1,0:T(8,128)(2,1)}), bf16[8,96,128]{2,1,0:T(8,128)(2,1)S(1)}, u32[]{:S(2)}, u32[]{:S(2)}) %all-to-all-start) | async-done | bytes 196640 | tf_op jit(solution)/shard_map/all_to_all | solution.py:698
  16.2 0.0 collective-permute-done.1.refs_1_
  16.2 1.5 %combine_rows.1 = (bf16[16,32,128]{2,1,0:T(8,128)(2,1)S(1)}, bf16[256,384]{1,0:T(8,128)(2,1)S(1)}) custom-call(bf16[8,96,128]{2,1,0:T(8,128)(2,1)S(1)} %all-to-all-done.sent_ref, s32[16,320]{1,0:T(8,128)S(1)} %bitcast.14, bf16[384,768]{1,0:T(8,128)(2,1)S(1)} %copy-done, bf16[256,256]{1,0:T(8,128)(2,1)S(1)} %copy-done.6, bf16[256,256]{1,0:T(8,128)(2,1)S(1)} %copy-done.14, ...), custom_call_target="tpu_custom_call" | custom-call | flops 603979776 | bytes 1888256 | tf_op jit(solution)/shard_map/combine_rows/pallas_call | solution.py:653
  17.7 0.0 copy-start.8
  17.7 7.8 %all_to_all.20.sent_ref = bf16[16,32,128]{2,1,0:T(8,128)(2,1)S(1)} all-to-all(bf16[16,32,128]{2,1,0:T(8,128)(2,1)S(1)} %get-tuple-element.24), channel_id=1, replica_groups={{15,14,13,12,11,10,9,8,7,6,5,4,3,2,1,0},{31,30,29,28,27,26,25,24,23,22,..., dimensions={0} | all-to-all | bytes 262144 | tf_op jit(solution)/shard_map/all_to_all | solution.py:698
  25.5 1.9 %refine_and_back.1 = (bf16[8,24,128]{2,1,0:T(8,128)(2,1)S(1)}, f32[32,384]{1,0:T(8,128)S(1)}) custom-call(bf16[16,32,128]{2,1,0:T(8,128)(2,1)S(1)} %all_to_all.20.sent_ref, bf16[16,640]{1,0:T(8,128)(2,1)S(1)} %bitcast.18, bf16[2,288,128]{2,1,0:T(8,128)(2,1)S(1)} %get-tuple-element.25.first_ref, bf16[2,96,288]{2,1,0:T(8,128)(2,1)S(1)} %get-tuple-element.26.first_t_ref, ...), custom_call_target="tpu_custom_call" | custom-call | flops 198180864 | bytes 913408 | tf_op jit(solution)/shard_map/refine_and_back/pallas_call | solution.py:653
  27.4 6.8 %all_to_all.21.sent_ref = bf16[8,24,128]{2,1,0:T(8,128)(2,1)S(1)} all-to-all(bf16[8,24,128]{2,1,0:T(8,128)(2,1)S(1)} %get-tuple-element.29), channel_id=1, replica_groups={{14,0,2,4,6,8,10,12},{30,16,18,20,22,24,26,28},{15,1,3,5,7,9,11,13},{31..., dimensions={0} | all-to-all | bytes 98304 | tf_op jit(solution)/shard_map/all_to_all | solution.py:698
  34.2 0.1 hand_on.1
  34.3 1.4 %collective-permute-start.2 = (bf16[72,640]{1,0:T(8,128)(2,1)S(1)}, bf16[72,640]{1,0:T(8,128)(2,1)S(1)}, u32[]{:S(2)}, u32[]{:S(2)}) collective-permute-start(bf16[72,640]{1,0:T(8,128)(2,1)S(1)} %get-tuple-element.33), channel_id=1, source_target_pairs={{0,16},{2,18},{4,20},{6,22},{8,24},{10,26},{12,28},{14,30},{16,0},... | collective-permute-start | bytes 276488 | tf_op jit(solution)/shard_map/ppermute | solution.py:692
  35.7 1.2 %masked_normal.1 = bf16[16,10,128]{2,1,0:T(8,128)(2,1)S(1)} custom-call(bf16[8,24,128]{2,1,0:T(8,128)(2,1)S(1)} %all_to_all.21.sent_ref, bf16[256,384]{1,0:T(8,128)(2,1)S(1)} %get-tuple-element.30.maps_ref, s32[16,320]{1,0:T(8,128)S(1)} %bitcast.15, bf16[384,768]{1,0:T(8,128)(2,1)S(1)} %copy-done, bf16[256,256]{1,0:T(8,128)(2,1)S(1)} %copy-done.6, ...), custom_call_target="tpu_custom_call" | custom-call | flops 452984832 | bytes 1159168 | tf_op jit(solution)/shard_map/masked_normal/pallas_call | solution.py:653
  36.8 7.3 %all_to_all.22.sent_ref = bf16[16,10,128]{2,1,0:T(8,128)(2,1)S(1)} all-to-all(bf16[16,10,128]{2,1,0:T(8,128)(2,1)S(1)} %masked_normal.1), channel_id=1, replica_groups={{15,14,13,12,11,10,9,8,7,6,5,4,3,2,1,0},{31,30,29,28,27,26,25,24,23,22,..., dimensions={0} | all-to-all | bytes 81920 | tf_op jit(solution)/shard_map/all_to_all | solution.py:698
  44.2 0.0 collective-permute-done.2.refs_1_
  44.2 1.6 %outputs.1 = (f32[16,640]{1,0:T(8,128)}, f32[640,128]{1,0:T(8,128)}) custom-call(f32[288,128]{1,0:T(8,128)S(1)} %get-tuple-element.21.columns_ref, bf16[16,10,128]{2,1,0:T(8,128)(2,1)S(1)} %all_to_all.22.sent_ref, f32[32,384]{1,0:T(8,128)S(1)} %get-tuple-element.31.image_ref, s32[16,320]{1,0:T(8,128)S(1)} %bitcast.16, bf16[384,768]{1,0:T(8,128)(2,1)S(1)} %copy-done, ...), custom_call_target="tpu_custom_call" | custom-call | flops 301989888 | bytes 1531904 | tf_op jit(solution)/shard_map/outputs/pallas_call | solution.py:653
  (18 shorter events, 0.0 us)
Async XLA Ops:
  0.6 11.7 %copy-start.2 = (bf16[128,1536]{1,0:T(8,128)(2,1)S(1)}, bf16[128,1536]{1,0:T(8,128)(2,1)}, u32[]{:S(2)}) copy-start(bf16[128,1536]{1,0:T(8,128)(2,1)} %constant.19.clone.place_ref) | copy-start | bytes 1179652
  0.6 11.7 %copy-start.4 = (f32[288,128]{1,0:T(8,128)S(1)}, f32[288,128]{1,0:T(8,128)}, u32[]{:S(2)}) copy-start(f32[288,128]{1,0:T(8,128)} %constant.20.clone.offset_ref) | copy-start | bytes 442372
  0.7 11.7 %copy-start.5 = (f32[288,128]{1,0:T(8,128)S(1)}, f32[288,128]{1,0:T(8,128)}, u32[]{:S(2)}) copy-start(f32[288,128]{1,0:T(8,128)} %constant.18.clone.repeat_ref) | copy-start | bytes 442372
  0.7 11.7 %copy-start.9 = (f32[2,9,18,2]{2,3,1,0:T(2,128)S(1)}, f32[2,9,18,2]{2,3,1,0:T(2,128)}, u32[]{:S(2)}) copy-start(f32[2,9,18,2]{2,3,1,0:T(2,128)} %param.20) | copy-start | bytes 7780
  0.7 11.7 %copy-start.10 = (f32[2,9,2,18]{3,2,1,0:T(2,128)S(1)}, f32[2,9,2,18]{3,2,1,0:T(2,128)}, u32[]{:S(2)}) copy-start(f32[2,9,2,18]{3,2,1,0:T(2,128)} %param.22) | copy-start | bytes 7780
  0.7 11.7 %copy-start.11 = (f32[2,18]{1,0:T(2,128)S(1)}, f32[2,18]{1,0:T(2,128)}, u32[]{:S(2)}) copy-start(f32[2,18]{1,0:T(2,128)} %bias_in_ref.1) | copy-start | bytes 436
  0.7 11.7 %copy-start.12 = (f32[2,2]{1,0:T(2,128)S(1)}, f32[2,2]{1,0:T(2,128)}, u32[]{:S(2)}) copy-start(f32[2,2]{1,0:T(2,128)} %bias_out_ref.1) | copy-start | bytes 52
  0.7 11.7 %copy-start.13 = (f32[2]{0:T(128)S(1)}, f32[2]{0:T(128)}, u32[]{:S(2)}) copy-start(f32[2]{0:T(128)} %weight_ref.1) | copy-start | bytes 28
  2.7 11.2 %copy-start = (bf16[384,768]{1,0:T(8,128)(2,1)S(1)}, bf16[384,768]{1,0:T(8,128)(2,1)}, u32[]{:S(2)}) copy-start(bf16[384,768]{1,0:T(8,128)(2,1)} %constant.14.clone.table_ref) | copy-start | bytes 1769476
  2.7 11.2 %collective-permute-start = (bf16[64,640]{1,0:T(8,128)(2,1)}, bf16[64,640]{1,0:T(8,128)(2,1)S(1)}, u32[]{:S(2)}, u32[]{:S(2)}) collective-permute-start(bf16[64,640]{1,0:T(8,128)(2,1)} %get-tuple-element.19), channel_id=1, source_target_pairs={{0,18},{2,16},{4,22},{6,20},{8,26},{10,24},{12,30},{14,28},{16,2},... | collective-permute-start | bytes 245768 | tf_op jit(solution)/shard_map/ppermute | solution.py:692
  6.2 10.0 %all-to-all-start = ((bf16[8,96,128]{2,1,0:T(8,128)(2,1)}), bf16[8,96,128]{2,1,0:T(8,128)(2,1)S(1)}, u32[]{:S(2)}, u32[]{:S(2)}) async-start(bf16[8,96,128]{2,1,0:T(8,128)(2,1)} %get-tuple-element.22), calls=%async_computation | async-start | bytes 393216 | tf_op jit(solution)/shard_map/all_to_all | solution.py:698
  12.4 1.6 %copy-start.3 = (s32[2,8,320]{2,1,0:T(8,128)S(1)}, s32[2,8,320]{2,1,0:T(8,128)}, u32[]{:S(2)}) copy-start(s32[2,8,320]{2,1,0:T(8,128)} %param.18) | copy-start | bytes 61444
  12.4 1.6 %copy-start.7 = (bf16[128,128]{1,0:T(8,128)(2,1)S(1)}, bf16[128,128]{1,0:T(8,128)(2,1)}, u32[]{:S(2)}) copy-start(bf16[128,128]{1,0:T(8,128)(2,1)} %constant.17.clone.plus_ref) | copy-start | bytes 98308
  14.0 0.9 %copy-start.1 = (bf16[8,16,1,640]{3,1,2,0:T(8,128)(2,1)S(1)}, bf16[8,16,1,640]{3,1,2,0:T(8,128)(2,1)}, u32[]{:S(2)}) copy-start(bf16[8,16,1,640]{3,1,2,0:T(8,128)(2,1)} %param.16) | copy-start | bytes 491524
  14.4 1.8 %copy-start.6 = (bf16[256,256]{1,0:T(8,128)(2,1)S(1)}, bf16[256,256]{1,0:T(8,128)(2,1)}, u32[]{:S(2)}) copy-start(bf16[256,256]{1,0:T(8,128)(2,1)} %constant.15.clone.minus_ref) | copy-start | bytes 393220
  14.4 1.8 %copy-start.14 = (bf16[256,256]{1,0:T(8,128)(2,1)S(1)}, bf16[256,256]{1,0:T(8,128)(2,1)}, u32[]{:S(2)}) copy-start(bf16[256,256]{1,0:T(8,128)(2,1)} %constant.16.clone.plus_ref) | copy-start | bytes 393220
  14.4 1.8 %collective-permute-start.1 = (f32[192,384]{1,0:T(8,128)S(1)}, f32[192,384]{1,0:T(8,128)S(1)}, u32[]{:S(2)}, u32[]{:S(2)}) collective-permute-start(f32[192,384]{1,0:T(8,128)S(1)} %far_images.1), channel_id=1, source_target_pairs={{0,2},{2,0},{4,6},{6,4},{8,10},{10,8},{12,14},{14,12},{16,18},{18,... | collective-permute-start | bytes 884744 | tf_op jit(solution)/shard_map/ppermute | solution.py:695
  17.7 7.8 %copy-start.8 = (bf16[1,16,640]{2,1,0:T(8,128)(2,1)S(1)}, bf16[1,16,640]{2,1,0:T(8,128)(2,1)}, u32[]{:S(2)}) copy-start(bf16[1,16,640]{2,1,0:T(8,128)(2,1)} %param.24) | copy-start | bytes 61444
  34.3 9.8 %collective-permute-start.2 = (bf16[72,640]{1,0:T(8,128)(2,1)S(1)}, bf16[72,640]{1,0:T(8,128)(2,1)S(1)}, u32[]{:S(2)}, u32[]{:S(2)}) collective-permute-start(bf16[72,640]{1,0:T(8,128)(2,1)S(1)} %get-tuple-element.33), channel_id=1, source_target_pairs={{0,16},{2,18},{4,20},{6,22},{8,24},{10,26},{12,28},{14,30},{16,0},... | collective-permute-start | bytes 276488 | tf_op jit(solution)/shard_map/ppermute | solution.py:692

commit v11 on v10

--- a/solution.py
+++ b/solution.py
@@ -378,7 +378,8 @@
 ):
     arrival_refs, refs = refs[:volumes], refs[volumes:]
     out_ref, maps_ref, arrived, leaving = refs
-    depth, pitch = sent_ref.shape[:2]
+    depth = sent_ref.shape[0]
+    pitch = arrived.shape[0] // depth
     volume = own_volume(depth)
     mask = pick(blocks(read_mask(mask_ref, table_ref.shape[0]), volumes), volume)
     mask = over_coils(mask, volumes * coils)
@@ -417,10 +418,10 @@
     ]
     leaving[...] = jnp.zeros_like(leaving)
     sums = [row_sums(value, volumes, coils) for value in found]
-    pitch = out_ref.shape[1]
+    pitch = leaving.shape[0] // depth
     for place in range(volumes):
         chunks = [chunk for value in sums for chunk in lane_chunks(value[place])]
-        write_rows(leaving, pitch, chunks, place * (pitch // volumes))
+        write_rows(leaving, pitch, chunks, place * len(chunks))
     put_messages(out_ref, leaving, to_places)
 
 
@@ -459,13 +460,14 @@
     leaving,
 ):
     take_messages(arrived, sent_ref, from_places)
-    depth, pitch = len(from_places), sent_ref.shape[1]
+    depth = len(from_places)
+    pitch = arrived.shape[0] // depth
     rows = depth * volumes
     width = padded(lines, LANES)
     count = width // LANES
-    begun = read_complex(arrived, pitch, 0, pitch // volumes, count, depth, volumes)
-    turned = read_complex(arrived, pitch, 2 * count, pitch // volumes, count, depth, volumes)
-    power = read_places(arrived, pitch, 4 * count, pitch // volumes, count, depth, volumes)
+    begun = read_complex(arrived, pitch, 0, 5 * count, count, depth, volumes)
+    turned = read_complex(arrived, pitch, 2 * count, 5 * count, count, depth, volumes)
+    power = read_places(arrived, pitch, 4 * count, 5 * count, count, depth, volumes)
     power = jnp.concatenate([power, power], axis=0)
     cotangent = jnp.concatenate(
         split_complex(lane_chunks(cotangent_ref[...].astype(F32)), lines), axis=0
@@ -692,7 +694,7 @@
         return lax.ppermute(value, "section", pairs)
 
     def between_cores(value):
-        return lax.ppermute(value, "section", [(s, s ^ 1) for s in range(sections)])
+        return lax.ppermute(value, "section", [(s, s) for s in range(sections)])
 
     def exchange(value, axes, groups):
         return lax.all_to_all(value, axes, 0, 0, tiled=True, axis_index_groups=groups)
@@ -709,7 +711,8 @@
 
     line_flops = 2 * (2 * planes) * width * (2 * width)
 
-    pitch = padded(volumes * (coils + 1) * whole_count, 16)
+    maps_lines = volumes * (coils + 1) * whole_count
+    pitch = padded(maps_lines, 8)
     packed, *samples = call(
         functools.partial(pack_kernel, coils, volumes, pitch, near_places),
         "pack_maps",
@@ -718,13 +721,13 @@
             coil_maps.reshape(coils * rows, two_lines),
             cotangent.reshape(rows, two_lines),
         ),
-        [shape(depth, pitch, LANES, kind=BF16)]
+        [shape(depth, maps_lines, LANES, kind=BF16)]
         + [shape(coils * depth, two_lines, kind=BF16)] * (volumes - 1),
         [(depth * pitch, LANES)],
         1000,
         LARGE_VMEM_BYTES,
     )
-    samples = [from_group(value, step, 1) for step, value in enumerate(samples, 1)]
+    samples = [from_group(value, step) for step, value in enumerate(samples, 1)]
     tall, wide = channels * rows, offset.shape[1]
     first, first_t, second, second_t, columns = call(
         functools.partial(taps_kernel, rows),
@@ -772,13 +775,14 @@
         images.append(between_cores(image))
     arrived = exchange(packed, "section", near)
 
-    depth_pitch = padded(volumes * 5 * count, 16 * volumes)
+    sums_lines = volumes * 5 * count
+    depth_pitch = padded(sums_lines, 8)
     partial, maps = call(
         functools.partial(rows_kernel, coils, lines, volumes, near_places, both_places),
         "combine_rows",
         (arrived, mask, table, minus, plus, *images),
         [
-            shape(span, depth_pitch, LANES, kind=BF16),
+            shape(span, sums_lines, LANES, kind=BF16),
             shape(2 * planes, width, kind=BF16),
         ],
         [(depth * pitch, LANES), (depth * depth_pitch, LANES)],

time: 46.1 us -> 45.4 us (0.985)
  starting transfers between devices: 11.2 us -> 10.2 us
    all_to_all x1, starting transfers between devices: 6.11 us -> 4.99 us  [exchange(): lax.all_to_all(value, axes, 0, 0, tiled=True, axis_index_groups=groups)]
where the time goes in v11:
time: 45.4 us; the launch traced here: 45 us
  blocking collectives  21.9 us (48%)
  Pallas kernels  10.6 us (23%)
  starting transfers between devices  10.2 us (22%)
  waiting for transfers between devices  0.89 us (2%)
  between operations  0.89 us (2%)
  local copies, waits for them, and re-layouts  0.48 us (1%)
    all_to_all x3, blocking collectives, exchange(): lax.all_to_all(value, axes, 0, 0, tiled=True, axis_index_groups=groups)  21.9 us
    pallas_call x9, Pallas kernels, call(): pl.pallas_call(kernel, name=name, out_shape=tuple(outs), in_specs=[pl.Blo...  10.6 us
    ppermute x2, starting transfers between devices, from_group(): return lax.ppermute(value, 'section', pairs)  5.21 us
    all_to_all x1, starting transfers between devices, exchange(): lax.all_to_all(value, axes, 0, 0, tiled=True, axis_index_groups=groups)  4.99 us
  transfers between devices with their start and end apart: 4, of which 1 were waited for; matrix products, arithmetic and copies ran while one was open for 0% of the time, Pallas kernels for 8%

profile of v11, /device:TPU:0, one launch (start us, length us, event | category | flops | bytes accessed | tf_op | source)
XLA Modules:
  0.0 45.0 jit_solution(653300987108046384)
XLA Ops:
  0.6 0.0 copy-start.2
  0.6 0.0 copy-start.4
  0.7 0.0 copy-start.5
  0.7 2.0 %pack_maps.1 = (bf16[8,90,128]{2,1,0:T(8,128)(2,1)}, bf16[64,640]{1,0:T(8,128)(2,1)}) custom-call(bf16[128,640]{1,0:T(8,128)(2,1)} %bitcast.10, bf16[128,640]{1,0:T(8,128)(2,1)} %bitcast.21, bf16[16,640]{1,0:T(8,128)(2,1)} %bitcast.17), custom_call_target="tpu_custom_call" | custom-call | flops 1000 | bytes 614400 | tf_op jit(solution)/shard_map/pack_maps/pallas_call | solution.py:655
  2.7 4.0 %collective-permute-start = (bf16[64,640]{1,0:T(8,128)(2,1)}, bf16[64,640]{1,0:T(8,128)(2,1)S(1)}, u32[]{:S(2)}, u32[]{:S(2)}) collective-permute-start(bf16[64,640]{1,0:T(8,128)(2,1)} %get-tuple-element.19), channel_id=1, source_target_pairs={{0,16},{2,18},{4,20},{6,22},{8,24},{10,26},{12,28},{14,30},{16,0},... | collective-permute-start | bytes 245768 | tf_op jit(solution)/shard_map/ppermute | solution.py:694
  6.8 5.0 %all-to-all-start = ((bf16[8,90,128]{2,1,0:T(8,128)(2,1)}), bf16[8,90,128]{2,1,0:T(8,128)(2,1)S(1)}, u32[]{:S(2)}, u32[]{:S(2)}) async-start(bf16[8,90,128]{2,1,0:T(8,128)(2,1)} %get-tuple-element.22), calls=%async_computation | async-start | bytes 393216 | tf_op jit(solution)/shard_map/all_to_all | solution.py:700
  11.8 0.0 copy-start.3
  11.8 0.0 copy-start.7
  11.8 1.5 %lay_out_taps.1 = (bf16[2,288,128]{2,1,0:T(8,128)(2,1)S(1)}, bf16[2,96,288]{2,1,0:T(8,128)(2,1)S(1)}, bf16[2,96,288]{2,1,0:T(8,128)(2,1)S(1)}, bf16[2,288,128]{2,1,0:T(8,128)(2,1)S(1)}, f32[288,128]{1,0:T(8,128)S(1)}) custom-call(f32[2]{0:T(128)S(1)} %copy-done.13, f32[18,2,18]{2,1,0:T(2,128)S(1)} %bitcast.19, f32[18,2,18]{2,1,0:T(2,128)S(1)} %bitcast.20, ...), custom_call_target="tpu_custom_call" | custom-call | flops 113246208 | bytes 1357032 | tf_op jit(solution)/shard_map/lay_out_taps/pallas_call | solution.py:655
  13.4 0.0 collective-permute-done.kspace_ref
  13.4 0.0 copy-start.1
  13.4 0.4 far_images.1
  13.9 0.0 copy-start.6
  13.9 0.0 copy-start.14
  13.9 0.0 collective-permute-start.1
  13.9 0.4 copy-done.1
  14.3 0.5 %own_images.1.refs_0_ = f32[128,384]{1,0:T(8,128)S(1)} custom-call(bf16[128,640]{1,0:T(8,128)(2,1)S(1)} %bitcast.11, s32[16,320]{1,0:T(8,128)S(1)} %bitcast.13, bf16[384,768]{1,0:T(8,128)(2,1)S(1)} %copy-done, bf16[128,128]{1,0:T(8,128)(2,1)S(1)} %copy-done.7), custom_call_target="tpu_custom_call" | custom-call | flops 150994944 | bytes 1003520 | tf_op jit(solution)/shard_map/own_images/pallas_call | solution.py:655
  14.8 0.9 %all-to-all-done.sent_ref = bf16[8,90,128]{2,1,0:T(8,128)(2,1)S(1)} async-done(((bf16[8,90,128]{2,1,0:T(8,128)(2,1)}), bf16[8,90,128]{2,1,0:T(8,128)(2,1)S(1)}, u32[]{:S(2)}, u32[]{:S(2)}) %all-to-all-start) | async-done | bytes 184352 | tf_op jit(solution)/shard_map/all_to_all | solution.py:700
  15.7 0.0 collective-permute-done.1.refs_1_
  15.7 0.0 copy-done.6
  15.7 1.5 %combine_rows.1 = (bf16[16,30,128]{2,1,0:T(8,128)(2,1)S(1)}, bf16[256,384]{1,0:T(8,128)(2,1)S(1)}) custom-call(bf16[8,90,128]{2,1,0:T(8,128)(2,1)S(1)} %all-to-all-done.sent_ref, s32[16,320]{1,0:T(8,128)S(1)} %bitcast.14, bf16[384,768]{1,0:T(8,128)(2,1)S(1)} %copy-done, bf16[256,256]{1,0:T(8,128)(2,1)S(1)} %copy-done.6, bf16[256,256]{1,0:T(8,128)(2,1)S(1)} %copy-done.14, ...), custom_call_target="tpu_custom_call" | custom-call | flops 603979776 | bytes 1867776 | tf_op jit(solution)/shard_map/combine_rows/pallas_call | solution.py:655
  17.1 0.0 copy-start.8
  17.1 7.8 %all_to_all.20.sent_ref = bf16[16,30,128]{2,1,0:T(8,128)(2,1)S(1)} all-to-all(bf16[16,30,128]{2,1,0:T(8,128)(2,1)S(1)} %get-tuple-element.24), channel_id=1, replica_groups={{15,14,13,12,11,10,9,8,7,6,5,4,3,2,1,0},{31,30,29,28,27,26,25,24,23,22,..., dimensions={0} | all-to-all | bytes 245760 | tf_op jit(solution)/shard_map/all_to_all | solution.py:700
  24.9 0.0 copy-done.8
  24.9 1.9 %refine_and_back.1 = (bf16[8,24,128]{2,1,0:T(8,128)(2,1)S(1)}, f32[32,384]{1,0:T(8,128)S(1)}) custom-call(bf16[16,30,128]{2,1,0:T(8,128)(2,1)S(1)} %all_to_all.20.sent_ref, bf16[16,640]{1,0:T(8,128)(2,1)S(1)} %bitcast.18, bf16[2,288,128]{2,1,0:T(8,128)(2,1)S(1)} %get-tuple-element.25.first_ref, bf16[2,96,288]{2,1,0:T(8,128)(2,1)S(1)} %get-tuple-element.26.first_t_ref, ...), custom_call_target="tpu_custom_call" | custom-call | flops 198180864 | bytes 905216 | tf_op jit(solution)/shard_map/refine_and_back/pallas_call | solution.py:655
  26.9 6.8 %all_to_all.21.sent_ref = bf16[8,24,128]{2,1,0:T(8,128)(2,1)S(1)} all-to-all(bf16[8,24,128]{2,1,0:T(8,128)(2,1)S(1)} %get-tuple-element.29), channel_id=1, replica_groups={{14,0,2,4,6,8,10,12},{30,16,18,20,22,24,26,28},{15,1,3,5,7,9,11,13},{31..., dimensions={0} | all-to-all | bytes 98304 | tf_op jit(solution)/shard_map/all_to_all | solution.py:700
  33.6 0.1 hand_on.1
  33.8 1.2 %collective-permute-start.2 = (bf16[72,640]{1,0:T(8,128)(2,1)S(1)}, bf16[72,640]{1,0:T(8,128)(2,1)S(1)}, u32[]{:S(2)}, u32[]{:S(2)}) collective-permute-start(bf16[72,640]{1,0:T(8,128)(2,1)S(1)} %get-tuple-element.33), channel_id=1, source_target_pairs={{0,16},{2,18},{4,20},{6,22},{8,24},{10,26},{12,28},{14,30},{16,0},... | collective-permute-start | bytes 276488 | tf_op jit(solution)/shard_map/ppermute | solution.py:694
  34.9 1.2 %masked_normal.1 = bf16[16,10,128]{2,1,0:T(8,128)(2,1)S(1)} custom-call(bf16[8,24,128]{2,1,0:T(8,128)(2,1)S(1)} %all_to_all.21.sent_ref, bf16[256,384]{1,0:T(8,128)(2,1)S(1)} %get-tuple-element.30.maps_ref, s32[16,320]{1,0:T(8,128)S(1)} %bitcast.15, bf16[384,768]{1,0:T(8,128)(2,1)S(1)} %copy-done, bf16[256,256]{1,0:T(8,128)(2,1)S(1)} %copy-done.6, ...), custom_call_target="tpu_custom_call" | custom-call | flops 452984832 | bytes 1159168 | tf_op jit(solution)/shard_map/masked_normal/pallas_call | solution.py:655
  36.1 7.3 %all_to_all.22.sent_ref = bf16[16,10,128]{2,1,0:T(8,128)(2,1)S(1)} all-to-all(bf16[16,10,128]{2,1,0:T(8,128)(2,1)S(1)} %masked_normal.1), channel_id=1, replica_groups={{15,14,13,12,11,10,9,8,7,6,5,4,3,2,1,0},{31,30,29,28,27,26,25,24,23,22,..., dimensions={0} | all-to-all | bytes 81920 | tf_op jit(solution)/shard_map/all_to_all | solution.py:700
  43.4 0.0 collective-permute-done.2.refs_1_
  43.4 1.6 %outputs.1 = (f32[16,640]{1,0:T(8,128)}, f32[640,128]{1,0:T(8,128)}) custom-call(f32[288,128]{1,0:T(8,128)S(1)} %get-tuple-element.21.columns_ref, bf16[16,10,128]{2,1,0:T(8,128)(2,1)S(1)} %all_to_all.22.sent_ref, f32[32,384]{1,0:T(8,128)S(1)} %get-tuple-element.31.image_ref, s32[16,320]{1,0:T(8,128)S(1)} %bitcast.16, bf16[384,768]{1,0:T(8,128)(2,1)S(1)} %copy-done, ...), custom_call_target="tpu_custom_call" | custom-call | flops 301989888 | bytes 1531904 | tf_op jit(solution)/shard_map/outputs/pallas_call | solution.py:655
  (18 shorter events, 0.0 us)
Async XLA Ops:
  0.6 11.1 %copy-start.2 = (bf16[128,1536]{1,0:T(8,128)(2,1)S(1)}, bf16[128,1536]{1,0:T(8,128)(2,1)}, u32[]{:S(2)}) copy-start(bf16[128,1536]{1,0:T(8,128)(2,1)} %constant.19.clone.place_ref) | copy-start | bytes 1179652
  0.6 11.1 %copy-start.4 = (f32[288,128]{1,0:T(8,128)S(1)}, f32[288,128]{1,0:T(8,128)}, u32[]{:S(2)}) copy-start(f32[288,128]{1,0:T(8,128)} %constant.20.clone.offset_ref) | copy-start | bytes 442372
  0.7 11.1 %copy-start.5 = (f32[288,128]{1,0:T(8,128)S(1)}, f32[288,128]{1,0:T(8,128)}, u32[]{:S(2)}) copy-start(f32[288,128]{1,0:T(8,128)} %constant.18.clone.repeat_ref) | copy-start | bytes 442372
  0.7 11.1 %copy-start.9 = (f32[2,9,18,2]{2,3,1,0:T(2,128)S(1)}, f32[2,9,18,2]{2,3,1,0:T(2,128)}, u32[]{:S(2)}) copy-start(f32[2,9,18,2]{2,3,1,0:T(2,128)} %param.20) | copy-start | bytes 7780
  0.7 11.1 %copy-start.10 = (f32[2,9,2,18]{3,2,1,0:T(2,128)S(1)}, f32[2,9,2,18]{3,2,1,0:T(2,128)}, u32[]{:S(2)}) copy-start(f32[2,9,2,18]{3,2,1,0:T(2,128)} %param.22) | copy-start | bytes 7780
  0.7 11.1 %copy-start.11 = (f32[2,18]{1,0:T(2,128)S(1)}, f32[2,18]{1,0:T(2,128)}, u32[]{:S(2)}) copy-start(f32[2,18]{1,0:T(2,128)} %bias_in_ref.1) | copy-start | bytes 436
  0.7 11.1 %copy-start.12 = (f32[2,2]{1,0:T(2,128)S(1)}, f32[2,2]{1,0:T(2,128)}, u32[]{:S(2)}) copy-start(f32[2,2]{1,0:T(2,128)} %bias_out_ref.1) | copy-start | bytes 52
  0.7 11.1 %copy-start.13 = (f32[2]{0:T(128)S(1)}, f32[2]{0:T(128)}, u32[]{:S(2)}) copy-start(f32[2]{0:T(128)} %weight_ref.1) | copy-start | bytes 28
  2.7 10.6 %copy-start = (bf16[384,768]{1,0:T(8,128)(2,1)S(1)}, bf16[384,768]{1,0:T(8,128)(2,1)}, u32[]{:S(2)}) copy-start(bf16[384,768]{1,0:T(8,128)(2,1)} %constant.14.clone.table_ref) | copy-start | bytes 1769476
  2.7 10.6 %collective-permute-start = (bf16[64,640]{1,0:T(8,128)(2,1)}, bf16[64,640]{1,0:T(8,128)(2,1)S(1)}, u32[]{:S(2)}, u32[]{:S(2)}) collective-permute-start(bf16[64,640]{1,0:T(8,128)(2,1)} %get-tuple-element.19), channel_id=1, source_target_pairs={{0,16},{2,18},{4,20},{6,22},{8,24},{10,26},{12,28},{14,30},{16,0},... | collective-permute-start | bytes 245768 | tf_op jit(solution)/shard_map/ppermute | solution.py:694
  6.8 8.9 %all-to-all-start = ((bf16[8,90,128]{2,1,0:T(8,128)(2,1)}), bf16[8,90,128]{2,1,0:T(8,128)(2,1)S(1)}, u32[]{:S(2)}, u32[]{:S(2)}) async-start(bf16[8,90,128]{2,1,0:T(8,128)(2,1)} %get-tuple-element.22), calls=%async_computation | async-start | bytes 393216 | tf_op jit(solution)/shard_map/all_to_all | solution.py:700
  11.8 1.6 %copy-start.3 = (s32[2,8,320]{2,1,0:T(8,128)S(1)}, s32[2,8,320]{2,1,0:T(8,128)}, u32[]{:S(2)}) copy-start(s32[2,8,320]{2,1,0:T(8,128)} %param.18) | copy-start | bytes 61444
  11.8 1.6 %copy-start.7 = (bf16[128,128]{1,0:T(8,128)(2,1)S(1)}, bf16[128,128]{1,0:T(8,128)(2,1)}, u32[]{:S(2)}) copy-start(bf16[128,128]{1,0:T(8,128)(2,1)} %constant.17.clone.plus_ref) | copy-start | bytes 98308
  13.4 0.9 %copy-start.1 = (bf16[8,16,1,640]{3,1,2,0:T(8,128)(2,1)S(1)}, bf16[8,16,1,640]{3,1,2,0:T(8,128)(2,1)}, u32[]{:S(2)}) copy-start(bf16[8,16,1,640]{3,1,2,0:T(8,128)(2,1)} %param.16) | copy-start | bytes 491524
  13.9 1.8 %copy-start.6 = (bf16[256,256]{1,0:T(8,128)(2,1)S(1)}, bf16[256,256]{1,0:T(8,128)(2,1)}, u32[]{:S(2)}) copy-start(bf16[256,256]{1,0:T(8,128)(2,1)} %constant.15.clone.minus_ref) | copy-start | bytes 393220
  13.9 1.8 %copy-start.14 = (bf16[256,256]{1,0:T(8,128)(2,1)S(1)}, bf16[256,256]{1,0:T(8,128)(2,1)}, u32[]{:S(2)}) copy-start(bf16[256,256]{1,0:T(8,128)(2,1)} %constant.16.clone.plus_ref) | copy-start | bytes 393220
  13.9 1.8 %collective-permute-start.1 = (f32[192,384]{1,0:T(8,128)S(1)}, f32[192,384]{1,0:T(8,128)S(1)}, u32[]{:S(2)}, u32[]{:S(2)}) collective-permute-start(f32[192,384]{1,0:T(8,128)S(1)} %far_images.1), channel_id=1, source_target_pairs={{0,0},{2,2},{4,4},{6,6},{8,8},{10,10},{12,12},{14,14},{16,16},{18,... | collective-permute-start | bytes 884744 | tf_op jit(solution)/shard_map/ppermute | solution.py:697
  17.1 7.8 %copy-start.8 = (bf16[1,16,640]{2,1,0:T(8,128)(2,1)S(1)}, bf16[1,16,640]{2,1,0:T(8,128)(2,1)}, u32[]{:S(2)}) copy-start(bf16[1,16,640]{2,1,0:T(8,128)(2,1)} %param.24) | copy-start | bytes 61444
  33.8 9.7 %collective-permute-start.2 = (bf16[72,640]{1,0:T(8,128)(2,1)S(1)}, bf16[72,640]{1,0:T(8,128)(2,1)S(1)}, u32[]{:S(2)}, u32[]{:S(2)}) collective-permute-start(bf16[72,640]{1,0:T(8,128)(2,1)S(1)} %get-tuple-element.33), channel_id=1, source_target_pairs={{0,16},{2,18},{4,20},{6,22},{8,24},{10,26},{12,28},{14,30},{16,0},... | collective-permute-start | bytes 276488 | tf_op jit(solution)/shard_map/ppermute | solution.py:694

commit v12 on v11

--- a/solution.py
+++ b/solution.py
@@ -355,14 +355,6 @@
         out_ref[images.shape[0] :] = jnp.zeros_like(out_ref[images.shape[0] :])
 
 
-def own_kernel(coils, lines, volumes, kspace_ref, mask_ref, table_ref, plus_ref, out_ref):
-    parts = blocks(read_mask(mask_ref, table_ref.shape[0]), volumes)
-    volume = own_volume(parts[0].shape[0])
-    kspace = choose_volume(kspace_ref[...].astype(F32), coils, volumes, volume)
-    mask = over_coils(pick(parts, volume), coils)
-    out_ref[...] = line_images(kspace, mask, lines, table_ref, plus_ref)
-
-
 def rows_kernel(
     coils,
     lines,
@@ -370,13 +362,15 @@
     from_places,
     to_places,
     sent_ref,
+    kspace_ref,
     mask_ref,
     table_ref,
     minus_ref,
     plus_ref,
+    near_ref,
     *refs,
 ):
-    arrival_refs, refs = refs[:volumes], refs[volumes:]
+    arrival_refs, refs = refs[: volumes - 1], refs[volumes - 1 :]
     out_ref, maps_ref, arrived, leaving = refs
     depth = sent_ref.shape[0]
     pitch = arrived.shape[0] // depth
@@ -384,7 +378,9 @@
     mask = pick(blocks(read_mask(mask_ref, table_ref.shape[0]), volumes), volume)
     mask = over_coils(mask, volumes * coils)
 
-    arrivals = [halves(ref[: 2 * coils * depth]) for ref in arrival_refs]
+    own = choose_volume(kspace_ref[...].astype(F32), coils, volumes, volume)
+    own = line_images(own, mask[: coils * depth], lines, table_ref, near_ref)
+    arrivals = [halves(own)] + [halves(ref[: 2 * coils * depth]) for ref in arrival_refs]
     measured = []
     for part in range(2):
         for place in range(volumes):
@@ -754,15 +750,7 @@
         scalars=1,
     )
     *samples, columns = lax.optimization_barrier((*samples, columns))
-    (own,) = call(
-        functools.partial(own_kernel, coils, lines, volumes),
-        "own_images",
-        (kspace.reshape(planes, two_lines), mask, table, near_plus),
-        [shape(2 * coils * depth, width)],
-        [],
-        line_flops,
-    )
-    images = [own]
+    images = []
     for value in samples:
         (image,) = call(
             functools.partial(far_kernel, coils, lines, volumes),
@@ -780,7 +768,7 @@
     partial, maps = call(
         functools.partial(rows_kernel, coils, lines, volumes, near_places, both_places),
         "combine_rows",
-        (arrived, mask, table, minus, plus, *images),
+        (arrived, kspace.reshape(planes, two_lines), mask, table, minus, plus, near_plus, *images),
         [
             shape(span, sums_lines, LANES, kind=BF16),
             shape(2 * planes, width, kind=BF16),

time: 45.4 us -> 45.5 us (level)
  waiting for transfers between devices: 0.89 us -> 1.75 us
    all_to_all x1, waiting for transfers between devices: 0.88 us -> 1.74 us  [exchange(): lax.all_to_all(value, axes, 0, 0, tiled=True, axis_index_groups=groups)]
    pallas_call x9 -> x8, Pallas kernels: 10.6 us -> 10.3 us  [call(): pl.pallas_call(kernel, name=name, out_shape=tuple(outs), in_specs=[pl.Blo...]
  transfers between devices with their start and end apart: 4 -> 4, of which waited for: 1 -> 1; matrix products, arithmetic and copies ran while one was open for 0% -> 0% of each run, Pallas kernels for 8% -> 7%
where the time goes in v12:
time: 45.5 us; the launch traced here: 45.1 us
  blocking collectives  21.9 us (48%)
  Pallas kernels  10.3 us (23%)
  starting transfers between devices  10.2 us (22%)
  waiting for transfers between devices  1.75 us (4%)
  between operations  0.89 us (2%)
    all_to_all x3, blocking collectives, exchange(): lax.all_to_all(value, axes, 0, 0, tiled=True, axis_index_groups=groups)  21.9 us
    pallas_call x8, Pallas kernels, call(): pl.pallas_call(kernel, name=name, out_shape=tuple(outs), in_specs=[pl.Blo...  10.3 us
    ppermute x2, starting transfers between devices, from_group(): return lax.ppermute(value, 'section', pairs)  5.22 us
    all_to_all x1, starting transfers between devices, exchange(): lax.all_to_all(value, axes, 0, 0, tiled=True, axis_index_groups=groups)  4.99 us
    all_to_all x1, waiting for transfers between devices, exchange(): lax.all_to_all(value, axes, 0, 0, tiled=True, axis_index_groups=groups)  1.74 us
  transfers between devices with their start and end apart: 4, of which 1 were waited for; matrix products, arithmetic and copies ran while one was open for 0% of the time, Pallas kernels for 7%

profile of v12, /device:TPU:0, one launch (start us, length us, event | category | flops | bytes accessed | tf_op | source)
XLA Modules:
  0.0 45.1 jit_solution(4987087456918486355)
XLA Ops:
  0.6 0.0 copy-start.1
  0.6 0.0 copy-start.3
  0.7 0.0 copy-start.4
  0.7 0.0 copy-start.9
  0.7 0.0 copy-start.10
  0.7 0.0 copy-start.11
  0.7 0.0 copy-start.12
  0.7 2.0 %pack_maps.1 = (bf16[8,90,128]{2,1,0:T(8,128)(2,1)}, bf16[64,640]{1,0:T(8,128)(2,1)}) custom-call(bf16[128,640]{1,0:T(8,128)(2,1)} %bitcast.10, bf16[128,640]{1,0:T(8,128)(2,1)} %bitcast.20, bf16[16,640]{1,0:T(8,128)(2,1)} %bitcast.16), custom_call_target="tpu_custom_call" | custom-call | flops 1000 | bytes 614400 | tf_op jit(solution)/shard_map/pack_maps/pallas_call | solution.py:651
  2.7 4.0 %collective-permute-start = (bf16[64,640]{1,0:T(8,128)(2,1)}, bf16[64,640]{1,0:T(8,128)(2,1)S(1)}, u32[]{:S(2)}, u32[]{:S(2)}) collective-permute-start(bf16[64,640]{1,0:T(8,128)(2,1)} %get-tuple-element.19), channel_id=1, source_target_pairs={{0,16},{2,18},{4,20},{6,22},{8,24},{10,26},{12,28},{14,30},{16,0},... | collective-permute-start | bytes 245768 | tf_op jit(solution)/shard_map/ppermute | solution.py:690
  6.8 5.0 %all-to-all-start = ((bf16[8,90,128]{2,1,0:T(8,128)(2,1)}), bf16[8,90,128]{2,1,0:T(8,128)(2,1)S(1)}, u32[]{:S(2)}, u32[]{:S(2)}) async-start(bf16[8,90,128]{2,1,0:T(8,128)(2,1)} %get-tuple-element.22), calls=%async_computation | async-start | bytes 393216 | tf_op jit(solution)/shard_map/all_to_all | solution.py:696
  11.8 0.0 copy-start.6
  11.8 0.0 copy-start.8
  11.8 1.5 %lay_out_taps.1 = (bf16[2,288,128]{2,1,0:T(8,128)(2,1)S(1)}, bf16[2,96,288]{2,1,0:T(8,128)(2,1)S(1)}, bf16[2,96,288]{2,1,0:T(8,128)(2,1)S(1)}, bf16[2,288,128]{2,1,0:T(8,128)(2,1)S(1)}, f32[288,128]{1,0:T(8,128)S(1)}) custom-call(f32[2]{0:T(128)S(1)} %copy-done.13, f32[18,2,18]{2,1,0:T(2,128)S(1)} %bitcast.18, f32[18,2,18]{2,1,0:T(2,128)S(1)} %bitcast.19, ...), custom_call_target="tpu_custom_call" | custom-call | flops 113246208 | bytes 1357032 | tf_op jit(solution)/shard_map/lay_out_taps/pallas_call | solution.py:651
  13.4 0.0 collective-permute-done.kspace_ref
  13.4 0.0 copy-start.2
  13.4 0.0 copy-start.5
  13.4 0.0 copy-start.14
  13.4 0.4 far_images.1
  13.9 0.0 collective-permute-start.1
  13.9 1.7 %all-to-all-done.sent_ref = bf16[8,90,128]{2,1,0:T(8,128)(2,1)S(1)} async-done(((bf16[8,90,128]{2,1,0:T(8,128)(2,1)}), bf16[8,90,128]{2,1,0:T(8,128)(2,1)S(1)}, u32[]{:S(2)}, u32[]{:S(2)}) %all-to-all-start) | async-done | bytes 184352 | tf_op jit(solution)/shard_map/all_to_all | solution.py:696
  15.7 0.0 collective-permute-done.1.refs_0_
  15.7 1.5 %combine_rows.1 = (bf16[16,30,128]{2,1,0:T(8,128)(2,1)S(1)}, bf16[256,384]{1,0:T(8,128)(2,1)S(1)}) custom-call(bf16[8,90,128]{2,1,0:T(8,128)(2,1)S(1)} %all-to-all-done.sent_ref, bf16[128,640]{1,0:T(8,128)(2,1)S(1)} %bitcast.11, s32[16,320]{1,0:T(8,128)S(1)} %bitcast.13, bf16[384,768]{1,0:T(8,128)(2,1)S(1)} %copy-done, bf16[256,256]{1,0:T(8,128)(2,1)S(1)} %copy-done.5, ...), custom_call_target="tpu_custom_call" | custom-call | flops 603979776 | bytes 1867776 | tf_op jit(solution)/shard_map/combine_rows/pallas_call | solution.py:651
  17.2 0.0 copy-start.7
  17.2 7.8 %all_to_all.20.sent_ref = bf16[16,30,128]{2,1,0:T(8,128)(2,1)S(1)} all-to-all(bf16[16,30,128]{2,1,0:T(8,128)(2,1)S(1)} %get-tuple-element.24), channel_id=1, replica_groups={{15,14,13,12,11,10,9,8,7,6,5,4,3,2,1,0},{31,30,29,28,27,26,25,24,23,22,..., dimensions={0} | all-to-all | bytes 245760 | tf_op jit(solution)/shard_map/all_to_all | solution.py:696
  25.0 1.9 %refine_and_back.1 = (bf16[8,24,128]{2,1,0:T(8,128)(2,1)S(1)}, f32[32,384]{1,0:T(8,128)S(1)}) custom-call(bf16[16,30,128]{2,1,0:T(8,128)(2,1)S(1)} %all_to_all.20.sent_ref, bf16[16,640]{1,0:T(8,128)(2,1)S(1)} %bitcast.17, bf16[2,288,128]{2,1,0:T(8,128)(2,1)S(1)} %get-tuple-element.25.first_ref, bf16[2,96,288]{2,1,0:T(8,128)(2,1)S(1)} %get-tuple-element.26.first_t_ref, ...), custom_call_target="tpu_custom_call" | custom-call | flops 198180864 | bytes 905216 | tf_op jit(solution)/shard_map/refine_and_back/pallas_call | solution.py:651
  26.9 6.7 %all_to_all.21.sent_ref = bf16[8,24,128]{2,1,0:T(8,128)(2,1)S(1)} all-to-all(bf16[8,24,128]{2,1,0:T(8,128)(2,1)S(1)} %get-tuple-element.29), channel_id=1, replica_groups={{14,0,2,4,6,8,10,12},{30,16,18,20,22,24,26,28},{15,1,3,5,7,9,11,13},{31..., dimensions={0} | all-to-all | bytes 98304 | tf_op jit(solution)/shard_map/all_to_all | solution.py:696
  33.7 0.1 hand_on.1
  33.8 1.2 %collective-permute-start.2 = (bf16[72,640]{1,0:T(8,128)(2,1)S(1)}, bf16[72,640]{1,0:T(8,128)(2,1)S(1)}, u32[]{:S(2)}, u32[]{:S(2)}) collective-permute-start(bf16[72,640]{1,0:T(8,128)(2,1)S(1)} %get-tuple-element.33), channel_id=1, source_target_pairs={{0,16},{2,18},{4,20},{6,22},{8,24},{10,26},{12,28},{14,30},{16,0},... | collective-permute-start | bytes 276488 | tf_op jit(solution)/shard_map/ppermute | solution.py:690
  35.0 1.2 %masked_normal.1 = bf16[16,10,128]{2,1,0:T(8,128)(2,1)S(1)} custom-call(bf16[8,24,128]{2,1,0:T(8,128)(2,1)S(1)} %all_to_all.21.sent_ref, bf16[256,384]{1,0:T(8,128)(2,1)S(1)} %get-tuple-element.30.maps_ref, s32[16,320]{1,0:T(8,128)S(1)} %bitcast.14, bf16[384,768]{1,0:T(8,128)(2,1)S(1)} %copy-done, bf16[256,256]{1,0:T(8,128)(2,1)S(1)} %copy-done.5, ...), custom_call_target="tpu_custom_call" | custom-call | flops 452984832 | bytes 1159168 | tf_op jit(solution)/shard_map/masked_normal/pallas_call | solution.py:651
  36.2 7.3 %all_to_all.22.sent_ref = bf16[16,10,128]{2,1,0:T(8,128)(2,1)S(1)} all-to-all(bf16[16,10,128]{2,1,0:T(8,128)(2,1)S(1)} %masked_normal.1), channel_id=1, replica_groups={{15,14,13,12,11,10,9,8,7,6,5,4,3,2,1,0},{31,30,29,28,27,26,25,24,23,22,..., dimensions={0} | all-to-all | bytes 81920 | tf_op jit(solution)/shard_map/all_to_all | solution.py:696
  43.5 0.0 collective-permute-done.2.refs_1_
  43.5 1.6 %outputs.1 = (f32[16,640]{1,0:T(8,128)}, f32[640,128]{1,0:T(8,128)}) custom-call(f32[288,128]{1,0:T(8,128)S(1)} %get-tuple-element.21.columns_ref, bf16[16,10,128]{2,1,0:T(8,128)(2,1)S(1)} %all_to_all.22.sent_ref, f32[32,384]{1,0:T(8,128)S(1)} %get-tuple-element.31.image_ref, s32[16,320]{1,0:T(8,128)S(1)} %bitcast.15, bf16[384,768]{1,0:T(8,128)(2,1)S(1)} %copy-done, ...), custom_call_target="tpu_custom_call" | custom-call | flops 301989888 | bytes 1531904 | tf_op jit(solution)/shard_map/outputs/pallas_call | solution.py:651
  (17 shorter events, 0.0 us)
Async XLA Ops:
  0.6 11.1 %copy-start.1 = (bf16[128,1536]{1,0:T(8,128)(2,1)S(1)}, bf16[128,1536]{1,0:T(8,128)(2,1)}, u32[]{:S(2)}) copy-start(bf16[128,1536]{1,0:T(8,128)(2,1)} %constant.19.clone.place_ref) | copy-start | bytes 1179652
  0.6 11.1 %copy-start.3 = (f32[288,128]{1,0:T(8,128)S(1)}, f32[288,128]{1,0:T(8,128)}, u32[]{:S(2)}) copy-start(f32[288,128]{1,0:T(8,128)} %constant.20.clone.offset_ref) | copy-start | bytes 442372
  0.7 11.1 %copy-start.4 = (f32[288,128]{1,0:T(8,128)S(1)}, f32[288,128]{1,0:T(8,128)}, u32[]{:S(2)}) copy-start(f32[288,128]{1,0:T(8,128)} %constant.18.clone.repeat_ref) | copy-start | bytes 442372
  0.7 11.1 %copy-start.9 = (f32[2,9,18,2]{2,3,1,0:T(2,128)S(1)}, f32[2,9,18,2]{2,3,1,0:T(2,128)}, u32[]{:S(2)}) copy-start(f32[2,9,18,2]{2,3,1,0:T(2,128)} %param.20) | copy-start | bytes 7780
  0.7 11.1 %copy-start.10 = (f32[2,9,2,18]{3,2,1,0:T(2,128)S(1)}, f32[2,9,2,18]{3,2,1,0:T(2,128)}, u32[]{:S(2)}) copy-start(f32[2,9,2,18]{3,2,1,0:T(2,128)} %param.22) | copy-start | bytes 7780
  0.7 11.1 %copy-start.11 = (f32[2,18]{1,0:T(2,128)S(1)}, f32[2,18]{1,0:T(2,128)}, u32[]{:S(2)}) copy-start(f32[2,18]{1,0:T(2,128)} %bias_in_ref.1) | copy-start | bytes 436
  0.7 11.1 %copy-start.12 = (f32[2,2]{1,0:T(2,128)S(1)}, f32[2,2]{1,0:T(2,128)}, u32[]{:S(2)}) copy-start(f32[2,2]{1,0:T(2,128)} %bias_out_ref.1) | copy-start | bytes 52
  0.7 11.1 %copy-start.13 = (f32[2]{0:T(128)S(1)}, f32[2]{0:T(128)}, u32[]{:S(2)}) copy-start(f32[2]{0:T(128)} %weight_ref.1) | copy-start | bytes 28
  2.7 10.6 %copy-start = (bf16[384,768]{1,0:T(8,128)(2,1)S(1)}, bf16[384,768]{1,0:T(8,128)(2,1)}, u32[]{:S(2)}) copy-start(bf16[384,768]{1,0:T(8,128)(2,1)} %constant.14.clone.table_ref) | copy-start | bytes 1769476
  2.7 10.6 %collective-permute-start = (bf16[64,640]{1,0:T(8,128)(2,1)}, bf16[64,640]{1,0:T(8,128)(2,1)S(1)}, u32[]{:S(2)}, u32[]{:S(2)}) collective-permute-start(bf16[64,640]{1,0:T(8,128)(2,1)} %get-tuple-element.19), channel_id=1, source_target_pairs={{0,16},{2,18},{4,20},{6,22},{8,24},{10,26},{12,28},{14,30},{16,0},... | collective-permute-start | bytes 245768 | tf_op jit(solution)/shard_map/ppermute | solution.py:690
  6.8 8.9 %all-to-all-start = ((bf16[8,90,128]{2,1,0:T(8,128)(2,1)}), bf16[8,90,128]{2,1,0:T(8,128)(2,1)S(1)}, u32[]{:S(2)}, u32[]{:S(2)}) async-start(bf16[8,90,128]{2,1,0:T(8,128)(2,1)} %get-tuple-element.22), calls=%async_computation | async-start | bytes 393216 | tf_op jit(solution)/shard_map/all_to_all | solution.py:696
  11.8 1.6 %copy-start.6 = (s32[2,8,320]{2,1,0:T(8,128)S(1)}, s32[2,8,320]{2,1,0:T(8,128)}, u32[]{:S(2)}) copy-start(s32[2,8,320]{2,1,0:T(8,128)} %param.18) | copy-start | bytes 61444
  11.8 1.6 %copy-start.8 = (bf16[128,128]{1,0:T(8,128)(2,1)S(1)}, bf16[128,128]{1,0:T(8,128)(2,1)}, u32[]{:S(2)}) copy-start(bf16[128,128]{1,0:T(8,128)(2,1)} %constant.17.clone.plus_ref.near_ref) | copy-start | bytes 98308
  13.4 2.3 %copy-start.2 = (bf16[8,16,1,640]{3,1,2,0:T(8,128)(2,1)S(1)}, bf16[8,16,1,640]{3,1,2,0:T(8,128)(2,1)}, u32[]{:S(2)}) copy-start(bf16[8,16,1,640]{3,1,2,0:T(8,128)(2,1)} %param.16) | copy-start | bytes 491524
  13.4 2.3 %copy-start.5 = (bf16[256,256]{1,0:T(8,128)(2,1)S(1)}, bf16[256,256]{1,0:T(8,128)(2,1)}, u32[]{:S(2)}) copy-start(bf16[256,256]{1,0:T(8,128)(2,1)} %constant.15.clone.minus_ref) | copy-start | bytes 393220
  13.4 2.2 %copy-start.14 = (bf16[256,256]{1,0:T(8,128)(2,1)S(1)}, bf16[256,256]{1,0:T(8,128)(2,1)}, u32[]{:S(2)}) copy-start(bf16[256,256]{1,0:T(8,128)(2,1)} %constant.16.clone.plus_ref) | copy-start | bytes 393220
  13.9 1.8 %collective-permute-start.1 = (f32[192,384]{1,0:T(8,128)S(1)}, f32[192,384]{1,0:T(8,128)S(1)}, u32[]{:S(2)}, u32[]{:S(2)}) collective-permute-start(f32[192,384]{1,0:T(8,128)S(1)} %far_images.1), channel_id=1, source_target_pairs={{0,0},{2,2},{4,4},{6,6},{8,8},{10,10},{12,12},{14,14},{16,16},{18,... | collective-permute-start | bytes 884744 | tf_op jit(solution)/shard_map/ppermute | solution.py:693
  17.2 7.8 %copy-start.7 = (bf16[1,16,640]{2,1,0:T(8,128)(2,1)S(1)}, bf16[1,16,640]{2,1,0:T(8,128)(2,1)}, u32[]{:S(2)}) copy-start(bf16[1,16,640]{2,1,0:T(8,128)(2,1)} %param.24) | copy-start | bytes 61444
  33.8 9.7 %collective-permute-start.2 = (bf16[72,640]{1,0:T(8,128)(2,1)S(1)}, bf16[72,640]{1,0:T(8,128)(2,1)S(1)}, u32[]{:S(2)}, u32[]{:S(2)}) collective-permute-start(bf16[72,640]{1,0:T(8,128)(2,1)S(1)} %get-tuple-element.33), channel_id=1, source_target_pairs={{0,16},{2,18},{4,20},{6,22},{8,24},{10,26},{12,28},{14,30},{16,0},... | collective-permute-start | bytes 276488 | tf_op jit(solution)/shard_map/ppermute | solution.py:690

commit v13 on v12

--- a/solution.py
+++ b/solution.py
@@ -277,7 +277,6 @@
         other = lax.rem(volume + step, jnp.int32(volumes))
         ref[...] = choose_volume(kspace, coils, volumes, other).astype(BF16)
     count = maps_ref.shape[1] // LANES
-    scratch[...] = jnp.zeros_like(scratch)
     image = image_ref[...].astype(F32)
     for coil in range(coils + 1):
         value = maps_ref[coil * rows : (coil + 1) * rows, :].astype(F32) if coil < coils else image
@@ -412,7 +411,6 @@
         *collect(maps_real, maps_imag, images),
         maps_real * maps_real + maps_imag * maps_imag,
     ]
-    leaving[...] = jnp.zeros_like(leaving)
     sums = [row_sums(value, volumes, coils) for value in found]
     pitch = leaving.shape[0] // depth
     for place in range(volumes):
@@ -502,7 +500,6 @@
     of_cotangent = weight[1] + weight[0] * kept[1] + kept[0] * kept[1]
     of_second = weight[0] + kept[0]
     pulled = of_cotangent * cotangent + of_second * back_second + back_first
-    leaving[...] = jnp.zeros_like(leaving)
     parts = [blocks(part, volumes) for value in (model, pulled) for part in halves(value)]
     for place in range(volumes):
         chunks = [chunk for part in parts for chunk in lane_chunks(part[place])]
@@ -513,7 +510,8 @@
 def hand_kernel(lines, volumes, from_places, sent_ref, maps_ref, *refs):
     outs, (arrived,) = refs[:-1], refs[-1:]
     take_messages(arrived, sent_ref, from_places)
-    depth, pitch = sent_ref.shape[:2]
+    depth = sent_ref.shape[0]
+    pitch = arrived.shape[0] // depth
     volume = own_volume(depth)
     count = maps_ref.shape[1] // LANES
     maps = [blocks(part, volumes) for part in halves(maps_ref[...].astype(F32))]
@@ -548,7 +546,8 @@
     leaving,
 ):
     take_messages(arrived, sent_ref, from_places)
-    depth, pitch = sent_ref.shape[:2]
+    depth = sent_ref.shape[0]
+    pitch = arrived.shape[0] // depth
     volume = own_volume(depth)
     count = maps_ref.shape[1] // LANES
     fields = [
@@ -564,7 +563,6 @@
     images = spread(maps_real, maps_imag, over_rows(reals, coils), over_rows(imags, coils))
     images = masked_normal(images, table_ref, minus_ref, plus_ref, mask)
     found = [row_sums(value, volumes, coils) for value in collect(maps_real, maps_imag, images)]
-    leaving[...] = jnp.zeros_like(leaving)
     for place in range(volumes):
         chunks = join_complex(found[0][place], found[1][place], lines)
         write_rows(leaving, leaving.shape[0] // depth, chunks, place * len(chunks))
@@ -779,7 +777,8 @@
 
     partial = exchange(partial, both, near_both)
 
-    model_pitch = padded(volumes * 4 * count, 8)
+    model_lines = volumes * 4 * count
+    model_pitch = padded(model_lines, 8)
     moved, image = call(
         functools.partial(refine_kernel, lines, volumes, both_places, near_places),
         "refine_and_back",
@@ -792,7 +791,7 @@
             second_t,
             columns,
         ),
-        [shape(depth, model_pitch, LANES, kind=BF16), shape(2 * rows, width)],
+        [shape(depth, model_lines, LANES, kind=BF16), shape(2 * rows, width)],
         [(depth * depth_pitch, LANES), (depth * model_pitch, LANES)],
         14 * tall * wide * width,
     )

time: 45.5 us -> 45.4 us (level)
  no operation moved by 1% of the time
where the time goes in v13:
time: 45.4 us; the launch traced here: 45 us
  blocking collectives  21.9 us (48%)
  Pallas kernels  10.2 us (22%)
  starting transfers between devices  10.2 us (22%)
  waiting for transfers between devices  1.75 us (4%)
  between operations  0.89 us (2%)
    all_to_all x3, blocking collectives, exchange(): lax.all_to_all(value, axes, 0, 0, tiled=True, axis_index_groups=groups)  21.9 us
    pallas_call x8, Pallas kernels, call(): pl.pallas_call(kernel, name=name, out_shape=tuple(outs), in_specs=[pl.Blo...  10.2 us
    ppermute x2, starting transfers between devices, from_group(): return lax.ppermute(value, 'section', pairs)  5.2 us
    all_to_all x1, starting transfers between devices, exchange(): lax.all_to_all(value, axes, 0, 0, tiled=True, axis_index_groups=groups)  4.99 us
    all_to_all x1, waiting for transfers between devices, exchange(): lax.all_to_all(value, axes, 0, 0, tiled=True, axis_index_groups=groups)  1.74 us
  transfers between devices with their start and end apart: 4, of which 1 were waited for; matrix products, arithmetic and copies ran while one was open for 0% of the time, Pallas kernels for 7%

profile of v13, /device:TPU:0, one launch (start us, length us, event | category | flops | bytes accessed | tf_op | source)
XLA Modules:
  0.0 45.0 jit_solution(10435044782268905935)
XLA Ops:
  0.6 0.0 copy-start.1
  0.6 0.0 copy-start.3
  0.7 0.0 copy-start.4
  0.7 2.0 %pack_maps.1 = (bf16[8,90,128]{2,1,0:T(8,128)(2,1)}, bf16[64,640]{1,0:T(8,128)(2,1)}) custom-call(bf16[128,640]{1,0:T(8,128)(2,1)} %bitcast.10, bf16[128,640]{1,0:T(8,128)(2,1)} %bitcast.20, bf16[16,640]{1,0:T(8,128)(2,1)} %bitcast.16), custom_call_target="tpu_custom_call" | custom-call | flops 1000 | bytes 614400 | tf_op jit(solution)/shard_map/pack_maps/pallas_call | solution.py:649
  2.7 4.0 %collective-permute-start = (bf16[64,640]{1,0:T(8,128)(2,1)}, bf16[64,640]{1,0:T(8,128)(2,1)S(1)}, u32[]{:S(2)}, u32[]{:S(2)}) collective-permute-start(bf16[64,640]{1,0:T(8,128)(2,1)} %get-tuple-element.19), channel_id=1, source_target_pairs={{0,16},{2,18},{4,20},{6,22},{8,24},{10,26},{12,28},{14,30},{16,0},... | collective-permute-start | bytes 245768 | tf_op jit(solution)/shard_map/ppermute | solution.py:688
  6.7 5.0 %all-to-all-start = ((bf16[8,90,128]{2,1,0:T(8,128)(2,1)}), bf16[8,90,128]{2,1,0:T(8,128)(2,1)S(1)}, u32[]{:S(2)}, u32[]{:S(2)}) async-start(bf16[8,90,128]{2,1,0:T(8,128)(2,1)} %get-tuple-element.22), calls=%async_computation | async-start | bytes 393216 | tf_op jit(solution)/shard_map/all_to_all | solution.py:694
  11.8 0.0 copy-start.6
  11.8 0.0 copy-start.8
  11.8 1.5 %lay_out_taps.1 = (bf16[2,288,128]{2,1,0:T(8,128)(2,1)S(1)}, bf16[2,96,288]{2,1,0:T(8,128)(2,1)S(1)}, bf16[2,96,288]{2,1,0:T(8,128)(2,1)S(1)}, bf16[2,288,128]{2,1,0:T(8,128)(2,1)S(1)}, f32[288,128]{1,0:T(8,128)S(1)}) custom-call(f32[2]{0:T(128)S(1)} %copy-done.13, f32[18,2,18]{2,1,0:T(2,128)S(1)} %bitcast.18, f32[18,2,18]{2,1,0:T(2,128)S(1)} %bitcast.19, ...), custom_call_target="tpu_custom_call" | custom-call | flops 113246208 | bytes 1357032 | tf_op jit(solution)/shard_map/lay_out_taps/pallas_call | solution.py:649
  13.3 0.0 collective-permute-done.kspace_ref
  13.3 0.0 copy-done
  13.4 0.0 copy-done.6
  13.4 0.0 copy-done.8
  13.4 0.0 copy-start.2
  13.4 0.0 copy-start.5
  13.4 0.0 copy-start.14
  13.4 0.4 far_images.1
  13.9 0.0 collective-permute-start.1
  13.9 1.7 %all-to-all-done.sent_ref = bf16[8,90,128]{2,1,0:T(8,128)(2,1)S(1)} async-done(((bf16[8,90,128]{2,1,0:T(8,128)(2,1)}), bf16[8,90,128]{2,1,0:T(8,128)(2,1)S(1)}, u32[]{:S(2)}, u32[]{:S(2)}) %all-to-all-start) | async-done | bytes 184352 | tf_op jit(solution)/shard_map/all_to_all | solution.py:694
  15.6 0.0 collective-permute-done.1.refs_0_
  15.7 1.5 %combine_rows.1 = (bf16[16,30,128]{2,1,0:T(8,128)(2,1)S(1)}, bf16[256,384]{1,0:T(8,128)(2,1)S(1)}) custom-call(bf16[8,90,128]{2,1,0:T(8,128)(2,1)S(1)} %all-to-all-done.sent_ref, bf16[128,640]{1,0:T(8,128)(2,1)S(1)} %bitcast.11, s32[16,320]{1,0:T(8,128)S(1)} %bitcast.13, bf16[384,768]{1,0:T(8,128)(2,1)S(1)} %copy-done, bf16[256,256]{1,0:T(8,128)(2,1)S(1)} %copy-done.5, ...), custom_call_target="tpu_custom_call" | custom-call | flops 603979776 | bytes 1867776 | tf_op jit(solution)/shard_map/combine_rows/pallas_call | solution.py:649
  17.2 0.0 copy-start.7
  17.2 7.8 %all_to_all.20.sent_ref = bf16[16,30,128]{2,1,0:T(8,128)(2,1)S(1)} all-to-all(bf16[16,30,128]{2,1,0:T(8,128)(2,1)S(1)} %get-tuple-element.24), channel_id=1, replica_groups={{15,14,13,12,11,10,9,8,7,6,5,4,3,2,1,0},{31,30,29,28,27,26,25,24,23,22,..., dimensions={0} | all-to-all | bytes 245760 | tf_op jit(solution)/shard_map/all_to_all | solution.py:694
  25.0 0.0 copy-done.7
  25.0 1.9 %refine_and_back.1 = (bf16[8,24,128]{2,1,0:T(8,128)(2,1)S(1)}, f32[32,384]{1,0:T(8,128)S(1)}) custom-call(bf16[16,30,128]{2,1,0:T(8,128)(2,1)S(1)} %all_to_all.20.sent_ref, bf16[16,640]{1,0:T(8,128)(2,1)S(1)} %bitcast.17, bf16[2,288,128]{2,1,0:T(8,128)(2,1)S(1)} %get-tuple-element.25.first_ref, bf16[2,96,288]{2,1,0:T(8,128)(2,1)S(1)} %get-tuple-element.26.first_t_ref, ...), custom_call_target="tpu_custom_call" | custom-call | flops 198180864 | bytes 905216 | tf_op jit(solution)/shard_map/refine_and_back/pallas_call | solution.py:649
  26.9 6.8 %all_to_all.21.sent_ref = bf16[8,24,128]{2,1,0:T(8,128)(2,1)S(1)} all-to-all(bf16[8,24,128]{2,1,0:T(8,128)(2,1)S(1)} %get-tuple-element.29), channel_id=1, replica_groups={{14,0,2,4,6,8,10,12},{30,16,18,20,22,24,26,28},{15,1,3,5,7,9,11,13},{31..., dimensions={0} | all-to-all | bytes 98304 | tf_op jit(solution)/shard_map/all_to_all | solution.py:694
  33.7 0.1 hand_on.1
  33.8 1.2 %collective-permute-start.2 = (bf16[72,640]{1,0:T(8,128)(2,1)S(1)}, bf16[72,640]{1,0:T(8,128)(2,1)S(1)}, u32[]{:S(2)}, u32[]{:S(2)}) collective-permute-start(bf16[72,640]{1,0:T(8,128)(2,1)S(1)} %get-tuple-element.33), channel_id=1, source_target_pairs={{0,16},{2,18},{4,20},{6,22},{8,24},{10,26},{12,28},{14,30},{16,0},... | collective-permute-start | bytes 276488 | tf_op jit(solution)/shard_map/ppermute | solution.py:688
  35.0 1.2 %masked_normal.1 = bf16[16,10,128]{2,1,0:T(8,128)(2,1)S(1)} custom-call(bf16[8,24,128]{2,1,0:T(8,128)(2,1)S(1)} %all_to_all.21.sent_ref, bf16[256,384]{1,0:T(8,128)(2,1)S(1)} %get-tuple-element.30.maps_ref, s32[16,320]{1,0:T(8,128)S(1)} %bitcast.14, bf16[384,768]{1,0:T(8,128)(2,1)S(1)} %copy-done, bf16[256,256]{1,0:T(8,128)(2,1)S(1)} %copy-done.5, ...), custom_call_target="tpu_custom_call" | custom-call | flops 452984832 | bytes 1159168 | tf_op jit(solution)/shard_map/masked_normal/pallas_call | solution.py:649
  36.1 7.3 %all_to_all.22.sent_ref = bf16[16,10,128]{2,1,0:T(8,128)(2,1)S(1)} all-to-all(bf16[16,10,128]{2,1,0:T(8,128)(2,1)S(1)} %masked_normal.1), channel_id=1, replica_groups={{15,14,13,12,11,10,9,8,7,6,5,4,3,2,1,0},{31,30,29,28,27,26,25,24,23,22,..., dimensions={0} | all-to-all | bytes 81920 | tf_op jit(solution)/shard_map/all_to_all | solution.py:694
  43.5 0.0 collective-permute-done.2.refs_1_
  43.5 1.6 %outputs.1 = (f32[16,640]{1,0:T(8,128)}, f32[640,128]{1,0:T(8,128)}) custom-call(f32[288,128]{1,0:T(8,128)S(1)} %get-tuple-element.21.columns_ref, bf16[16,10,128]{2,1,0:T(8,128)(2,1)S(1)} %all_to_all.22.sent_ref, f32[32,384]{1,0:T(8,128)S(1)} %get-tuple-element.31.image_ref, s32[16,320]{1,0:T(8,128)S(1)} %bitcast.15, bf16[384,768]{1,0:T(8,128)(2,1)S(1)} %copy-done, ...), custom_call_target="tpu_custom_call" | custom-call | flops 301989888 | bytes 1531904 | tf_op jit(solution)/shard_map/outputs/pallas_call | solution.py:649
  (17 shorter events, 0.0 us)
Async XLA Ops:
  0.6 11.1 %copy-start.1 = (bf16[128,1536]{1,0:T(8,128)(2,1)S(1)}, bf16[128,1536]{1,0:T(8,128)(2,1)}, u32[]{:S(2)}) copy-start(bf16[128,1536]{1,0:T(8,128)(2,1)} %constant.19.clone.place_ref) | copy-start | bytes 1179652
  0.6 11.1 %copy-start.3 = (f32[288,128]{1,0:T(8,128)S(1)}, f32[288,128]{1,0:T(8,128)}, u32[]{:S(2)}) copy-start(f32[288,128]{1,0:T(8,128)} %constant.20.clone.offset_ref) | copy-start | bytes 442372
  0.7 11.1 %copy-start.4 = (f32[288,128]{1,0:T(8,128)S(1)}, f32[288,128]{1,0:T(8,128)}, u32[]{:S(2)}) copy-start(f32[288,128]{1,0:T(8,128)} %constant.18.clone.repeat_ref) | copy-start | bytes 442372
  0.7 11.1 %copy-start.9 = (f32[2,9,18,2]{2,3,1,0:T(2,128)S(1)}, f32[2,9,18,2]{2,3,1,0:T(2,128)}, u32[]{:S(2)}) copy-start(f32[2,9,18,2]{2,3,1,0:T(2,128)} %param.20) | copy-start | bytes 7780
  0.7 11.1 %copy-start.10 = (f32[2,9,2,18]{3,2,1,0:T(2,128)S(1)}, f32[2,9,2,18]{3,2,1,0:T(2,128)}, u32[]{:S(2)}) copy-start(f32[2,9,2,18]{3,2,1,0:T(2,128)} %param.22) | copy-start | bytes 7780
  0.7 11.1 %copy-start.11 = (f32[2,18]{1,0:T(2,128)S(1)}, f32[2,18]{1,0:T(2,128)}, u32[]{:S(2)}) copy-start(f32[2,18]{1,0:T(2,128)} %bias_in_ref.1) | copy-start | bytes 436
  0.7 11.1 %copy-start.12 = (f32[2,2]{1,0:T(2,128)S(1)}, f32[2,2]{1,0:T(2,128)}, u32[]{:S(2)}) copy-start(f32[2,2]{1,0:T(2,128)} %bias_out_ref.1) | copy-start | bytes 52
  0.7 11.1 %copy-start.13 = (f32[2]{0:T(128)S(1)}, f32[2]{0:T(128)}, u32[]{:S(2)}) copy-start(f32[2]{0:T(128)} %weight_ref.1) | copy-start | bytes 28
  2.7 10.6 %copy-start = (bf16[384,768]{1,0:T(8,128)(2,1)S(1)}, bf16[384,768]{1,0:T(8,128)(2,1)}, u32[]{:S(2)}) copy-start(bf16[384,768]{1,0:T(8,128)(2,1)} %constant.14.clone.table_ref) | copy-start | bytes 1769476
  2.7 10.6 %collective-permute-start = (bf16[64,640]{1,0:T(8,128)(2,1)}, bf16[64,640]{1,0:T(8,128)(2,1)S(1)}, u32[]{:S(2)}, u32[]{:S(2)}) collective-permute-start(bf16[64,640]{1,0:T(8,128)(2,1)} %get-tuple-element.19), channel_id=1, source_target_pairs={{0,16},{2,18},{4,20},{6,22},{8,24},{10,26},{12,28},{14,30},{16,0},... | collective-permute-start | bytes 245768 | tf_op jit(solution)/shard_map/ppermute | solution.py:688
  6.7 8.9 %all-to-all-start = ((bf16[8,90,128]{2,1,0:T(8,128)(2,1)}), bf16[8,90,128]{2,1,0:T(8,128)(2,1)S(1)}, u32[]{:S(2)}, u32[]{:S(2)}) async-start(bf16[8,90,128]{2,1,0:T(8,128)(2,1)} %get-tuple-element.22), calls=%async_computation | async-start | bytes 393216 | tf_op jit(solution)/shard_map/all_to_all | solution.py:694
  11.8 1.6 %copy-start.6 = (s32[2,8,320]{2,1,0:T(8,128)S(1)}, s32[2,8,320]{2,1,0:T(8,128)}, u32[]{:S(2)}) copy-start(s32[2,8,320]{2,1,0:T(8,128)} %param.18) | copy-start | bytes 61444
  11.8 1.6 %copy-start.8 = (bf16[128,128]{1,0:T(8,128)(2,1)S(1)}, bf16[128,128]{1,0:T(8,128)(2,1)}, u32[]{:S(2)}) copy-start(bf16[128,128]{1,0:T(8,128)(2,1)} %constant.17.clone.plus_ref.near_ref) | copy-start | bytes 98308
  13.4 2.3 %copy-start.2 = (bf16[8,16,1,640]{3,1,2,0:T(8,128)(2,1)S(1)}, bf16[8,16,1,640]{3,1,2,0:T(8,128)(2,1)}, u32[]{:S(2)}) copy-start(bf16[8,16,1,640]{3,1,2,0:T(8,128)(2,1)} %param.16) | copy-start | bytes 491524
  13.4 2.3 %copy-start.5 = (bf16[256,256]{1,0:T(8,128)(2,1)S(1)}, bf16[256,256]{1,0:T(8,128)(2,1)}, u32[]{:S(2)}) copy-start(bf16[256,256]{1,0:T(8,128)(2,1)} %constant.15.clone.minus_ref) | copy-start | bytes 393220
  13.4 2.2 %copy-start.14 = (bf16[256,256]{1,0:T(8,128)(2,1)S(1)}, bf16[256,256]{1,0:T(8,128)(2,1)}, u32[]{:S(2)}) copy-start(bf16[256,256]{1,0:T(8,128)(2,1)} %constant.16.clone.plus_ref) | copy-start | bytes 393220
  13.9 1.8 %collective-permute-start.1 = (f32[192,384]{1,0:T(8,128)S(1)}, f32[192,384]{1,0:T(8,128)S(1)}, u32[]{:S(2)}, u32[]{:S(2)}) collective-permute-start(f32[192,384]{1,0:T(8,128)S(1)} %far_images.1), channel_id=1, source_target_pairs={{0,0},{2,2},{4,4},{6,6},{8,8},{10,10},{12,12},{14,14},{16,16},{18,... | collective-permute-start | bytes 884744 | tf_op jit(solution)/shard_map/ppermute | solution.py:691
  17.2 7.8 %copy-start.7 = (bf16[1,16,640]{2,1,0:T(8,128)(2,1)S(1)}, bf16[1,16,640]{2,1,0:T(8,128)(2,1)}, u32[]{:S(2)}) copy-start(bf16[1,16,640]{2,1,0:T(8,128)(2,1)} %param.24) | copy-start | bytes 61444
  33.8 9.6 %collective-permute-start.2 = (bf16[72,640]{1,0:T(8,128)(2,1)S(1)}, bf16[72,640]{1,0:T(8,128)(2,1)S(1)}, u32[]{:S(2)}, u32[]{:S(2)}) collective-permute-start(bf16[72,640]{1,0:T(8,128)(2,1)S(1)} %get-tuple-element.33), channel_id=1, source_target_pairs={{0,16},{2,18},{4,20},{6,22},{8,24},{10,26},{12,28},{14,30},{16,0},... | collective-permute-start | bytes 276488 | tf_op jit(solution)/shard_map/ppermute | solution.py:688

commit v14 on v13

--- a/solution.py
+++ b/solution.py
@@ -525,6 +525,9 @@
     for step, ref in enumerate(outs):
         place = lax.rem(volume + step, jnp.int32(volumes))
         chosen = [jnp.concatenate([pick(a, place), pick(b, place)]) for a, b in zip(maps, pulled)]
+        if step == 0:
+            ref[...] = jnp.concatenate(chosen, axis=0).astype(BF16)
+            continue
         for index, chunk in enumerate(join_complex(*chosen, lines)):
             ref[:, index * LANES : (index + 1) * LANES] = chunk.astype(BF16)
 
@@ -590,8 +593,9 @@
     handed, (grad_ref,) = refs[:volumes], refs[volumes:]
     depth = mask_ref.shape[0] // volumes
     volume = own_volume(depth)
-    handed = [split_complex(lane_chunks(ref[...].astype(F32)), lines) for ref in handed]
-    handed = [jnp.concatenate(parts, axis=0) for parts in handed]
+    own, *handed = [ref[...].astype(F32) for ref in handed]
+    handed = [split_complex(lane_chunks(value), lines) for value in handed]
+    handed = [own] + [jnp.concatenate(parts, axis=0) for parts in handed]
     found = from_volumes(handed, volume, 2 * (coils + 1), volumes)
     maps, pulled = [], []
     for first in (0, coils + 1):
@@ -803,7 +807,8 @@
         functools.partial(hand_kernel, lines, volumes, near_places),
         "hand_on",
         (moved, maps),
-        [shape((coils + 1) * depth, two_lines, kind=BF16)] * volumes,
+        [shape(2 * (coils + 1) * depth, width, kind=BF16)]
+        + [shape((coils + 1) * depth, two_lines, kind=BF16)] * (volumes - 1),
         [(depth * model_pitch, LANES)],
         1000,
     )

time: 45.4 us -> 45.4 us (level)
  no operation moved by 1% of the time
where the time goes in v14:
time: 45.4 us; the launch traced here: 45 us
  blocking collectives  21.9 us (48%)
  Pallas kernels  10.2 us (22%)
  starting transfers between devices  10.2 us (22%)
  waiting for transfers between devices  1.75 us (4%)
  between operations  0.88 us (2%)
    all_to_all x3, blocking collectives, exchange(): lax.all_to_all(value, axes, 0, 0, tiled=True, axis_index_groups=groups)  21.9 us
    pallas_call x8, Pallas kernels, call(): pl.pallas_call(kernel, name=name, out_shape=tuple(outs), in_specs=[pl.Blo...  10.2 us
    ppermute x2, starting transfers between devices, from_group(): return lax.ppermute(value, 'section', pairs)  5.2 us
    all_to_all x1, starting transfers between devices, exchange(): lax.all_to_all(value, axes, 0, 0, tiled=True, axis_index_groups=groups)  4.99 us
    all_to_all x1, waiting for transfers between devices, exchange(): lax.all_to_all(value, axes, 0, 0, tiled=True, axis_index_groups=groups)  1.74 us
  transfers between devices with their start and end apart: 4, of which 1 were waited for; matrix products, arithmetic and copies ran while one was open for 0% of the time, Pallas kernels for 7%

profile of v14, /device:TPU:0, one launch (start us, length us, event | category | flops | bytes accessed | tf_op | source)
XLA Modules:
  0.0 45.0 jit_solution(6896614067771458074)
XLA Ops:
  0.6 0.0 copy-start.1
  0.6 0.0 copy-start.3
  0.7 0.0 copy-start.4
  0.7 0.0 copy-start.9
  0.7 0.0 copy-start.10
  0.7 0.0 copy-start.11
  0.7 0.0 copy-start.12
  0.7 2.0 %pack_maps.1 = (bf16[8,90,128]{2,1,0:T(8,128)(2,1)}, bf16[64,640]{1,0:T(8,128)(2,1)}) custom-call(bf16[128,640]{1,0:T(8,128)(2,1)} %bitcast.10, bf16[128,640]{1,0:T(8,128)(2,1)} %bitcast.20, bf16[16,640]{1,0:T(8,128)(2,1)} %bitcast.16), custom_call_target="tpu_custom_call" | custom-call | flops 1000 | bytes 614400 | tf_op jit(solution)/shard_map/pack_maps/pallas_call | solution.py:653
  2.7 4.0 %collective-permute-start = (bf16[64,640]{1,0:T(8,128)(2,1)}, bf16[64,640]{1,0:T(8,128)(2,1)S(1)}, u32[]{:S(2)}, u32[]{:S(2)}) collective-permute-start(bf16[64,640]{1,0:T(8,128)(2,1)} %get-tuple-element.19), channel_id=1, source_target_pairs={{0,16},{2,18},{4,20},{6,22},{8,24},{10,26},{12,28},{14,30},{16,0},... | collective-permute-start | bytes 245768 | tf_op jit(solution)/shard_map/ppermute | solution.py:692
  6.7 5.0 %all-to-all-start = ((bf16[8,90,128]{2,1,0:T(8,128)(2,1)}), bf16[8,90,128]{2,1,0:T(8,128)(2,1)S(1)}, u32[]{:S(2)}, u32[]{:S(2)}) async-start(bf16[8,90,128]{2,1,0:T(8,128)(2,1)} %get-tuple-element.22), calls=%async_computation | async-start | bytes 393216 | tf_op jit(solution)/shard_map/all_to_all | solution.py:698
  11.8 0.0 copy-start.6
  11.8 0.0 copy-start.8
  11.8 1.5 %lay_out_taps.1 = (bf16[2,288,128]{2,1,0:T(8,128)(2,1)S(1)}, bf16[2,96,288]{2,1,0:T(8,128)(2,1)S(1)}, bf16[2,96,288]{2,1,0:T(8,128)(2,1)S(1)}, bf16[2,288,128]{2,1,0:T(8,128)(2,1)S(1)}, f32[288,128]{1,0:T(8,128)S(1)}) custom-call(f32[2]{0:T(128)S(1)} %copy-done.13, f32[18,2,18]{2,1,0:T(2,128)S(1)} %bitcast.18, f32[18,2,18]{2,1,0:T(2,128)S(1)} %bitcast.19, ...), custom_call_target="tpu_custom_call" | custom-call | flops 113246208 | bytes 1357032 | tf_op jit(solution)/shard_map/lay_out_taps/pallas_call | solution.py:653
  13.3 0.0 collective-permute-done.kspace_ref
  13.4 0.0 copy-start.2
  13.4 0.0 copy-start.5
  13.4 0.0 copy-start.14
  13.4 0.4 far_images.1
  13.9 0.0 collective-permute-start.1
  13.9 1.7 %all-to-all-done.sent_ref = bf16[8,90,128]{2,1,0:T(8,128)(2,1)S(1)} async-done(((bf16[8,90,128]{2,1,0:T(8,128)(2,1)}), bf16[8,90,128]{2,1,0:T(8,128)(2,1)S(1)}, u32[]{:S(2)}, u32[]{:S(2)}) %all-to-all-start) | async-done | bytes 184352 | tf_op jit(solution)/shard_map/all_to_all | solution.py:698
  15.6 0.0 collective-permute-done.1.refs_0_
  15.7 1.5 %combine_rows.1 = (bf16[16,30,128]{2,1,0:T(8,128)(2,1)S(1)}, bf16[256,384]{1,0:T(8,128)(2,1)S(1)}) custom-call(bf16[8,90,128]{2,1,0:T(8,128)(2,1)S(1)} %all-to-all-done.sent_ref, bf16[128,640]{1,0:T(8,128)(2,1)S(1)} %bitcast.11, s32[16,320]{1,0:T(8,128)S(1)} %bitcast.13, bf16[384,768]{1,0:T(8,128)(2,1)S(1)} %copy-done, bf16[256,256]{1,0:T(8,128)(2,1)S(1)} %copy-done.5, ...), custom_call_target="tpu_custom_call" | custom-call | flops 603979776 | bytes 1867776 | tf_op jit(solution)/shard_map/combine_rows/pallas_call | solution.py:653
  17.2 0.0 copy-start.7
  17.2 7.8 %all_to_all.20.sent_ref = bf16[16,30,128]{2,1,0:T(8,128)(2,1)S(1)} all-to-all(bf16[16,30,128]{2,1,0:T(8,128)(2,1)S(1)} %get-tuple-element.24), channel_id=1, replica_groups={{15,14,13,12,11,10,9,8,7,6,5,4,3,2,1,0},{31,30,29,28,27,26,25,24,23,22,..., dimensions={0} | all-to-all | bytes 245760 | tf_op jit(solution)/shard_map/all_to_all | solution.py:698
  25.0 1.9 %refine_and_back.1 = (bf16[8,24,128]{2,1,0:T(8,128)(2,1)S(1)}, f32[32,384]{1,0:T(8,128)S(1)}) custom-call(bf16[16,30,128]{2,1,0:T(8,128)(2,1)S(1)} %all_to_all.20.sent_ref, bf16[16,640]{1,0:T(8,128)(2,1)S(1)} %bitcast.17, bf16[2,288,128]{2,1,0:T(8,128)(2,1)S(1)} %get-tuple-element.25.first_ref, bf16[2,96,288]{2,1,0:T(8,128)(2,1)S(1)} %get-tuple-element.26.first_t_ref, ...), custom_call_target="tpu_custom_call" | custom-call | flops 198180864 | bytes 905216 | tf_op jit(solution)/shard_map/refine_and_back/pallas_call | solution.py:653
  26.9 6.8 %all_to_all.21.sent_ref = bf16[8,24,128]{2,1,0:T(8,128)(2,1)S(1)} all-to-all(bf16[8,24,128]{2,1,0:T(8,128)(2,1)S(1)} %get-tuple-element.29), channel_id=1, replica_groups={{14,0,2,4,6,8,10,12},{30,16,18,20,22,24,26,28},{15,1,3,5,7,9,11,13},{31..., dimensions={0} | all-to-all | bytes 98304 | tf_op jit(solution)/shard_map/all_to_all | solution.py:698
  33.7 0.1 hand_on.1
  33.8 1.2 %collective-permute-start.2 = (bf16[72,640]{1,0:T(8,128)(2,1)S(1)}, bf16[72,640]{1,0:T(8,128)(2,1)S(1)}, u32[]{:S(2)}, u32[]{:S(2)}) collective-permute-start(bf16[72,640]{1,0:T(8,128)(2,1)S(1)} %get-tuple-element.33), channel_id=1, source_target_pairs={{0,16},{2,18},{4,20},{6,22},{8,24},{10,26},{12,28},{14,30},{16,0},... | collective-permute-start | bytes 276488 | tf_op jit(solution)/shard_map/ppermute | solution.py:692
  35.0 1.2 %masked_normal.1 = bf16[16,10,128]{2,1,0:T(8,128)(2,1)S(1)} custom-call(bf16[8,24,128]{2,1,0:T(8,128)(2,1)S(1)} %all_to_all.21.sent_ref, bf16[256,384]{1,0:T(8,128)(2,1)S(1)} %get-tuple-element.30.maps_ref, s32[16,320]{1,0:T(8,128)S(1)} %bitcast.14, bf16[384,768]{1,0:T(8,128)(2,1)S(1)} %copy-done, bf16[256,256]{1,0:T(8,128)(2,1)S(1)} %copy-done.5, ...), custom_call_target="tpu_custom_call" | custom-call | flops 452984832 | bytes 1159168 | tf_op jit(solution)/shard_map/masked_normal/pallas_call | solution.py:653
  36.1 7.3 %all_to_all.22.sent_ref = bf16[16,10,128]{2,1,0:T(8,128)(2,1)S(1)} all-to-all(bf16[16,10,128]{2,1,0:T(8,128)(2,1)S(1)} %masked_normal.1), channel_id=1, replica_groups={{15,14,13,12,11,10,9,8,7,6,5,4,3,2,1,0},{31,30,29,28,27,26,25,24,23,22,..., dimensions={0} | all-to-all | bytes 81920 | tf_op jit(solution)/shard_map/all_to_all | solution.py:698
  43.4 0.0 collective-permute-done.2.refs_1_
  43.4 1.6 %outputs.1 = (f32[16,640]{1,0:T(8,128)}, f32[640,128]{1,0:T(8,128)}) custom-call(f32[288,128]{1,0:T(8,128)S(1)} %get-tuple-element.21.columns_ref, bf16[16,10,128]{2,1,0:T(8,128)(2,1)S(1)} %all_to_all.22.sent_ref, f32[32,384]{1,0:T(8,128)S(1)} %get-tuple-element.31.image_ref, s32[16,320]{1,0:T(8,128)S(1)} %bitcast.15, bf16[384,768]{1,0:T(8,128)(2,1)S(1)} %copy-done, ...), custom_call_target="tpu_custom_call" | custom-call | flops 301989888 | bytes 1550336 | tf_op jit(solution)/shard_map/outputs/pallas_call | solution.py:653
  (17 shorter events, 0.0 us)
Async XLA Ops:
  0.6 11.1 %copy-start.1 = (bf16[128,1536]{1,0:T(8,128)(2,1)S(1)}, bf16[128,1536]{1,0:T(8,128)(2,1)}, u32[]{:S(2)}) copy-start(bf16[128,1536]{1,0:T(8,128)(2,1)} %constant.19.clone.place_ref) | copy-start | bytes 1179652
  0.6 11.1 %copy-start.3 = (f32[288,128]{1,0:T(8,128)S(1)}, f32[288,128]{1,0:T(8,128)}, u32[]{:S(2)}) copy-start(f32[288,128]{1,0:T(8,128)} %constant.20.clone.offset_ref) | copy-start | bytes 442372
  0.7 11.1 %copy-start.4 = (f32[288,128]{1,0:T(8,128)S(1)}, f32[288,128]{1,0:T(8,128)}, u32[]{:S(2)}) copy-start(f32[288,128]{1,0:T(8,128)} %constant.18.clone.repeat_ref) | copy-start | bytes 442372
  0.7 11.1 %copy-start.9 = (f32[2,9,18,2]{2,3,1,0:T(2,128)S(1)}, f32[2,9,18,2]{2,3,1,0:T(2,128)}, u32[]{:S(2)}) copy-start(f32[2,9,18,2]{2,3,1,0:T(2,128)} %param.20) | copy-start | bytes 7780
  0.7 11.1 %copy-start.10 = (f32[2,9,2,18]{3,2,1,0:T(2,128)S(1)}, f32[2,9,2,18]{3,2,1,0:T(2,128)}, u32[]{:S(2)}) copy-start(f32[2,9,2,18]{3,2,1,0:T(2,128)} %param.22) | copy-start | bytes 7780
  0.7 11.1 %copy-start.11 = (f32[2,18]{1,0:T(2,128)S(1)}, f32[2,18]{1,0:T(2,128)}, u32[]{:S(2)}) copy-start(f32[2,18]{1,0:T(2,128)} %bias_in_ref.1) | copy-start | bytes 436
  0.7 11.1 %copy-start.12 = (f32[2,2]{1,0:T(2,128)S(1)}, f32[2,2]{1,0:T(2,128)}, u32[]{:S(2)}) copy-start(f32[2,2]{1,0:T(2,128)} %bias_out_ref.1) | copy-start | bytes 52
  0.7 11.1 %copy-start.13 = (f32[2]{0:T(128)S(1)}, f32[2]{0:T(128)}, u32[]{:S(2)}) copy-start(f32[2]{0:T(128)} %weight_ref.1) | copy-start | bytes 28
  2.7 10.6 %copy-start = (bf16[384,768]{1,0:T(8,128)(2,1)S(1)}, bf16[384,768]{1,0:T(8,128)(2,1)}, u32[]{:S(2)}) copy-start(bf16[384,768]{1,0:T(8,128)(2,1)} %constant.14.clone.table_ref) | copy-start | bytes 1769476
  2.7 10.6 %collective-permute-start = (bf16[64,640]{1,0:T(8,128)(2,1)}, bf16[64,640]{1,0:T(8,128)(2,1)S(1)}, u32[]{:S(2)}, u32[]{:S(2)}) collective-permute-start(bf16[64,640]{1,0:T(8,128)(2,1)} %get-tuple-element.19), channel_id=1, source_target_pairs={{0,16},{2,18},{4,20},{6,22},{8,24},{10,26},{12,28},{14,30},{16,0},... | collective-permute-start | bytes 245768 | tf_op jit(solution)/shard_map/ppermute | solution.py:692
  6.7 8.9 %all-to-all-start = ((bf16[8,90,128]{2,1,0:T(8,128)(2,1)}), bf16[8,90,128]{2,1,0:T(8,128)(2,1)S(1)}, u32[]{:S(2)}, u32[]{:S(2)}) async-start(bf16[8,90,128]{2,1,0:T(8,128)(2,1)} %get-tuple-element.22), calls=%async_computation | async-start | bytes 393216 | tf_op jit(solution)/shard_map/all_to_all | solution.py:698
  11.8 1.6 %copy-start.6 = (s32[2,8,320]{2,1,0:T(8,128)S(1)}, s32[2,8,320]{2,1,0:T(8,128)}, u32[]{:S(2)}) copy-start(s32[2,8,320]{2,1,0:T(8,128)} %param.18) | copy-start | bytes 61444
  11.8 1.6 %copy-start.8 = (bf16[128,128]{1,0:T(8,128)(2,1)S(1)}, bf16[128,128]{1,0:T(8,128)(2,1)}, u32[]{:S(2)}) copy-start(bf16[128,128]{1,0:T(8,128)(2,1)} %constant.17.clone.plus_ref.near_ref) | copy-start | bytes 98308
  13.4 2.3 %copy-start.2 = (bf16[8,16,1,640]{3,1,2,0:T(8,128)(2,1)S(1)}, bf16[8,16,1,640]{3,1,2,0:T(8,128)(2,1)}, u32[]{:S(2)}) copy-start(bf16[8,16,1,640]{3,1,2,0:T(8,128)(2,1)} %param.16) | copy-start | bytes 491524
  13.4 2.3 %copy-start.5 = (bf16[256,256]{1,0:T(8,128)(2,1)S(1)}, bf16[256,256]{1,0:T(8,128)(2,1)}, u32[]{:S(2)}) copy-start(bf16[256,256]{1,0:T(8,128)(2,1)} %constant.15.clone.minus_ref) | copy-start | bytes 393220
  13.4 2.2 %copy-start.14 = (bf16[256,256]{1,0:T(8,128)(2,1)S(1)}, bf16[256,256]{1,0:T(8,128)(2,1)}, u32[]{:S(2)}) copy-start(bf16[256,256]{1,0:T(8,128)(2,1)} %constant.16.clone.plus_ref) | copy-start | bytes 393220
  13.9 1.8 %collective-permute-start.1 = (f32[192,384]{1,0:T(8,128)S(1)}, f32[192,384]{1,0:T(8,128)S(1)}, u32[]{:S(2)}, u32[]{:S(2)}) collective-permute-start(f32[192,384]{1,0:T(8,128)S(1)} %far_images.1), channel_id=1, source_target_pairs={{0,0},{2,2},{4,4},{6,6},{8,8},{10,10},{12,12},{14,14},{16,16},{18,... | collective-permute-start | bytes 884744 | tf_op jit(solution)/shard_map/ppermute | solution.py:695
  17.2 7.8 %copy-start.7 = (bf16[1,16,640]{2,1,0:T(8,128)(2,1)S(1)}, bf16[1,16,640]{2,1,0:T(8,128)(2,1)}, u32[]{:S(2)}) copy-start(bf16[1,16,640]{2,1,0:T(8,128)(2,1)} %param.24) | copy-start | bytes 61444
  33.8 9.6 %collective-permute-start.2 = (bf16[72,640]{1,0:T(8,128)(2,1)S(1)}, bf16[72,640]{1,0:T(8,128)(2,1)S(1)}, u32[]{:S(2)}, u32[]{:S(2)}) collective-permute-start(bf16[72,640]{1,0:T(8,128)(2,1)S(1)} %get-tuple-element.33), channel_id=1, source_target_pairs={{0,16},{2,18},{4,20},{6,22},{8,24},{10,26},{12,28},{14,30},{16,0},... | collective-permute-start | bytes 276488 | tf_op jit(solution)/shard_map/ppermute | solution.py:692

commit v15 on v12

--- a/solution.py
+++ b/solution.py
@@ -676,7 +676,7 @@
     both = ("section", "coil")
     span = depth * coil_devices
     near_order = [depth - 1] + list(range(depth - 1))
-    both_order = list(range(span))[::-1]
+    both_order = [m for m in range(span)[::-1] if m // coil_devices % 2] + [m for m in range(span)[::-1] if not m // coil_devices % 2]
     near = [[group * depth + member for member in near_order] for group in range(volumes)]
     near_both = [[group * span + member for member in both_order] for group in range(volumes)]
     near_places = [[near_order.index(member)] for member in range(depth)]

time: 45.5 us -> 45.5 us (level)
  no operation moved by 1% of the time
where the time goes in v15:
time: 45.5 us; the launch traced here: 45.1 us
  blocking collectives  21.9 us (48%)
  Pallas kernels  10.3 us (23%)
  starting transfers between devices  10.2 us (22%)
  waiting for transfers between devices  1.75 us (4%)
  between operations  0.89 us (2%)
    all_to_all x3, blocking collectives, exchange(): lax.all_to_all(value, axes, 0, 0, tiled=True, axis_index_groups=groups)  21.9 us
    pallas_call x8, Pallas kernels, call(): pl.pallas_call(kernel, name=name, out_shape=tuple(outs), in_specs=[pl.Blo...  10.3 us
    ppermute x2, starting transfers between devices, from_group(): return lax.ppermute(value, 'section', pairs)  5.19 us
    all_to_all x1, starting transfers between devices, exchange(): lax.all_to_all(value, axes, 0, 0, tiled=True, axis_index_groups=groups)  4.99 us
    all_to_all x1, waiting for transfers between devices, exchange(): lax.all_to_all(value, axes, 0, 0, tiled=True, axis_index_groups=groups)  1.74 us
  transfers between devices with their start and end apart: 4, of which 1 were waited for; matrix products, arithmetic and copies ran while one was open for 0% of the time, Pallas kernels for 7%

profile of v15, /device:TPU:0, one launch (start us, length us, event | category | flops | bytes accessed | tf_op | source)
XLA Modules:
  0.0 45.1 jit_solution(11895927665192358645)
XLA Ops:
  0.6 0.0 copy-start.1
  0.6 0.0 copy-start.3
  0.7 0.0 copy-start.4
  0.7 2.0 %pack_maps.1 = (bf16[8,90,128]{2,1,0:T(8,128)(2,1)}, bf16[64,640]{1,0:T(8,128)(2,1)}) custom-call(bf16[128,640]{1,0:T(8,128)(2,1)} %bitcast.10, bf16[128,640]{1,0:T(8,128)(2,1)} %bitcast.20, bf16[16,640]{1,0:T(8,128)(2,1)} %bitcast.16), custom_call_target="tpu_custom_call" | custom-call | flops 1000 | bytes 614400 | tf_op jit(solution)/shard_map/pack_maps/pallas_call | solution.py:651
  2.7 4.0 %collective-permute-start = (bf16[64,640]{1,0:T(8,128)(2,1)}, bf16[64,640]{1,0:T(8,128)(2,1)S(1)}, u32[]{:S(2)}, u32[]{:S(2)}) collective-permute-start(bf16[64,640]{1,0:T(8,128)(2,1)} %get-tuple-element.19), channel_id=1, source_target_pairs={{0,16},{2,18},{4,20},{6,22},{8,24},{10,26},{12,28},{14,30},{16,0},... | collective-permute-start | bytes 245768 | tf_op jit(solution)/shard_map/ppermute | solution.py:690
  6.8 5.0 %all-to-all-start = ((bf16[8,90,128]{2,1,0:T(8,128)(2,1)}), bf16[8,90,128]{2,1,0:T(8,128)(2,1)S(1)}, u32[]{:S(2)}, u32[]{:S(2)}) async-start(bf16[8,90,128]{2,1,0:T(8,128)(2,1)} %get-tuple-element.22), calls=%async_computation | async-start | bytes 393216 | tf_op jit(solution)/shard_map/all_to_all | solution.py:696
  11.8 0.0 copy-done.3
  11.8 0.0 copy-done.4
  11.8 0.0 copy-done.9
  11.8 0.0 copy-done.10
  11.8 0.0 copy-start.6
  11.8 0.0 copy-start.8
  11.8 1.5 %lay_out_taps.1 = (bf16[2,288,128]{2,1,0:T(8,128)(2,1)S(1)}, bf16[2,96,288]{2,1,0:T(8,128)(2,1)S(1)}, bf16[2,96,288]{2,1,0:T(8,128)(2,1)S(1)}, bf16[2,288,128]{2,1,0:T(8,128)(2,1)S(1)}, f32[288,128]{1,0:T(8,128)S(1)}) custom-call(f32[2]{0:T(128)S(1)} %copy-done.13, f32[18,2,18]{2,1,0:T(2,128)S(1)} %bitcast.18, f32[18,2,18]{2,1,0:T(2,128)S(1)} %bitcast.19, ...), custom_call_target="tpu_custom_call" | custom-call | flops 113246208 | bytes 1357032 | tf_op jit(solution)/shard_map/lay_out_taps/pallas_call | solution.py:651
  13.4 0.0 collective-permute-done.kspace_ref
  13.4 0.0 copy-start.2
  13.4 0.0 copy-start.5
  13.4 0.0 copy-start.14
  13.4 0.4 far_images.1
  13.9 0.0 collective-permute-start.1
  13.9 1.7 %all-to-all-done.sent_ref = bf16[8,90,128]{2,1,0:T(8,128)(2,1)S(1)} async-done(((bf16[8,90,128]{2,1,0:T(8,128)(2,1)}), bf16[8,90,128]{2,1,0:T(8,128)(2,1)S(1)}, u32[]{:S(2)}, u32[]{:S(2)}) %all-to-all-start) | async-done | bytes 184352 | tf_op jit(solution)/shard_map/all_to_all | solution.py:696
  15.7 0.0 collective-permute-done.1.refs_0_
  15.7 1.5 %combine_rows.1 = (bf16[16,30,128]{2,1,0:T(8,128)(2,1)S(1)}, bf16[256,384]{1,0:T(8,128)(2,1)S(1)}) custom-call(bf16[8,90,128]{2,1,0:T(8,128)(2,1)S(1)} %all-to-all-done.sent_ref, bf16[128,640]{1,0:T(8,128)(2,1)S(1)} %bitcast.11, s32[16,320]{1,0:T(8,128)S(1)} %bitcast.13, bf16[384,768]{1,0:T(8,128)(2,1)S(1)} %copy-done, bf16[256,256]{1,0:T(8,128)(2,1)S(1)} %copy-done.5, ...), custom_call_target="tpu_custom_call" | custom-call | flops 603979776 | bytes 1867776 | tf_op jit(solution)/shard_map/combine_rows/pallas_call | solution.py:651
  17.2 0.0 copy-start.7
  17.2 7.7 %all_to_all.20.sent_ref = bf16[16,30,128]{2,1,0:T(8,128)(2,1)S(1)} all-to-all(bf16[16,30,128]{2,1,0:T(8,128)(2,1)S(1)} %get-tuple-element.24), channel_id=1, replica_groups={{15,14,11,10,7,6,3,2,13,12,9,8,5,4,1,0},{31,30,27,26,23,22,19,18,29,28,..., dimensions={0} | all-to-all | bytes 245760 | tf_op jit(solution)/shard_map/all_to_all | solution.py:696
  24.9 1.9 %refine_and_back.1 = (bf16[8,24,128]{2,1,0:T(8,128)(2,1)S(1)}, f32[32,384]{1,0:T(8,128)S(1)}) custom-call(bf16[16,30,128]{2,1,0:T(8,128)(2,1)S(1)} %all_to_all.20.sent_ref, bf16[16,640]{1,0:T(8,128)(2,1)S(1)} %bitcast.17, bf16[2,288,128]{2,1,0:T(8,128)(2,1)S(1)} %get-tuple-element.25.first_ref, bf16[2,96,288]{2,1,0:T(8,128)(2,1)S(1)} %get-tuple-element.26.first_t_ref, ...), custom_call_target="tpu_custom_call" | custom-call | flops 198180864 | bytes 905216 | tf_op jit(solution)/shard_map/refine_and_back/pallas_call | solution.py:651
  26.8 6.9 %all_to_all.21.sent_ref = bf16[8,24,128]{2,1,0:T(8,128)(2,1)S(1)} all-to-all(bf16[8,24,128]{2,1,0:T(8,128)(2,1)S(1)} %get-tuple-element.29), channel_id=1, replica_groups={{14,0,2,4,6,8,10,12},{30,16,18,20,22,24,26,28},{15,1,3,5,7,9,11,13},{31..., dimensions={0} | all-to-all | bytes 98304 | tf_op jit(solution)/shard_map/all_to_all | solution.py:696
  33.8 0.1 hand_on.1
  33.9 1.1 %collective-permute-start.2 = (bf16[72,640]{1,0:T(8,128)(2,1)S(1)}, bf16[72,640]{1,0:T(8,128)(2,1)S(1)}, u32[]{:S(2)}, u32[]{:S(2)}) collective-permute-start(bf16[72,640]{1,0:T(8,128)(2,1)S(1)} %get-tuple-element.33), channel_id=1, source_target_pairs={{0,16},{2,18},{4,20},{6,22},{8,24},{10,26},{12,28},{14,30},{16,0},... | collective-permute-start | bytes 276488 | tf_op jit(solution)/shard_map/ppermute | solution.py:690
  35.1 1.2 %masked_normal.1 = bf16[16,10,128]{2,1,0:T(8,128)(2,1)S(1)} custom-call(bf16[8,24,128]{2,1,0:T(8,128)(2,1)S(1)} %all_to_all.21.sent_ref, bf16[256,384]{1,0:T(8,128)(2,1)S(1)} %get-tuple-element.30.maps_ref, s32[16,320]{1,0:T(8,128)S(1)} %bitcast.14, bf16[384,768]{1,0:T(8,128)(2,1)S(1)} %copy-done, bf16[256,256]{1,0:T(8,128)(2,1)S(1)} %copy-done.5, ...), custom_call_target="tpu_custom_call" | custom-call | flops 452984832 | bytes 1159168 | tf_op jit(solution)/shard_map/masked_normal/pallas_call | solution.py:651
  36.2 7.3 %all_to_all.22.sent_ref = bf16[16,10,128]{2,1,0:T(8,128)(2,1)S(1)} all-to-all(bf16[16,10,128]{2,1,0:T(8,128)(2,1)S(1)} %masked_normal.1), channel_id=1, replica_groups={{15,14,11,10,7,6,3,2,13,12,9,8,5,4,1,0},{31,30,27,26,23,22,19,18,29,28,..., dimensions={0} | all-to-all | bytes 81920 | tf_op jit(solution)/shard_map/all_to_all | solution.py:696
  43.5 0.0 collective-permute-done.2.refs_1_
  43.5 1.6 %outputs.1 = (f32[16,640]{1,0:T(8,128)}, f32[640,128]{1,0:T(8,128)}) custom-call(f32[288,128]{1,0:T(8,128)S(1)} %get-tuple-element.21.columns_ref, bf16[16,10,128]{2,1,0:T(8,128)(2,1)S(1)} %all_to_all.22.sent_ref, f32[32,384]{1,0:T(8,128)S(1)} %get-tuple-element.31.image_ref, s32[16,320]{1,0:T(8,128)S(1)} %bitcast.15, bf16[384,768]{1,0:T(8,128)(2,1)S(1)} %copy-done, ...), custom_call_target="tpu_custom_call" | custom-call | flops 301989888 | bytes 1531904 | tf_op jit(solution)/shard_map/outputs/pallas_call | solution.py:651
  (17 shorter events, 0.0 us)
Async XLA Ops:
  0.6 11.1 %copy-start.1 = (bf16[128,1536]{1,0:T(8,128)(2,1)S(1)}, bf16[128,1536]{1,0:T(8,128)(2,1)}, u32[]{:S(2)}) copy-start(bf16[128,1536]{1,0:T(8,128)(2,1)} %constant.19.clone.place_ref) | copy-start | bytes 1179652
  0.6 11.1 %copy-start.3 = (f32[288,128]{1,0:T(8,128)S(1)}, f32[288,128]{1,0:T(8,128)}, u32[]{:S(2)}) copy-start(f32[288,128]{1,0:T(8,128)} %constant.20.clone.offset_ref) | copy-start | bytes 442372
  0.7 11.1 %copy-start.4 = (f32[288,128]{1,0:T(8,128)S(1)}, f32[288,128]{1,0:T(8,128)}, u32[]{:S(2)}) copy-start(f32[288,128]{1,0:T(8,128)} %constant.18.clone.repeat_ref) | copy-start | bytes 442372
  0.7 11.1 %copy-start.9 = (f32[2,9,18,2]{2,3,1,0:T(2,128)S(1)}, f32[2,9,18,2]{2,3,1,0:T(2,128)}, u32[]{:S(2)}) copy-start(f32[2,9,18,2]{2,3,1,0:T(2,128)} %param.20) | copy-start | bytes 7780
  0.7 11.1 %copy-start.10 = (f32[2,9,2,18]{3,2,1,0:T(2,128)S(1)}, f32[2,9,2,18]{3,2,1,0:T(2,128)}, u32[]{:S(2)}) copy-start(f32[2,9,2,18]{3,2,1,0:T(2,128)} %param.22) | copy-start | bytes 7780
  0.7 11.1 %copy-start.11 = (f32[2,18]{1,0:T(2,128)S(1)}, f32[2,18]{1,0:T(2,128)}, u32[]{:S(2)}) copy-start(f32[2,18]{1,0:T(2,128)} %bias_in_ref.1) | copy-start | bytes 436
  0.7 11.1 %copy-start.12 = (f32[2,2]{1,0:T(2,128)S(1)}, f32[2,2]{1,0:T(2,128)}, u32[]{:S(2)}) copy-start(f32[2,2]{1,0:T(2,128)} %bias_out_ref.1) | copy-start | bytes 52
  0.7 11.1 %copy-start.13 = (f32[2]{0:T(128)S(1)}, f32[2]{0:T(128)}, u32[]{:S(2)}) copy-start(f32[2]{0:T(128)} %weight_ref.1) | copy-start | bytes 28
  2.7 10.6 %copy-start = (bf16[384,768]{1,0:T(8,128)(2,1)S(1)}, bf16[384,768]{1,0:T(8,128)(2,1)}, u32[]{:S(2)}) copy-start(bf16[384,768]{1,0:T(8,128)(2,1)} %constant.14.clone.table_ref) | copy-start | bytes 1769476
  2.7 10.6 %collective-permute-start = (bf16[64,640]{1,0:T(8,128)(2,1)}, bf16[64,640]{1,0:T(8,128)(2,1)S(1)}, u32[]{:S(2)}, u32[]{:S(2)}) collective-permute-start(bf16[64,640]{1,0:T(8,128)(2,1)} %get-tuple-element.19), channel_id=1, source_target_pairs={{0,16},{2,18},{4,20},{6,22},{8,24},{10,26},{12,28},{14,30},{16,0},... | collective-permute-start | bytes 245768 | tf_op jit(solution)/shard_map/ppermute | solution.py:690
  6.8 8.9 %all-to-all-start = ((bf16[8,90,128]{2,1,0:T(8,128)(2,1)}), bf16[8,90,128]{2,1,0:T(8,128)(2,1)S(1)}, u32[]{:S(2)}, u32[]{:S(2)}) async-start(bf16[8,90,128]{2,1,0:T(8,128)(2,1)} %get-tuple-element.22), calls=%async_computation | async-start | bytes 393216 | tf_op jit(solution)/shard_map/all_to_all | solution.py:696
  11.8 1.6 %copy-start.6 = (s32[2,8,320]{2,1,0:T(8,128)S(1)}, s32[2,8,320]{2,1,0:T(8,128)}, u32[]{:S(2)}) copy-start(s32[2,8,320]{2,1,0:T(8,128)} %param.18) | copy-start | bytes 61444
  11.8 1.6 %copy-start.8 = (bf16[128,128]{1,0:T(8,128)(2,1)S(1)}, bf16[128,128]{1,0:T(8,128)(2,1)}, u32[]{:S(2)}) copy-start(bf16[128,128]{1,0:T(8,128)(2,1)} %constant.17.clone.plus_ref.near_ref) | copy-start | bytes 98308
  13.4 2.3 %copy-start.2 = (bf16[8,16,1,640]{3,1,2,0:T(8,128)(2,1)S(1)}, bf16[8,16,1,640]{3,1,2,0:T(8,128)(2,1)}, u32[]{:S(2)}) copy-start(bf16[8,16,1,640]{3,1,2,0:T(8,128)(2,1)} %param.16) | copy-start | bytes 491524
  13.4 2.3 %copy-start.5 = (bf16[256,256]{1,0:T(8,128)(2,1)S(1)}, bf16[256,256]{1,0:T(8,128)(2,1)}, u32[]{:S(2)}) copy-start(bf16[256,256]{1,0:T(8,128)(2,1)} %constant.15.clone.minus_ref) | copy-start | bytes 393220
  13.4 2.2 %copy-start.14 = (bf16[256,256]{1,0:T(8,128)(2,1)S(1)}, bf16[256,256]{1,0:T(8,128)(2,1)}, u32[]{:S(2)}) copy-start(bf16[256,256]{1,0:T(8,128)(2,1)} %constant.16.clone.plus_ref) | copy-start | bytes 393220
  13.9 1.8 %collective-permute-start.1 = (f32[192,384]{1,0:T(8,128)S(1)}, f32[192,384]{1,0:T(8,128)S(1)}, u32[]{:S(2)}, u32[]{:S(2)}) collective-permute-start(f32[192,384]{1,0:T(8,128)S(1)} %far_images.1), channel_id=1, source_target_pairs={{0,0},{2,2},{4,4},{6,6},{8,8},{10,10},{12,12},{14,14},{16,16},{18,... | collective-permute-start | bytes 884744 | tf_op jit(solution)/shard_map/ppermute | solution.py:693
  17.2 7.7 %copy-start.7 = (bf16[1,16,640]{2,1,0:T(8,128)(2,1)S(1)}, bf16[1,16,640]{2,1,0:T(8,128)(2,1)}, u32[]{:S(2)}) copy-start(bf16[1,16,640]{2,1,0:T(8,128)(2,1)} %param.24) | copy-start | bytes 61444
  33.9 9.6 %collective-permute-start.2 = (bf16[72,640]{1,0:T(8,128)(2,1)S(1)}, bf16[72,640]{1,0:T(8,128)(2,1)S(1)}, u32[]{:S(2)}, u32[]{:S(2)}) collective-permute-start(bf16[72,640]{1,0:T(8,128)(2,1)S(1)} %get-tuple-element.33), channel_id=1, source_target_pairs={{0,16},{2,18},{4,20},{6,22},{8,24},{10,26},{12,28},{14,30},{16,0},... | collective-permute-start | bytes 276488 | tf_op jit(solution)/shard_map/ppermute | solution.py:690
